TPU v7x, 512 devices: a whole 4x4x16 slice. The times are simulated.
512 devices in a mesh: seq: 32 (over z_hi, x, core), ri: 4 (over z_lo), rj: 4 (over y).
Axes of the slice: x: 4, y: 4, z: 16 (z_hi: 4, z_lo: 4; z = z_hi * 4 + z_lo), core: 2. Of those that a mesh axis runs over, the one named last changes fastest.
Arguments:
- query_proj: bfloat16 [64, 1024, 256], P('seq', 'ri', 'rj'), may hold values from -8 to 8
- key_proj: bfloat16 [64, 1024, 256], P('seq', 'rj', 'ri'), may hold values from -8 to 8
- value_proj: bfloat16 [64, 1024, 256], P('seq', 'rj', 'ri'), may hold values from -6 to 6
- pair_bias: bfloat16 [8, 1024, 1024], P(None, 'ri', 'rj'), may hold values from -6 to 6
- attn_output: bfloat16 [64, 1024, 256], P('seq', 'ri', 'rj'), may hold values from -6 to 6
- output_grad: bfloat16 [64, 1024, 256], P('seq', 'ri', 'rj'), may hold values from -6 to 6
Outputs:
- query_grad: bfloat16 [64, 1024, 256], P('seq', 'ri', 'rj')
- key_grad: bfloat16 [64, 1024, 256], P('seq', 'rj', 'ri')
- value_grad: bfloat16 [64, 1024, 256], P('seq', 'rj', 'ri')
- bias_grad: float32 [8, 1024, 1024], P(None, 'ri', 'rj')
All inputs are finite; a program needn't handle non-finite values.
Results may differ from a plain program's by a relative error of at most 0.014.
Values may be sent and summed in bfloat16 or wider, within the bound.
No kernel may reach another device: no remote copies, remote signals or barrier semaphores. Data moves between devices by JAX's collectives and lax.ppermute only.
A program may use at most 64 MiB of HBM per device.

v0:
```python
import jax
import jax.numpy as jnp
from jax import lax
from jax.sharding import PartitionSpec as P

H = 8
HEAD = 32


def combined_all(part, axis, combine):
    gathered = jax.tree.map(lambda a: lax.all_gather(a, axis), part)

    def take(source):
        return jax.tree.map(lambda a: lax.dynamic_index_in_dim(a, source, 0, False), gathered)

    return lax.fori_loop(
        1, lax.axis_size(axis), lambda source, state: combine(state, take(source)), take(0)
    )


def head_dots(grads, saved):
    product = grads.astype(jnp.float32) * saved.astype(jnp.float32)
    return jnp.sum(product.reshape(product.shape[0], product.shape[1], -1, HEAD), axis=3)


def softmax_stats(logits):
    row_top = jnp.max(logits, axis=2)
    row_total = jnp.sum(jnp.exp(logits - row_top[:, :, None]), axis=2)
    return (row_top, row_total)


def combine_stats(first, second):
    row_top = jnp.maximum(first[0], second[0])
    row_total = first[1] * jnp.exp(first[0] - row_top) + second[1] * jnp.exp(second[0] - row_top)
    return (row_top, row_total)


def body(query_proj, key_proj, value_proj, pair_bias, attn_output, output_grad):
    softmax_scale = HEAD ** (-0.5)
    full_query, full_grad, full_saved = (
        lax.all_gather(query_proj, "rj", axis=2, tiled=True),
        lax.all_gather(output_grad, "rj", axis=2, tiled=True),
        lax.all_gather(attn_output, "rj", axis=2, tiled=True),
    )
    inner_dots = head_dots(full_grad, full_saved)
    full_key, full_value = (
        lax.all_gather(key_proj, "ri", axis=2, tiled=True),
        lax.all_gather(value_proj, "ri", axis=2, tiled=True),
    )
    query_parts = []
    key_parts = []
    value_parts = []
    bias_parts = []
    for head in range(H):
        lanes = slice(head * HEAD, (head + 1) * HEAD)
        head_lanes = slice(head * HEAD, (head + 1) * HEAD)
        raw = jnp.einsum(
            "sic,sjc->sij",
            full_query[:, :, head_lanes],
            full_key[:, :, head_lanes],
            preferred_element_type=jnp.float32,
        )
        logits = raw * softmax_scale + pair_bias[head].astype(jnp.float32)[None]
        row_top, row_total = combined_all(softmax_stats(logits), "rj", combine_stats)
        log_total = row_top + jnp.log(row_total)
        weights = jnp.exp(logits - log_total[:, :, None])
        weights_low = weights.astype(jnp.bfloat16)
        grad_head = full_grad[:, :, lanes]
        value_parts.append(
            jnp.einsum("sij,sic->sjc", weights_low, grad_head, preferred_element_type=jnp.float32)
        )
        grad_weights = jnp.einsum(
            "sic,sjc->sij", grad_head, full_value[:, :, lanes], preferred_element_type=jnp.float32
        )
        grad_logits = weights * (grad_weights - inner_dots[:, :, head][:, :, None])
        bias_part = jnp.sum(grad_logits, axis=0)
        bias_parts.append(bias_part)
        grad_low = grad_logits.astype(jnp.bfloat16)
        query_parts.append(
            jnp.einsum(
                "sij,sjc->sic", grad_low, full_key[:, :, lanes], preferred_element_type=jnp.float32
            )
            * softmax_scale
        )
        key_parts.append(
            jnp.einsum(
                "sij,sic->sjc",
                grad_low,
                full_query[:, :, lanes],
                preferred_element_type=jnp.float32,
            )
            * softmax_scale
        )
    query_grad = lax.psum_scatter(
        jnp.concatenate(query_parts, axis=2).astype(jnp.bfloat16),
        "rj",
        scatter_dimension=2,
        tiled=True,
    )
    key_sum, value_sum = (
        lax.psum_scatter(
            jnp.concatenate(key_parts, axis=2).astype(jnp.bfloat16),
            "ri",
            scatter_dimension=2,
            tiled=True,
        ).astype(jnp.float32),
        lax.psum_scatter(
            jnp.concatenate(value_parts, axis=2).astype(jnp.bfloat16),
            "ri",
            scatter_dimension=2,
            tiled=True,
        ).astype(jnp.float32),
    )
    bias_grad = jnp.stack(bias_parts)
    bias_grad = lax.psum(bias_grad, "seq")
    return (query_grad, key_sum.astype(jnp.bfloat16), value_sum.astype(jnp.bfloat16), bias_grad)


def solution(mesh):
    return jax.shard_map(
        body,
        mesh=mesh,
        in_specs=(
            P("seq", "ri", "rj"),
            P("seq", "rj", "ri"),
            P("seq", "rj", "ri"),
            P(None, "ri", "rj"),
            P("seq", "ri", "rj"),
            P("seq", "ri", "rj"),
        ),
        out_specs=(
            P("seq", "ri", "rj"),
            P("seq", "rj", "ri"),
            P("seq", "rj", "ri"),
            P(None, "ri", "rj"),
        ),
        check_vma=False,
    )
```

profile of v0, /device:TPU:1, one launch (start us, length us, event | category | flops | bytes accessed | tf_op | source)
XLA Modules:
  0.0 647.7 jit_solution(17903185240470392134)
XLA Ops:
  8.1 11.1 %all_gather.117 = bf16[2,256,256]{1,2,0:T(8,128)(2,1)S(1)} all-gather(bf16[2,256,64]{1,2,0:T(8,128)(2,1)} %param.27), channel_id=1, replica_groups=mesh['seq'=32,'ri'=4,'rj'=4] {'rj'}, dimensions={2}, use_global_device_ids=true | all-gather | bytes 327680 | tf_op jit(solution)/shard_map/all_gather | solution.py:42
  19.1 9.6 %all_gather.111 = bf16[2,256,256]{1,2,0:T(8,128)(2,1)S(1)} all-gather(bf16[2,256,64]{1,2,0:T(8,128)(2,1)} %param.22), channel_id=1, replica_groups=mesh['seq'=32,'ri'=4,'rj'=4] {'rj'}, dimensions={2}, use_global_device_ids=true | all-gather | bytes 327680 | tf_op jit(solution)/shard_map/all_gather | solution.py:41
  28.7 12.8 %all_gather.112 = bf16[2,256,256]{1,2,0:T(8,128)(2,1)S(1)} all-gather(bf16[2,256,64]{1,2,0:T(8,128)(2,1)} %param.23), channel_id=1, replica_groups=mesh['seq'=32,'ri'=4,'rj'=4] {'ri'}, dimensions={2}, use_global_device_ids=true | all-gather | bytes 327680 | tf_op jit(solution)/shard_map/all_gather | solution.py:47
  41.5 13.9 %all_gather.118 = bf16[2,256,256]{1,2,0:T(8,128)(2,1)} all-gather(bf16[2,256,64]{1,2,0:T(8,128)(2,1)} %param.24), channel_id=1, replica_groups=mesh['seq'=32,'ri'=4,'rj'=4] {'ri'}, dimensions={2}, use_global_device_ids=true | all-gather | bytes 327680 | tf_op jit(solution)/shard_map/all_gather | solution.py:48
  55.5 10.4 %all_gather.119 = bf16[2,256,256]{1,2,0:T(8,128)(2,1)S(1)} all-gather(bf16[2,256,64]{1,2,0:T(8,128)(2,1)} %param.26), channel_id=1, replica_groups=mesh['seq'=32,'ri'=4,'rj'=4] {'rj'}, dimensions={2}, use_global_device_ids=true | all-gather | bytes 327680 | tf_op jit(solution)/shard_map/all_gather | solution.py:43
  66.9 1.8 copy.71
  68.7 1.8 copy.65
  73.1 8.4 %all-gather.29 = f32[4,2,256]{2,1,0:T(2,128)S(1)} all-gather(f32[1,2,256]{2,1,0:T(2,128)S(1)} %bitcast.242), channel_id=15, replica_groups=mesh['seq'=32,'ri'=4,'rj'=4] {'rj'}, dimensions={0}, use_global_device_ids=true | all-gather | bytes 10240 | tf_op jit(solution)/shard_map/all_gather | solution.py:11
  81.5 8.1 %all-gather.28 = f32[4,2,256]{2,1,0:T(2,128)S(1)} all-gather(f32[1,2,256]{2,1,0:T(2,128)S(1)} %bitcast.234), channel_id=14, replica_groups=mesh['seq'=32,'ri'=4,'rj'=4] {'rj'}, dimensions={0}, use_global_device_ids=true | all-gather | bytes 10240 | tf_op jit(solution)/shard_map/all_gather | solution.py:11
  90.1 8.1 %all-gather.17 = f32[4,2,256]{2,1,0:T(2,128)S(1)} all-gather(f32[1,2,256]{2,1,0:T(2,128)S(1)} %bitcast.243), channel_id=3, replica_groups=mesh['seq'=32,'ri'=4,'rj'=4] {'rj'}, dimensions={0}, use_global_device_ids=true | all-gather | bytes 10240 | tf_op jit(solution)/shard_map/all_gather | solution.py:11
  98.2 8.1 %all-gather.16 = f32[4,2,256]{2,1,0:T(2,128)S(1)} all-gather(f32[1,2,256]{2,1,0:T(2,128)S(1)} %bitcast.235), channel_id=2, replica_groups=mesh['seq'=32,'ri'=4,'rj'=4] {'rj'}, dimensions={0}, use_global_device_ids=true | all-gather | bytes 10240 | tf_op jit(solution)/shard_map/all_gather | solution.py:11
  106.7 8.1 %all-gather.19 = f32[4,2,256]{2,1,0:T(2,128)S(1)} all-gather(f32[1,2,256]{2,1,0:T(2,128)S(1)} %bitcast.244), channel_id=5, replica_groups=mesh['seq'=32,'ri'=4,'rj'=4] {'rj'}, dimensions={0}, use_global_device_ids=true | all-gather | bytes 10240 | tf_op jit(solution)/shard_map/all_gather | solution.py:11
  114.8 8.1 %all-gather.18 = f32[4,2,256]{2,1,0:T(2,128)S(1)} all-gather(f32[1,2,256]{2,1,0:T(2,128)S(1)} %bitcast.236), channel_id=4, replica_groups=mesh['seq'=32,'ri'=4,'rj'=4] {'rj'}, dimensions={0}, use_global_device_ids=true | all-gather | bytes 10240 | tf_op jit(solution)/shard_map/all_gather | solution.py:11
  123.4 8.1 %all-gather.21 = f32[4,2,256]{2,1,0:T(2,128)S(1)} all-gather(f32[1,2,256]{2,1,0:T(2,128)S(1)} %bitcast.245), channel_id=7, replica_groups=mesh['seq'=32,'ri'=4,'rj'=4] {'rj'}, dimensions={0}, use_global_device_ids=true | all-gather | bytes 10240 | tf_op jit(solution)/shard_map/all_gather | solution.py:11
  131.5 8.1 %all-gather.20 = f32[4,2,256]{2,1,0:T(2,128)S(1)} all-gather(f32[1,2,256]{2,1,0:T(2,128)S(1)} %bitcast.237), channel_id=6, replica_groups=mesh['seq'=32,'ri'=4,'rj'=4] {'rj'}, dimensions={0}, use_global_device_ids=true | all-gather | bytes 10240 | tf_op jit(solution)/shard_map/all_gather | solution.py:11
  141.0 8.1 %all-gather.23 = f32[4,2,256]{2,1,0:T(2,128)S(1)} all-gather(f32[1,2,256]{2,1,0:T(2,128)S(1)} %bitcast.246), channel_id=9, replica_groups=mesh['seq'=32,'ri'=4,'rj'=4] {'rj'}, dimensions={0}, use_global_device_ids=true | all-gather | bytes 10240 | tf_op jit(solution)/shard_map/all_gather | solution.py:11
  149.1 8.1 %all-gather.22 = f32[4,2,256]{2,1,0:T(2,128)S(1)} all-gather(f32[1,2,256]{2,1,0:T(2,128)S(1)} %bitcast.238), channel_id=8, replica_groups=mesh['seq'=32,'ri'=4,'rj'=4] {'rj'}, dimensions={0}, use_global_device_ids=true | all-gather | bytes 10240 | tf_op jit(solution)/shard_map/all_gather | solution.py:11
  158.7 8.1 %all-gather.25 = f32[4,2,256]{2,1,0:T(2,128)S(1)} all-gather(f32[1,2,256]{2,1,0:T(2,128)S(1)} %bitcast.247), channel_id=11, replica_groups=mesh['seq'=32,'ri'=4,'rj'=4] {'rj'}, dimensions={0}, use_global_device_ids=true | all-gather | bytes 10240 | tf_op jit(solution)/shard_map/all_gather | solution.py:11
  166.8 8.1 %all-gather.24 = f32[4,2,256]{2,1,0:T(2,128)S(1)} all-gather(f32[1,2,256]{2,1,0:T(2,128)S(1)} %bitcast.239), channel_id=10, replica_groups=mesh['seq'=32,'ri'=4,'rj'=4] {'rj'}, dimensions={0}, use_global_device_ids=true | all-gather | bytes 10240 | tf_op jit(solution)/shard_map/all_gather | solution.py:11
  177.1 8.1 %all-gather.27 = f32[4,2,256]{2,1,0:T(2,128)S(1)} all-gather(f32[1,2,256]{2,1,0:T(2,128)S(1)} %bitcast.248), channel_id=13, replica_groups=mesh['seq'=32,'ri'=4,'rj'=4] {'rj'}, dimensions={0}, use_global_device_ids=true | all-gather | bytes 10240 | tf_op jit(solution)/shard_map/all_gather | solution.py:11
  185.2 8.1 %all-gather.26 = f32[4,2,256]{2,1,0:T(2,128)S(1)} all-gather(f32[1,2,256]{2,1,0:T(2,128)S(1)} %bitcast.240), channel_id=12, replica_groups=mesh['seq'=32,'ri'=4,'rj'=4] {'rj'}, dimensions={0}, use_global_device_ids=true | all-gather | bytes 10240 | tf_op jit(solution)/shard_map/all_gather | solution.py:11
  195.6 8.1 %all-gather.31 = f32[4,2,256]{2,1,0:T(2,128)S(1)} all-gather(f32[1,2,256]{2,1,0:T(2,128)S(1)} %bitcast.249), channel_id=17, replica_groups=mesh['seq'=32,'ri'=4,'rj'=4] {'rj'}, dimensions={0}, use_global_device_ids=true | all-gather | bytes 10240 | tf_op jit(solution)/shard_map/all_gather | solution.py:11
  203.7 8.1 %all-gather.30 = f32[4,2,256]{2,1,0:T(2,128)S(1)} all-gather(f32[1,2,256]{2,1,0:T(2,128)S(1)} %bitcast.241), channel_id=16, replica_groups=mesh['seq'=32,'ri'=4,'rj'=4] {'rj'}, dimensions={0}, use_global_device_ids=true | all-gather | bytes 10240 | tf_op jit(solution)/shard_map/all_gather | solution.py:11
  211.9 1.8 fusion.177
  214.5 1.8 fusion.178
  227.6 1.8 fusion.49
  241.4 1.8 fusion.33
  246.7 1.8 fusion.39
  250.2 1.8 fusion.43
  252.0 1.8 fusion.45
  261.9 375.3 %all-reduce.2.cloned.1.call-done = f32[8,256,256]{1,2,0:T(8,128)} async-done(((f32[8,256,256]{1,2,0:T(8,128)}), f32[8,256,256]{1,2,0:T(8,128)}) %all-reduce.2.cloned.1.call-update) | async-done | bytes 2097168 | tf_op jit(solution)/shard_map/psum | solution.py:115
  637.2 2.9 copy.90
  (153 shorter events, 50.8 us)
Async XLA Ops:
  8.0 58.0 %copy-start.10 = (bf16[8,256,256]{2,1,0:T(8,128)(2,1)S(1)}, bf16[8,256,256]{2,1,0:T(8,128)(2,1)}, u32[]{:S(2)}) copy-start(bf16[8,256,256]{2,1,0:T(8,128)(2,1)} %param.25) | copy-start | bytes 3145732
  8.0 629.2 %all-reduce.2.cloned.1.call-start = ((), (), s32[]{:S(2)}) async-start(), calls=%async_computation.6 | async-start | bytes 4194304 | tf_op jit(solution)/shard_map/psum | solution.py:115
  28.7 111.0 %copy-start.8 = (bf16[2,256,256]{1,2,0:T(8,128)(2,1)}, bf16[2,256,256]{1,2,0:T(8,128)(2,1)S(1)}, u32[]{:S(2)}) copy-start(bf16[2,256,256]{1,2,0:T(8,128)(2,1)S(1)} %all_gather.111) | copy-start | bytes 786436
  41.5 98.2 %copy-start.9 = (bf16[2,256,256]{1,2,0:T(8,128)(2,1)}, bf16[2,256,256]{1,2,0:T(8,128)(2,1)S(1)}, u32[]{:S(2)}) copy-start(bf16[2,256,256]{1,2,0:T(8,128)(2,1)S(1)} %all_gather.112) | copy-start | bytes 786436
  176.2 0.8 copy-start
  194.7 0.8 copy-start.3
  211.9 4.5 copy-start.11
  214.5 4.9 copy-start.1
  217.4 4.1 copy-start.4
  227.5 412.6 %reduce-scatter.4.cloned.1.call-start = ((), (), s32[]{:S(2)}) async-start(), calls=%async_computation.3 | async-start | bytes 327680 | tf_op jit(solution)/shard_map/reduce_scatter | solution.py:94
  227.6 12.2 %copy-start.6 = (bf16[2,256,256]{1,2,0:T(8,128)(2,1)S(1)}, bf16[2,256,256]{1,2,0:T(8,128)(2,1)}, u32[]{:S(2)}) copy-start(bf16[2,256,256]{1,2,0:T(8,128)(2,1)} %get-tuple-element.1231) | copy-start | bytes 786436
  241.3 398.8 %reduce-scatter.6.cloned.1.call-start = ((), (), s32[]{:S(2)}) async-start(), calls=%async_computation.4 | async-start | bytes 327680 | tf_op jit(solution)/shard_map/reduce_scatter | solution.py:101
  241.4 12.3 %copy-start.7 = (bf16[2,256,256]{1,2,0:T(8,128)(2,1)S(1)}, bf16[2,256,256]{1,2,0:T(8,128)(2,1)}, u32[]{:S(2)}) copy-start(bf16[2,256,256]{1,2,0:T(8,128)(2,1)} %get-tuple-element.1231) | copy-start | bytes 786436
  255.3 384.8 %reduce-scatter.8.cloned.1.call-start = ((), (), s32[]{:S(2)}) async-start(), calls=%async_computation.5 | async-start | bytes 327680 | tf_op jit(solution)/shard_map/reduce_scatter | solution.py:107
  255.4 4.1 copy-start.2
  255.4 5.7 copy-start.5
Sparse Core Ops, SparseCore 0:
  227.6 409.5 all-reduce.1
Sparse Core Ops, SparseCore 1:
  241.4 77.2 reduce-scatter.3
  322.2 30.0 reduce-scatter.5
  355.5 28.6 reduce-scatter.7
where the time goes:
time: 649 us; the launch traced here: 648 us
  waiting for transfers between devices  375 us (58%)
  blocking collectives  187 us (29%)
  matrix products  50 us (8%)
  local copies, waits for them, and re-layouts  16.1 us (2%)
  between operations  16 us (2%)
    psum x1, waiting for transfers between devices, body(): bias_grad = lax.psum(bias_grad, 'seq')  375 us
    all_gather x16, blocking collectives, combined_all(): gathered = jax.tree.map(lambda a: lax.all_gather(a, axis), part)  130 us
    all_gather x1, blocking collectives, body(): lax.all_gather(value_proj, 'ri', axis=2, tiled=True)  13.9 us
    dot_general x8, matrix products, body(): jnp.einsum('sij,sic->sjc', grad_low, full_query[:, :, lanes], preferred_e...  13.9 us
    dot_general x8, matrix products, body(): jnp.einsum('sij,sjc->sic', grad_low, full_key[:, :, lanes], preferred_ele...  13.7 us
  transfers between devices with their start and end apart: 4, of which 1 were waited for; matrix products, arithmetic and copies ran while one was open for 6% of the time, Pallas kernels for 0%

commit v1 on v0

v1 whole, which is shorter than its diff:
```python
import jax
import jax.numpy as jnp
from jax import lax
from jax.experimental import pallas as pl
from jax.experimental.pallas import tpu as pltpu
from jax.sharding import Mesh
from jax.sharding import PartitionSpec as P

HEAD = 32
SCALE = HEAD**-0.5
N = 4
ROWS = 256
KEYS = N * ROWS
LANES = 128
CHUNK = 16
BF = jnp.bfloat16
F32 = jnp.float32
NT = (((1,), (1,)), ((), ()))
TN = (((0,), (0,)), ((), ()))


def attention_kernel(
    q_ref, g_ref, o_ref, kv0, kv1, kv2, kv3, bias_own, bias1, bias2, bias3,
    send, keep, dq_ref, d0, d1, d2, d3,
    kvs, bias, stack, raw, low, acc, dkv, sem_in, sem_out,
):
    ri, rj, core = (lax.axis_index(a) for a in ("ri", "rj", "core"))

    loads = []
    for t, src in enumerate((kv0, kv1, kv2, kv3)):
        block = lax.rem(ri + N - t, N)
        dst = kvs.at[:, pl.ds(pl.multiple_of(block * ROWS, ROWS), ROWS), :]
        loads.append(pltpu.make_async_copy(src, dst, sem_in.at[t]))
    for t, src in enumerate((bias_own.at[pl.ds(2 * rj, 2)], bias1, bias2, bias3)):
        block = lax.rem(rj + N - t, N)
        dst = bias.at[:, :, pl.ds(pl.multiple_of(block * ROWS, ROWS), ROWS)]
        loads.append(pltpu.make_async_copy(src, dst, sem_in.at[N + t]))
    for c in loads:
        c.start()

    lane = lax.broadcasted_iota(jnp.int32, (ROWS, LANES), 1) // HEAD
    for s in range(2):
        both = jnp.concatenate([q_ref[s], g_ref[s]], axis=1)
        for part in range(4):
            stack[s, part * ROWS : (part + 1) * ROWS, :] = jnp.where(lane == part, both, 0)
    for c in loads:
        c.wait()

    for s in range(2):

        @pl.loop(0, 4)
        def _(part):
            rows = pl.ds(pl.multiple_of(part * ROWS, ROWS), ROWS)
            raw[s, rows, :] = lax.dot_general(
                stack[s, rows, :], kvs[s], NT, preferred_element_type=F32
            )

    head_of = lax.broadcasted_iota(jnp.int32, (CHUNK, 2 * HEAD), 1) // HEAD
    for h in range(2):

        @pl.loop(0, ROWS // CHUNK)
        def _(i):
            r0 = pl.multiple_of(i * CHUNK, CHUNK)
            at_logits = pl.ds(pl.multiple_of(h * ROWS + r0, CHUNK), CHUNK)
            at_grads = pl.ds(pl.multiple_of((2 + h) * ROWS + r0, CHUNK), CHUNK)
            rows = pl.ds(r0, CHUNK)
            pair = bias[h, rows, :].astype(F32)
            total = None
            for s in range(2):
                logits = raw[s, at_logits, :] * SCALE + pair
                top = jnp.max(logits, axis=1, keepdims=True)
                weights = jnp.exp(logits - top)
                weights = weights * (1.0 / jnp.sum(weights, axis=1, keepdims=True))
                dots = g_ref[s, rows, :].astype(F32) * o_ref[s, rows, :].astype(F32)
                inner = jnp.sum(jnp.where(head_of == h, dots, 0.0), axis=1, keepdims=True)
                grad = weights * (raw[s, at_grads, :] - inner)
                low[s, at_logits, :] = grad.astype(BF)
                low[s, at_grads, :] = weights.astype(BF)
                total = grad if total is None else total + grad
            total = total.astype(BF)
            quarter = i // (64 // CHUNK)
            within = pl.ds(pl.multiple_of(lax.rem(i, 64 // CHUNK) * CHUNK, CHUNK), CHUNK)
            for j in range(N):
                acc[h, quarter * N + j, within, :] = total[:, j * ROWS : (j + 1) * ROWS]

    stores = [
        pltpu.make_async_copy(acc.at[1 - core], send, sem_out.at[N]),
        pltpu.make_async_copy(acc.at[core], keep, sem_out.at[N + 1]),
    ]
    for c in stores:
        c.start()

    for s in range(2):

        @pl.loop(0, N)
        def _(block):
            at = pl.ds(pl.multiple_of(block * ROWS, ROWS), ROWS)
            grads = lax.dot_general(stack[s], low[s, :, at], TN, preferred_element_type=F32)
            grads = grads.T
            grads = jnp.where(lane < 2, grads * SCALE, grads)
            dkv[s, at, :] = grads.astype(BF)

        half = [
            jnp.dot(
                low[s, h * ROWS : (h + 1) * ROWS, :], kvs[s], preferred_element_type=F32
            )
            for h in range(2)
        ]
        dq = jnp.where(lane == 0, half[0], half[1]) * SCALE
        dq_ref[s] = dq[:, : 2 * HEAD].astype(BF)

    for t, dst in enumerate((d0, d1, d2, d3)):
        block = lax.rem(ri + N - t, N)
        src = dkv.at[:, pl.ds(pl.multiple_of(block * ROWS, ROWS), ROWS), :]
        stores.append(pltpu.make_async_copy(src, dst, sem_out.at[t]))
        stores[-1].start()
    for c in stores:
        c.wait()


def attention(q, g, o, kvs, biases):
    seqs = q.shape[0]
    anywhere, vmem = pl.BlockSpec(memory_space=pl.ANY), pl.BlockSpec(memory_space=pltpu.VMEM)
    piece = jax.ShapeDtypeStruct((N * N, 64, ROWS), BF)
    grads = jax.ShapeDtypeStruct((seqs, ROWS, LANES), BF)
    return pl.pallas_call(
        attention_kernel,
        out_shape=(piece, piece, jax.ShapeDtypeStruct(q.shape, BF), *[grads] * N),
        in_specs=[vmem] * 3 + [anywhere] * 8,
        out_specs=(anywhere, anywhere, vmem, *[anywhere] * N),
        scratch_shapes=[
            pltpu.VMEM((seqs, KEYS, LANES), BF),
            pltpu.VMEM((2, ROWS, KEYS), BF),
            pltpu.VMEM((seqs, 4 * ROWS, LANES), BF),
            pltpu.VMEM((seqs, 4 * ROWS, KEYS), F32),
            pltpu.VMEM((seqs, 4 * ROWS, KEYS), BF),
            pltpu.VMEM((2, N * N, 64, ROWS), BF),
            pltpu.VMEM((seqs, KEYS, LANES), BF),
            pltpu.SemaphoreType.DMA((2 * N,)),
            pltpu.SemaphoreType.DMA((N + 2,)),
        ],
        compiler_params=pltpu.CompilerParams(vmem_limit_bytes=40 * 2**20),
        cost_estimate=pl.CostEstimate(
            flops=5 * 2 * 2**25, bytes_accessed=6 * 2**20, transcendentals=2**20
        ),
    )(q, g, o, *kvs, *biases)


def swap(x, axis, pairs):
    return lax.ppermute(x, axis, [(a, b) for a, b in pairs] + [(b, a) for a, b in pairs])


def body(query_proj, key_proj, value_proj, pair_bias, attn_output, output_grad):
    rj, core = lax.axis_index("rj"), lax.axis_index("core")

    kv = jnp.concatenate([key_proj, value_proj], axis=2)
    kvs = [
        lax.ppermute(
            kv,
            ("ri", "rj"),
            [(a * N + b, (b + t) % N * N + a) for a in range(N) for b in range(N)],
        )
        for t in range(N)
    ]
    biases = [pair_bias]
    for t in range(1, N):
        chunk = lax.dynamic_slice_in_dim(pair_bias, 2 * lax.rem(rj + t, N), 2, 0)
        biases.append(lax.ppermute(chunk, "rj", [(a, (a + t) % N) for a in range(N)]))

    send, keep, query_grad, *parts = attention(query_proj, output_grad, attn_output, kvs, biases)

    other = swap(send, "core", [(0, 1)])
    total = (keep.astype(F32) + other.astype(F32)).astype(BF)
    spread = lax.all_to_all(total, ("x", "rj"), 0, 0, tiled=True)
    total = jnp.sum(spread.reshape(N, N, 64, ROWS).astype(F32), axis=0).astype(BF)
    for pairs in ([(0, 1), (2, 3)], [(1, 2), (3, 0)]):
        other = swap(total, "zh", pairs)
        total = (total.astype(F32) + other.astype(F32)).astype(BF)
    mine = lax.all_gather(total, "x", axis=0)
    other = swap(mine, "core", [(0, 1)])
    even = jnp.where(core == 0, mine, other).astype(F32)
    odd = jnp.where(core == 0, other, mine).astype(F32)
    bias_grad = jnp.stack([even, odd], axis=2)
    bias_grad = bias_grad.transpose(1, 2, 0, 3, 4).reshape(2 * N, ROWS, ROWS)

    back = [
        lax.ppermute(
            parts[t],
            ("ri", "rj"),
            [((b + t) % N * N + a, a * N + b) for a in range(N) for b in range(N)],
        )
        for t in range(N)
    ]
    kv_grad = sum(x.astype(F32) for x in back).astype(BF)
    width = key_proj.shape[2]
    return query_grad, kv_grad[:, :, :width], kv_grad[:, :, width:], bias_grad


def solution(mesh):
    split = Mesh(
        mesh.devices.reshape(N, N, 2, N, N), ("zh", "x", "core", "ri", "rj")
    )
    seq = ("zh", "x", "core")
    rows, keys, tile = P(seq, "ri", "rj"), P(seq, "rj", "ri"), P(None, "ri", "rj")
    return jax.shard_map(
        body,
        mesh=split,
        in_specs=(rows, keys, keys, tile, rows, rows),
        out_specs=(rows, keys, keys, tile),
        check_vma=False,
    )
```

time: 649 us -> 148 us (0.23)
  the two profiles are of different devices: /device:TPU:1 before, /device:TPU:163 now
where the time goes in v1:
time: 148 us; the launch traced here: 147 us
  starting transfers between devices  64.2 us (43%)
  blocking collectives  43.7 us (30%)
  waiting for transfers between devices  15.5 us (10%)
  Pallas kernels  13.9 us (9%)
  local copies, waits for them, and re-layouts  8.02 us (5%)
    all_gather x1, blocking collectives, body(): mine = lax.all_gather(total, 'x', axis=0)  28.7 us
    ppermute x4, starting transfers between devices, swap(): lax.ppermute(x, axis, [(a, b) for a, b in pairs] + [(b, a) for a, b in pa...  27.1 us
    ppermute x4, starting transfers between devices, body(): lax.ppermute(kv, ('ri', 'rj'), [(a * N + b, (b + t) % N * N + a) for a in...  15.2 us
    all_to_all x1, blocking collectives, body(): spread = lax.all_to_all(total, ('x', 'rj'), 0, 0, tiled=True)  15 us
    pallas_call x1, Pallas kernels, attention(): pl.pallas_call(attention_kernel, out_shape=(piece, piece, jax.ShapeDtypeS...  13.9 us
    ppermute x4, starting transfers between devices, body(): lax.ppermute(parts[t], ('ri', 'rj'), [((b + t) % N * N + a, a * N + b) fo...  13.6 us
    ppermute x4, waiting for transfers between devices, swap(): lax.ppermute(x, axis, [(a, b) for a, b in pairs] + [(b, a) for a, b in pa...  9.85 us
    ppermute x3, starting transfers between devices, body(): lax.ppermute(chunk, 'rj', [(a, (a + t) % N) for a in range(N)])  8.43 us
  transfers between devices with their start and end apart: 15, of which 3 were waited for; matrix products, arithmetic and copies ran while one was open for 3% of the time, Pallas kernels for 0%

profile of v1, /device:TPU:163, one launch (start us, length us, event | category | flops | bytes accessed | tf_op | source)
XLA Modules:
  0.0 147.0 jit_solution(4658347345213059523)
XLA Ops:
  0.7 1.1 copy.36
  1.7 1.0 copy.37
  2.8 5.9 %collective-permute-start.3 = (bf16[2,256,128]{2,1,0:T(8,128)(2,1)S(1)}, bf16[2,256,128]{2,1,0:T(8,128)(2,1)S(1)}, u32[]{:S(2)}, u32[]{:S(2)}) collective-permute-start(bf16[2,256,128]{2,1,0:T(8,128)(2,1)S(1)} %pad_maximum_fusion), channel_id=1, source_target_pairs={{0,12},{1,0},{2,4},{3,8},{4,13},{5,1},{6,5},{7,9},{8,14},{9,2},{10... | collective-permute-start | bytes 393224 | tf_op jit(solution)/shard_map/ppermute | solution.py:158
  8.7 1.9 %collective-permute-start.2 = (bf16[2,256,128]{2,1,0:T(8,128)(2,1)S(1)}, bf16[2,256,128]{2,1,0:T(8,128)(2,1)S(1)}, u32[]{:S(2)}, u32[]{:S(2)}) collective-permute-start(bf16[2,256,128]{2,1,0:T(8,128)(2,1)S(1)} %pad_maximum_fusion), channel_id=1, source_target_pairs={{0,8},{1,12},{2,0},{3,4},{4,9},{5,13},{6,1},{7,5},{8,10},{9,14},{1... | collective-permute-start | bytes 393224 | tf_op jit(solution)/shard_map/ppermute | solution.py:158
  10.7 1.9 %constant_dynamic-slice_fusion = (bf16[2,256,256]{2,1,0:T(8,128)(2,1)}, bf16[2,256,256]{2,1,0:T(8,128)(2,1)S(1)}, bf16[2,256,256]{2,1,0:T(8,128)(2,1)S(1)}) fusion(bf16[8,256,256]{2,1,0:T(8,128)(2,1)} %bias_own.1, s32[]{:T(128)S(6)} %select_n.23, s32[]{:T(128)S(6)} %select_n.22, s32[]{:T(128)S(6)} %select_n.21), kind=kLoop, calls=%fused_computation.8 | loop fusion | bytes 1572876 | tf_op jit(solution)/shard_map/dynamic_slice | solution.py:167
  12.6 2.9 %collective-permute-start.6 = (bf16[2,256,256]{2,1,0:T(8,128)(2,1)}, bf16[2,256,256]{2,1,0:T(8,128)(2,1)S(1)}, u32[]{:S(2)}, u32[]{:S(2)}) collective-permute-start(bf16[2,256,256]{2,1,0:T(8,128)(2,1)} %get-tuple-element.36), channel_id=1, source_target_pairs={{0,3},{1,0},{2,1},{3,2},{4,7},{5,4},{6,5},{7,6},{8,11},{9,8},{10,9... | collective-permute-start | bytes 786440 | tf_op jit(solution)/shard_map/ppermute | solution.py:168
  15.5 3.6 %collective-permute-start.5 = (bf16[2,256,256]{2,1,0:T(8,128)(2,1)S(1)}, bf16[2,256,256]{2,1,0:T(8,128)(2,1)S(1)}, u32[]{:S(2)}, u32[]{:S(2)}) collective-permute-start(bf16[2,256,256]{2,1,0:T(8,128)(2,1)S(1)} %get-tuple-element.37), channel_id=1, source_target_pairs={{0,2},{1,3},{2,0},{3,1},{4,6},{5,7},{6,4},{7,5},{8,10},{9,11},{10,... | collective-permute-start | bytes 786440 | tf_op jit(solution)/shard_map/ppermute | solution.py:168
  19.1 1.9 %collective-permute-start.4 = (bf16[2,256,256]{2,1,0:T(8,128)(2,1)S(1)}, bf16[2,256,256]{2,1,0:T(8,128)(2,1)S(1)}, u32[]{:S(2)}, u32[]{:S(2)}) collective-permute-start(bf16[2,256,256]{2,1,0:T(8,128)(2,1)S(1)} %get-tuple-element.38), channel_id=1, source_target_pairs={{0,1},{1,2},{2,3},{3,0},{4,5},{5,6},{6,7},{7,4},{8,9},{9,10},{10,1... | collective-permute-start | bytes 786440 | tf_op jit(solution)/shard_map/ppermute | solution.py:168
  21.0 2.9 %collective-permute-start.1 = (bf16[2,256,128]{2,1,0:T(8,128)(2,1)S(1)}, bf16[2,256,128]{2,1,0:T(8,128)(2,1)S(1)}, u32[]{:S(2)}, u32[]{:S(2)}) collective-permute-start(bf16[2,256,128]{2,1,0:T(8,128)(2,1)S(1)} %pad_maximum_fusion), channel_id=1, source_target_pairs={{0,4},{1,8},{2,12},{3,0},{4,5},{5,9},{6,13},{7,1},{8,6},{9,10},{10... | collective-permute-start | bytes 393224 | tf_op jit(solution)/shard_map/ppermute | solution.py:158
  23.9 4.4 %collective-permute-start = (bf16[2,256,128]{2,1,0:T(8,128)(2,1)S(1)}, bf16[2,256,128]{2,1,0:T(8,128)(2,1)S(1)}, u32[]{:S(2)}, u32[]{:S(2)}) collective-permute-start(bf16[2,256,128]{2,1,0:T(8,128)(2,1)S(1)} %pad_maximum_fusion), channel_id=1, source_target_pairs={{0,0},{1,4},{2,8},{3,12},{4,1},{5,5},{6,9},{7,13},{8,2},{9,6},{10,... | collective-permute-start | bytes 393224 | tf_op jit(solution)/shard_map/ppermute | solution.py:158
  28.4 0.1 copy.38.q_ref
  28.5 0.1 copy.40.o_ref
  28.8 5.6 %collective-permute-done.1.kv1 = bf16[2,256,128]{2,1,0:T(8,128)(2,1)S(1)} collective-permute-done((bf16[2,256,128]{2,1,0:T(8,128)(2,1)S(1)}, bf16[2,256,128]{2,1,0:T(8,128)(2,1)S(1)}, u32[]{:S(2)}, u32[]{:S(2)}) %collective-permute-start.1) | collective-permute-done | bytes 131104 | tf_op jit(solution)/shard_map/ppermute | solution.py:158
  34.5 13.9 %shard_map.93 = (bf16[16,64,256]{2,1,0:T(8,128)(2,1)S(1)}, bf16[16,64,256]{2,1,0:T(8,128)(2,1)S(1)}, bf16[2,256,64]{2,1,0:T(8,128)(2,1)S(1)}, bf16[2,256,128]{2,...) custom-call(bf16[2,256,64]{2,1,0:T(8,128)(2,1)S(1)} %copy.38.q_ref, ...), custom_call_target="tpu_custom_call" | custom-call | flops 335544320 | bytes 6291456 | tf_op jit(solution)/shard_map/pallas_call | solution.py:126
  48.3 6.4 %collective-permute-start.11 = (bf16[16,64,256]{2,1,0:T(8,128)(2,1)S(1)}, bf16[16,64,256]{2,1,0:T(8,128)(2,1)S(1)}, u32[]{:S(2)}, u32[]{:S(2)}) collective-permute-start(bf16[16,64,256]{2,1,0:T(8,128)(2,1)S(1)} %get-tuple-element.17), channel_id=1, source_target_pairs={{0,16},{16,0},{1,17},{17,1},{2,18},{18,2},{3,19},{19,3},{4,20},{20... | collective-permute-start | bytes 1572872 | tf_op jit(solution)/shard_map/ppermute | solution.py:150
  54.8 1.5 %collective-permute-done.11 = bf16[16,64,256]{2,1,0:T(8,128)(2,1)S(1)} collective-permute-done((bf16[16,64,256]{2,1,0:T(8,128)(2,1)S(1)}, bf16[16,64,256]{2,1,0:T(8,128)(2,1)S(1)}, u32[]{:S(2)}, u32[]{:S(2)}) %collective-permute-start.11) | collective-permute-done | bytes 524320 | tf_op jit(solution)/shard_map/ppermute | solution.py:150
  56.3 0.1 add_convert_fusion
  56.4 15.0 %all_to_all.5 = bf16[16,64,256]{2,1,0:T(8,128)(2,1)S(1)} all-to-all(bf16[16,64,256]{2,1,0:T(8,128)(2,1)S(1)} %add_convert_fusion), channel_id=1, replica_groups=mesh['zh'=4,'x'=4,'core'=2,'ri'=4,'rj'=4] {'x','rj'}, dimensions={0} | all-to-all | bytes 1048576 | tf_op jit(solution)/shard_map/all_to_all | solution.py:174
  71.5 1.9 %collective-permute-start.12 = (bf16[4,64,256]{2,1,0:T(8,128)(2,1)S(1)}, bf16[4,64,256]{2,1,0:T(8,128)(2,1)S(1)}, u32[]{:S(2)}, u32[]{:S(2)}) collective-permute-start(bf16[4,64,256]{2,1,0:T(8,128)(2,1)S(1)} %reduce_sum.12), channel_id=1, source_target_pairs={{0,128},{256,384},{128,0},{384,256},{1,129},{257,385},{129,1},{385... | collective-permute-start | bytes 393224 | tf_op jit(solution)/shard_map/ppermute | solution.py:150
  73.4 8.3 %collective-permute-done.12 = bf16[4,64,256]{2,1,0:T(8,128)(2,1)S(1)} collective-permute-done((bf16[4,64,256]{2,1,0:T(8,128)(2,1)S(1)}, bf16[4,64,256]{2,1,0:T(8,128)(2,1)S(1)}, u32[]{:S(2)}, u32[]{:S(2)}) %collective-permute-start.12) | collective-permute-done | bytes 131104 | tf_op jit(solution)/shard_map/ppermute | solution.py:150
  81.8 12.7 %collective-permute-start.13 = (bf16[4,64,256]{2,1,0:T(8,128)(2,1)S(1)}, bf16[4,64,256]{2,1,0:T(8,128)(2,1)S(1)}, u32[]{:S(2)}, u32[]{:S(2)}) collective-permute-start(bf16[4,64,256]{2,1,0:T(8,128)(2,1)S(1)} %add_convert_fusion.2), channel_id=1, source_target_pairs={{128,256},{384,0},{256,128},{0,384},{129,257},{385,1},{257,129},{1... | collective-permute-start | bytes 393224 | tf_op jit(solution)/shard_map/ppermute | solution.py:150
  94.5 6.7 %collective-permute-start.7 = (bf16[2,256,128]{2,1,0:T(8,128)(2,1)S(1)}, bf16[2,256,128]{2,1,0:T(8,128)(2,1)S(1)}, u32[]{:S(2)}, u32[]{:S(2)}) collective-permute-start(bf16[2,256,128]{2,1,0:T(8,128)(2,1)S(1)} %get-tuple-element.12), channel_id=1, source_target_pairs={{0,0},{4,1},{8,2},{12,3},{1,4},{5,5},{9,6},{13,7},{2,8},{6,9},{10,... | collective-permute-start | bytes 393224 | tf_op jit(solution)/shard_map/ppermute | solution.py:187
  101.2 1.9 %collective-permute-start.8 = (bf16[2,256,128]{2,1,0:T(8,128)(2,1)S(1)}, bf16[2,256,128]{2,1,0:T(8,128)(2,1)S(1)}, u32[]{:S(2)}, u32[]{:S(2)}) collective-permute-start(bf16[2,256,128]{2,1,0:T(8,128)(2,1)S(1)} %get-tuple-element.13), channel_id=1, source_target_pairs={{4,0},{8,1},{12,2},{0,3},{5,4},{9,5},{13,6},{1,7},{6,8},{10,9},{14... | collective-permute-start | bytes 393224 | tf_op jit(solution)/shard_map/ppermute | solution.py:187
  103.2 2.4 %collective-permute-start.9 = (bf16[2,256,128]{2,1,0:T(8,128)(2,1)S(1)}, bf16[2,256,128]{2,1,0:T(8,128)(2,1)S(1)}, u32[]{:S(2)}, u32[]{:S(2)}) collective-permute-start(bf16[2,256,128]{2,1,0:T(8,128)(2,1)S(1)} %get-tuple-element.14), channel_id=1, source_target_pairs={{8,0},{12,1},{0,2},{4,3},{9,4},{13,5},{1,6},{5,7},{10,8},{14,9},{2... | collective-permute-start | bytes 393224 | tf_op jit(solution)/shard_map/ppermute | solution.py:187
  105.6 2.5 %collective-permute-start.10 = (bf16[2,256,128]{2,1,0:T(8,128)(2,1)S(1)}, bf16[2,256,128]{2,1,0:T(8,128)(2,1)S(1)}, u32[]{:S(2)}, u32[]{:S(2)}) collective-permute-start(bf16[2,256,128]{2,1,0:T(8,128)(2,1)S(1)} %get-tuple-element.15), channel_id=1, source_target_pairs={{12,0},{0,1},{4,2},{8,3},{13,4},{1,5},{5,6},{9,7},{14,8},{2,9},{6,... | collective-permute-start | bytes 393224 | tf_op jit(solution)/shard_map/ppermute | solution.py:187
  108.2 28.7 %all-gather = bf16[16,64,256]{2,1,0:T(8,128)(2,1)S(1)} all-gather(bf16[4,64,256]{2,1,0:T(8,128)(2,1)S(1)} %add_convert_fusion.1), channel_id=2, replica_groups=mesh['zh'=4,'x'=4,'core'=2,'ri'=4,'rj'=4] {'x'}, dimensions={0}, use_global_device_ids=true | all-gather | bytes 655360 | tf_op jit(solution)/shard_map/all_gather | solution.py:179
  136.9 6.0 %collective-permute-start.14 = (bf16[4,4,64,256]{3,2,1,0:T(8,128)(2,1)S(1)}, bf16[4,4,64,256]{3,2,1,0:T(8,128)(2,1)S(1)}, u32[]{:S(2)}, u32[]{:S(2)}) collective-permute-start(bf16[4,4,64,256]{3,2,1,0:T(8,128)(2,1)S(1)} %bitcast.9), channel_id=1, source_target_pairs={{0,16},{16,0},{1,17},{17,1},{2,18},{18,2},{3,19},{19,3},{4,20},{20... | collective-permute-start | bytes 1572872 | tf_op jit(solution)/shard_map/ppermute | solution.py:150
  142.9 0.7 copy.42
  143.9 0.7 copy.44
  144.6 0.7 copy.43
  145.4 0.1 convert_bitcast_fusion
  145.5 1.5 copy.41
  (28 shorter events, 0.7 us)
Async XLA Ops:
  0.6 33.8 %copy-start = (bf16[8,256,256]{2,1,0:T(8,128)(2,1)S(1)}, bf16[8,256,256]{2,1,0:T(8,128)(2,1)}, u32[]{:S(2)}) copy-start(bf16[8,256,256]{2,1,0:T(8,128)(2,1)} %bias_own.1) | copy-start | bytes 3145732
  0.6 27.7 %copy-start.1 = (bf16[2,256,64]{1,2,0:T(8,128)(2,1)S(1)}, bf16[2,256,64]{1,2,0:T(8,128)(2,1)}, u32[]{:S(2)}) copy-start(bf16[2,256,64]{1,2,0:T(8,128)(2,1)} %param.6) | copy-start | bytes 196612
  0.7 27.9 %copy-start.2 = (bf16[2,256,64]{1,2,0:T(8,128)(2,1)S(1)}, bf16[2,256,64]{1,2,0:T(8,128)(2,1)}, u32[]{:S(2)}) copy-start(bf16[2,256,64]{1,2,0:T(8,128)(2,1)} %param.10) | copy-start | bytes 196612
  0.7 28.0 %copy-start.3 = (bf16[2,256,64]{1,2,0:T(8,128)(2,1)S(1)}, bf16[2,256,64]{1,2,0:T(8,128)(2,1)}, u32[]{:S(2)}) copy-start(bf16[2,256,64]{1,2,0:T(8,128)(2,1)} %param.11) | copy-start | bytes 196612
  2.8 18.2 %collective-permute-start.3 = (bf16[2,256,128]{2,1,0:T(8,128)(2,1)S(1)}, bf16[2,256,128]{2,1,0:T(8,128)(2,1)S(1)}, u32[]{:S(2)}, u32[]{:S(2)}) collective-permute-start(bf16[2,256,128]{2,1,0:T(8,128)(2,1)S(1)} %pad_maximum_fusion), channel_id=1, source_target_pairs={{0,12},{1,0},{2,4},{3,8},{4,13},{5,1},{6,5},{7,9},{8,14},{9,2},{10... | collective-permute-start | bytes 393224 | tf_op jit(solution)/shard_map/ppermute | solution.py:158
  8.7 15.2 %collective-permute-start.2 = (bf16[2,256,128]{2,1,0:T(8,128)(2,1)S(1)}, bf16[2,256,128]{2,1,0:T(8,128)(2,1)S(1)}, u32[]{:S(2)}, u32[]{:S(2)}) collective-permute-start(bf16[2,256,128]{2,1,0:T(8,128)(2,1)S(1)} %pad_maximum_fusion), channel_id=1, source_target_pairs={{0,8},{1,12},{2,0},{3,4},{4,9},{5,13},{6,1},{7,5},{8,10},{9,14},{1... | collective-permute-start | bytes 393224 | tf_op jit(solution)/shard_map/ppermute | solution.py:158
  12.6 21.9 %collective-permute-start.6 = (bf16[2,256,256]{2,1,0:T(8,128)(2,1)}, bf16[2,256,256]{2,1,0:T(8,128)(2,1)S(1)}, u32[]{:S(2)}, u32[]{:S(2)}) collective-permute-start(bf16[2,256,256]{2,1,0:T(8,128)(2,1)} %get-tuple-element.36), channel_id=1, source_target_pairs={{0,3},{1,0},{2,1},{3,2},{4,7},{5,4},{6,5},{7,6},{8,11},{9,8},{10,9... | collective-permute-start | bytes 786440 | tf_op jit(solution)/shard_map/ppermute | solution.py:168
  15.5 18.9 %collective-permute-start.5 = (bf16[2,256,256]{2,1,0:T(8,128)(2,1)S(1)}, bf16[2,256,256]{2,1,0:T(8,128)(2,1)S(1)}, u32[]{:S(2)}, u32[]{:S(2)}) collective-permute-start(bf16[2,256,256]{2,1,0:T(8,128)(2,1)S(1)} %get-tuple-element.37), channel_id=1, source_target_pairs={{0,2},{1,3},{2,0},{3,1},{4,6},{5,7},{6,4},{7,5},{8,10},{9,11},{10,... | collective-permute-start | bytes 786440 | tf_op jit(solution)/shard_map/ppermute | solution.py:168
  19.1 15.4 %collective-permute-start.4 = (bf16[2,256,256]{2,1,0:T(8,128)(2,1)S(1)}, bf16[2,256,256]{2,1,0:T(8,128)(2,1)S(1)}, u32[]{:S(2)}, u32[]{:S(2)}) collective-permute-start(bf16[2,256,256]{2,1,0:T(8,128)(2,1)S(1)} %get-tuple-element.38), channel_id=1, source_target_pairs={{0,1},{1,2},{2,3},{3,0},{4,5},{5,6},{6,7},{7,4},{8,9},{9,10},{10,1... | collective-permute-start | bytes 786440 | tf_op jit(solution)/shard_map/ppermute | solution.py:168
  21.0 13.4 %collective-permute-start.1 = (bf16[2,256,128]{2,1,0:T(8,128)(2,1)S(1)}, bf16[2,256,128]{2,1,0:T(8,128)(2,1)S(1)}, u32[]{:S(2)}, u32[]{:S(2)}) collective-permute-start(bf16[2,256,128]{2,1,0:T(8,128)(2,1)S(1)} %pad_maximum_fusion), channel_id=1, source_target_pairs={{0,4},{1,8},{2,12},{3,0},{4,5},{5,9},{6,13},{7,1},{8,6},{9,10},{10... | collective-permute-start | bytes 393224 | tf_op jit(solution)/shard_map/ppermute | solution.py:158
  23.9 10.5 %collective-permute-start = (bf16[2,256,128]{2,1,0:T(8,128)(2,1)S(1)}, bf16[2,256,128]{2,1,0:T(8,128)(2,1)S(1)}, u32[]{:S(2)}, u32[]{:S(2)}) collective-permute-start(bf16[2,256,128]{2,1,0:T(8,128)(2,1)S(1)} %pad_maximum_fusion), channel_id=1, source_target_pairs={{0,0},{1,4},{2,8},{3,12},{4,1},{5,5},{6,9},{7,13},{8,2},{9,6},{10,... | collective-permute-start | bytes 393224 | tf_op jit(solution)/shard_map/ppermute | solution.py:158
  48.3 7.9 %collective-permute-start.11 = (bf16[16,64,256]{2,1,0:T(8,128)(2,1)S(1)}, bf16[16,64,256]{2,1,0:T(8,128)(2,1)S(1)}, u32[]{:S(2)}, u32[]{:S(2)}) collective-permute-start(bf16[16,64,256]{2,1,0:T(8,128)(2,1)S(1)} %get-tuple-element.17), channel_id=1, source_target_pairs={{0,16},{16,0},{1,17},{17,1},{2,18},{18,2},{3,19},{19,3},{4,20},{20... | collective-permute-start | bytes 1572872 | tf_op jit(solution)/shard_map/ppermute | solution.py:150
  71.5 10.3 %collective-permute-start.12 = (bf16[4,64,256]{2,1,0:T(8,128)(2,1)S(1)}, bf16[4,64,256]{2,1,0:T(8,128)(2,1)S(1)}, u32[]{:S(2)}, u32[]{:S(2)}) collective-permute-start(bf16[4,64,256]{2,1,0:T(8,128)(2,1)S(1)} %reduce_sum.12), channel_id=1, source_target_pairs={{0,128},{256,384},{128,0},{384,256},{1,129},{257,385},{129,1},{385... | collective-permute-start | bytes 393224 | tf_op jit(solution)/shard_map/ppermute | solution.py:150
  81.8 26.4 %collective-permute-start.13 = (bf16[4,64,256]{2,1,0:T(8,128)(2,1)S(1)}, bf16[4,64,256]{2,1,0:T(8,128)(2,1)S(1)}, u32[]{:S(2)}, u32[]{:S(2)}) collective-permute-start(bf16[4,64,256]{2,1,0:T(8,128)(2,1)S(1)} %add_convert_fusion.2), channel_id=1, source_target_pairs={{128,256},{384,0},{256,128},{0,384},{129,257},{385,1},{257,129},{1... | collective-permute-start | bytes 393224 | tf_op jit(solution)/shard_map/ppermute | solution.py:150
  94.5 49.1 %collective-permute-start.7 = (bf16[2,256,128]{2,1,0:T(8,128)(2,1)S(1)}, bf16[2,256,128]{2,1,0:T(8,128)(2,1)S(1)}, u32[]{:S(2)}, u32[]{:S(2)}) collective-permute-start(bf16[2,256,128]{2,1,0:T(8,128)(2,1)S(1)} %get-tuple-element.12), channel_id=1, source_target_pairs={{0,0},{4,1},{8,2},{12,3},{1,4},{5,5},{9,6},{13,7},{2,8},{6,9},{10,... | collective-permute-start | bytes 393224 | tf_op jit(solution)/shard_map/ppermute | solution.py:187
  101.2 42.4 %collective-permute-start.8 = (bf16[2,256,128]{2,1,0:T(8,128)(2,1)S(1)}, bf16[2,256,128]{2,1,0:T(8,128)(2,1)S(1)}, u32[]{:S(2)}, u32[]{:S(2)}) collective-permute-start(bf16[2,256,128]{2,1,0:T(8,128)(2,1)S(1)} %get-tuple-element.13), channel_id=1, source_target_pairs={{4,0},{8,1},{12,2},{0,3},{5,4},{9,5},{13,6},{1,7},{6,8},{10,9},{14... | collective-permute-start | bytes 393224 | tf_op jit(solution)/shard_map/ppermute | solution.py:187
  103.2 40.5 %collective-permute-start.9 = (bf16[2,256,128]{2,1,0:T(8,128)(2,1)S(1)}, bf16[2,256,128]{2,1,0:T(8,128)(2,1)S(1)}, u32[]{:S(2)}, u32[]{:S(2)}) collective-permute-start(bf16[2,256,128]{2,1,0:T(8,128)(2,1)S(1)} %get-tuple-element.14), channel_id=1, source_target_pairs={{8,0},{12,1},{0,2},{4,3},{9,4},{13,5},{1,6},{5,7},{10,8},{14,9},{2... | collective-permute-start | bytes 393224 | tf_op jit(solution)/shard_map/ppermute | solution.py:187
  105.6 38.1 %collective-permute-start.10 = (bf16[2,256,128]{2,1,0:T(8,128)(2,1)S(1)}, bf16[2,256,128]{2,1,0:T(8,128)(2,1)S(1)}, u32[]{:S(2)}, u32[]{:S(2)}) collective-permute-start(bf16[2,256,128]{2,1,0:T(8,128)(2,1)S(1)} %get-tuple-element.15), channel_id=1, source_target_pairs={{12,0},{0,1},{4,2},{8,3},{13,4},{1,5},{5,6},{9,7},{14,8},{2,9},{6,... | collective-permute-start | bytes 393224 | tf_op jit(solution)/shard_map/ppermute | solution.py:187
  136.9 8.4 %collective-permute-start.14 = (bf16[4,4,64,256]{3,2,1,0:T(8,128)(2,1)S(1)}, bf16[4,4,64,256]{3,2,1,0:T(8,128)(2,1)S(1)}, u32[]{:S(2)}, u32[]{:S(2)}) collective-permute-start(bf16[4,4,64,256]{3,2,1,0:T(8,128)(2,1)S(1)} %bitcast.9), channel_id=1, source_target_pairs={{0,16},{16,0},{1,17},{17,1},{2,18},{18,2},{3,19},{19,3},{4,20},{20... | collective-permute-start | bytes 1572872 | tf_op jit(solution)/shard_map/ppermute | solution.py:150

commit v2 on v1

v2 whole, which is shorter than its diff:
```python
import functools

import jax
import jax.numpy as jnp
from jax import lax
from jax.experimental import pallas as pl
from jax.experimental.pallas import tpu as pltpu
from jax.sharding import Mesh
from jax.sharding import PartitionSpec as P

HEAD = 32
SCALE = HEAD**-0.5
N = 4
ROWS = 256
KEYS = N * ROWS
LANES = 128
CHUNK = 32
UNROLL = 4
BF = jnp.bfloat16
F32 = jnp.float32
NT = (((1,), (1,)), ((), ()))
NN = (((1,), (0,)), ((), ()))


def attention_kernel(
    q_ref, g_ref, o_ref, kv0, kv1, kv2, kv3, bias,
    send, keep, dq_ref, d0, d1, d2, d3,
    stack, wide, raw, low, inner,
):
    ri, core = lax.axis_index("ri"), lax.axis_index("core")
    kvs = (kv0, kv1, kv2, kv3)
    blocks = [lax.rem(ri + N - t, N) for t in range(N)]
    channel = lax.broadcasted_iota(jnp.int32, (LANES, ROWS), 0) // HEAD

    for s in range(2):
        both = jnp.concatenate([q_ref[s], g_ref[s]], axis=0)
        for part in range(4):
            at = slice(part * ROWS, (part + 1) * ROWS)
            one = jnp.where(channel == part, both, 0)
            wide[s, :, at] = one
            stack[s, at, :] = one.T
        dots = g_ref[s].astype(F32) * o_ref[s].astype(F32)
        for h in range(2):
            sums = jnp.sum(dots[h * HEAD : (h + 1) * HEAD], axis=0, keepdims=True)
            inner[s, h] = jnp.broadcast_to(sums, (LANES, ROWS)).T

    for s in range(2):
        for t in range(N):
            at = slice(t * ROWS, (t + 1) * ROWS)
            raw[s, :, at] = lax.dot_general(stack[s], kvs[t][s], NN, preferred_element_type=F32)

    for out, h in ((send, 1 - core), (keep, core)):

        @pl.loop(0, ROWS // CHUNK, unroll=UNROLL)
        def _(i):
            r0 = pl.multiple_of(i * CHUNK, CHUNK)
            at_logits = pl.ds(pl.multiple_of(h * ROWS + r0, CHUNK), CHUNK)
            at_grads = pl.ds(pl.multiple_of((2 + h) * ROWS + r0, CHUNK), CHUNK)
            rows = pl.ds(r0, CHUNK)
            pair = jnp.concatenate([bias[b, h, rows, :] for b in blocks], axis=1).astype(F32)
            total = None
            for s in range(2):
                logits = raw[s, at_logits, :] * SCALE + pair
                top = jnp.max(logits, axis=1, keepdims=True)
                weights = jnp.exp(logits - top)
                weights = weights * (1.0 / jnp.sum(weights, axis=1, keepdims=True))
                dots = jnp.concatenate([inner[s, h, rows, :]] * (KEYS // LANES), axis=1)
                grad = weights * (raw[s, at_grads, :] - dots)
                low[s, at_logits, :] = grad.astype(BF)
                low[s, at_grads, :] = weights.astype(BF)
                total = grad if total is None else total + grad
            total = total.astype(BF)
            quarter = i // (64 // CHUNK)
            within = pl.ds(pl.multiple_of(lax.rem(i, 64 // CHUNK) * CHUNK, CHUNK), CHUNK)
            for t, b in enumerate(blocks):
                out[quarter * N + b, within, :] = total[:, t * ROWS : (t + 1) * ROWS]

    for s in range(2):
        for t, out in enumerate((d0, d1, d2, d3)):
            at = slice(t * ROWS, (t + 1) * ROWS)
            grads = lax.dot_general(wide[s], low[s, :, at], NN, preferred_element_type=F32)
            out[s] = jnp.where(channel < 2, grads * SCALE, grads).astype(BF)
        grads = None
        for t in range(N):
            at = slice(t * ROWS, (t + 1) * ROWS)
            term = lax.dot_general(
                low[s, : 2 * ROWS, at], kvs[t][s], NT, preferred_element_type=F32
            )
            grads = term if grads is None else grads + term
        for h in range(2):
            mine = grads[h * ROWS : (h + 1) * ROWS].T[h * HEAD : (h + 1) * HEAD]
            dq_ref[s, h * HEAD : (h + 1) * HEAD, :] = (mine * SCALE).astype(BF)


def attention(q, g, o, kvs, bias):
    seqs = q.shape[0]
    vmem = pl.BlockSpec(memory_space=pltpu.VMEM)
    piece = jax.ShapeDtypeStruct((N * N, 64, ROWS), BF)
    grads = jax.ShapeDtypeStruct((seqs, LANES, ROWS), BF)
    return pl.pallas_call(
        attention_kernel,
        out_shape=(piece, piece, jax.ShapeDtypeStruct(q.shape, BF), *[grads] * N),
        in_specs=[vmem] * 8,
        out_specs=(vmem,) * 7,
        scratch_shapes=[
            pltpu.VMEM((seqs, 4 * ROWS, LANES), BF),
            pltpu.VMEM((seqs, LANES, 4 * ROWS), BF),
            pltpu.VMEM((seqs, 4 * ROWS, KEYS), F32),
            pltpu.VMEM((seqs, 4 * ROWS, KEYS), BF),
            pltpu.VMEM((seqs, 2, ROWS, LANES), F32),
        ],
        compiler_params=pltpu.CompilerParams(vmem_limit_bytes=32 * 2**20),
        cost_estimate=pl.CostEstimate(
            flops=5 * 2 * 2**25, bytes_accessed=6 * 2**20, transcendentals=2**20
        ),
    )(q, g, o, *kvs, bias)


def hand_on_kernel(n, *refs):
    for src, dst in zip(refs[-2 * n : -n], refs[-n:]):
        dst[...] = src[...]


def hand_on(parts, after):
    anywhere, vmem = pl.BlockSpec(memory_space=pl.ANY), pl.BlockSpec(memory_space=pltpu.VMEM)
    return pl.pallas_call(
        functools.partial(hand_on_kernel, len(parts)),
        out_shape=[jax.ShapeDtypeStruct(x.shape, x.dtype) for x in parts],
        in_specs=[anywhere] * len(after) + [vmem] * len(parts),
        out_specs=[vmem] * len(parts),
        compiler_params=pltpu.CompilerParams(vmem_limit_bytes=8 * 2**20),
        cost_estimate=pl.CostEstimate(flops=0, bytes_accessed=2**20, transcendentals=0),
    )(*after, *parts)


def place_kernel(first, x_ref, *refs):
    out_ref, wide, sem = refs[-3:]
    core = lax.axis_index("core")
    head = core if first else 1 - core
    copies = []
    for j in range(N):
        for x in range(N):
            wide[j, x * 64 : (x + 1) * 64, :] = x_ref[x, j].astype(F32)
        copies.append(pltpu.make_async_copy(wide.at[j], out_ref.at[2 * j + head], sem.at[j]))
        copies[-1].start()
    for c in copies:
        c.wait()


def place(x, before=None):
    first = before is None
    anywhere, vmem = pl.BlockSpec(memory_space=pl.ANY), pl.BlockSpec(memory_space=pltpu.VMEM)
    return pl.pallas_call(
        lambda *refs: place_kernel(first, *refs),
        out_shape=jax.ShapeDtypeStruct((2 * N, ROWS, ROWS), F32),
        in_specs=[vmem] if first else [vmem, anywhere],
        out_specs=anywhere,
        scratch_shapes=[pltpu.VMEM((N, ROWS, ROWS), F32), pltpu.SemaphoreType.DMA((N,))],
        input_output_aliases={} if first else {1: 0},
        compiler_params=pltpu.CompilerParams(vmem_limit_bytes=8 * 2**20),
        cost_estimate=pl.CostEstimate(flops=2**18, bytes_accessed=3 * 2**19, transcendentals=0),
    )(*([x] if first else [x, before]))


def swap(x, axis, pairs):
    return lax.ppermute(x, axis, [(a, b) for a, b in pairs] + [(b, a) for a, b in pairs])


def add(a, b):
    return (a.astype(F32) + b.astype(F32)).astype(BF)


def body(query_proj, key_proj, value_proj, pair_bias, attn_output, output_grad):
    q, k, v, o, g = (
        jnp.swapaxes(x, 1, 2)
        for x in (query_proj, key_proj, value_proj, attn_output, output_grad)
    )
    grid = [(a, b) for a in range(N) for b in range(N)]

    kv = jnp.concatenate([k, v], axis=1)
    kvs = [
        lax.ppermute(kv, ("ri", "rj"), [(a * N + b, (b + t) % N * N + a) for a, b in grid])
        for t in range(N)
    ]
    bias = lax.all_to_all(pair_bias, "rj", 0, 0, tiled=True).reshape(N, 2, ROWS, ROWS)

    send, keep, dq, *parts = attention(q, g, o, kvs, bias)

    def home(part, t):
        return lax.ppermute(
            part, ("ri", "rj"), [((b + t) % N * N + a, a * N + b) for a, b in grid]
        )

    total = add(keep, swap(send, "core", [(0, 1)]))
    spread = lax.all_to_all(total, ("x", "rj"), 0, 0, tiled=True)
    total = jnp.sum(spread.reshape(N, N, 64, ROWS).astype(F32), axis=0).astype(BF)
    back = []
    for first, pairs in ((0, [(0, 1), (2, 3)]), (2, [(1, 2), (3, 0)])):
        other = swap(total, "zh", pairs)
        near = hand_on(parts[first : first + 2], (total, *back))
        homes = [home(part, first + t) for t, part in enumerate(near)]
        total = add(total, other)
        back += homes
    mine = lax.all_gather(total, "x", axis=0)
    bias_grad = place(swap(mine, "core", [(0, 1)]), place(mine))

    kv_grad = sum(x.astype(F32) for x in back).astype(BF)
    width = k.shape[1]
    grads = (dq, kv_grad[:, :width], kv_grad[:, width:])
    return *(jnp.swapaxes(x, 1, 2) for x in grads), bias_grad


def solution(mesh):
    split = Mesh(mesh.devices.reshape(N, N, 2, N, N), ("zh", "x", "core", "ri", "rj"))
    seq = ("zh", "x", "core")
    rows, keys, tile = P(seq, "ri", "rj"), P(seq, "rj", "ri"), P(None, "ri", "rj")
    return jax.shard_map(
        body,
        mesh=split,
        in_specs=(rows, keys, keys, tile, rows, rows),
        out_specs=(rows, keys, keys, tile),
        check_vma=False,
    )
```

time: 148 us -> 129 us (0.87)
  the two profiles are of different devices: /device:TPU:163 before, /device:TPU:161 now
where the time goes in v2:
time: 129 us
  starting transfers between devices  68.2 us (53%)
  blocking collectives  26.7 us (21%)
  waiting for transfers between devices  23.8 us (18%)
  Pallas kernels  7.86 us (6%)
    ppermute x4, starting transfers between devices, swap(): lax.ppermute(x, axis, [(a, b) for a, b in pairs] + [(b, a) for a, b in pa...  39.1 us
    ppermute x4, waiting for transfers between devices, swap(): lax.ppermute(x, axis, [(a, b) for a, b in pairs] + [(b, a) for a, b in pa...  18.9 us
    all_to_all x1, blocking collectives, body(): spread = lax.all_to_all(total, ('x', 'rj'), 0, 0, tiled=True)  16.3 us
    ppermute x4, starting transfers between devices, body(): lax.ppermute(kv, ('ri', 'rj'), [(a * N + b, (b + t) % N * N + a) for a, b...  15.7 us
    all_gather x1, blocking collectives, body(): mine = lax.all_gather(total, 'x', axis=0)  10.4 us
    ppermute x4, starting transfers between devices, home(): lax.ppermute(part, ('ri', 'rj'), [((b + t) % N * N + a, a * N + b) for a,...  9.09 us
    pallas_call x1, Pallas kernels, attention(): pl.pallas_call(attention_kernel, out_shape=(piece, piece, jax.ShapeDtypeS...  5.79 us
    ppermute x4, waiting for transfers between devices, body(): lax.ppermute(kv, ('ri', 'rj'), [(a * N + b, (b + t) % N * N + a) for a, b...  4.95 us
  transfers between devices with their start and end apart: 13, of which 5 were waited for; matrix products, arithmetic and copies ran while one was open for 1% of the time, Pallas kernels for 1%

profile of v2, /device:TPU:161, one launch (start us, length us, event | category | flops | bytes accessed | tf_op | source)
XLA Modules:
  0.0 128.5 jit_solution(16830319872667398683)
XLA Ops:
  0.7 4.3 %all-to-all-start = ((bf16[8,256,256]{2,1,0:T(8,128)(2,1)}), bf16[8,256,256]{2,1,0:T(8,128)(2,1)S(1)}, u32[]{:S(2)}, u32[]{:S(2)}) async-start(bf16[8,256,256]{2,1,0:T(8,128)(2,1)} %param.9), calls=%async_computation | async-start | bytes 2097152 | tf_op jit(solution)/shard_map/all_to_all | solution.py:185
  5.0 6.1 %collective-permute-start.3 = (bf16[2,128,256]{2,1,0:T(8,128)(2,1)S(1)}, bf16[2,128,256]{2,1,0:T(8,128)(2,1)S(1)}, u32[]{:S(2)}, u32[]{:S(2)}) collective-permute-start(bf16[2,128,256]{2,1,0:T(8,128)(2,1)S(1)} %pad_maximum_fusion), channel_id=1, source_target_pairs={{0,12},{1,0},{2,4},{3,8},{4,13},{5,1},{6,5},{7,9},{8,14},{9,2},{10... | collective-permute-start | bytes 393224 | tf_op jit(solution)/shard_map/ppermute | solution.py:182
  11.1 1.9 %collective-permute-start.2 = (bf16[2,128,256]{2,1,0:T(8,128)(2,1)S(1)}, bf16[2,128,256]{2,1,0:T(8,128)(2,1)S(1)}, u32[]{:S(2)}, u32[]{:S(2)}) collective-permute-start(bf16[2,128,256]{2,1,0:T(8,128)(2,1)S(1)} %pad_maximum_fusion), channel_id=1, source_target_pairs={{0,8},{1,12},{2,0},{3,4},{4,9},{5,13},{6,1},{7,5},{8,10},{9,14},{1... | collective-permute-start | bytes 393224 | tf_op jit(solution)/shard_map/ppermute | solution.py:182
  13.0 2.6 %collective-permute-start.1 = (bf16[2,128,256]{2,1,0:T(8,128)(2,1)S(1)}, bf16[2,128,256]{2,1,0:T(8,128)(2,1)S(1)}, u32[]{:S(2)}, u32[]{:S(2)}) collective-permute-start(bf16[2,128,256]{2,1,0:T(8,128)(2,1)S(1)} %pad_maximum_fusion), channel_id=1, source_target_pairs={{0,4},{1,8},{2,12},{3,0},{4,5},{5,9},{6,13},{7,1},{8,6},{9,10},{10... | collective-permute-start | bytes 393224 | tf_op jit(solution)/shard_map/ppermute | solution.py:182
  15.7 5.1 %collective-permute-start = (bf16[2,128,256]{2,1,0:T(8,128)(2,1)S(1)}, bf16[2,128,256]{2,1,0:T(8,128)(2,1)S(1)}, u32[]{:S(2)}, u32[]{:S(2)}) collective-permute-start(bf16[2,128,256]{2,1,0:T(8,128)(2,1)S(1)} %pad_maximum_fusion), channel_id=1, source_target_pairs={{0,0},{1,4},{2,8},{3,12},{4,1},{5,5},{6,9},{7,13},{8,2},{9,6},{10,... | collective-permute-start | bytes 393224 | tf_op jit(solution)/shard_map/ppermute | solution.py:182
  20.8 1.8 %collective-permute-done.2.kv2 = bf16[2,128,256]{2,1,0:T(8,128)(2,1)S(1)} collective-permute-done((bf16[2,128,256]{2,1,0:T(8,128)(2,1)S(1)}, bf16[2,128,256]{2,1,0:T(8,128)(2,1)S(1)}, u32[]{:S(2)}, u32[]{:S(2)}) %collective-permute-start.2) | collective-permute-done | bytes 131104 | tf_op jit(solution)/shard_map/ppermute | solution.py:182
  22.5 3.2 %collective-permute-done.kv0 = bf16[2,128,256]{2,1,0:T(8,128)(2,1)S(1)} collective-permute-done((bf16[2,128,256]{2,1,0:T(8,128)(2,1)S(1)}, bf16[2,128,256]{2,1,0:T(8,128)(2,1)S(1)}, u32[]{:S(2)}, u32[]{:S(2)}) %collective-permute-start) | collective-permute-done | bytes 131104 | tf_op jit(solution)/shard_map/ppermute | solution.py:182
  25.7 0.0 all-to-all-done
  25.7 5.8 %shard_map.93 = (bf16[16,64,256]{2,1,0:T(8,128)(2,1)S(1)}, bf16[16,64,256]{2,1,0:T(8,128)(2,1)S(1)}, bf16[2,64,256]{2,1,0:T(8,128)(2,1)}, bf16[2,128,256]{2,1,0:...) custom-call(bf16[2,64,256]{2,1,0:T(8,128)(2,1)S(1)} %bitcast.16, ...), custom_call_target="tpu_custom_call" | custom-call | flops 335544320 | bytes 6291456 | tf_op jit(solution)/shard_map/pallas_call | solution.py:100
  31.5 7.1 %collective-permute-start.4 = (bf16[16,64,256]{2,1,0:T(8,128)(2,1)S(1)}, bf16[16,64,256]{2,1,0:T(8,128)(2,1)S(1)}, u32[]{:S(2)}, u32[]{:S(2)}) collective-permute-start(bf16[16,64,256]{2,1,0:T(8,128)(2,1)S(1)} %get-tuple-element.17), channel_id=1, source_target_pairs={{0,16},{16,0},{1,17},{17,1},{2,18},{18,2},{3,19},{19,3},{4,20},{20... | collective-permute-start | bytes 1572872 | tf_op jit(solution)/shard_map/ppermute | solution.py:166
  38.6 1.5 %collective-permute-done.4 = bf16[16,64,256]{2,1,0:T(8,128)(2,1)S(1)} collective-permute-done((bf16[16,64,256]{2,1,0:T(8,128)(2,1)S(1)}, bf16[16,64,256]{2,1,0:T(8,128)(2,1)S(1)}, u32[]{:S(2)}, u32[]{:S(2)}) %collective-permute-start.4) | collective-permute-done | bytes 524320 | tf_op jit(solution)/shard_map/ppermute | solution.py:166
  40.1 0.1 add_convert_fusion
  40.2 16.3 %all_to_all.10 = bf16[16,64,256]{2,1,0:T(8,128)(2,1)S(1)} all-to-all(bf16[16,64,256]{2,1,0:T(8,128)(2,1)S(1)} %add_convert_fusion), channel_id=1, replica_groups=mesh['zh'=4,'x'=4,'core'=2,'ri'=4,'rj'=4] {'x','rj'}, dimensions={0} | all-to-all | bytes 1048576 | tf_op jit(solution)/shard_map/all_to_all | solution.py:195
  56.5 0.1 reduce_sum.12.refs_0_
  56.6 1.9 %collective-permute-start.7 = (bf16[4,64,256]{2,1,0:T(8,128)(2,1)S(1)}, bf16[4,64,256]{2,1,0:T(8,128)(2,1)S(1)}, u32[]{:S(2)}, u32[]{:S(2)}) collective-permute-start(bf16[4,64,256]{2,1,0:T(8,128)(2,1)S(1)} %reduce_sum.12.refs_0_), channel_id=1, source_target_pairs={{0,128},{256,384},{128,0},{384,256},{1,129},{257,385},{129,1},{385... | collective-permute-start | bytes 393224 | tf_op jit(solution)/shard_map/ppermute | solution.py:166
  58.6 3.3 %collective-permute-start.5 = (bf16[2,128,256]{2,1,0:T(8,128)(2,1)S(1)}, bf16[2,128,256]{2,1,0:T(8,128)(2,1)S(1)}, u32[]{:S(2)}, u32[]{:S(2)}) collective-permute-start(bf16[2,128,256]{2,1,0:T(8,128)(2,1)S(1)} %get-tuple-element.20), channel_id=1, source_target_pairs={{0,0},{4,1},{8,2},{12,3},{1,4},{5,5},{9,6},{13,7},{2,8},{6,9},{10,... | collective-permute-start | bytes 393224 | tf_op jit(solution)/shard_map/ppermute | solution.py:190
  61.9 1.9 %collective-permute-start.6 = (bf16[2,128,256]{2,1,0:T(8,128)(2,1)S(1)}, bf16[2,128,256]{2,1,0:T(8,128)(2,1)S(1)}, u32[]{:S(2)}, u32[]{:S(2)}) collective-permute-start(bf16[2,128,256]{2,1,0:T(8,128)(2,1)S(1)} %get-tuple-element.21), channel_id=1, source_target_pairs={{4,0},{8,1},{12,2},{0,3},{5,4},{9,5},{13,6},{1,7},{6,8},{10,9},{14... | collective-permute-start | bytes 393224 | tf_op jit(solution)/shard_map/ppermute | solution.py:190
  63.8 13.0 %collective-permute-done.7 = bf16[4,64,256]{2,1,0:T(8,128)(2,1)S(1)} collective-permute-done((bf16[4,64,256]{2,1,0:T(8,128)(2,1)S(1)}, bf16[4,64,256]{2,1,0:T(8,128)(2,1)S(1)}, u32[]{:S(2)}, u32[]{:S(2)}) %collective-permute-start.7) | collective-permute-done | bytes 131104 | tf_op jit(solution)/shard_map/ppermute | solution.py:166
  76.9 16.9 %collective-permute-start.10 = (bf16[4,64,256]{2,1,0:T(8,128)(2,1)S(1)}, bf16[4,64,256]{2,1,0:T(8,128)(2,1)S(1)}, u32[]{:S(2)}, u32[]{:S(2)}) collective-permute-start(bf16[4,64,256]{2,1,0:T(8,128)(2,1)S(1)} %add_convert_fusion.3.refs_0_), channel_id=1, source_target_pairs={{128,256},{384,0},{256,128},{0,384},{129,257},{385,1},{257,129},{1... | collective-permute-start | bytes 393224 | tf_op jit(solution)/shard_map/ppermute | solution.py:166
  93.8 0.0 collective-permute-done.6.refs_2_
  93.9 1.9 %collective-permute-start.8 = (bf16[2,128,256]{2,1,0:T(8,128)(2,1)S(1)}, bf16[2,128,256]{2,1,0:T(8,128)(2,1)S(1)}, u32[]{:S(2)}, u32[]{:S(2)}) collective-permute-start(bf16[2,128,256]{2,1,0:T(8,128)(2,1)S(1)} %get-tuple-element.24), channel_id=1, source_target_pairs={{8,0},{12,1},{0,2},{4,3},{9,4},{13,5},{1,6},{5,7},{10,8},{14,9},{2... | collective-permute-start | bytes 393224 | tf_op jit(solution)/shard_map/ppermute | solution.py:190
  95.8 1.9 %collective-permute-start.9 = (bf16[2,128,256]{2,1,0:T(8,128)(2,1)S(1)}, bf16[2,128,256]{2,1,0:T(8,128)(2,1)S(1)}, u32[]{:S(2)}, u32[]{:S(2)}) collective-permute-start(bf16[2,128,256]{2,1,0:T(8,128)(2,1)S(1)} %get-tuple-element.25), channel_id=1, source_target_pairs={{12,0},{0,1},{4,2},{8,3},{13,4},{1,5},{5,6},{9,7},{14,8},{2,9},{6,... | collective-permute-start | bytes 393224 | tf_op jit(solution)/shard_map/ppermute | solution.py:190
  97.7 4.3 %collective-permute-done.10 = bf16[4,64,256]{2,1,0:T(8,128)(2,1)S(1)} collective-permute-done((bf16[4,64,256]{2,1,0:T(8,128)(2,1)S(1)}, bf16[4,64,256]{2,1,0:T(8,128)(2,1)S(1)}, u32[]{:S(2)}, u32[]{:S(2)}) %collective-permute-start.10) | collective-permute-done | bytes 131104 | tf_op jit(solution)/shard_map/ppermute | solution.py:166
  102.1 10.4 %all-gather = bf16[16,64,256]{2,1,0:T(8,128)(2,1)S(1)} all-gather(bf16[4,64,256]{2,1,0:T(8,128)(2,1)S(1)} %add_convert_fusion.1), channel_id=2, replica_groups=mesh['zh'=4,'x'=4,'core'=2,'ri'=4,'rj'=4] {'x'}, dimensions={0}, use_global_device_ids=true | all-gather | bytes 655360 | tf_op jit(solution)/shard_map/all_gather | solution.py:204
  112.5 13.3 %collective-permute-start.11 = (bf16[4,4,64,256]{3,2,1,0:T(8,128)(2,1)S(1)}, bf16[4,4,64,256]{3,2,1,0:T(8,128)(2,1)S(1)}, u32[]{:S(2)}, u32[]{:S(2)}) collective-permute-start(bf16[4,4,64,256]{3,2,1,0:T(8,128)(2,1)S(1)} %bitcast.13), channel_id=1, source_target_pairs={{0,16},{16,0},{1,17},{17,1},{2,18},{18,2},{3,19},{19,3},{4,20},{20... | collective-permute-start | bytes 1572872 | tf_op jit(solution)/shard_map/ppermute | solution.py:166
  125.7 1.0 shard_map.96.refs_1_
  126.8 0.0 collective-permute-done.8
  126.8 0.0 collective-permute-done.9
  126.8 0.1 add_convert_fusion.2
  126.9 0.7 slice_bitcast_fusion
  127.5 0.0 collective-permute-done.11.refs_0_
  127.5 1.0 shard_map.97
  (18 shorter events, 0.1 us)
Async XLA Ops:
  0.6 4.4 %copy-start.3 = (bf16[2,256,64]{1,2,0:T(8,128)(2,1)S(1)}, bf16[2,256,64]{1,2,0:T(8,128)(2,1)}, u32[]{:S(2)}) copy-start(bf16[2,256,64]{1,2,0:T(8,128)(2,1)} %param.8) | copy-start | bytes 196612
  0.6 4.4 %copy-start.4 = (bf16[2,256,64]{1,2,0:T(8,128)(2,1)S(1)}, bf16[2,256,64]{1,2,0:T(8,128)(2,1)}, u32[]{:S(2)}) copy-start(bf16[2,256,64]{1,2,0:T(8,128)(2,1)} %param.7) | copy-start | bytes 196612
  0.7 25.1 %copy-start.1 = (bf16[2,256,64]{1,2,0:T(8,128)(2,1)S(1)}, bf16[2,256,64]{1,2,0:T(8,128)(2,1)}, u32[]{:S(2)}) copy-start(bf16[2,256,64]{1,2,0:T(8,128)(2,1)} %param.11) | copy-start | bytes 196612
  0.7 25.1 %copy-start.2 = (bf16[2,256,64]{1,2,0:T(8,128)(2,1)S(1)}, bf16[2,256,64]{1,2,0:T(8,128)(2,1)}, u32[]{:S(2)}) copy-start(bf16[2,256,64]{1,2,0:T(8,128)(2,1)} %param.10) | copy-start | bytes 196612
  0.7 25.0 %copy-start = (bf16[2,256,64]{1,2,0:T(8,128)(2,1)S(1)}, bf16[2,256,64]{1,2,0:T(8,128)(2,1)}, u32[]{:S(2)}) copy-start(bf16[2,256,64]{1,2,0:T(8,128)(2,1)} %param.6) | copy-start | bytes 196612
  0.7 25.0 %all-to-all-start = ((bf16[8,256,256]{2,1,0:T(8,128)(2,1)}), bf16[8,256,256]{2,1,0:T(8,128)(2,1)S(1)}, u32[]{:S(2)}, u32[]{:S(2)}) async-start(bf16[8,256,256]{2,1,0:T(8,128)(2,1)} %param.9), calls=%async_computation | async-start | bytes 2097152 | tf_op jit(solution)/shard_map/all_to_all | solution.py:185
  5.0 15.7 %collective-permute-start.3 = (bf16[2,128,256]{2,1,0:T(8,128)(2,1)S(1)}, bf16[2,128,256]{2,1,0:T(8,128)(2,1)S(1)}, u32[]{:S(2)}, u32[]{:S(2)}) collective-permute-start(bf16[2,128,256]{2,1,0:T(8,128)(2,1)S(1)} %pad_maximum_fusion), channel_id=1, source_target_pairs={{0,12},{1,0},{2,4},{3,8},{4,13},{5,1},{6,5},{7,9},{8,14},{9,2},{10... | collective-permute-start | bytes 393224 | tf_op jit(solution)/shard_map/ppermute | solution.py:182
  11.1 11.4 %collective-permute-start.2 = (bf16[2,128,256]{2,1,0:T(8,128)(2,1)S(1)}, bf16[2,128,256]{2,1,0:T(8,128)(2,1)S(1)}, u32[]{:S(2)}, u32[]{:S(2)}) collective-permute-start(bf16[2,128,256]{2,1,0:T(8,128)(2,1)S(1)} %pad_maximum_fusion), channel_id=1, source_target_pairs={{0,8},{1,12},{2,0},{3,4},{4,9},{5,13},{6,1},{7,5},{8,10},{9,14},{1... | collective-permute-start | bytes 393224 | tf_op jit(solution)/shard_map/ppermute | solution.py:182
  13.0 9.5 %collective-permute-start.1 = (bf16[2,128,256]{2,1,0:T(8,128)(2,1)S(1)}, bf16[2,128,256]{2,1,0:T(8,128)(2,1)S(1)}, u32[]{:S(2)}, u32[]{:S(2)}) collective-permute-start(bf16[2,128,256]{2,1,0:T(8,128)(2,1)S(1)} %pad_maximum_fusion), channel_id=1, source_target_pairs={{0,4},{1,8},{2,12},{3,0},{4,5},{5,9},{6,13},{7,1},{8,6},{9,10},{10... | collective-permute-start | bytes 393224 | tf_op jit(solution)/shard_map/ppermute | solution.py:182
  15.7 10.1 %collective-permute-start = (bf16[2,128,256]{2,1,0:T(8,128)(2,1)S(1)}, bf16[2,128,256]{2,1,0:T(8,128)(2,1)S(1)}, u32[]{:S(2)}, u32[]{:S(2)}) collective-permute-start(bf16[2,128,256]{2,1,0:T(8,128)(2,1)S(1)} %pad_maximum_fusion), channel_id=1, source_target_pairs={{0,0},{1,4},{2,8},{3,12},{4,1},{5,5},{6,9},{7,13},{8,2},{9,6},{10,... | collective-permute-start | bytes 393224 | tf_op jit(solution)/shard_map/ppermute | solution.py:182
  31.5 8.6 %collective-permute-start.4 = (bf16[16,64,256]{2,1,0:T(8,128)(2,1)S(1)}, bf16[16,64,256]{2,1,0:T(8,128)(2,1)S(1)}, u32[]{:S(2)}, u32[]{:S(2)}) collective-permute-start(bf16[16,64,256]{2,1,0:T(8,128)(2,1)S(1)} %get-tuple-element.17), channel_id=1, source_target_pairs={{0,16},{16,0},{1,17},{17,1},{2,18},{18,2},{3,19},{19,3},{4,20},{20... | collective-permute-start | bytes 1572872 | tf_op jit(solution)/shard_map/ppermute | solution.py:166
  56.6 20.2 %collective-permute-start.7 = (bf16[4,64,256]{2,1,0:T(8,128)(2,1)S(1)}, bf16[4,64,256]{2,1,0:T(8,128)(2,1)S(1)}, u32[]{:S(2)}, u32[]{:S(2)}) collective-permute-start(bf16[4,64,256]{2,1,0:T(8,128)(2,1)S(1)} %reduce_sum.12.refs_0_), channel_id=1, source_target_pairs={{0,128},{256,384},{128,0},{384,256},{1,129},{257,385},{129,1},{385... | collective-permute-start | bytes 393224 | tf_op jit(solution)/shard_map/ppermute | solution.py:166
  58.6 35.3 %collective-permute-start.5 = (bf16[2,128,256]{2,1,0:T(8,128)(2,1)S(1)}, bf16[2,128,256]{2,1,0:T(8,128)(2,1)S(1)}, u32[]{:S(2)}, u32[]{:S(2)}) collective-permute-start(bf16[2,128,256]{2,1,0:T(8,128)(2,1)S(1)} %get-tuple-element.20), channel_id=1, source_target_pairs={{0,0},{4,1},{8,2},{12,3},{1,4},{5,5},{9,6},{13,7},{2,8},{6,9},{10,... | collective-permute-start | bytes 393224 | tf_op jit(solution)/shard_map/ppermute | solution.py:190
  61.9 31.9 %collective-permute-start.6 = (bf16[2,128,256]{2,1,0:T(8,128)(2,1)S(1)}, bf16[2,128,256]{2,1,0:T(8,128)(2,1)S(1)}, u32[]{:S(2)}, u32[]{:S(2)}) collective-permute-start(bf16[2,128,256]{2,1,0:T(8,128)(2,1)S(1)} %get-tuple-element.21), channel_id=1, source_target_pairs={{4,0},{8,1},{12,2},{0,3},{5,4},{9,5},{13,6},{1,7},{6,8},{10,9},{14... | collective-permute-start | bytes 393224 | tf_op jit(solution)/shard_map/ppermute | solution.py:190
  76.9 25.2 %collective-permute-start.10 = (bf16[4,64,256]{2,1,0:T(8,128)(2,1)S(1)}, bf16[4,64,256]{2,1,0:T(8,128)(2,1)S(1)}, u32[]{:S(2)}, u32[]{:S(2)}) collective-permute-start(bf16[4,64,256]{2,1,0:T(8,128)(2,1)S(1)} %add_convert_fusion.3.refs_0_), channel_id=1, source_target_pairs={{128,256},{384,0},{256,128},{0,384},{129,257},{385,1},{257,129},{1... | collective-permute-start | bytes 393224 | tf_op jit(solution)/shard_map/ppermute | solution.py:166
  93.9 32.9 %collective-permute-start.8 = (bf16[2,128,256]{2,1,0:T(8,128)(2,1)S(1)}, bf16[2,128,256]{2,1,0:T(8,128)(2,1)S(1)}, u32[]{:S(2)}, u32[]{:S(2)}) collective-permute-start(bf16[2,128,256]{2,1,0:T(8,128)(2,1)S(1)} %get-tuple-element.24), channel_id=1, source_target_pairs={{8,0},{12,1},{0,2},{4,3},{9,4},{13,5},{1,6},{5,7},{10,8},{14,9},{2... | collective-permute-start | bytes 393224 | tf_op jit(solution)/shard_map/ppermute | solution.py:190
  95.8 31.0 %collective-permute-start.9 = (bf16[2,128,256]{2,1,0:T(8,128)(2,1)S(1)}, bf16[2,128,256]{2,1,0:T(8,128)(2,1)S(1)}, u32[]{:S(2)}, u32[]{:S(2)}) collective-permute-start(bf16[2,128,256]{2,1,0:T(8,128)(2,1)S(1)} %get-tuple-element.25), channel_id=1, source_target_pairs={{12,0},{0,1},{4,2},{8,3},{13,4},{1,5},{5,6},{9,7},{14,8},{2,9},{6,... | collective-permute-start | bytes 393224 | tf_op jit(solution)/shard_map/ppermute | solution.py:190
  112.5 15.0 %collective-permute-start.11 = (bf16[4,4,64,256]{3,2,1,0:T(8,128)(2,1)S(1)}, bf16[4,4,64,256]{3,2,1,0:T(8,128)(2,1)S(1)}, u32[]{:S(2)}, u32[]{:S(2)}) collective-permute-start(bf16[4,4,64,256]{3,2,1,0:T(8,128)(2,1)S(1)} %bitcast.13), channel_id=1, source_target_pairs={{0,16},{16,0},{1,17},{17,1},{2,18},{18,2},{3,19},{19,3},{4,20},{20... | collective-permute-start | bytes 1572872 | tf_op jit(solution)/shard_map/ppermute | solution.py:166

commit v3 on v2

--- a/solution.py
+++ b/solution.py
@@ -1,5 +1,3 @@
-import functools
-
 import jax
 import jax.numpy as jnp
 from jax import lax
@@ -116,23 +114,6 @@
     )(q, g, o, *kvs, bias)
 
 
-def hand_on_kernel(n, *refs):
-    for src, dst in zip(refs[-2 * n : -n], refs[-n:]):
-        dst[...] = src[...]
-
-
-def hand_on(parts, after):
-    anywhere, vmem = pl.BlockSpec(memory_space=pl.ANY), pl.BlockSpec(memory_space=pltpu.VMEM)
-    return pl.pallas_call(
-        functools.partial(hand_on_kernel, len(parts)),
-        out_shape=[jax.ShapeDtypeStruct(x.shape, x.dtype) for x in parts],
-        in_specs=[anywhere] * len(after) + [vmem] * len(parts),
-        out_specs=[vmem] * len(parts),
-        compiler_params=pltpu.CompilerParams(vmem_limit_bytes=8 * 2**20),
-        cost_estimate=pl.CostEstimate(flops=0, bytes_accessed=2**20, transcendentals=0),
-    )(*after, *parts)
-
-
 def place_kernel(first, x_ref, *refs):
     out_ref, wide, sem = refs[-3:]
     core = lax.axis_index("core")
@@ -192,15 +173,12 @@
         )
 
     total = add(keep, swap(send, "core", [(0, 1)]))
+    back = [home(part, t) for t, part in enumerate(parts)]
     spread = lax.all_to_all(total, ("x", "rj"), 0, 0, tiled=True)
+    spread, *back = lax.optimization_barrier((spread, *back))
     total = jnp.sum(spread.reshape(N, N, 64, ROWS).astype(F32), axis=0).astype(BF)
-    back = []
-    for first, pairs in ((0, [(0, 1), (2, 3)]), (2, [(1, 2), (3, 0)])):
-        other = swap(total, "zh", pairs)
-        near = hand_on(parts[first : first + 2], (total, *back))
-        homes = [home(part, first + t) for t, part in enumerate(near)]
-        total = add(total, other)
-        back += homes
+    for pairs in ([(0, 1), (2, 3)], [(1, 2), (3, 0)]):
+        total = add(total, swap(total, "zh", pairs))
     mine = lax.all_gather(total, "x", axis=0)
     bias_grad = place(swap(mine, "core", [(0, 1)]), place(mine))
 

time: 129 us -> 143 us (1.11)
  the two profiles are of different devices: /device:TPU:161 before, /device:TPU:17 now
where the time goes in v3:
time: 143 us
  starting transfers between devices  73.1 us (51%)
  waiting for transfers between devices  47.1 us (33%)
  blocking collectives  11.9 us (8%)
  Pallas kernels  7.82 us (5%)
    ppermute x4, starting transfers between devices, swap(): lax.ppermute(x, axis, [(a, b) for a, b in pairs] + [(b, a) for a, b in pa...  37.5 us
    ppermute x4, waiting for transfers between devices, home(): lax.ppermute(part, ('ri', 'rj'), [((b + t) % N * N + a, a * N + b) for a,...  28.1 us
    ppermute x4, starting transfers between devices, body(): lax.ppermute(kv, ('ri', 'rj'), [(a * N + b, (b + t) % N * N + a) for a, b...  14.7 us
    ppermute x4, waiting for transfers between devices, body(): lax.ppermute(kv, ('ri', 'rj'), [(a * N + b, (b + t) % N * N + a) for a, b...  12.7 us
    all_gather x1, blocking collectives, body(): mine = lax.all_gather(total, 'x', axis=0)  11.9 us
    ppermute x4, starting transfers between devices, home(): lax.ppermute(part, ('ri', 'rj'), [((b + t) % N * N + a, a * N + b) for a,...  11.2 us
    ppermute x4, waiting for transfers between devices, swap(): lax.ppermute(x, axis, [(a, b) for a, b in pairs] + [(b, a) for a, b in pa...  6.3 us
    pallas_call x1, Pallas kernels, attention(): pl.pallas_call(attention_kernel, out_shape=(piece, piece, jax.ShapeDtypeS...  5.79 us
  transfers between devices with their start and end apart: 14, of which 7 were waited for; matrix products, arithmetic and copies ran while one was open for 1% of the time, Pallas kernels for 1%

profile of v3, /device:TPU:17, one launch (start us, length us, event | category | flops | bytes accessed | tf_op | source)
XLA Modules:
  0.0 142.7 jit_solution(9260068630418342696)
XLA Ops:
  0.7 4.4 %all-to-all-start = ((bf16[8,256,256]{2,1,0:T(8,128)(2,1)}), bf16[8,256,256]{2,1,0:T(8,128)(2,1)S(1)}, u32[]{:S(2)}, u32[]{:S(2)}) async-start(bf16[8,256,256]{2,1,0:T(8,128)(2,1)} %param.9), calls=%async_computation | async-start | bytes 2097152 | tf_op jit(solution)/shard_map/all_to_all | solution.py:166
  5.1 3.3 %collective-permute-start.3 = (bf16[2,128,256]{2,1,0:T(8,128)(2,1)S(1)}, bf16[2,128,256]{2,1,0:T(8,128)(2,1)S(1)}, u32[]{:S(2)}, u32[]{:S(2)}) collective-permute-start(bf16[2,128,256]{2,1,0:T(8,128)(2,1)S(1)} %pad_maximum_fusion), channel_id=1, source_target_pairs={{0,12},{1,0},{2,4},{3,8},{4,13},{5,1},{6,5},{7,9},{8,14},{9,2},{10... | collective-permute-start | bytes 393224 | tf_op jit(solution)/shard_map/ppermute | solution.py:163
  8.4 4.9 %collective-permute-start.2 = (bf16[2,128,256]{2,1,0:T(8,128)(2,1)S(1)}, bf16[2,128,256]{2,1,0:T(8,128)(2,1)S(1)}, u32[]{:S(2)}, u32[]{:S(2)}) collective-permute-start(bf16[2,128,256]{2,1,0:T(8,128)(2,1)S(1)} %pad_maximum_fusion), channel_id=1, source_target_pairs={{0,8},{1,12},{2,0},{3,4},{4,9},{5,13},{6,1},{7,5},{8,10},{9,14},{1... | collective-permute-start | bytes 393224 | tf_op jit(solution)/shard_map/ppermute | solution.py:163
  13.3 4.4 %collective-permute-start.1 = (bf16[2,128,256]{2,1,0:T(8,128)(2,1)S(1)}, bf16[2,128,256]{2,1,0:T(8,128)(2,1)S(1)}, u32[]{:S(2)}, u32[]{:S(2)}) collective-permute-start(bf16[2,128,256]{2,1,0:T(8,128)(2,1)S(1)} %pad_maximum_fusion), channel_id=1, source_target_pairs={{0,4},{1,8},{2,12},{3,0},{4,5},{5,9},{6,13},{7,1},{8,6},{9,10},{10... | collective-permute-start | bytes 393224 | tf_op jit(solution)/shard_map/ppermute | solution.py:163
  17.7 2.1 %collective-permute-start = (bf16[2,128,256]{2,1,0:T(8,128)(2,1)S(1)}, bf16[2,128,256]{2,1,0:T(8,128)(2,1)S(1)}, u32[]{:S(2)}, u32[]{:S(2)}) collective-permute-start(bf16[2,128,256]{2,1,0:T(8,128)(2,1)S(1)} %pad_maximum_fusion), channel_id=1, source_target_pairs={{0,0},{1,4},{2,8},{3,12},{4,1},{5,5},{6,9},{7,13},{8,2},{9,6},{10,... | collective-permute-start | bytes 393224 | tf_op jit(solution)/shard_map/ppermute | solution.py:163
  19.8 0.0 collective-permute-done.3.kv3
  19.8 0.0 collective-permute-done.2.kv2
  19.8 3.5 %collective-permute-done.1.kv1 = bf16[2,128,256]{2,1,0:T(8,128)(2,1)S(1)} collective-permute-done((bf16[2,128,256]{2,1,0:T(8,128)(2,1)S(1)}, bf16[2,128,256]{2,1,0:T(8,128)(2,1)S(1)}, u32[]{:S(2)}, u32[]{:S(2)}) %collective-permute-start.1) | collective-permute-done | bytes 131104 | tf_op jit(solution)/shard_map/ppermute | solution.py:163
  23.4 9.1 %collective-permute-done.kv0 = bf16[2,128,256]{2,1,0:T(8,128)(2,1)S(1)} collective-permute-done((bf16[2,128,256]{2,1,0:T(8,128)(2,1)S(1)}, bf16[2,128,256]{2,1,0:T(8,128)(2,1)S(1)}, u32[]{:S(2)}, u32[]{:S(2)}) %collective-permute-start) | collective-permute-done | bytes 131104 | tf_op jit(solution)/shard_map/ppermute | solution.py:163
  32.5 5.8 %shard_map.93 = (bf16[16,64,256]{2,1,0:T(8,128)(2,1)S(1)}, bf16[16,64,256]{2,1,0:T(8,128)(2,1)S(1)}, bf16[2,64,256]{2,1,0:T(8,128)(2,1)}, bf16[2,128,256]{2,1,0:...) custom-call(bf16[2,64,256]{2,1,0:T(8,128)(2,1)S(1)} %bitcast.16, ...), custom_call_target="tpu_custom_call" | custom-call | flops 335544320 | bytes 6291456 | tf_op jit(solution)/shard_map/pallas_call | solution.py:98
  38.3 2.4 %collective-permute-start.4 = (bf16[16,64,256]{2,1,0:T(8,128)(2,1)S(1)}, bf16[16,64,256]{2,1,0:T(8,128)(2,1)S(1)}, u32[]{:S(2)}, u32[]{:S(2)}) collective-permute-start(bf16[16,64,256]{2,1,0:T(8,128)(2,1)S(1)} %get-tuple-element.18), channel_id=1, source_target_pairs={{0,16},{16,0},{1,17},{17,1},{2,18},{18,2},{3,19},{19,3},{4,20},{20... | collective-permute-start | bytes 1572872 | tf_op jit(solution)/shard_map/ppermute | solution.py:147
  40.8 1.5 %collective-permute-done.4 = bf16[16,64,256]{2,1,0:T(8,128)(2,1)S(1)} collective-permute-done((bf16[16,64,256]{2,1,0:T(8,128)(2,1)S(1)}, bf16[16,64,256]{2,1,0:T(8,128)(2,1)S(1)}, u32[]{:S(2)}, u32[]{:S(2)}) %collective-permute-start.4) | collective-permute-done | bytes 524320 | tf_op jit(solution)/shard_map/ppermute | solution.py:147
  42.3 0.9 add_convert_fusion
  43.2 5.4 %all-to-all-start.1 = ((bf16[16,64,256]{2,1,0:T(8,128)(2,1)}), bf16[16,64,256]{2,1,0:T(8,128)(2,1)S(1)}, u32[]{:S(2)}, u32[]{:S(2)}) async-start(bf16[16,64,256]{2,1,0:T(8,128)(2,1)} %add_convert_fusion), calls=%async_computation.1 | async-start | bytes 1048576 | tf_op jit(solution)/shard_map/all_to_all | solution.py:177
  48.6 1.9 %collective-permute-start.5 = (bf16[2,128,256]{2,1,0:T(8,128)(2,1)S(1)}, bf16[2,128,256]{2,1,0:T(8,128)(2,1)S(1)}, u32[]{:S(2)}, u32[]{:S(2)}) collective-permute-start(bf16[2,128,256]{2,1,0:T(8,128)(2,1)S(1)} %get-tuple-element.19), channel_id=1, source_target_pairs={{0,0},{4,1},{8,2},{12,3},{1,4},{5,5},{9,6},{13,7},{2,8},{6,9},{10,... | collective-permute-start | bytes 393224 | tf_op jit(solution)/shard_map/ppermute | solution.py:171
  50.5 4.7 %collective-permute-start.6 = (bf16[2,128,256]{2,1,0:T(8,128)(2,1)S(1)}, bf16[2,128,256]{2,1,0:T(8,128)(2,1)S(1)}, u32[]{:S(2)}, u32[]{:S(2)}) collective-permute-start(bf16[2,128,256]{2,1,0:T(8,128)(2,1)S(1)} %get-tuple-element.20), channel_id=1, source_target_pairs={{4,0},{8,1},{12,2},{0,3},{5,4},{9,5},{13,6},{1,7},{6,8},{10,9},{14... | collective-permute-start | bytes 393224 | tf_op jit(solution)/shard_map/ppermute | solution.py:171
  55.3 1.9 %collective-permute-start.7 = (bf16[2,128,256]{2,1,0:T(8,128)(2,1)S(1)}, bf16[2,128,256]{2,1,0:T(8,128)(2,1)S(1)}, u32[]{:S(2)}, u32[]{:S(2)}) collective-permute-start(bf16[2,128,256]{2,1,0:T(8,128)(2,1)S(1)} %get-tuple-element.21), channel_id=1, source_target_pairs={{8,0},{12,1},{0,2},{4,3},{9,4},{13,5},{1,6},{5,7},{10,8},{14,9},{2... | collective-permute-start | bytes 393224 | tf_op jit(solution)/shard_map/ppermute | solution.py:171
  57.2 2.6 %collective-permute-start.8 = (bf16[2,128,256]{2,1,0:T(8,128)(2,1)S(1)}, bf16[2,128,256]{2,1,0:T(8,128)(2,1)S(1)}, u32[]{:S(2)}, u32[]{:S(2)}) collective-permute-start(bf16[2,128,256]{2,1,0:T(8,128)(2,1)S(1)} %get-tuple-element.22), channel_id=1, source_target_pairs={{12,0},{0,1},{4,2},{8,3},{13,4},{1,5},{5,6},{9,7},{14,8},{2,9},{6,... | collective-permute-start | bytes 393224 | tf_op jit(solution)/shard_map/ppermute | solution.py:171
  59.8 11.0 %collective-permute-done.5 = bf16[2,128,256]{2,1,0:T(8,128)(2,1)S(1)} collective-permute-done((bf16[2,128,256]{2,1,0:T(8,128)(2,1)S(1)}, bf16[2,128,256]{2,1,0:T(8,128)(2,1)S(1)}, u32[]{:S(2)}, u32[]{:S(2)}) %collective-permute-start.5) | collective-permute-done | bytes 131104 | tf_op jit(solution)/shard_map/ppermute | solution.py:171
  70.8 17.1 %collective-permute-done.8 = bf16[2,128,256]{2,1,0:T(8,128)(2,1)S(1)} collective-permute-done((bf16[2,128,256]{2,1,0:T(8,128)(2,1)S(1)}, bf16[2,128,256]{2,1,0:T(8,128)(2,1)S(1)}, u32[]{:S(2)}, u32[]{:S(2)}) %collective-permute-start.8) | collective-permute-done | bytes 131104 | tf_op jit(solution)/shard_map/ppermute | solution.py:171
  88.0 0.0 all-to-all-done.1
  88.0 0.1 reduce_sum.12
  88.0 11.6 %collective-permute-start.9 = (bf16[4,64,256]{2,1,0:T(8,128)(2,1)S(1)}, bf16[4,64,256]{2,1,0:T(8,128)(2,1)S(1)}, u32[]{:S(2)}, u32[]{:S(2)}) collective-permute-start(bf16[4,64,256]{2,1,0:T(8,128)(2,1)S(1)} %reduce_sum.12), channel_id=1, source_target_pairs={{0,128},{256,384},{128,0},{384,256},{1,129},{257,385},{129,1},{385... | collective-permute-start | bytes 393224 | tf_op jit(solution)/shard_map/ppermute | solution.py:147
  99.7 2.4 %collective-permute-done.9 = bf16[4,64,256]{2,1,0:T(8,128)(2,1)S(1)} collective-permute-done((bf16[4,64,256]{2,1,0:T(8,128)(2,1)S(1)}, bf16[4,64,256]{2,1,0:T(8,128)(2,1)S(1)}, u32[]{:S(2)}, u32[]{:S(2)}) %collective-permute-start.9) | collective-permute-done | bytes 131104 | tf_op jit(solution)/shard_map/ppermute | solution.py:147
  102.2 17.1 %collective-permute-start.10 = (bf16[4,64,256]{2,1,0:T(8,128)(2,1)S(1)}, bf16[4,64,256]{2,1,0:T(8,128)(2,1)S(1)}, u32[]{:S(2)}, u32[]{:S(2)}) collective-permute-start(bf16[4,64,256]{2,1,0:T(8,128)(2,1)S(1)} %add_convert_fusion.2), channel_id=1, source_target_pairs={{128,256},{384,0},{256,128},{0,384},{129,257},{385,1},{257,129},{1... | collective-permute-start | bytes 393224 | tf_op jit(solution)/shard_map/ppermute | solution.py:147
  119.3 2.3 %collective-permute-done.10 = bf16[4,64,256]{2,1,0:T(8,128)(2,1)S(1)} collective-permute-done((bf16[4,64,256]{2,1,0:T(8,128)(2,1)S(1)}, bf16[4,64,256]{2,1,0:T(8,128)(2,1)S(1)}, u32[]{:S(2)}, u32[]{:S(2)}) %collective-permute-start.10) | collective-permute-done | bytes 131104 | tf_op jit(solution)/shard_map/ppermute | solution.py:147
  121.6 11.9 %all-gather = bf16[16,64,256]{2,1,0:T(8,128)(2,1)S(1)} all-gather(bf16[4,64,256]{2,1,0:T(8,128)(2,1)S(1)} %add_convert_fusion.1), channel_id=2, replica_groups=mesh['zh'=4,'x'=4,'core'=2,'ri'=4,'rj'=4] {'x'}, dimensions={0}, use_global_device_ids=true | all-gather | bytes 655360 | tf_op jit(solution)/shard_map/all_gather | solution.py:182
  133.5 6.3 %collective-permute-start.11 = (bf16[4,4,64,256]{3,2,1,0:T(8,128)(2,1)S(1)}, bf16[4,4,64,256]{3,2,1,0:T(8,128)(2,1)S(1)}, u32[]{:S(2)}, u32[]{:S(2)}) collective-permute-start(bf16[4,4,64,256]{3,2,1,0:T(8,128)(2,1)S(1)} %bitcast.13), channel_id=1, source_target_pairs={{0,16},{16,0},{1,17},{17,1},{2,18},{18,2},{3,19},{19,3},{4,20},{20... | collective-permute-start | bytes 1572872 | tf_op jit(solution)/shard_map/ppermute | solution.py:147
  139.9 0.1 add_convert_fusion.3
  139.9 0.7 slice_bitcast_fusion
  140.6 1.0 shard_map.94.refs_1_
  141.6 1.0 shard_map.95
  (17 shorter events, 0.1 us)
Async XLA Ops:
  0.6 4.4 %copy-start.3 = (bf16[2,256,64]{1,2,0:T(8,128)(2,1)S(1)}, bf16[2,256,64]{1,2,0:T(8,128)(2,1)}, u32[]{:S(2)}) copy-start(bf16[2,256,64]{1,2,0:T(8,128)(2,1)} %param.8) | copy-start | bytes 196612
  0.6 4.4 %copy-start.4 = (bf16[2,256,64]{1,2,0:T(8,128)(2,1)S(1)}, bf16[2,256,64]{1,2,0:T(8,128)(2,1)}, u32[]{:S(2)}) copy-start(bf16[2,256,64]{1,2,0:T(8,128)(2,1)} %param.7) | copy-start | bytes 196612
  0.7 31.9 %copy-start.1 = (bf16[2,256,64]{1,2,0:T(8,128)(2,1)S(1)}, bf16[2,256,64]{1,2,0:T(8,128)(2,1)}, u32[]{:S(2)}) copy-start(bf16[2,256,64]{1,2,0:T(8,128)(2,1)} %param.11) | copy-start | bytes 196612
  0.7 31.9 %copy-start.2 = (bf16[2,256,64]{1,2,0:T(8,128)(2,1)S(1)}, bf16[2,256,64]{1,2,0:T(8,128)(2,1)}, u32[]{:S(2)}) copy-start(bf16[2,256,64]{1,2,0:T(8,128)(2,1)} %param.10) | copy-start | bytes 196612
  0.7 31.8 %copy-start = (bf16[2,256,64]{1,2,0:T(8,128)(2,1)S(1)}, bf16[2,256,64]{1,2,0:T(8,128)(2,1)}, u32[]{:S(2)}) copy-start(bf16[2,256,64]{1,2,0:T(8,128)(2,1)} %param.6) | copy-start | bytes 196612
  0.7 31.8 %all-to-all-start = ((bf16[8,256,256]{2,1,0:T(8,128)(2,1)}), bf16[8,256,256]{2,1,0:T(8,128)(2,1)S(1)}, u32[]{:S(2)}, u32[]{:S(2)}) async-start(bf16[8,256,256]{2,1,0:T(8,128)(2,1)} %param.9), calls=%async_computation | async-start | bytes 2097152 | tf_op jit(solution)/shard_map/all_to_all | solution.py:166
  5.1 14.7 %collective-permute-start.3 = (bf16[2,128,256]{2,1,0:T(8,128)(2,1)S(1)}, bf16[2,128,256]{2,1,0:T(8,128)(2,1)S(1)}, u32[]{:S(2)}, u32[]{:S(2)}) collective-permute-start(bf16[2,128,256]{2,1,0:T(8,128)(2,1)S(1)} %pad_maximum_fusion), channel_id=1, source_target_pairs={{0,12},{1,0},{2,4},{3,8},{4,13},{5,1},{6,5},{7,9},{8,14},{9,2},{10... | collective-permute-start | bytes 393224 | tf_op jit(solution)/shard_map/ppermute | solution.py:163
  8.4 11.5 %collective-permute-start.2 = (bf16[2,128,256]{2,1,0:T(8,128)(2,1)S(1)}, bf16[2,128,256]{2,1,0:T(8,128)(2,1)S(1)}, u32[]{:S(2)}, u32[]{:S(2)}) collective-permute-start(bf16[2,128,256]{2,1,0:T(8,128)(2,1)S(1)} %pad_maximum_fusion), channel_id=1, source_target_pairs={{0,8},{1,12},{2,0},{3,4},{4,9},{5,13},{6,1},{7,5},{8,10},{9,14},{1... | collective-permute-start | bytes 393224 | tf_op jit(solution)/shard_map/ppermute | solution.py:163
  13.3 10.1 %collective-permute-start.1 = (bf16[2,128,256]{2,1,0:T(8,128)(2,1)S(1)}, bf16[2,128,256]{2,1,0:T(8,128)(2,1)S(1)}, u32[]{:S(2)}, u32[]{:S(2)}) collective-permute-start(bf16[2,128,256]{2,1,0:T(8,128)(2,1)S(1)} %pad_maximum_fusion), channel_id=1, source_target_pairs={{0,4},{1,8},{2,12},{3,0},{4,5},{5,9},{6,13},{7,1},{8,6},{9,10},{10... | collective-permute-start | bytes 393224 | tf_op jit(solution)/shard_map/ppermute | solution.py:163
  17.7 14.8 %collective-permute-start = (bf16[2,128,256]{2,1,0:T(8,128)(2,1)S(1)}, bf16[2,128,256]{2,1,0:T(8,128)(2,1)S(1)}, u32[]{:S(2)}, u32[]{:S(2)}) collective-permute-start(bf16[2,128,256]{2,1,0:T(8,128)(2,1)S(1)} %pad_maximum_fusion), channel_id=1, source_target_pairs={{0,0},{1,4},{2,8},{3,12},{4,1},{5,5},{6,9},{7,13},{8,2},{9,6},{10,... | collective-permute-start | bytes 393224 | tf_op jit(solution)/shard_map/ppermute | solution.py:163
  38.3 4.0 %collective-permute-start.4 = (bf16[16,64,256]{2,1,0:T(8,128)(2,1)S(1)}, bf16[16,64,256]{2,1,0:T(8,128)(2,1)S(1)}, u32[]{:S(2)}, u32[]{:S(2)}) collective-permute-start(bf16[16,64,256]{2,1,0:T(8,128)(2,1)S(1)} %get-tuple-element.18), channel_id=1, source_target_pairs={{0,16},{16,0},{1,17},{17,1},{2,18},{18,2},{3,19},{19,3},{4,20},{20... | collective-permute-start | bytes 1572872 | tf_op jit(solution)/shard_map/ppermute | solution.py:147
  43.2 44.7 %all-to-all-start.1 = ((bf16[16,64,256]{2,1,0:T(8,128)(2,1)}), bf16[16,64,256]{2,1,0:T(8,128)(2,1)S(1)}, u32[]{:S(2)}, u32[]{:S(2)}) async-start(bf16[16,64,256]{2,1,0:T(8,128)(2,1)} %add_convert_fusion), calls=%async_computation.1 | async-start | bytes 1048576 | tf_op jit(solution)/shard_map/all_to_all | solution.py:177
  48.6 22.2 %collective-permute-start.5 = (bf16[2,128,256]{2,1,0:T(8,128)(2,1)S(1)}, bf16[2,128,256]{2,1,0:T(8,128)(2,1)S(1)}, u32[]{:S(2)}, u32[]{:S(2)}) collective-permute-start(bf16[2,128,256]{2,1,0:T(8,128)(2,1)S(1)} %get-tuple-element.19), channel_id=1, source_target_pairs={{0,0},{4,1},{8,2},{12,3},{1,4},{5,5},{9,6},{13,7},{2,8},{6,9},{10,... | collective-permute-start | bytes 393224 | tf_op jit(solution)/shard_map/ppermute | solution.py:171
  50.5 20.3 %collective-permute-start.6 = (bf16[2,128,256]{2,1,0:T(8,128)(2,1)S(1)}, bf16[2,128,256]{2,1,0:T(8,128)(2,1)S(1)}, u32[]{:S(2)}, u32[]{:S(2)}) collective-permute-start(bf16[2,128,256]{2,1,0:T(8,128)(2,1)S(1)} %get-tuple-element.20), channel_id=1, source_target_pairs={{4,0},{8,1},{12,2},{0,3},{5,4},{9,5},{13,6},{1,7},{6,8},{10,9},{14... | collective-permute-start | bytes 393224 | tf_op jit(solution)/shard_map/ppermute | solution.py:171
  55.3 15.6 %collective-permute-start.7 = (bf16[2,128,256]{2,1,0:T(8,128)(2,1)S(1)}, bf16[2,128,256]{2,1,0:T(8,128)(2,1)S(1)}, u32[]{:S(2)}, u32[]{:S(2)}) collective-permute-start(bf16[2,128,256]{2,1,0:T(8,128)(2,1)S(1)} %get-tuple-element.21), channel_id=1, source_target_pairs={{8,0},{12,1},{0,2},{4,3},{9,4},{13,5},{1,6},{5,7},{10,8},{14,9},{2... | collective-permute-start | bytes 393224 | tf_op jit(solution)/shard_map/ppermute | solution.py:171
  57.2 30.8 %collective-permute-start.8 = (bf16[2,128,256]{2,1,0:T(8,128)(2,1)S(1)}, bf16[2,128,256]{2,1,0:T(8,128)(2,1)S(1)}, u32[]{:S(2)}, u32[]{:S(2)}) collective-permute-start(bf16[2,128,256]{2,1,0:T(8,128)(2,1)S(1)} %get-tuple-element.22), channel_id=1, source_target_pairs={{12,0},{0,1},{4,2},{8,3},{13,4},{1,5},{5,6},{9,7},{14,8},{2,9},{6,... | collective-permute-start | bytes 393224 | tf_op jit(solution)/shard_map/ppermute | solution.py:171
  88.0 14.1 %collective-permute-start.9 = (bf16[4,64,256]{2,1,0:T(8,128)(2,1)S(1)}, bf16[4,64,256]{2,1,0:T(8,128)(2,1)S(1)}, u32[]{:S(2)}, u32[]{:S(2)}) collective-permute-start(bf16[4,64,256]{2,1,0:T(8,128)(2,1)S(1)} %reduce_sum.12), channel_id=1, source_target_pairs={{0,128},{256,384},{128,0},{384,256},{1,129},{257,385},{129,1},{385... | collective-permute-start | bytes 393224 | tf_op jit(solution)/shard_map/ppermute | solution.py:147
  102.2 19.5 %collective-permute-start.10 = (bf16[4,64,256]{2,1,0:T(8,128)(2,1)S(1)}, bf16[4,64,256]{2,1,0:T(8,128)(2,1)S(1)}, u32[]{:S(2)}, u32[]{:S(2)}) collective-permute-start(bf16[4,64,256]{2,1,0:T(8,128)(2,1)S(1)} %add_convert_fusion.2), channel_id=1, source_target_pairs={{128,256},{384,0},{256,128},{0,384},{129,257},{385,1},{257,129},{1... | collective-permute-start | bytes 393224 | tf_op jit(solution)/shard_map/ppermute | solution.py:147
  133.5 8.1 %collective-permute-start.11 = (bf16[4,4,64,256]{3,2,1,0:T(8,128)(2,1)S(1)}, bf16[4,4,64,256]{3,2,1,0:T(8,128)(2,1)S(1)}, u32[]{:S(2)}, u32[]{:S(2)}) collective-permute-start(bf16[4,4,64,256]{3,2,1,0:T(8,128)(2,1)S(1)} %bitcast.13), channel_id=1, source_target_pairs={{0,16},{16,0},{1,17},{17,1},{2,18},{18,2},{3,19},{19,3},{4,20},{20... | collective-permute-start | bytes 1572872 | tf_op jit(solution)/shard_map/ppermute | solution.py:147

commit v4 on v3

--- a/solution.py
+++ b/solution.py
@@ -22,10 +22,10 @@
 
 def attention_kernel(
     q_ref, g_ref, o_ref, kv0, kv1, kv2, kv3, bias,
-    send, keep, dq_ref, d0, d1, d2, d3,
+    send, keep, dq_ref, dkv_ref,
     stack, wide, raw, low, inner,
 ):
-    ri, core = lax.axis_index("ri"), lax.axis_index("core")
+    ri, rj, core = (lax.axis_index(a) for a in ("ri", "rj", "core"))
     kvs = (kv0, kv1, kv2, kv3)
     blocks = [lax.rem(ri + N - t, N) for t in range(N)]
     channel = lax.broadcasted_iota(jnp.int32, (LANES, ROWS), 0) // HEAD
@@ -74,10 +74,11 @@
                 out[quarter * N + b, within, :] = total[:, t * ROWS : (t + 1) * ROWS]
 
     for s in range(2):
-        for t, out in enumerate((d0, d1, d2, d3)):
+        for t, b in enumerate(blocks):
             at = slice(t * ROWS, (t + 1) * ROWS)
             grads = lax.dot_general(wide[s], low[s, :, at], NN, preferred_element_type=F32)
-            out[s] = jnp.where(channel < 2, grads * SCALE, grads).astype(BF)
+            grads = jnp.where(channel < 2, grads * SCALE, grads)
+            dkv_ref[lax.rem(b + N - rj, N), s] = grads.astype(BF)
         grads = None
         for t in range(N):
             at = slice(t * ROWS, (t + 1) * ROWS)
@@ -94,12 +95,12 @@
     seqs = q.shape[0]
     vmem = pl.BlockSpec(memory_space=pltpu.VMEM)
     piece = jax.ShapeDtypeStruct((N * N, 64, ROWS), BF)
-    grads = jax.ShapeDtypeStruct((seqs, LANES, ROWS), BF)
+    grads = jax.ShapeDtypeStruct((N, seqs, LANES, ROWS), BF)
     return pl.pallas_call(
         attention_kernel,
-        out_shape=(piece, piece, jax.ShapeDtypeStruct(q.shape, BF), *[grads] * N),
+        out_shape=(piece, piece, jax.ShapeDtypeStruct(q.shape, BF), grads),
         in_specs=[vmem] * 8,
-        out_specs=(vmem,) * 7,
+        out_specs=(vmem,) * 4,
         scratch_shapes=[
             pltpu.VMEM((seqs, 4 * ROWS, LANES), BF),
             pltpu.VMEM((seqs, LANES, 4 * ROWS), BF),
@@ -112,6 +113,34 @@
             flops=5 * 2 * 2**25, bytes_accessed=6 * 2**20, transcendentals=2**20
         ),
     )(q, g, o, *kvs, bias)
+
+
+def split_kernel(after, x_ref, *outs):
+    for t, out in enumerate(outs):
+        out[...] = x_ref[t]
+
+
+def choose_kernel(after, *refs):
+    ri, rj = lax.axis_index("ri"), lax.axis_index("rj")
+    for t, out in enumerate(refs[N:]):
+        wanted = lax.rem(rj + 2 * N - ri - t, N)
+        for source, x_ref in enumerate(refs[:N]):
+
+            @pl.when(wanted == source)
+            def _():
+                out[...] = x_ref[...]
+
+
+def hand_on(kernel, after, *args):
+    anywhere, vmem = pl.BlockSpec(memory_space=pl.ANY), pl.BlockSpec(memory_space=pltpu.VMEM)
+    return pl.pallas_call(
+        kernel,
+        out_shape=[jax.ShapeDtypeStruct(args[0].shape[-3:], BF)] * N,
+        in_specs=[anywhere] + [vmem] * len(args),
+        out_specs=[vmem] * N,
+        compiler_params=pltpu.CompilerParams(vmem_limit_bytes=8 * 2**20),
+        cost_estimate=pl.CostEstimate(flops=0, bytes_accessed=2**21, transcendentals=0),
+    )(after, *args)
 
 
 def place_kernel(first, x_ref, *refs):
@@ -165,24 +194,27 @@
     ]
     bias = lax.all_to_all(pair_bias, "rj", 0, 0, tiled=True).reshape(N, 2, ROWS, ROWS)
 
-    send, keep, dq, *parts = attention(q, g, o, kvs, bias)
-
-    def home(part, t):
-        return lax.ppermute(
-            part, ("ri", "rj"), [((b + t) % N * N + a, a * N + b) for a, b in grid]
-        )
+    send, keep, dq, dkv = attention(q, g, o, kvs, bias)
+
+    def spread_out(parts, axis):
+        return [parts[0]] + [
+            lax.ppermute(parts[t], axis, [(a, (a + t) % N) for a in range(N)])
+            for t in range(1, N)
+        ]
 
     total = add(keep, swap(send, "core", [(0, 1)]))
-    back = [home(part, t) for t, part in enumerate(parts)]
     spread = lax.all_to_all(total, ("x", "rj"), 0, 0, tiled=True)
-    spread, *back = lax.optimization_barrier((spread, *back))
     total = jnp.sum(spread.reshape(N, N, 64, ROWS).astype(F32), axis=0).astype(BF)
-    for pairs in ([(0, 1), (2, 3)], [(1, 2), (3, 0)]):
-        total = add(total, swap(total, "zh", pairs))
+    other = swap(total, "zh", [(0, 1), (2, 3)])
+    parts = spread_out(hand_on(split_kernel, total, dkv), "rj")
+    total = add(total, other)
+    other = swap(total, "zh", [(1, 2), (3, 0)])
+    parts = spread_out(hand_on(choose_kernel, total, *parts), "ri")
+    total = add(total, other)
     mine = lax.all_gather(total, "x", axis=0)
     bias_grad = place(swap(mine, "core", [(0, 1)]), place(mine))
 
-    kv_grad = sum(x.astype(F32) for x in back).astype(BF)
+    kv_grad = sum(x.astype(F32) for x in parts).astype(BF)
     width = k.shape[1]
     grads = (dq, kv_grad[:, :width], kv_grad[:, width:])
     return *(jnp.swapaxes(x, 1, 2) for x in grads), bias_grad

time: 143 us -> 116 us (0.81)
  the two profiles are of different devices: /device:TPU:17 before, /device:TPU:1 now
where the time goes in v4:
time: 116 us
  starting transfers between devices  65 us (56%)
  blocking collectives  31.3 us (27%)
  waiting for transfers between devices  9.34 us (8%)
  Pallas kernels  7.96 us (7%)
    ppermute x4, starting transfers between devices, swap(): lax.ppermute(x, axis, [(a, b) for a, b in pairs] + [(b, a) for a, b in pa...  26.9 us
    all_to_all x1, blocking collectives, body(): spread = lax.all_to_all(total, ('x', 'rj'), 0, 0, tiled=True)  20.3 us
    ppermute x6, starting transfers between devices, spread_out(): lax.ppermute(parts[t], axis, [(a, (a + t) % N) for a in range(N)])  19.2 us
    ppermute x4, starting transfers between devices, body(): lax.ppermute(kv, ('ri', 'rj'), [(a * N + b, (b + t) % N * N + a) for a, b...  13.7 us
    all_gather x1, blocking collectives, body(): mine = lax.all_gather(total, 'x', axis=0)  11 us
    pallas_call x1, Pallas kernels, attention(): pl.pallas_call(attention_kernel, out_shape=(piece, piece, jax.ShapeDtypeS...  5.78 us
    ppermute x4, waiting for transfers between devices, body(): lax.ppermute(kv, ('ri', 'rj'), [(a * N + b, (b + t) % N * N + a) for a, b...  5.46 us
    all_to_all x1, starting transfers between devices, body(): lax.all_to_all(pair_bias, 'rj', 0, 0, tiled=True).reshape(N, 2, ROWS, ROWS)  5.16 us
  transfers between devices with their start and end apart: 15, of which 4 were waited for; matrix products, arithmetic and copies ran while one was open for 1% of the time, Pallas kernels for 1%

profile of v4, /device:TPU:1, one launch (start us, length us, event | category | flops | bytes accessed | tf_op | source)
XLA Modules:
  0.0 115.6 jit_solution(14648270387512344969)
XLA Ops:
  0.7 5.2 %all-to-all-start = ((bf16[8,256,256]{2,1,0:T(8,128)(2,1)}), bf16[8,256,256]{2,1,0:T(8,128)(2,1)S(1)}, u32[]{:S(2)}, u32[]{:S(2)}) async-start(bf16[8,256,256]{2,1,0:T(8,128)(2,1)} %param.9), calls=%async_computation | async-start | bytes 2097152 | tf_op jit(solution)/shard_map/all_to_all | solution.py:195
  5.9 6.3 %collective-permute-start.3 = (bf16[2,128,256]{2,1,0:T(8,128)(2,1)S(1)}, bf16[2,128,256]{2,1,0:T(8,128)(2,1)S(1)}, u32[]{:S(2)}, u32[]{:S(2)}) collective-permute-start(bf16[2,128,256]{2,1,0:T(8,128)(2,1)S(1)} %pad_maximum_fusion), channel_id=1, source_target_pairs={{0,12},{1,0},{2,4},{3,8},{4,13},{5,1},{6,5},{7,9},{8,14},{9,2},{10... | collective-permute-start | bytes 393224 | tf_op jit(solution)/shard_map/ppermute | solution.py:192
  12.1 4.9 %collective-permute-start.2 = (bf16[2,128,256]{2,1,0:T(8,128)(2,1)S(1)}, bf16[2,128,256]{2,1,0:T(8,128)(2,1)S(1)}, u32[]{:S(2)}, u32[]{:S(2)}) collective-permute-start(bf16[2,128,256]{2,1,0:T(8,128)(2,1)S(1)} %pad_maximum_fusion), channel_id=1, source_target_pairs={{0,8},{1,12},{2,0},{3,4},{4,9},{5,13},{6,1},{7,5},{8,10},{9,14},{1... | collective-permute-start | bytes 393224 | tf_op jit(solution)/shard_map/ppermute | solution.py:192
  17.0 1.9 %collective-permute-start.1 = (bf16[2,128,256]{2,1,0:T(8,128)(2,1)S(1)}, bf16[2,128,256]{2,1,0:T(8,128)(2,1)S(1)}, u32[]{:S(2)}, u32[]{:S(2)}) collective-permute-start(bf16[2,128,256]{2,1,0:T(8,128)(2,1)S(1)} %pad_maximum_fusion), channel_id=1, source_target_pairs={{0,4},{1,8},{2,12},{3,0},{4,5},{5,9},{6,13},{7,1},{8,6},{9,10},{10... | collective-permute-start | bytes 393224 | tf_op jit(solution)/shard_map/ppermute | solution.py:192
  18.9 0.7 collective-permute-start
  19.6 2.9 %collective-permute-done.2.kv2 = bf16[2,128,256]{2,1,0:T(8,128)(2,1)S(1)} collective-permute-done((bf16[2,128,256]{2,1,0:T(8,128)(2,1)S(1)}, bf16[2,128,256]{2,1,0:T(8,128)(2,1)S(1)}, u32[]{:S(2)}, u32[]{:S(2)}) %collective-permute-start.2) | collective-permute-done | bytes 131104 | tf_op jit(solution)/shard_map/ppermute | solution.py:192
  22.5 2.6 %collective-permute-done.1.kv1 = bf16[2,128,256]{2,1,0:T(8,128)(2,1)S(1)} collective-permute-done((bf16[2,128,256]{2,1,0:T(8,128)(2,1)S(1)}, bf16[2,128,256]{2,1,0:T(8,128)(2,1)S(1)}, u32[]{:S(2)}, u32[]{:S(2)}) %collective-permute-start.1) | collective-permute-done | bytes 131104 | tf_op jit(solution)/shard_map/ppermute | solution.py:192
  25.1 0.0 collective-permute-done.kv0
  25.1 0.0 all-to-all-done
  25.1 5.8 %shard_map.93 = (bf16[16,64,256]{2,1,0:T(8,128)(2,1)S(1)}, bf16[16,64,256]{2,1,0:T(8,128)(2,1)S(1)}, bf16[2,64,256]{2,1,0:T(8,128)(2,1)}, bf16[4,2,128,256]{3,2,1,0:T(8,128)(2,1)S(1)}) custom-call(bf16[2,64,256]{2,1,0:T(8,128)(2,1)S(1)} %bitcast.16, bf16[2,64,256]{2,1,0:T(8,128)(2,1)S(1)} %bitcast.17, bf16[2,64,256]{2,1,0:T(8,128)(2,1)S(1)} %bitcast.18, ...), custom_call_target="tpu_custom_call" | custom-call | flops 335544320 | bytes 6291456 | tf_op jit(solution)/shard_map/pallas_call | solution.py:99
  30.9 5.9 %collective-permute-start.4 = (bf16[16,64,256]{2,1,0:T(8,128)(2,1)S(1)}, bf16[16,64,256]{2,1,0:T(8,128)(2,1)S(1)}, u32[]{:S(2)}, u32[]{:S(2)}) collective-permute-start(bf16[16,64,256]{2,1,0:T(8,128)(2,1)S(1)} %get-tuple-element.18), channel_id=1, source_target_pairs={{0,16},{16,0},{1,17},{17,1},{2,18},{18,2},{3,19},{19,3},{4,20},{20... | collective-permute-start | bytes 1572872 | tf_op jit(solution)/shard_map/ppermute | solution.py:176
  36.8 1.5 %collective-permute-done.4 = bf16[16,64,256]{2,1,0:T(8,128)(2,1)S(1)} collective-permute-done((bf16[16,64,256]{2,1,0:T(8,128)(2,1)S(1)}, bf16[16,64,256]{2,1,0:T(8,128)(2,1)S(1)}, u32[]{:S(2)}, u32[]{:S(2)}) %collective-permute-start.4) | collective-permute-done | bytes 524320 | tf_op jit(solution)/shard_map/ppermute | solution.py:176
  38.3 0.1 add_convert_fusion
  38.5 20.3 %all_to_all.10 = bf16[16,64,256]{2,1,0:T(8,128)(2,1)S(1)} all-to-all(bf16[16,64,256]{2,1,0:T(8,128)(2,1)S(1)} %add_convert_fusion), channel_id=1, replica_groups=mesh['zh'=4,'x'=4,'core'=2,'ri'=4,'rj'=4] {'x','rj'}, dimensions={0} | all-to-all | bytes 1048576 | tf_op jit(solution)/shard_map/all_to_all | solution.py:206
  58.8 0.1 reduce_sum.12.after
  58.9 8.8 %collective-permute-start.5 = (bf16[4,64,256]{2,1,0:T(8,128)(2,1)S(1)}, bf16[4,64,256]{2,1,0:T(8,128)(2,1)S(1)}, u32[]{:S(2)}, u32[]{:S(2)}) collective-permute-start(bf16[4,64,256]{2,1,0:T(8,128)(2,1)S(1)} %reduce_sum.12.after), channel_id=1, source_target_pairs={{0,128},{256,384},{128,0},{384,256},{1,129},{257,385},{129,1},{385... | collective-permute-start | bytes 393224 | tf_op jit(solution)/shard_map/ppermute | solution.py:176
  67.8 2.3 %collective-permute-start.6 = (bf16[2,128,256]{2,1,0:T(8,128)(2,1)S(1)}, bf16[2,128,256]{2,1,0:T(8,128)(2,1)S(1)}, u32[]{:S(2)}, u32[]{:S(2)}) collective-permute-start(bf16[2,128,256]{2,1,0:T(8,128)(2,1)S(1)} %get-tuple-element.21), channel_id=1, source_target_pairs={{0,1},{1,2},{2,3},{3,0},{4,5},{5,6},{6,7},{7,4},{8,9},{9,10},{10,1... | collective-permute-start | bytes 393224 | tf_op jit(solution)/shard_map/ppermute | solution.py:201
  70.1 3.6 %collective-permute-start.7 = (bf16[2,128,256]{2,1,0:T(8,128)(2,1)S(1)}, bf16[2,128,256]{2,1,0:T(8,128)(2,1)S(1)}, u32[]{:S(2)}, u32[]{:S(2)}) collective-permute-start(bf16[2,128,256]{2,1,0:T(8,128)(2,1)S(1)} %get-tuple-element.22), channel_id=1, source_target_pairs={{0,2},{1,3},{2,0},{3,1},{4,6},{5,7},{6,4},{7,5},{8,10},{9,11},{10,... | collective-permute-start | bytes 393224 | tf_op jit(solution)/shard_map/ppermute | solution.py:201
  73.7 3.1 %collective-permute-start.8 = (bf16[2,128,256]{2,1,0:T(8,128)(2,1)S(1)}, bf16[2,128,256]{2,1,0:T(8,128)(2,1)S(1)}, u32[]{:S(2)}, u32[]{:S(2)}) collective-permute-start(bf16[2,128,256]{2,1,0:T(8,128)(2,1)S(1)} %get-tuple-element.23), channel_id=1, source_target_pairs={{0,3},{1,0},{2,1},{3,2},{4,7},{5,4},{6,5},{7,6},{8,11},{9,8},{10,9... | collective-permute-start | bytes 393224 | tf_op jit(solution)/shard_map/ppermute | solution.py:201
  76.8 2.3 %collective-permute-done.5 = bf16[4,64,256]{2,1,0:T(8,128)(2,1)S(1)} collective-permute-done((bf16[4,64,256]{2,1,0:T(8,128)(2,1)S(1)}, bf16[4,64,256]{2,1,0:T(8,128)(2,1)S(1)}, u32[]{:S(2)}, u32[]{:S(2)}) %collective-permute-start.5) | collective-permute-done | bytes 131104 | tf_op jit(solution)/shard_map/ppermute | solution.py:176
  79.2 6.5 %collective-permute-start.12 = (bf16[4,64,256]{2,1,0:T(8,128)(2,1)S(1)}, bf16[4,64,256]{2,1,0:T(8,128)(2,1)S(1)}, u32[]{:S(2)}, u32[]{:S(2)}) collective-permute-start(bf16[4,64,256]{2,1,0:T(8,128)(2,1)S(1)} %add_convert_fusion.3.after), channel_id=1, source_target_pairs={{128,256},{384,0},{256,128},{0,384},{129,257},{385,1},{257,129},{1... | collective-permute-start | bytes 393224 | tf_op jit(solution)/shard_map/ppermute | solution.py:176
  85.7 0.0 collective-permute-done.8.refs_3_
  85.7 0.1 shard_map.95
  85.8 1.9 %collective-permute-start.9 = (bf16[2,128,256]{2,1,0:T(8,128)(2,1)S(1)}, bf16[2,128,256]{2,1,0:T(8,128)(2,1)S(1)}, u32[]{:S(2)}, u32[]{:S(2)}) collective-permute-start(bf16[2,128,256]{2,1,0:T(8,128)(2,1)S(1)} %get-tuple-element.25), channel_id=1, source_target_pairs={{0,4},{4,8},{8,12},{12,0},{1,5},{5,9},{9,13},{13,1},{2,6},{6,10},{... | collective-permute-start | bytes 393224 | tf_op jit(solution)/shard_map/ppermute | solution.py:201
  87.7 6.3 %collective-permute-start.10 = (bf16[2,128,256]{2,1,0:T(8,128)(2,1)S(1)}, bf16[2,128,256]{2,1,0:T(8,128)(2,1)S(1)}, u32[]{:S(2)}, u32[]{:S(2)}) collective-permute-start(bf16[2,128,256]{2,1,0:T(8,128)(2,1)S(1)} %get-tuple-element.26), channel_id=1, source_target_pairs={{0,8},{4,12},{8,0},{12,4},{1,9},{5,13},{9,1},{13,5},{2,10},{6,14},... | collective-permute-start | bytes 393224 | tf_op jit(solution)/shard_map/ppermute | solution.py:201
  94.1 1.9 %collective-permute-start.11 = (bf16[2,128,256]{2,1,0:T(8,128)(2,1)S(1)}, bf16[2,128,256]{2,1,0:T(8,128)(2,1)S(1)}, u32[]{:S(2)}, u32[]{:S(2)}) collective-permute-start(bf16[2,128,256]{2,1,0:T(8,128)(2,1)S(1)} %get-tuple-element.27), channel_id=1, source_target_pairs={{0,12},{4,0},{8,4},{12,8},{1,13},{5,1},{9,5},{13,9},{2,14},{6,2},{... | collective-permute-start | bytes 393224 | tf_op jit(solution)/shard_map/ppermute | solution.py:201
  96.0 11.0 %all-gather = bf16[16,64,256]{2,1,0:T(8,128)(2,1)S(1)} all-gather(bf16[4,64,256]{2,1,0:T(8,128)(2,1)S(1)} %add_convert_fusion.1), channel_id=2, replica_groups=mesh['zh'=4,'x'=4,'core'=2,'ri'=4,'rj'=4] {'x'}, dimensions={0}, use_global_device_ids=true | all-gather | bytes 655360 | tf_op jit(solution)/shard_map/all_gather | solution.py:214
  107.0 5.7 %collective-permute-start.13 = (bf16[4,4,64,256]{3,2,1,0:T(8,128)(2,1)S(1)}, bf16[4,4,64,256]{3,2,1,0:T(8,128)(2,1)S(1)}, u32[]{:S(2)}, u32[]{:S(2)}) collective-permute-start(bf16[4,4,64,256]{3,2,1,0:T(8,128)(2,1)S(1)} %bitcast.13), channel_id=1, source_target_pairs={{0,16},{16,0},{1,17},{17,1},{2,18},{18,2},{3,19},{19,3},{4,20},{20... | collective-permute-start | bytes 1572872 | tf_op jit(solution)/shard_map/ppermute | solution.py:176
  112.8 1.0 shard_map.96.refs_1_
  113.8 0.1 add_convert_fusion.2
  113.9 0.7 slice_bitcast_fusion
  114.6 1.0 shard_map.97
  (22 shorter events, 0.2 us)
Async XLA Ops:
  0.6 5.2 %copy-start.3 = (bf16[2,256,64]{1,2,0:T(8,128)(2,1)S(1)}, bf16[2,256,64]{1,2,0:T(8,128)(2,1)}, u32[]{:S(2)}) copy-start(bf16[2,256,64]{1,2,0:T(8,128)(2,1)} %param.8) | copy-start | bytes 196612
  0.6 5.2 %copy-start.4 = (bf16[2,256,64]{1,2,0:T(8,128)(2,1)S(1)}, bf16[2,256,64]{1,2,0:T(8,128)(2,1)}, u32[]{:S(2)}) copy-start(bf16[2,256,64]{1,2,0:T(8,128)(2,1)} %param.7) | copy-start | bytes 196612
  0.7 24.4 %copy-start.1 = (bf16[2,256,64]{1,2,0:T(8,128)(2,1)S(1)}, bf16[2,256,64]{1,2,0:T(8,128)(2,1)}, u32[]{:S(2)}) copy-start(bf16[2,256,64]{1,2,0:T(8,128)(2,1)} %param.11) | copy-start | bytes 196612
  0.7 24.4 %copy-start.2 = (bf16[2,256,64]{1,2,0:T(8,128)(2,1)S(1)}, bf16[2,256,64]{1,2,0:T(8,128)(2,1)}, u32[]{:S(2)}) copy-start(bf16[2,256,64]{1,2,0:T(8,128)(2,1)} %param.10) | copy-start | bytes 196612
  0.7 24.4 %copy-start = (bf16[2,256,64]{1,2,0:T(8,128)(2,1)S(1)}, bf16[2,256,64]{1,2,0:T(8,128)(2,1)}, u32[]{:S(2)}) copy-start(bf16[2,256,64]{1,2,0:T(8,128)(2,1)} %param.6) | copy-start | bytes 196612
  0.7 24.4 %all-to-all-start = ((bf16[8,256,256]{2,1,0:T(8,128)(2,1)}), bf16[8,256,256]{2,1,0:T(8,128)(2,1)S(1)}, u32[]{:S(2)}, u32[]{:S(2)}) async-start(bf16[8,256,256]{2,1,0:T(8,128)(2,1)} %param.9), calls=%async_computation | async-start | bytes 2097152 | tf_op jit(solution)/shard_map/all_to_all | solution.py:195
  5.9 13.8 %collective-permute-start.3 = (bf16[2,128,256]{2,1,0:T(8,128)(2,1)S(1)}, bf16[2,128,256]{2,1,0:T(8,128)(2,1)S(1)}, u32[]{:S(2)}, u32[]{:S(2)}) collective-permute-start(bf16[2,128,256]{2,1,0:T(8,128)(2,1)S(1)} %pad_maximum_fusion), channel_id=1, source_target_pairs={{0,12},{1,0},{2,4},{3,8},{4,13},{5,1},{6,5},{7,9},{8,14},{9,2},{10... | collective-permute-start | bytes 393224 | tf_op jit(solution)/shard_map/ppermute | solution.py:192
  12.1 10.4 %collective-permute-start.2 = (bf16[2,128,256]{2,1,0:T(8,128)(2,1)S(1)}, bf16[2,128,256]{2,1,0:T(8,128)(2,1)S(1)}, u32[]{:S(2)}, u32[]{:S(2)}) collective-permute-start(bf16[2,128,256]{2,1,0:T(8,128)(2,1)S(1)} %pad_maximum_fusion), channel_id=1, source_target_pairs={{0,8},{1,12},{2,0},{3,4},{4,9},{5,13},{6,1},{7,5},{8,10},{9,14},{1... | collective-permute-start | bytes 393224 | tf_op jit(solution)/shard_map/ppermute | solution.py:192
  17.0 8.1 %collective-permute-start.1 = (bf16[2,128,256]{2,1,0:T(8,128)(2,1)S(1)}, bf16[2,128,256]{2,1,0:T(8,128)(2,1)S(1)}, u32[]{:S(2)}, u32[]{:S(2)}) collective-permute-start(bf16[2,128,256]{2,1,0:T(8,128)(2,1)S(1)} %pad_maximum_fusion), channel_id=1, source_target_pairs={{0,4},{1,8},{2,12},{3,0},{4,5},{5,9},{6,13},{7,1},{8,6},{9,10},{10... | collective-permute-start | bytes 393224 | tf_op jit(solution)/shard_map/ppermute | solution.py:192
  18.9 6.2 %collective-permute-start = (bf16[2,128,256]{2,1,0:T(8,128)(2,1)S(1)}, bf16[2,128,256]{2,1,0:T(8,128)(2,1)S(1)}, u32[]{:S(2)}, u32[]{:S(2)}) collective-permute-start(bf16[2,128,256]{2,1,0:T(8,128)(2,1)S(1)} %pad_maximum_fusion), channel_id=1, source_target_pairs={{0,0},{1,4},{2,8},{3,12},{4,1},{5,5},{6,9},{7,13},{8,2},{9,6},{10,... | collective-permute-start | bytes 393224 | tf_op jit(solution)/shard_map/ppermute | solution.py:192
  30.9 7.4 %collective-permute-start.4 = (bf16[16,64,256]{2,1,0:T(8,128)(2,1)S(1)}, bf16[16,64,256]{2,1,0:T(8,128)(2,1)S(1)}, u32[]{:S(2)}, u32[]{:S(2)}) collective-permute-start(bf16[16,64,256]{2,1,0:T(8,128)(2,1)S(1)} %get-tuple-element.18), channel_id=1, source_target_pairs={{0,16},{16,0},{1,17},{17,1},{2,18},{18,2},{3,19},{19,3},{4,20},{20... | collective-permute-start | bytes 1572872 | tf_op jit(solution)/shard_map/ppermute | solution.py:176
  58.9 20.2 %collective-permute-start.5 = (bf16[4,64,256]{2,1,0:T(8,128)(2,1)S(1)}, bf16[4,64,256]{2,1,0:T(8,128)(2,1)S(1)}, u32[]{:S(2)}, u32[]{:S(2)}) collective-permute-start(bf16[4,64,256]{2,1,0:T(8,128)(2,1)S(1)} %reduce_sum.12.after), channel_id=1, source_target_pairs={{0,128},{256,384},{128,0},{384,256},{1,129},{257,385},{129,1},{385... | collective-permute-start | bytes 393224 | tf_op jit(solution)/shard_map/ppermute | solution.py:176
  67.8 17.9 %collective-permute-start.6 = (bf16[2,128,256]{2,1,0:T(8,128)(2,1)S(1)}, bf16[2,128,256]{2,1,0:T(8,128)(2,1)S(1)}, u32[]{:S(2)}, u32[]{:S(2)}) collective-permute-start(bf16[2,128,256]{2,1,0:T(8,128)(2,1)S(1)} %get-tuple-element.21), channel_id=1, source_target_pairs={{0,1},{1,2},{2,3},{3,0},{4,5},{5,6},{6,7},{7,4},{8,9},{9,10},{10,1... | collective-permute-start | bytes 393224 | tf_op jit(solution)/shard_map/ppermute | solution.py:201
  70.1 15.6 %collective-permute-start.7 = (bf16[2,128,256]{2,1,0:T(8,128)(2,1)S(1)}, bf16[2,128,256]{2,1,0:T(8,128)(2,1)S(1)}, u32[]{:S(2)}, u32[]{:S(2)}) collective-permute-start(bf16[2,128,256]{2,1,0:T(8,128)(2,1)S(1)} %get-tuple-element.22), channel_id=1, source_target_pairs={{0,2},{1,3},{2,0},{3,1},{4,6},{5,7},{6,4},{7,5},{8,10},{9,11},{10,... | collective-permute-start | bytes 393224 | tf_op jit(solution)/shard_map/ppermute | solution.py:201
  73.7 12.0 %collective-permute-start.8 = (bf16[2,128,256]{2,1,0:T(8,128)(2,1)S(1)}, bf16[2,128,256]{2,1,0:T(8,128)(2,1)S(1)}, u32[]{:S(2)}, u32[]{:S(2)}) collective-permute-start(bf16[2,128,256]{2,1,0:T(8,128)(2,1)S(1)} %get-tuple-element.23), channel_id=1, source_target_pairs={{0,3},{1,0},{2,1},{3,2},{4,7},{5,4},{6,5},{7,6},{8,11},{9,8},{10,9... | collective-permute-start | bytes 393224 | tf_op jit(solution)/shard_map/ppermute | solution.py:201
  79.2 16.8 %collective-permute-start.12 = (bf16[4,64,256]{2,1,0:T(8,128)(2,1)S(1)}, bf16[4,64,256]{2,1,0:T(8,128)(2,1)S(1)}, u32[]{:S(2)}, u32[]{:S(2)}) collective-permute-start(bf16[4,64,256]{2,1,0:T(8,128)(2,1)S(1)} %add_convert_fusion.3.after), channel_id=1, source_target_pairs={{128,256},{384,0},{256,128},{0,384},{129,257},{385,1},{257,129},{1... | collective-permute-start | bytes 393224 | tf_op jit(solution)/shard_map/ppermute | solution.py:176
  85.8 28.0 %collective-permute-start.9 = (bf16[2,128,256]{2,1,0:T(8,128)(2,1)S(1)}, bf16[2,128,256]{2,1,0:T(8,128)(2,1)S(1)}, u32[]{:S(2)}, u32[]{:S(2)}) collective-permute-start(bf16[2,128,256]{2,1,0:T(8,128)(2,1)S(1)} %get-tuple-element.25), channel_id=1, source_target_pairs={{0,4},{4,8},{8,12},{12,0},{1,5},{5,9},{9,13},{13,1},{2,6},{6,10},{... | collective-permute-start | bytes 393224 | tf_op jit(solution)/shard_map/ppermute | solution.py:201
  87.7 26.1 %collective-permute-start.10 = (bf16[2,128,256]{2,1,0:T(8,128)(2,1)S(1)}, bf16[2,128,256]{2,1,0:T(8,128)(2,1)S(1)}, u32[]{:S(2)}, u32[]{:S(2)}) collective-permute-start(bf16[2,128,256]{2,1,0:T(8,128)(2,1)S(1)} %get-tuple-element.26), channel_id=1, source_target_pairs={{0,8},{4,12},{8,0},{12,4},{1,9},{5,13},{9,1},{13,5},{2,10},{6,14},... | collective-permute-start | bytes 393224 | tf_op jit(solution)/shard_map/ppermute | solution.py:201
  94.1 19.7 %collective-permute-start.11 = (bf16[2,128,256]{2,1,0:T(8,128)(2,1)S(1)}, bf16[2,128,256]{2,1,0:T(8,128)(2,1)S(1)}, u32[]{:S(2)}, u32[]{:S(2)}) collective-permute-start(bf16[2,128,256]{2,1,0:T(8,128)(2,1)S(1)} %get-tuple-element.27), channel_id=1, source_target_pairs={{0,12},{4,0},{8,4},{12,8},{1,13},{5,1},{9,5},{13,9},{2,14},{6,2},{... | collective-permute-start | bytes 393224 | tf_op jit(solution)/shard_map/ppermute | solution.py:201
  107.0 7.6 %collective-permute-start.13 = (bf16[4,4,64,256]{3,2,1,0:T(8,128)(2,1)S(1)}, bf16[4,4,64,256]{3,2,1,0:T(8,128)(2,1)S(1)}, u32[]{:S(2)}, u32[]{:S(2)}) collective-permute-start(bf16[4,4,64,256]{3,2,1,0:T(8,128)(2,1)S(1)} %bitcast.13), channel_id=1, source_target_pairs={{0,16},{16,0},{1,17},{17,1},{2,18},{18,2},{3,19},{19,3},{4,20},{20... | collective-permute-start | bytes 1572872 | tf_op jit(solution)/shard_map/ppermute | solution.py:176

commit v5 on v4

--- a/solution.py
+++ b/solution.py
@@ -180,6 +180,12 @@
     return (a.astype(F32) + b.astype(F32)).astype(BF)
 
 
+def spread_out(parts, axis):
+    steps = ([(a, (a + t) % N) for a in range(N)] for t in range(N))
+    moved = [lax.ppermute(part, axis, step) for part, step in zip(parts[1:], list(steps)[1:])]
+    return [parts[0], *moved]
+
+
 def body(query_proj, key_proj, value_proj, pair_bias, attn_output, output_grad):
     q, k, v, o, g = (
         jnp.swapaxes(x, 1, 2)
@@ -188,19 +194,11 @@
     grid = [(a, b) for a in range(N) for b in range(N)]
 
     kv = jnp.concatenate([k, v], axis=1)
-    kvs = [
-        lax.ppermute(kv, ("ri", "rj"), [(a * N + b, (b + t) % N * N + a) for a, b in grid])
-        for t in range(N)
-    ]
+    kv = lax.ppermute(kv, ("ri", "rj"), [(a * N + b, b * N + a) for a, b in grid])
+    kvs = spread_out([kv] * N, "ri")
     bias = lax.all_to_all(pair_bias, "rj", 0, 0, tiled=True).reshape(N, 2, ROWS, ROWS)
 
     send, keep, dq, dkv = attention(q, g, o, kvs, bias)
-
-    def spread_out(parts, axis):
-        return [parts[0]] + [
-            lax.ppermute(parts[t], axis, [(a, (a + t) % N) for a in range(N)])
-            for t in range(1, N)
-        ]
 
     total = add(keep, swap(send, "core", [(0, 1)]))
     spread = lax.all_to_all(total, ("x", "rj"), 0, 0, tiled=True)

time: 116 us -> 122 us (1.052)
  starting transfers between devices: 65 us -> 72.3 us
  blocking collectives: 31.3 us -> 30 us
    ppermute x10, starting transfers between devices: 32.9 us -> 41.3 us  [the longest x9 40.6 us: spread_out(): lax.ppermute(part, axis, step)]
    all_to_all x1, blocking collectives: 20.3 us -> 19.1 us  [body(): spread = lax.all_to_all(total, ('x', 'rj'), 0, 0, tiled=True)]
  transfers between devices with their start and end apart: 15 -> 15, of which waited for: 4 -> 3; matrix products, arithmetic and copies ran while one was open for 1% -> 1% of each run, Pallas kernels for 1% -> 1%
where the time goes in v5:
time: 122 us
  starting transfers between devices  72.3 us (59%)
  blocking collectives  30 us (25%)
  waiting for transfers between devices  9.47 us (8%)
  Pallas kernels  7.97 us (7%)
    ppermute x9, starting transfers between devices, spread_out(): lax.ppermute(part, axis, step)  40.6 us
    ppermute x4, starting transfers between devices, swap(): lax.ppermute(x, axis, [(a, b) for a, b in pairs] + [(b, a) for a, b in pa...  25.9 us
    all_to_all x1, blocking collectives, body(): spread = lax.all_to_all(total, ('x', 'rj'), 0, 0, tiled=True)  19.1 us
    all_gather x1, blocking collectives, body(): mine = lax.all_gather(total, 'x', axis=0)  10.9 us
    pallas_call x1, Pallas kernels, attention(): pl.pallas_call(attention_kernel, out_shape=(piece, piece, jax.ShapeDtypeS...  5.79 us
    ppermute x9, waiting for transfers between devices, spread_out(): lax.ppermute(part, axis, step)  5.77 us
    all_to_all x1, starting transfers between devices, body(): lax.all_to_all(pair_bias, 'rj', 0, 0, tiled=True).reshape(N, 2, ROWS, ROWS)  5.16 us
    ppermute x4, waiting for transfers between devices, swap(): lax.ppermute(x, axis, [(a, b) for a, b in pairs] + [(b, a) for a, b in pa...  3.69 us
  transfers between devices with their start and end apart: 15, of which 3 were waited for; matrix products, arithmetic and copies ran while one was open for 1% of the time, Pallas kernels for 1%

profile of v5, /device:TPU:1, one launch (start us, length us, event | category | flops | bytes accessed | tf_op | source)
XLA Modules:
  0.0 121.8 jit_solution(18386954478580729210)
XLA Ops:
  0.7 5.2 %all-to-all-start = ((bf16[8,256,256]{2,1,0:T(8,128)(2,1)}), bf16[8,256,256]{2,1,0:T(8,128)(2,1)S(1)}, u32[]{:S(2)}, u32[]{:S(2)}) async-start(bf16[8,256,256]{2,1,0:T(8,128)(2,1)} %param.9), calls=%async_computation | async-start | bytes 2097152 | tf_op jit(solution)/shard_map/all_to_all | solution.py:199
  5.9 0.7 collective-permute-start
  6.5 16.0 %collective-permute-start.3 = (bf16[2,128,256]{2,1,0:T(8,128)(2,1)S(1)}, bf16[2,128,256]{2,1,0:T(8,128)(2,1)S(1)}, u32[]{:S(2)}, u32[]{:S(2)}) collective-permute-start(bf16[2,128,256]{2,1,0:T(8,128)(2,1)S(1)} %collective-permute-done.kv0), channel_id=1, source_target_pairs={{0,12},{4,0},{8,4},{12,8},{1,13},{5,1},{9,5},{13,9},{2,14},{6,2},{... | collective-permute-start | bytes 393224 | tf_op jit(solution)/shard_map/ppermute | solution.py:185
  22.6 1.9 %collective-permute-start.2 = (bf16[2,128,256]{2,1,0:T(8,128)(2,1)S(1)}, bf16[2,128,256]{2,1,0:T(8,128)(2,1)S(1)}, u32[]{:S(2)}, u32[]{:S(2)}) collective-permute-start(bf16[2,128,256]{2,1,0:T(8,128)(2,1)S(1)} %collective-permute-done.kv0), channel_id=1, source_target_pairs={{0,8},{4,12},{8,0},{12,4},{1,9},{5,13},{9,1},{13,5},{2,10},{6,14},... | collective-permute-start | bytes 393224 | tf_op jit(solution)/shard_map/ppermute | solution.py:185
  24.5 2.2 %collective-permute-start.1 = (bf16[2,128,256]{2,1,0:T(8,128)(2,1)S(1)}, bf16[2,128,256]{2,1,0:T(8,128)(2,1)S(1)}, u32[]{:S(2)}, u32[]{:S(2)}) collective-permute-start(bf16[2,128,256]{2,1,0:T(8,128)(2,1)S(1)} %collective-permute-done.kv0), channel_id=1, source_target_pairs={{0,4},{4,8},{8,12},{12,0},{1,5},{5,9},{9,13},{13,1},{2,6},{6,10},{... | collective-permute-start | bytes 393224 | tf_op jit(solution)/shard_map/ppermute | solution.py:185
  26.7 0.0 collective-permute-done.3.kv3
  26.7 5.7 %collective-permute-done.2.kv2 = bf16[2,128,256]{2,1,0:T(8,128)(2,1)S(1)} collective-permute-done((bf16[2,128,256]{2,1,0:T(8,128)(2,1)S(1)}, bf16[2,128,256]{2,1,0:T(8,128)(2,1)S(1)}, u32[]{:S(2)}, u32[]{:S(2)}) %collective-permute-start.2) | collective-permute-done | bytes 131104 | tf_op jit(solution)/shard_map/ppermute | solution.py:185
  32.5 0.0 collective-permute-done.1.kv1
  32.5 0.0 all-to-all-done
  32.5 5.8 %shard_map.93 = (bf16[16,64,256]{2,1,0:T(8,128)(2,1)S(1)}, bf16[16,64,256]{2,1,0:T(8,128)(2,1)S(1)}, bf16[2,64,256]{2,1,0:T(8,128)(2,1)}, bf16[4,2,128,256]{3,2,1,0:T(8,128)(2,1)S(1)}) custom-call(bf16[2,64,256]{2,1,0:T(8,128)(2,1)S(1)} %bitcast.16, bf16[2,64,256]{2,1,0:T(8,128)(2,1)S(1)} %bitcast.17, bf16[2,64,256]{2,1,0:T(8,128)(2,1)S(1)} %bitcast.18, ...), custom_call_target="tpu_custom_call" | custom-call | flops 335544320 | bytes 6291456 | tf_op jit(solution)/shard_map/pallas_call | solution.py:99
  38.3 6.1 %collective-permute-start.4 = (bf16[16,64,256]{2,1,0:T(8,128)(2,1)S(1)}, bf16[16,64,256]{2,1,0:T(8,128)(2,1)S(1)}, u32[]{:S(2)}, u32[]{:S(2)}) collective-permute-start(bf16[16,64,256]{2,1,0:T(8,128)(2,1)S(1)} %get-tuple-element.18), channel_id=1, source_target_pairs={{0,16},{16,0},{1,17},{17,1},{2,18},{18,2},{3,19},{19,3},{4,20},{20... | collective-permute-start | bytes 1572872 | tf_op jit(solution)/shard_map/ppermute | solution.py:176
  44.4 1.5 %collective-permute-done.4 = bf16[16,64,256]{2,1,0:T(8,128)(2,1)S(1)} collective-permute-done((bf16[16,64,256]{2,1,0:T(8,128)(2,1)S(1)}, bf16[16,64,256]{2,1,0:T(8,128)(2,1)S(1)}, u32[]{:S(2)}, u32[]{:S(2)}) %collective-permute-start.4) | collective-permute-done | bytes 524320 | tf_op jit(solution)/shard_map/ppermute | solution.py:176
  46.0 0.1 add_convert_fusion
  46.1 19.1 %all_to_all.10 = bf16[16,64,256]{2,1,0:T(8,128)(2,1)S(1)} all-to-all(bf16[16,64,256]{2,1,0:T(8,128)(2,1)S(1)} %add_convert_fusion), channel_id=1, replica_groups=mesh['zh'=4,'x'=4,'core'=2,'ri'=4,'rj'=4] {'x','rj'}, dimensions={0} | all-to-all | bytes 1048576 | tf_op jit(solution)/shard_map/all_to_all | solution.py:204
  65.2 0.1 reduce_sum.12.after
  65.3 8.8 %collective-permute-start.5 = (bf16[4,64,256]{2,1,0:T(8,128)(2,1)S(1)}, bf16[4,64,256]{2,1,0:T(8,128)(2,1)S(1)}, u32[]{:S(2)}, u32[]{:S(2)}) collective-permute-start(bf16[4,64,256]{2,1,0:T(8,128)(2,1)S(1)} %reduce_sum.12.after), channel_id=1, source_target_pairs={{0,128},{256,384},{128,0},{384,256},{1,129},{257,385},{129,1},{385... | collective-permute-start | bytes 393224 | tf_op jit(solution)/shard_map/ppermute | solution.py:176
  74.2 2.3 %collective-permute-start.6 = (bf16[2,128,256]{2,1,0:T(8,128)(2,1)S(1)}, bf16[2,128,256]{2,1,0:T(8,128)(2,1)S(1)}, u32[]{:S(2)}, u32[]{:S(2)}) collective-permute-start(bf16[2,128,256]{2,1,0:T(8,128)(2,1)S(1)} %get-tuple-element.21), channel_id=1, source_target_pairs={{0,1},{1,2},{2,3},{3,0},{4,5},{5,6},{6,7},{7,4},{8,9},{9,10},{10,1... | collective-permute-start | bytes 393224 | tf_op jit(solution)/shard_map/ppermute | solution.py:185
  76.5 3.6 %collective-permute-start.7 = (bf16[2,128,256]{2,1,0:T(8,128)(2,1)S(1)}, bf16[2,128,256]{2,1,0:T(8,128)(2,1)S(1)}, u32[]{:S(2)}, u32[]{:S(2)}) collective-permute-start(bf16[2,128,256]{2,1,0:T(8,128)(2,1)S(1)} %get-tuple-element.22), channel_id=1, source_target_pairs={{0,2},{1,3},{2,0},{3,1},{4,6},{5,7},{6,4},{7,5},{8,10},{9,11},{10,... | collective-permute-start | bytes 393224 | tf_op jit(solution)/shard_map/ppermute | solution.py:185
  80.1 3.1 %collective-permute-start.8 = (bf16[2,128,256]{2,1,0:T(8,128)(2,1)S(1)}, bf16[2,128,256]{2,1,0:T(8,128)(2,1)S(1)}, u32[]{:S(2)}, u32[]{:S(2)}) collective-permute-start(bf16[2,128,256]{2,1,0:T(8,128)(2,1)S(1)} %get-tuple-element.23), channel_id=1, source_target_pairs={{0,3},{1,0},{2,1},{3,2},{4,7},{5,4},{6,5},{7,6},{8,11},{9,8},{10,9... | collective-permute-start | bytes 393224 | tf_op jit(solution)/shard_map/ppermute | solution.py:185
  83.2 2.2 %collective-permute-done.5 = bf16[4,64,256]{2,1,0:T(8,128)(2,1)S(1)} collective-permute-done((bf16[4,64,256]{2,1,0:T(8,128)(2,1)S(1)}, bf16[4,64,256]{2,1,0:T(8,128)(2,1)S(1)}, u32[]{:S(2)}, u32[]{:S(2)}) %collective-permute-start.5) | collective-permute-done | bytes 131104 | tf_op jit(solution)/shard_map/ppermute | solution.py:176
  85.4 5.1 %collective-permute-start.12 = (bf16[4,64,256]{2,1,0:T(8,128)(2,1)S(1)}, bf16[4,64,256]{2,1,0:T(8,128)(2,1)S(1)}, u32[]{:S(2)}, u32[]{:S(2)}) collective-permute-start(bf16[4,64,256]{2,1,0:T(8,128)(2,1)S(1)} %add_convert_fusion.3.after), channel_id=1, source_target_pairs={{128,256},{384,0},{256,128},{0,384},{129,257},{385,1},{257,129},{1... | collective-permute-start | bytes 393224 | tf_op jit(solution)/shard_map/ppermute | solution.py:176
  90.5 0.0 collective-permute-done.8.refs_3_
  90.5 0.1 shard_map.95
  90.7 1.9 %collective-permute-start.9 = (bf16[2,128,256]{2,1,0:T(8,128)(2,1)S(1)}, bf16[2,128,256]{2,1,0:T(8,128)(2,1)S(1)}, u32[]{:S(2)}, u32[]{:S(2)}) collective-permute-start(bf16[2,128,256]{2,1,0:T(8,128)(2,1)S(1)} %get-tuple-element.25), channel_id=1, source_target_pairs={{0,4},{4,8},{8,12},{12,0},{1,5},{5,9},{9,13},{13,1},{2,6},{6,10},{... | collective-permute-start | bytes 393224 | tf_op jit(solution)/shard_map/ppermute | solution.py:185
  92.6 7.6 %collective-permute-start.10 = (bf16[2,128,256]{2,1,0:T(8,128)(2,1)S(1)}, bf16[2,128,256]{2,1,0:T(8,128)(2,1)S(1)}, u32[]{:S(2)}, u32[]{:S(2)}) collective-permute-start(bf16[2,128,256]{2,1,0:T(8,128)(2,1)S(1)} %get-tuple-element.26), channel_id=1, source_target_pairs={{0,8},{4,12},{8,0},{12,4},{1,9},{5,13},{9,1},{13,5},{2,10},{6,14},... | collective-permute-start | bytes 393224 | tf_op jit(solution)/shard_map/ppermute | solution.py:185
  100.2 1.9 %collective-permute-start.11 = (bf16[2,128,256]{2,1,0:T(8,128)(2,1)S(1)}, bf16[2,128,256]{2,1,0:T(8,128)(2,1)S(1)}, u32[]{:S(2)}, u32[]{:S(2)}) collective-permute-start(bf16[2,128,256]{2,1,0:T(8,128)(2,1)S(1)} %get-tuple-element.27), channel_id=1, source_target_pairs={{0,12},{4,0},{8,4},{12,8},{1,13},{5,1},{9,5},{13,9},{2,14},{6,2},{... | collective-permute-start | bytes 393224 | tf_op jit(solution)/shard_map/ppermute | solution.py:185
  102.2 10.9 %all-gather = bf16[16,64,256]{2,1,0:T(8,128)(2,1)S(1)} all-gather(bf16[4,64,256]{2,1,0:T(8,128)(2,1)S(1)} %add_convert_fusion.1), channel_id=2, replica_groups=mesh['zh'=4,'x'=4,'core'=2,'ri'=4,'rj'=4] {'x'}, dimensions={0}, use_global_device_ids=true | all-gather | bytes 655360 | tf_op jit(solution)/shard_map/all_gather | solution.py:212
  113.1 5.8 %collective-permute-start.13 = (bf16[4,4,64,256]{3,2,1,0:T(8,128)(2,1)S(1)}, bf16[4,4,64,256]{3,2,1,0:T(8,128)(2,1)S(1)}, u32[]{:S(2)}, u32[]{:S(2)}) collective-permute-start(bf16[4,4,64,256]{3,2,1,0:T(8,128)(2,1)S(1)} %bitcast.13), channel_id=1, source_target_pairs={{0,16},{16,0},{1,17},{17,1},{2,18},{18,2},{3,19},{19,3},{4,20},{20... | collective-permute-start | bytes 1572872 | tf_op jit(solution)/shard_map/ppermute | solution.py:176
  119.0 1.0 shard_map.96.refs_1_
  120.0 0.1 add_convert_fusion.2
  120.1 0.7 slice_bitcast_fusion
  120.8 1.0 shard_map.97
  (22 shorter events, 0.2 us)
Async XLA Ops:
  0.6 5.2 %copy-start.3 = (bf16[2,256,64]{1,2,0:T(8,128)(2,1)S(1)}, bf16[2,256,64]{1,2,0:T(8,128)(2,1)}, u32[]{:S(2)}) copy-start(bf16[2,256,64]{1,2,0:T(8,128)(2,1)} %param.8) | copy-start | bytes 196612
  0.6 5.2 %copy-start.4 = (bf16[2,256,64]{1,2,0:T(8,128)(2,1)S(1)}, bf16[2,256,64]{1,2,0:T(8,128)(2,1)}, u32[]{:S(2)}) copy-start(bf16[2,256,64]{1,2,0:T(8,128)(2,1)} %param.7) | copy-start | bytes 196612
  0.7 31.8 %copy-start.1 = (bf16[2,256,64]{1,2,0:T(8,128)(2,1)S(1)}, bf16[2,256,64]{1,2,0:T(8,128)(2,1)}, u32[]{:S(2)}) copy-start(bf16[2,256,64]{1,2,0:T(8,128)(2,1)} %param.11) | copy-start | bytes 196612
  0.7 31.8 %copy-start.2 = (bf16[2,256,64]{1,2,0:T(8,128)(2,1)S(1)}, bf16[2,256,64]{1,2,0:T(8,128)(2,1)}, u32[]{:S(2)}) copy-start(bf16[2,256,64]{1,2,0:T(8,128)(2,1)} %param.10) | copy-start | bytes 196612
  0.7 31.8 %copy-start = (bf16[2,256,64]{1,2,0:T(8,128)(2,1)S(1)}, bf16[2,256,64]{1,2,0:T(8,128)(2,1)}, u32[]{:S(2)}) copy-start(bf16[2,256,64]{1,2,0:T(8,128)(2,1)} %param.6) | copy-start | bytes 196612
  0.7 31.8 %all-to-all-start = ((bf16[8,256,256]{2,1,0:T(8,128)(2,1)}), bf16[8,256,256]{2,1,0:T(8,128)(2,1)S(1)}, u32[]{:S(2)}, u32[]{:S(2)}) async-start(bf16[8,256,256]{2,1,0:T(8,128)(2,1)} %param.9), calls=%async_computation | async-start | bytes 2097152 | tf_op jit(solution)/shard_map/all_to_all | solution.py:199
  5.9 0.7 collective-permute-start
  6.5 20.2 %collective-permute-start.3 = (bf16[2,128,256]{2,1,0:T(8,128)(2,1)S(1)}, bf16[2,128,256]{2,1,0:T(8,128)(2,1)S(1)}, u32[]{:S(2)}, u32[]{:S(2)}) collective-permute-start(bf16[2,128,256]{2,1,0:T(8,128)(2,1)S(1)} %collective-permute-done.kv0), channel_id=1, source_target_pairs={{0,12},{4,0},{8,4},{12,8},{1,13},{5,1},{9,5},{13,9},{2,14},{6,2},{... | collective-permute-start | bytes 393224 | tf_op jit(solution)/shard_map/ppermute | solution.py:185
  22.6 9.9 %collective-permute-start.2 = (bf16[2,128,256]{2,1,0:T(8,128)(2,1)S(1)}, bf16[2,128,256]{2,1,0:T(8,128)(2,1)S(1)}, u32[]{:S(2)}, u32[]{:S(2)}) collective-permute-start(bf16[2,128,256]{2,1,0:T(8,128)(2,1)S(1)} %collective-permute-done.kv0), channel_id=1, source_target_pairs={{0,8},{4,12},{8,0},{12,4},{1,9},{5,13},{9,1},{13,5},{2,10},{6,14},... | collective-permute-start | bytes 393224 | tf_op jit(solution)/shard_map/ppermute | solution.py:185
  24.5 8.0 %collective-permute-start.1 = (bf16[2,128,256]{2,1,0:T(8,128)(2,1)S(1)}, bf16[2,128,256]{2,1,0:T(8,128)(2,1)S(1)}, u32[]{:S(2)}, u32[]{:S(2)}) collective-permute-start(bf16[2,128,256]{2,1,0:T(8,128)(2,1)S(1)} %collective-permute-done.kv0), channel_id=1, source_target_pairs={{0,4},{4,8},{8,12},{12,0},{1,5},{5,9},{9,13},{13,1},{2,6},{6,10},{... | collective-permute-start | bytes 393224 | tf_op jit(solution)/shard_map/ppermute | solution.py:185
  38.3 7.7 %collective-permute-start.4 = (bf16[16,64,256]{2,1,0:T(8,128)(2,1)S(1)}, bf16[16,64,256]{2,1,0:T(8,128)(2,1)S(1)}, u32[]{:S(2)}, u32[]{:S(2)}) collective-permute-start(bf16[16,64,256]{2,1,0:T(8,128)(2,1)S(1)} %get-tuple-element.18), channel_id=1, source_target_pairs={{0,16},{16,0},{1,17},{17,1},{2,18},{18,2},{3,19},{19,3},{4,20},{20... | collective-permute-start | bytes 1572872 | tf_op jit(solution)/shard_map/ppermute | solution.py:176
  65.3 20.1 %collective-permute-start.5 = (bf16[4,64,256]{2,1,0:T(8,128)(2,1)S(1)}, bf16[4,64,256]{2,1,0:T(8,128)(2,1)S(1)}, u32[]{:S(2)}, u32[]{:S(2)}) collective-permute-start(bf16[4,64,256]{2,1,0:T(8,128)(2,1)S(1)} %reduce_sum.12.after), channel_id=1, source_target_pairs={{0,128},{256,384},{128,0},{384,256},{1,129},{257,385},{129,1},{385... | collective-permute-start | bytes 393224 | tf_op jit(solution)/shard_map/ppermute | solution.py:176
  74.2 16.4 %collective-permute-start.6 = (bf16[2,128,256]{2,1,0:T(8,128)(2,1)S(1)}, bf16[2,128,256]{2,1,0:T(8,128)(2,1)S(1)}, u32[]{:S(2)}, u32[]{:S(2)}) collective-permute-start(bf16[2,128,256]{2,1,0:T(8,128)(2,1)S(1)} %get-tuple-element.21), channel_id=1, source_target_pairs={{0,1},{1,2},{2,3},{3,0},{4,5},{5,6},{6,7},{7,4},{8,9},{9,10},{10,1... | collective-permute-start | bytes 393224 | tf_op jit(solution)/shard_map/ppermute | solution.py:185
  76.5 14.0 %collective-permute-start.7 = (bf16[2,128,256]{2,1,0:T(8,128)(2,1)S(1)}, bf16[2,128,256]{2,1,0:T(8,128)(2,1)S(1)}, u32[]{:S(2)}, u32[]{:S(2)}) collective-permute-start(bf16[2,128,256]{2,1,0:T(8,128)(2,1)S(1)} %get-tuple-element.22), channel_id=1, source_target_pairs={{0,2},{1,3},{2,0},{3,1},{4,6},{5,7},{6,4},{7,5},{8,10},{9,11},{10,... | collective-permute-start | bytes 393224 | tf_op jit(solution)/shard_map/ppermute | solution.py:185
  80.1 10.5 %collective-permute-start.8 = (bf16[2,128,256]{2,1,0:T(8,128)(2,1)S(1)}, bf16[2,128,256]{2,1,0:T(8,128)(2,1)S(1)}, u32[]{:S(2)}, u32[]{:S(2)}) collective-permute-start(bf16[2,128,256]{2,1,0:T(8,128)(2,1)S(1)} %get-tuple-element.23), channel_id=1, source_target_pairs={{0,3},{1,0},{2,1},{3,2},{4,7},{5,4},{6,5},{7,6},{8,11},{9,8},{10,9... | collective-permute-start | bytes 393224 | tf_op jit(solution)/shard_map/ppermute | solution.py:185
  85.4 16.7 %collective-permute-start.12 = (bf16[4,64,256]{2,1,0:T(8,128)(2,1)S(1)}, bf16[4,64,256]{2,1,0:T(8,128)(2,1)S(1)}, u32[]{:S(2)}, u32[]{:S(2)}) collective-permute-start(bf16[4,64,256]{2,1,0:T(8,128)(2,1)S(1)} %add_convert_fusion.3.after), channel_id=1, source_target_pairs={{128,256},{384,0},{256,128},{0,384},{129,257},{385,1},{257,129},{1... | collective-permute-start | bytes 393224 | tf_op jit(solution)/shard_map/ppermute | solution.py:176
  90.7 29.3 %collective-permute-start.9 = (bf16[2,128,256]{2,1,0:T(8,128)(2,1)S(1)}, bf16[2,128,256]{2,1,0:T(8,128)(2,1)S(1)}, u32[]{:S(2)}, u32[]{:S(2)}) collective-permute-start(bf16[2,128,256]{2,1,0:T(8,128)(2,1)S(1)} %get-tuple-element.25), channel_id=1, source_target_pairs={{0,4},{4,8},{8,12},{12,0},{1,5},{5,9},{9,13},{13,1},{2,6},{6,10},{... | collective-permute-start | bytes 393224 | tf_op jit(solution)/shard_map/ppermute | solution.py:185
  92.6 27.4 %collective-permute-start.10 = (bf16[2,128,256]{2,1,0:T(8,128)(2,1)S(1)}, bf16[2,128,256]{2,1,0:T(8,128)(2,1)S(1)}, u32[]{:S(2)}, u32[]{:S(2)}) collective-permute-start(bf16[2,128,256]{2,1,0:T(8,128)(2,1)S(1)} %get-tuple-element.26), channel_id=1, source_target_pairs={{0,8},{4,12},{8,0},{12,4},{1,9},{5,13},{9,1},{13,5},{2,10},{6,14},... | collective-permute-start | bytes 393224 | tf_op jit(solution)/shard_map/ppermute | solution.py:185
  100.2 19.8 %collective-permute-start.11 = (bf16[2,128,256]{2,1,0:T(8,128)(2,1)S(1)}, bf16[2,128,256]{2,1,0:T(8,128)(2,1)S(1)}, u32[]{:S(2)}, u32[]{:S(2)}) collective-permute-start(bf16[2,128,256]{2,1,0:T(8,128)(2,1)S(1)} %get-tuple-element.27), channel_id=1, source_target_pairs={{0,12},{4,0},{8,4},{12,8},{1,13},{5,1},{9,5},{13,9},{2,14},{6,2},{... | collective-permute-start | bytes 393224 | tf_op jit(solution)/shard_map/ppermute | solution.py:185
  113.1 7.6 %collective-permute-start.13 = (bf16[4,4,64,256]{3,2,1,0:T(8,128)(2,1)S(1)}, bf16[4,4,64,256]{3,2,1,0:T(8,128)(2,1)S(1)}, u32[]{:S(2)}, u32[]{:S(2)}) collective-permute-start(bf16[4,4,64,256]{3,2,1,0:T(8,128)(2,1)S(1)} %bitcast.13), channel_id=1, source_target_pairs={{0,16},{16,0},{1,17},{17,1},{2,18},{18,2},{3,19},{19,3},{4,20},{20... | collective-permute-start | bytes 1572872 | tf_op jit(solution)/shard_map/ppermute | solution.py:176

commit v6 on v5

--- a/solution.py
+++ b/solution.py
@@ -195,6 +195,7 @@
 
     kv = jnp.concatenate([k, v], axis=1)
     kv = lax.ppermute(kv, ("ri", "rj"), [(a * N + b, b * N + a) for a, b in grid])
+    pair_bias, kv = lax.optimization_barrier((pair_bias, kv))
     kvs = spread_out([kv] * N, "ri")
     bias = lax.all_to_all(pair_bias, "rj", 0, 0, tiled=True).reshape(N, 2, ROWS, ROWS)
 

time: 122 us -> 123 us (level)
  blocking collectives: 30 us -> 28.3 us
  waiting for transfers between devices: 9.47 us -> 10.9 us
    all_to_all x1, starting transfers between devices: 5.16 us -> 17.1 us  [body(): lax.all_to_all(pair_bias, 'rj', 0, 0, tiled=True).reshape(N, 2, ROWS, ROWS)]
    ppermute x9, starting transfers between devices: 40.6 us -> 29.3 us  [spread_out(): lax.ppermute(part, axis, step)]
    all_to_all x1, blocking collectives: 19.1 us -> 16.9 us  [body(): spread = lax.all_to_all(total, ('x', 'rj'), 0, 0, tiled=True)]
where the time goes in v6:
time: 123 us; the launch traced here: 122 us
  starting transfers between devices  71.9 us (58%)
  blocking collectives  28.3 us (23%)
  waiting for transfers between devices  10.9 us (9%)
  Pallas kernels  7.97 us (6%)
  other arithmetic  1.3 us (1%)
    ppermute x9, starting transfers between devices, spread_out(): lax.ppermute(part, axis, step)  29.3 us
    ppermute x4, starting transfers between devices, swap(): lax.ppermute(x, axis, [(a, b) for a, b in pairs] + [(b, a) for a, b in pa...  24.9 us
    all_to_all x1, starting transfers between devices, body(): lax.all_to_all(pair_bias, 'rj', 0, 0, tiled=True).reshape(N, 2, ROWS, ROWS)  17.1 us
    all_to_all x1, blocking collectives, body(): spread = lax.all_to_all(total, ('x', 'rj'), 0, 0, tiled=True)  16.9 us
    all_gather x1, blocking collectives, body(): mine = lax.all_gather(total, 'x', axis=0)  11.4 us
    ppermute x9, waiting for transfers between devices, spread_out(): lax.ppermute(part, axis, step)  6.16 us
    pallas_call x1, Pallas kernels, attention(): pl.pallas_call(attention_kernel, out_shape=(piece, piece, jax.ShapeDtypeS...  5.79 us
    ppermute x4, waiting for transfers between devices, swap(): lax.ppermute(x, axis, [(a, b) for a, b in pairs] + [(b, a) for a, b in pa...  4.77 us
  transfers between devices with their start and end apart: 15, of which 3 were waited for; matrix products, arithmetic and copies ran while one was open for 1% of the time, Pallas kernels for 1%

profile of v6, /device:TPU:1, one launch (start us, length us, event | category | flops | bytes accessed | tf_op | source)
XLA Modules:
  0.0 122.0 jit_solution(13833374762938128308)
XLA Ops:
  0.7 0.9 pad_maximum_fusion
  1.6 0.7 collective-permute-start
  2.3 17.1 %all-to-all-start = ((bf16[8,256,256]{2,1,0:T(8,128)(2,1)}), bf16[8,256,256]{2,1,0:T(8,128)(2,1)S(1)}, u32[]{:S(2)}, u32[]{:S(2)}) async-start(bf16[8,256,256]{2,1,0:T(8,128)(2,1)} %param.9), calls=%async_computation | async-start | bytes 2097152 | tf_op jit(solution)/shard_map/all_to_all | solution.py:200
  19.3 6.3 %collective-permute-start.3 = (bf16[2,128,256]{2,1,0:T(8,128)(2,1)S(1)}, bf16[2,128,256]{2,1,0:T(8,128)(2,1)S(1)}, u32[]{:S(2)}, u32[]{:S(2)}) collective-permute-start(bf16[2,128,256]{2,1,0:T(8,128)(2,1)S(1)} %collective-permute-done.kv0), channel_id=1, source_target_pairs={{0,12},{4,0},{8,4},{12,8},{1,13},{5,1},{9,5},{13,9},{2,14},{6,2},{... | collective-permute-start | bytes 393224 | tf_op jit(solution)/shard_map/ppermute | solution.py:185
  25.6 1.9 %collective-permute-start.2 = (bf16[2,128,256]{2,1,0:T(8,128)(2,1)S(1)}, bf16[2,128,256]{2,1,0:T(8,128)(2,1)S(1)}, u32[]{:S(2)}, u32[]{:S(2)}) collective-permute-start(bf16[2,128,256]{2,1,0:T(8,128)(2,1)S(1)} %collective-permute-done.kv0), channel_id=1, source_target_pairs={{0,8},{4,12},{8,0},{12,4},{1,9},{5,13},{9,1},{13,5},{2,10},{6,14},... | collective-permute-start | bytes 393224 | tf_op jit(solution)/shard_map/ppermute | solution.py:185
  27.6 2.2 %collective-permute-start.1 = (bf16[2,128,256]{2,1,0:T(8,128)(2,1)S(1)}, bf16[2,128,256]{2,1,0:T(8,128)(2,1)S(1)}, u32[]{:S(2)}, u32[]{:S(2)}) collective-permute-start(bf16[2,128,256]{2,1,0:T(8,128)(2,1)S(1)} %collective-permute-done.kv0), channel_id=1, source_target_pairs={{0,4},{4,8},{8,12},{12,0},{1,5},{5,9},{9,13},{13,1},{2,6},{6,10},{... | collective-permute-start | bytes 393224 | tf_op jit(solution)/shard_map/ppermute | solution.py:185
  29.8 6.1 %collective-permute-done.2.kv2 = bf16[2,128,256]{2,1,0:T(8,128)(2,1)S(1)} collective-permute-done((bf16[2,128,256]{2,1,0:T(8,128)(2,1)S(1)}, bf16[2,128,256]{2,1,0:T(8,128)(2,1)S(1)}, u32[]{:S(2)}, u32[]{:S(2)}) %collective-permute-start.2) | collective-permute-done | bytes 131104 | tf_op jit(solution)/shard_map/ppermute | solution.py:185
  35.9 5.8 %shard_map.93 = (bf16[16,64,256]{2,1,0:T(8,128)(2,1)S(1)}, bf16[16,64,256]{2,1,0:T(8,128)(2,1)S(1)}, bf16[2,64,256]{2,1,0:T(8,128)(2,1)}, bf16[4,2,128,256]{3,2,1,0:T(8,128)(2,1)S(1)}) custom-call(bf16[2,64,256]{2,1,0:T(8,128)(2,1)S(1)} %bitcast.16, bf16[2,64,256]{2,1,0:T(8,128)(2,1)S(1)} %bitcast.17, bf16[2,64,256]{2,1,0:T(8,128)(2,1)S(1)} %bitcast.18, ...), custom_call_target="tpu_custom_call" | custom-call | flops 335544320 | bytes 6291456 | tf_op jit(solution)/shard_map/pallas_call | solution.py:99
  41.7 4.7 %collective-permute-start.4 = (bf16[16,64,256]{2,1,0:T(8,128)(2,1)S(1)}, bf16[16,64,256]{2,1,0:T(8,128)(2,1)S(1)}, u32[]{:S(2)}, u32[]{:S(2)}) collective-permute-start(bf16[16,64,256]{2,1,0:T(8,128)(2,1)S(1)} %get-tuple-element.22), channel_id=1, source_target_pairs={{0,16},{16,0},{1,17},{17,1},{2,18},{18,2},{3,19},{19,3},{4,20},{20... | collective-permute-start | bytes 1572872 | tf_op jit(solution)/shard_map/ppermute | solution.py:176
  46.5 1.5 %collective-permute-done.4 = bf16[16,64,256]{2,1,0:T(8,128)(2,1)S(1)} collective-permute-done((bf16[16,64,256]{2,1,0:T(8,128)(2,1)S(1)}, bf16[16,64,256]{2,1,0:T(8,128)(2,1)S(1)}, u32[]{:S(2)}, u32[]{:S(2)}) %collective-permute-start.4) | collective-permute-done | bytes 524320 | tf_op jit(solution)/shard_map/ppermute | solution.py:176
  48.0 0.1 add_convert_fusion
  48.1 16.9 %all_to_all.10 = bf16[16,64,256]{2,1,0:T(8,128)(2,1)S(1)} all-to-all(bf16[16,64,256]{2,1,0:T(8,128)(2,1)S(1)} %add_convert_fusion), channel_id=1, replica_groups=mesh['zh'=4,'x'=4,'core'=2,'ri'=4,'rj'=4] {'x','rj'}, dimensions={0} | all-to-all | bytes 1048576 | tf_op jit(solution)/shard_map/all_to_all | solution.py:205
  65.0 0.1 reduce_sum.12.after
  65.1 8.8 %collective-permute-start.5 = (bf16[4,64,256]{2,1,0:T(8,128)(2,1)S(1)}, bf16[4,64,256]{2,1,0:T(8,128)(2,1)S(1)}, u32[]{:S(2)}, u32[]{:S(2)}) collective-permute-start(bf16[4,64,256]{2,1,0:T(8,128)(2,1)S(1)} %reduce_sum.12.after), channel_id=1, source_target_pairs={{0,128},{256,384},{128,0},{384,256},{1,129},{257,385},{129,1},{385... | collective-permute-start | bytes 393224 | tf_op jit(solution)/shard_map/ppermute | solution.py:176
  74.0 2.3 %collective-permute-start.6 = (bf16[2,128,256]{2,1,0:T(8,128)(2,1)S(1)}, bf16[2,128,256]{2,1,0:T(8,128)(2,1)S(1)}, u32[]{:S(2)}, u32[]{:S(2)}) collective-permute-start(bf16[2,128,256]{2,1,0:T(8,128)(2,1)S(1)} %get-tuple-element.25), channel_id=1, source_target_pairs={{0,1},{1,2},{2,3},{3,0},{4,5},{5,6},{6,7},{7,4},{8,9},{9,10},{10,1... | collective-permute-start | bytes 393224 | tf_op jit(solution)/shard_map/ppermute | solution.py:185
  76.3 3.6 %collective-permute-start.7 = (bf16[2,128,256]{2,1,0:T(8,128)(2,1)S(1)}, bf16[2,128,256]{2,1,0:T(8,128)(2,1)S(1)}, u32[]{:S(2)}, u32[]{:S(2)}) collective-permute-start(bf16[2,128,256]{2,1,0:T(8,128)(2,1)S(1)} %get-tuple-element.26), channel_id=1, source_target_pairs={{0,2},{1,3},{2,0},{3,1},{4,6},{5,7},{6,4},{7,5},{8,10},{9,11},{10,... | collective-permute-start | bytes 393224 | tf_op jit(solution)/shard_map/ppermute | solution.py:185
  79.9 3.1 %collective-permute-start.8 = (bf16[2,128,256]{2,1,0:T(8,128)(2,1)S(1)}, bf16[2,128,256]{2,1,0:T(8,128)(2,1)S(1)}, u32[]{:S(2)}, u32[]{:S(2)}) collective-permute-start(bf16[2,128,256]{2,1,0:T(8,128)(2,1)S(1)} %get-tuple-element.27), channel_id=1, source_target_pairs={{0,3},{1,0},{2,1},{3,2},{4,7},{5,4},{6,5},{7,6},{8,11},{9,8},{10,9... | collective-permute-start | bytes 393224 | tf_op jit(solution)/shard_map/ppermute | solution.py:185
  83.0 3.3 %collective-permute-done.5 = bf16[4,64,256]{2,1,0:T(8,128)(2,1)S(1)} collective-permute-done((bf16[4,64,256]{2,1,0:T(8,128)(2,1)S(1)}, bf16[4,64,256]{2,1,0:T(8,128)(2,1)S(1)}, u32[]{:S(2)}, u32[]{:S(2)}) %collective-permute-start.5) | collective-permute-done | bytes 131104 | tf_op jit(solution)/shard_map/ppermute | solution.py:176
  86.3 5.4 %collective-permute-start.12 = (bf16[4,64,256]{2,1,0:T(8,128)(2,1)S(1)}, bf16[4,64,256]{2,1,0:T(8,128)(2,1)S(1)}, u32[]{:S(2)}, u32[]{:S(2)}) collective-permute-start(bf16[4,64,256]{2,1,0:T(8,128)(2,1)S(1)} %add_convert_fusion.3.after), channel_id=1, source_target_pairs={{128,256},{384,0},{256,128},{0,384},{129,257},{385,1},{257,129},{1... | collective-permute-start | bytes 393224 | tf_op jit(solution)/shard_map/ppermute | solution.py:176
  91.7 0.0 collective-permute-done.6.refs_1_
  91.8 0.0 collective-permute-done.8.refs_3_
  91.8 0.1 shard_map.95
  91.9 1.9 %collective-permute-start.9 = (bf16[2,128,256]{2,1,0:T(8,128)(2,1)S(1)}, bf16[2,128,256]{2,1,0:T(8,128)(2,1)S(1)}, u32[]{:S(2)}, u32[]{:S(2)}) collective-permute-start(bf16[2,128,256]{2,1,0:T(8,128)(2,1)S(1)} %get-tuple-element.29), channel_id=1, source_target_pairs={{0,4},{4,8},{8,12},{12,0},{1,5},{5,9},{9,13},{13,1},{2,6},{6,10},{... | collective-permute-start | bytes 393224 | tf_op jit(solution)/shard_map/ppermute | solution.py:185
  93.8 6.0 %collective-permute-start.10 = (bf16[2,128,256]{2,1,0:T(8,128)(2,1)S(1)}, bf16[2,128,256]{2,1,0:T(8,128)(2,1)S(1)}, u32[]{:S(2)}, u32[]{:S(2)}) collective-permute-start(bf16[2,128,256]{2,1,0:T(8,128)(2,1)S(1)} %get-tuple-element.30), channel_id=1, source_target_pairs={{0,8},{4,12},{8,0},{12,4},{1,9},{5,13},{9,1},{13,5},{2,10},{6,14},... | collective-permute-start | bytes 393224 | tf_op jit(solution)/shard_map/ppermute | solution.py:185
  99.9 1.9 %collective-permute-start.11 = (bf16[2,128,256]{2,1,0:T(8,128)(2,1)S(1)}, bf16[2,128,256]{2,1,0:T(8,128)(2,1)S(1)}, u32[]{:S(2)}, u32[]{:S(2)}) collective-permute-start(bf16[2,128,256]{2,1,0:T(8,128)(2,1)S(1)} %get-tuple-element.31), channel_id=1, source_target_pairs={{0,12},{4,0},{8,4},{12,8},{1,13},{5,1},{9,5},{13,9},{2,14},{6,2},{... | collective-permute-start | bytes 393224 | tf_op jit(solution)/shard_map/ppermute | solution.py:185
  101.9 11.4 %all-gather = bf16[16,64,256]{2,1,0:T(8,128)(2,1)S(1)} all-gather(bf16[4,64,256]{2,1,0:T(8,128)(2,1)S(1)} %add_convert_fusion.1), channel_id=2, replica_groups=mesh['zh'=4,'x'=4,'core'=2,'ri'=4,'rj'=4] {'x'}, dimensions={0}, use_global_device_ids=true | all-gather | bytes 655360 | tf_op jit(solution)/shard_map/all_gather | solution.py:213
  113.3 5.9 %collective-permute-start.13 = (bf16[4,4,64,256]{3,2,1,0:T(8,128)(2,1)S(1)}, bf16[4,4,64,256]{3,2,1,0:T(8,128)(2,1)S(1)}, u32[]{:S(2)}, u32[]{:S(2)}) collective-permute-start(bf16[4,4,64,256]{3,2,1,0:T(8,128)(2,1)S(1)} %bitcast.13), channel_id=1, source_target_pairs={{0,16},{16,0},{1,17},{17,1},{2,18},{18,2},{3,19},{19,3},{4,20},{20... | collective-permute-start | bytes 1572872 | tf_op jit(solution)/shard_map/ppermute | solution.py:176
  119.2 1.0 shard_map.96.refs_1_
  120.2 0.0 collective-permute-done.11
  120.2 0.1 add_convert_fusion.2
  120.3 0.7 slice_bitcast_fusion
  121.0 1.0 shard_map.97
  (18 shorter events, 0.1 us)
Async XLA Ops:
  0.6 35.3 %copy-start.1 = (bf16[2,256,64]{1,2,0:T(8,128)(2,1)S(1)}, bf16[2,256,64]{1,2,0:T(8,128)(2,1)}, u32[]{:S(2)}) copy-start(bf16[2,256,64]{1,2,0:T(8,128)(2,1)} %param.11) | copy-start | bytes 196612
  0.6 35.3 %copy-start.2 = (bf16[2,256,64]{1,2,0:T(8,128)(2,1)S(1)}, bf16[2,256,64]{1,2,0:T(8,128)(2,1)}, u32[]{:S(2)}) copy-start(bf16[2,256,64]{1,2,0:T(8,128)(2,1)} %param.10) | copy-start | bytes 196612
  0.7 35.3 %copy-start = (bf16[2,256,64]{1,2,0:T(8,128)(2,1)S(1)}, bf16[2,256,64]{1,2,0:T(8,128)(2,1)}, u32[]{:S(2)}) copy-start(bf16[2,256,64]{1,2,0:T(8,128)(2,1)} %param.6) | copy-start | bytes 196612
  1.6 0.7 collective-permute-start
  2.3 33.6 %all-to-all-start = ((bf16[8,256,256]{2,1,0:T(8,128)(2,1)}), bf16[8,256,256]{2,1,0:T(8,128)(2,1)S(1)}, u32[]{:S(2)}, u32[]{:S(2)}) async-start(bf16[8,256,256]{2,1,0:T(8,128)(2,1)} %param.9), calls=%async_computation | async-start | bytes 2097152 | tf_op jit(solution)/shard_map/all_to_all | solution.py:200
  19.3 10.4 %collective-permute-start.3 = (bf16[2,128,256]{2,1,0:T(8,128)(2,1)S(1)}, bf16[2,128,256]{2,1,0:T(8,128)(2,1)S(1)}, u32[]{:S(2)}, u32[]{:S(2)}) collective-permute-start(bf16[2,128,256]{2,1,0:T(8,128)(2,1)S(1)} %collective-permute-done.kv0), channel_id=1, source_target_pairs={{0,12},{4,0},{8,4},{12,8},{1,13},{5,1},{9,5},{13,9},{2,14},{6,2},{... | collective-permute-start | bytes 393224 | tf_op jit(solution)/shard_map/ppermute | solution.py:185
  25.6 10.3 %collective-permute-start.2 = (bf16[2,128,256]{2,1,0:T(8,128)(2,1)S(1)}, bf16[2,128,256]{2,1,0:T(8,128)(2,1)S(1)}, u32[]{:S(2)}, u32[]{:S(2)}) collective-permute-start(bf16[2,128,256]{2,1,0:T(8,128)(2,1)S(1)} %collective-permute-done.kv0), channel_id=1, source_target_pairs={{0,8},{4,12},{8,0},{12,4},{1,9},{5,13},{9,1},{13,5},{2,10},{6,14},... | collective-permute-start | bytes 393224 | tf_op jit(solution)/shard_map/ppermute | solution.py:185
  27.6 8.4 %collective-permute-start.1 = (bf16[2,128,256]{2,1,0:T(8,128)(2,1)S(1)}, bf16[2,128,256]{2,1,0:T(8,128)(2,1)S(1)}, u32[]{:S(2)}, u32[]{:S(2)}) collective-permute-start(bf16[2,128,256]{2,1,0:T(8,128)(2,1)S(1)} %collective-permute-done.kv0), channel_id=1, source_target_pairs={{0,4},{4,8},{8,12},{12,0},{1,5},{5,9},{9,13},{13,1},{2,6},{6,10},{... | collective-permute-start | bytes 393224 | tf_op jit(solution)/shard_map/ppermute | solution.py:185
  41.7 6.3 %collective-permute-start.4 = (bf16[16,64,256]{2,1,0:T(8,128)(2,1)S(1)}, bf16[16,64,256]{2,1,0:T(8,128)(2,1)S(1)}, u32[]{:S(2)}, u32[]{:S(2)}) collective-permute-start(bf16[16,64,256]{2,1,0:T(8,128)(2,1)S(1)} %get-tuple-element.22), channel_id=1, source_target_pairs={{0,16},{16,0},{1,17},{17,1},{2,18},{18,2},{3,19},{19,3},{4,20},{20... | collective-permute-start | bytes 1572872 | tf_op jit(solution)/shard_map/ppermute | solution.py:176
  65.1 21.2 %collective-permute-start.5 = (bf16[4,64,256]{2,1,0:T(8,128)(2,1)S(1)}, bf16[4,64,256]{2,1,0:T(8,128)(2,1)S(1)}, u32[]{:S(2)}, u32[]{:S(2)}) collective-permute-start(bf16[4,64,256]{2,1,0:T(8,128)(2,1)S(1)} %reduce_sum.12.after), channel_id=1, source_target_pairs={{0,128},{256,384},{128,0},{384,256},{1,129},{257,385},{129,1},{385... | collective-permute-start | bytes 393224 | tf_op jit(solution)/shard_map/ppermute | solution.py:176
  74.0 17.8 %collective-permute-start.6 = (bf16[2,128,256]{2,1,0:T(8,128)(2,1)S(1)}, bf16[2,128,256]{2,1,0:T(8,128)(2,1)S(1)}, u32[]{:S(2)}, u32[]{:S(2)}) collective-permute-start(bf16[2,128,256]{2,1,0:T(8,128)(2,1)S(1)} %get-tuple-element.25), channel_id=1, source_target_pairs={{0,1},{1,2},{2,3},{3,0},{4,5},{5,6},{6,7},{7,4},{8,9},{9,10},{10,1... | collective-permute-start | bytes 393224 | tf_op jit(solution)/shard_map/ppermute | solution.py:185
  76.3 15.5 %collective-permute-start.7 = (bf16[2,128,256]{2,1,0:T(8,128)(2,1)S(1)}, bf16[2,128,256]{2,1,0:T(8,128)(2,1)S(1)}, u32[]{:S(2)}, u32[]{:S(2)}) collective-permute-start(bf16[2,128,256]{2,1,0:T(8,128)(2,1)S(1)} %get-tuple-element.26), channel_id=1, source_target_pairs={{0,2},{1,3},{2,0},{3,1},{4,6},{5,7},{6,4},{7,5},{8,10},{9,11},{10,... | collective-permute-start | bytes 393224 | tf_op jit(solution)/shard_map/ppermute | solution.py:185
  79.9 11.9 %collective-permute-start.8 = (bf16[2,128,256]{2,1,0:T(8,128)(2,1)S(1)}, bf16[2,128,256]{2,1,0:T(8,128)(2,1)S(1)}, u32[]{:S(2)}, u32[]{:S(2)}) collective-permute-start(bf16[2,128,256]{2,1,0:T(8,128)(2,1)S(1)} %get-tuple-element.27), channel_id=1, source_target_pairs={{0,3},{1,0},{2,1},{3,2},{4,7},{5,4},{6,5},{7,6},{8,11},{9,8},{10,9... | collective-permute-start | bytes 393224 | tf_op jit(solution)/shard_map/ppermute | solution.py:185
  86.3 15.5 %collective-permute-start.12 = (bf16[4,64,256]{2,1,0:T(8,128)(2,1)S(1)}, bf16[4,64,256]{2,1,0:T(8,128)(2,1)S(1)}, u32[]{:S(2)}, u32[]{:S(2)}) collective-permute-start(bf16[4,64,256]{2,1,0:T(8,128)(2,1)S(1)} %add_convert_fusion.3.after), channel_id=1, source_target_pairs={{128,256},{384,0},{256,128},{0,384},{129,257},{385,1},{257,129},{1... | collective-permute-start | bytes 393224 | tf_op jit(solution)/shard_map/ppermute | solution.py:176
  91.9 28.3 %collective-permute-start.9 = (bf16[2,128,256]{2,1,0:T(8,128)(2,1)S(1)}, bf16[2,128,256]{2,1,0:T(8,128)(2,1)S(1)}, u32[]{:S(2)}, u32[]{:S(2)}) collective-permute-start(bf16[2,128,256]{2,1,0:T(8,128)(2,1)S(1)} %get-tuple-element.29), channel_id=1, source_target_pairs={{0,4},{4,8},{8,12},{12,0},{1,5},{5,9},{9,13},{13,1},{2,6},{6,10},{... | collective-permute-start | bytes 393224 | tf_op jit(solution)/shard_map/ppermute | solution.py:185
  93.8 26.4 %collective-permute-start.10 = (bf16[2,128,256]{2,1,0:T(8,128)(2,1)S(1)}, bf16[2,128,256]{2,1,0:T(8,128)(2,1)S(1)}, u32[]{:S(2)}, u32[]{:S(2)}) collective-permute-start(bf16[2,128,256]{2,1,0:T(8,128)(2,1)S(1)} %get-tuple-element.30), channel_id=1, source_target_pairs={{0,8},{4,12},{8,0},{12,4},{1,9},{5,13},{9,1},{13,5},{2,10},{6,14},... | collective-permute-start | bytes 393224 | tf_op jit(solution)/shard_map/ppermute | solution.py:185
  99.9 20.3 %collective-permute-start.11 = (bf16[2,128,256]{2,1,0:T(8,128)(2,1)S(1)}, bf16[2,128,256]{2,1,0:T(8,128)(2,1)S(1)}, u32[]{:S(2)}, u32[]{:S(2)}) collective-permute-start(bf16[2,128,256]{2,1,0:T(8,128)(2,1)S(1)} %get-tuple-element.31), channel_id=1, source_target_pairs={{0,12},{4,0},{8,4},{12,8},{1,13},{5,1},{9,5},{13,9},{2,14},{6,2},{... | collective-permute-start | bytes 393224 | tf_op jit(solution)/shard_map/ppermute | solution.py:185
  113.3 7.7 %collective-permute-start.13 = (bf16[4,4,64,256]{3,2,1,0:T(8,128)(2,1)S(1)}, bf16[4,4,64,256]{3,2,1,0:T(8,128)(2,1)S(1)}, u32[]{:S(2)}, u32[]{:S(2)}) collective-permute-start(bf16[4,4,64,256]{3,2,1,0:T(8,128)(2,1)S(1)} %bitcast.13), channel_id=1, source_target_pairs={{0,16},{16,0},{1,17},{17,1},{2,18},{18,2},{3,19},{19,3},{4,20},{20... | collective-permute-start | bytes 1572872 | tf_op jit(solution)/shard_map/ppermute | solution.py:176

commit v7 on v3

--- a/solution.py
+++ b/solution.py
@@ -22,7 +22,7 @@
 
 def attention_kernel(
     q_ref, g_ref, o_ref, kv0, kv1, kv2, kv3, bias,
-    send, keep, dq_ref, d0, d1, d2, d3,
+    send, keep, dq_ref, dkv_ref,
     stack, wide, raw, low, inner,
 ):
     ri, core = lax.axis_index("ri"), lax.axis_index("core")
@@ -74,10 +74,11 @@
                 out[quarter * N + b, within, :] = total[:, t * ROWS : (t + 1) * ROWS]
 
     for s in range(2):
-        for t, out in enumerate((d0, d1, d2, d3)):
+        for t, b in enumerate(blocks):
             at = slice(t * ROWS, (t + 1) * ROWS)
             grads = lax.dot_general(wide[s], low[s, :, at], NN, preferred_element_type=F32)
-            out[s] = jnp.where(channel < 2, grads * SCALE, grads).astype(BF)
+            grads = jnp.where(channel < 2, grads * SCALE, grads)
+            dkv_ref[b, s] = grads.astype(BF)
         grads = None
         for t in range(N):
             at = slice(t * ROWS, (t + 1) * ROWS)
@@ -94,12 +95,12 @@
     seqs = q.shape[0]
     vmem = pl.BlockSpec(memory_space=pltpu.VMEM)
     piece = jax.ShapeDtypeStruct((N * N, 64, ROWS), BF)
-    grads = jax.ShapeDtypeStruct((seqs, LANES, ROWS), BF)
+    grads = jax.ShapeDtypeStruct((N, seqs, LANES, ROWS), BF)
     return pl.pallas_call(
         attention_kernel,
-        out_shape=(piece, piece, jax.ShapeDtypeStruct(q.shape, BF), *[grads] * N),
+        out_shape=(piece, piece, jax.ShapeDtypeStruct(q.shape, BF), grads),
         in_specs=[vmem] * 8,
-        out_specs=(vmem,) * 7,
+        out_specs=(vmem,) * 4,
         scratch_shapes=[
             pltpu.VMEM((seqs, 4 * ROWS, LANES), BF),
             pltpu.VMEM((seqs, LANES, 4 * ROWS), BF),
@@ -165,24 +166,20 @@
     ]
     bias = lax.all_to_all(pair_bias, "rj", 0, 0, tiled=True).reshape(N, 2, ROWS, ROWS)
 
-    send, keep, dq, *parts = attention(q, g, o, kvs, bias)
-
-    def home(part, t):
-        return lax.ppermute(
-            part, ("ri", "rj"), [((b + t) % N * N + a, a * N + b) for a, b in grid]
-        )
+    send, keep, dq, dkv = attention(q, g, o, kvs, bias)
 
     total = add(keep, swap(send, "core", [(0, 1)]))
-    back = [home(part, t) for t, part in enumerate(parts)]
     spread = lax.all_to_all(total, ("x", "rj"), 0, 0, tiled=True)
-    spread, *back = lax.optimization_barrier((spread, *back))
     total = jnp.sum(spread.reshape(N, N, 64, ROWS).astype(F32), axis=0).astype(BF)
-    for pairs in ([(0, 1), (2, 3)], [(1, 2), (3, 0)]):
-        total = add(total, swap(total, "zh", pairs))
-    mine = lax.all_gather(total, "x", axis=0)
+    total = add(total, swap(total, "zh", [(0, 1), (2, 3)]))
+    back = lax.psum_scatter(dkv.reshape(-1, ROWS), "ri", scatter_dimension=0, tiled=True)
+    total, back = lax.optimization_barrier((total, back))
+    back = lax.ppermute(back, ("ri", "rj"), [(a * N + b, b * N + a) for a, b in grid])
+    total = add(total, swap(total, "zh", [(1, 2), (3, 0)]))
+    mine, back = lax.optimization_barrier((lax.all_gather(total, "x", axis=0), back))
     bias_grad = place(swap(mine, "core", [(0, 1)]), place(mine))
 
-    kv_grad = sum(x.astype(F32) for x in back).astype(BF)
+    kv_grad = back.reshape(dkv.shape[1:])
     width = k.shape[1]
     grads = (dq, kv_grad[:, :width], kv_grad[:, width:])
     return *(jnp.swapaxes(x, 1, 2) for x in grads), bias_grad

time: 143 us -> 133 us (0.930)
  the two profiles are of different devices: /device:TPU:17 before, /device:TPU:161 now
where the time goes in v7:
time: 133 us
  starting transfers between devices  41.4 us (31%)
  waiting for transfers between devices  37.4 us (28%)
  blocking collectives  30.8 us (23%)
  between operations  14.2 us (11%)
  Pallas kernels  7.82 us (6%)
    ppermute x4, waiting for transfers between devices, swap(): lax.ppermute(x, axis, [(a, b) for a, b in pairs] + [(b, a) for a, b in pa...  27.8 us
    ppermute x4, starting transfers between devices, swap(): lax.ppermute(x, axis, [(a, b) for a, b in pairs] + [(b, a) for a, b in pa...  19.4 us
    all_to_all x1, blocking collectives, body(): spread = lax.all_to_all(total, ('x', 'rj'), 0, 0, tiled=True)  16.3 us
    ppermute x4, starting transfers between devices, body(): lax.ppermute(kv, ('ri', 'rj'), [(a * N + b, (b + t) % N * N + a) for a, b...  15.7 us
    all_gather x1, blocking collectives, body(): lax.all_gather(total, 'x', axis=0)  14.5 us
    pallas_call x1, Pallas kernels, attention(): pl.pallas_call(attention_kernel, out_shape=(piece, piece, jax.ShapeDtypeS...  5.79 us
    ppermute x4, waiting for transfers between devices, body(): lax.ppermute(kv, ('ri', 'rj'), [(a * N + b, (b + t) % N * N + a) for a, b...  4.95 us
    reduce_scatter x1, waiting for transfers between devices, body(): lax.psum_scatter(dkv.reshape(-1, ROWS), 'ri', scatter_dimension=0, tiled=...  4.6 us
  transfers between devices with their start and end apart: 11, of which 6 were waited for; matrix products, arithmetic and copies ran while one was open for 1% of the time, Pallas kernels for 1%

profile of v7, /device:TPU:161, one launch (start us, length us, event | category | flops | bytes accessed | tf_op | source)
XLA Modules:
  0.0 132.6 jit_solution(6921546969662544331)
XLA Ops:
  7.2 4.3 %all-to-all-start = ((bf16[8,256,256]{2,1,0:T(8,128)(2,1)}), bf16[8,256,256]{2,1,0:T(8,128)(2,1)S(1)}, u32[]{:S(2)}, u32[]{:S(2)}) async-start(bf16[8,256,256]{2,1,0:T(8,128)(2,1)} %param.9), calls=%async_computation | async-start | bytes 2097152 | tf_op jit(solution)/shard_map/all_to_all | solution.py:167
  11.5 0.0 reduce-scatter.2.cloned.1.call-start
  11.6 6.1 %collective-permute-start.3 = (bf16[2,128,256]{2,1,0:T(8,128)(2,1)S(1)}, bf16[2,128,256]{2,1,0:T(8,128)(2,1)S(1)}, u32[]{:S(2)}, u32[]{:S(2)}) collective-permute-start(bf16[2,128,256]{2,1,0:T(8,128)(2,1)S(1)} %pad_maximum_fusion), channel_id=1, source_target_pairs={{0,12},{1,0},{2,4},{3,8},{4,13},{5,1},{6,5},{7,9},{8,14},{9,2},{10... | collective-permute-start | bytes 393224 | tf_op jit(solution)/shard_map/ppermute | solution.py:164
  17.7 1.9 %collective-permute-start.2 = (bf16[2,128,256]{2,1,0:T(8,128)(2,1)S(1)}, bf16[2,128,256]{2,1,0:T(8,128)(2,1)S(1)}, u32[]{:S(2)}, u32[]{:S(2)}) collective-permute-start(bf16[2,128,256]{2,1,0:T(8,128)(2,1)S(1)} %pad_maximum_fusion), channel_id=1, source_target_pairs={{0,8},{1,12},{2,0},{3,4},{4,9},{5,13},{6,1},{7,5},{8,10},{9,14},{1... | collective-permute-start | bytes 393224 | tf_op jit(solution)/shard_map/ppermute | solution.py:164
  19.6 2.6 %collective-permute-start.1 = (bf16[2,128,256]{2,1,0:T(8,128)(2,1)S(1)}, bf16[2,128,256]{2,1,0:T(8,128)(2,1)S(1)}, u32[]{:S(2)}, u32[]{:S(2)}) collective-permute-start(bf16[2,128,256]{2,1,0:T(8,128)(2,1)S(1)} %pad_maximum_fusion), channel_id=1, source_target_pairs={{0,4},{1,8},{2,12},{3,0},{4,5},{5,9},{6,13},{7,1},{8,6},{9,10},{10... | collective-permute-start | bytes 393224 | tf_op jit(solution)/shard_map/ppermute | solution.py:164
  22.2 5.1 %collective-permute-start = (bf16[2,128,256]{2,1,0:T(8,128)(2,1)S(1)}, bf16[2,128,256]{2,1,0:T(8,128)(2,1)S(1)}, u32[]{:S(2)}, u32[]{:S(2)}) collective-permute-start(bf16[2,128,256]{2,1,0:T(8,128)(2,1)S(1)} %pad_maximum_fusion), channel_id=1, source_target_pairs={{0,0},{1,4},{2,8},{3,12},{4,1},{5,5},{6,9},{7,13},{8,2},{9,6},{10,... | collective-permute-start | bytes 393224 | tf_op jit(solution)/shard_map/ppermute | solution.py:164
  27.3 0.0 collective-permute-done.3.kv3
  27.3 1.8 %collective-permute-done.2.kv2 = bf16[2,128,256]{2,1,0:T(8,128)(2,1)S(1)} collective-permute-done((bf16[2,128,256]{2,1,0:T(8,128)(2,1)S(1)}, bf16[2,128,256]{2,1,0:T(8,128)(2,1)S(1)}, u32[]{:S(2)}, u32[]{:S(2)}) %collective-permute-start.2) | collective-permute-done | bytes 131104 | tf_op jit(solution)/shard_map/ppermute | solution.py:164
  29.1 0.0 collective-permute-done.1.kv1
  29.1 3.2 %collective-permute-done.kv0 = bf16[2,128,256]{2,1,0:T(8,128)(2,1)S(1)} collective-permute-done((bf16[2,128,256]{2,1,0:T(8,128)(2,1)S(1)}, bf16[2,128,256]{2,1,0:T(8,128)(2,1)S(1)}, u32[]{:S(2)}, u32[]{:S(2)}) %collective-permute-start) | collective-permute-done | bytes 131104 | tf_op jit(solution)/shard_map/ppermute | solution.py:164
  32.3 0.0 all-to-all-done
  32.3 0.0 copy-done.2
  32.3 5.8 %shard_map.93 = (bf16[16,64,256]{2,1,0:T(8,128)(2,1)S(1)}, bf16[16,64,256]{2,1,0:T(8,128)(2,1)S(1)}, bf16[2,64,256]{2,1,0:T(8,128)(2,1)}, bf16[4,2,128,256]{3,2,1,0:T(8,128)(2,1)}) custom-call(bf16[2,64,256]{2,1,0:T(8,128)(2,1)S(1)} %bitcast.18, bf16[2,64,256]{2,1,0:T(8,128)(2,1)S(1)} %bitcast.19, bf16[2,64,256]{2,1,0:T(8,128)(2,1)S(1)} %bitcast.20, ...), custom_call_target="tpu_custom_call" | custom-call | flops 335544320 | bytes 6291456 | tf_op jit(solution)/shard_map/pallas_call | solution.py:99
  38.1 7.1 %collective-permute-start.4 = (bf16[16,64,256]{2,1,0:T(8,128)(2,1)S(1)}, bf16[16,64,256]{2,1,0:T(8,128)(2,1)S(1)}, u32[]{:S(2)}, u32[]{:S(2)}) collective-permute-start(bf16[16,64,256]{2,1,0:T(8,128)(2,1)S(1)} %get-tuple-element.14), channel_id=1, source_target_pairs={{0,16},{16,0},{1,17},{17,1},{2,18},{18,2},{3,19},{19,3},{4,20},{20... | collective-permute-start | bytes 1572872 | tf_op jit(solution)/shard_map/ppermute | solution.py:148
  45.1 0.0 reduce-scatter.2.cloned.1.call-update
  45.1 1.5 %collective-permute-done.4 = bf16[16,64,256]{2,1,0:T(8,128)(2,1)S(1)} collective-permute-done((bf16[16,64,256]{2,1,0:T(8,128)(2,1)S(1)}, bf16[16,64,256]{2,1,0:T(8,128)(2,1)S(1)}, u32[]{:S(2)}, u32[]{:S(2)}) %collective-permute-start.4) | collective-permute-done | bytes 524320 | tf_op jit(solution)/shard_map/ppermute | solution.py:148
  46.6 0.2 add_convert_fusion
  46.8 16.3 %all_to_all.10 = bf16[16,64,256]{2,1,0:T(8,128)(2,1)S(1)} all-to-all(bf16[16,64,256]{2,1,0:T(8,128)(2,1)S(1)} %add_convert_fusion), channel_id=1, replica_groups=mesh['zh'=4,'x'=4,'core'=2,'ri'=4,'rj'=4] {'x','rj'}, dimensions={0} | all-to-all | bytes 1048576 | tf_op jit(solution)/shard_map/all_to_all | solution.py:172
  63.1 0.1 reduce_sum.12
  63.2 1.9 %collective-permute-start.5 = (bf16[4,64,256]{2,1,0:T(8,128)(2,1)S(1)}, bf16[4,64,256]{2,1,0:T(8,128)(2,1)S(1)}, u32[]{:S(2)}, u32[]{:S(2)}) collective-permute-start(bf16[4,64,256]{2,1,0:T(8,128)(2,1)S(1)} %reduce_sum.12), channel_id=1, source_target_pairs={{0,128},{256,384},{128,0},{384,256},{1,129},{257,385},{129,1},{385... | collective-permute-start | bytes 393224 | tf_op jit(solution)/shard_map/ppermute | solution.py:148
  65.1 14.6 %collective-permute-done.5 = bf16[4,64,256]{2,1,0:T(8,128)(2,1)S(1)} collective-permute-done((bf16[4,64,256]{2,1,0:T(8,128)(2,1)S(1)}, bf16[4,64,256]{2,1,0:T(8,128)(2,1)S(1)}, u32[]{:S(2)}, u32[]{:S(2)}) %collective-permute-start.5) | collective-permute-done | bytes 131104 | tf_op jit(solution)/shard_map/ppermute | solution.py:148
  79.7 4.6 %reduce-scatter.2.cloned.1.call-done = bf16[256,256]{1,0:T(8,128)(2,1)} async-done(((bf16[1024,256]{1,0:T(8,128)(2,1)}), bf16[256,256]{1,0:T(8,128)(2,1)}) %reduce-scatter.2.cloned.1.call-update) | async-done | bytes 131088 | tf_op jit(solution)/shard_map/reduce_scatter | solution.py:175
  84.3 4.4 %collective-permute-start.6 = (bf16[4,64,256]{2,1,0:T(8,128)(2,1)S(1)}, bf16[4,64,256]{2,1,0:T(8,128)(2,1)S(1)}, u32[]{:S(2)}, u32[]{:S(2)}) collective-permute-start(bf16[4,64,256]{2,1,0:T(8,128)(2,1)S(1)} %add_convert_fusion.2), channel_id=1, source_target_pairs={{128,256},{384,0},{256,128},{0,384},{129,257},{385,1},{257,129},{1... | collective-permute-start | bytes 393224 | tf_op jit(solution)/shard_map/ppermute | solution.py:148
  88.8 1.9 %collective-permute-start.7 = (bf16[256,256]{1,0:T(8,128)(2,1)}, bf16[256,256]{1,0:T(8,128)(2,1)S(1)}, u32[]{:S(2)}, u32[]{:S(2)}) collective-permute-start(bf16[256,256]{1,0:T(8,128)(2,1)} %reduce-scatter.2.cloned.1.call-done), channel_id=1, source_target_pairs={{0,0},{1,4},{2,8},{3,12},{4,1},{5,5},{6,9},{7,13},{8,2},{9,6},{10,... | collective-permute-start | bytes 393224 | tf_op jit(solution)/shard_map/ppermute | solution.py:177
  90.7 11.8 %collective-permute-done.6 = bf16[4,64,256]{2,1,0:T(8,128)(2,1)S(1)} collective-permute-done((bf16[4,64,256]{2,1,0:T(8,128)(2,1)S(1)}, bf16[4,64,256]{2,1,0:T(8,128)(2,1)S(1)}, u32[]{:S(2)}, u32[]{:S(2)}) %collective-permute-start.6) | collective-permute-done | bytes 131104 | tf_op jit(solution)/shard_map/ppermute | solution.py:148
  102.5 14.5 %all-gather = bf16[16,64,256]{2,1,0:T(8,128)(2,1)S(1)} all-gather(bf16[4,64,256]{2,1,0:T(8,128)(2,1)S(1)} %add_convert_fusion.1), channel_id=2, replica_groups=mesh['zh'=4,'x'=4,'core'=2,'ri'=4,'rj'=4] {'x'}, dimensions={0}, use_global_device_ids=true | all-gather | bytes 655360 | tf_op jit(solution)/shard_map/all_gather | solution.py:179
  117.0 0.0 collective-permute-done.7
  117.0 6.0 %collective-permute-start.8 = (bf16[4,4,64,256]{3,2,1,0:T(8,128)(2,1)S(1)}, bf16[4,4,64,256]{3,2,1,0:T(8,128)(2,1)S(1)}, u32[]{:S(2)}, u32[]{:S(2)}) collective-permute-start(bf16[4,4,64,256]{3,2,1,0:T(8,128)(2,1)S(1)} %bitcast.15), channel_id=1, source_target_pairs={{0,16},{16,0},{1,17},{17,1},{2,18},{18,2},{3,19},{19,3},{4,20},{20... | collective-permute-start | bytes 1572872 | tf_op jit(solution)/shard_map/ppermute | solution.py:148
  123.1 1.0 shard_map.94.refs_1_
  124.1 0.7 slice_bitcast_fusion
  124.7 0.0 collective-permute-done.8.refs_0_
  124.7 1.0 shard_map.95
  (12 shorter events, 0.1 us)
Async XLA Ops:
  7.2 4.4 %copy-start.3 = (bf16[2,256,64]{1,2,0:T(8,128)(2,1)S(1)}, bf16[2,256,64]{1,2,0:T(8,128)(2,1)}, u32[]{:S(2)}) copy-start(bf16[2,256,64]{1,2,0:T(8,128)(2,1)} %param.8) | copy-start | bytes 196612
  7.2 4.4 %copy-start.4 = (bf16[2,256,64]{1,2,0:T(8,128)(2,1)S(1)}, bf16[2,256,64]{1,2,0:T(8,128)(2,1)}, u32[]{:S(2)}) copy-start(bf16[2,256,64]{1,2,0:T(8,128)(2,1)} %param.7) | copy-start | bytes 196612
  7.2 25.1 %copy-start.1 = (bf16[2,256,64]{1,2,0:T(8,128)(2,1)S(1)}, bf16[2,256,64]{1,2,0:T(8,128)(2,1)}, u32[]{:S(2)}) copy-start(bf16[2,256,64]{1,2,0:T(8,128)(2,1)} %param.11) | copy-start | bytes 196612
  7.2 25.1 %copy-start.2 = (bf16[2,256,64]{1,2,0:T(8,128)(2,1)S(1)}, bf16[2,256,64]{1,2,0:T(8,128)(2,1)}, u32[]{:S(2)}) copy-start(bf16[2,256,64]{1,2,0:T(8,128)(2,1)} %param.10) | copy-start | bytes 196612
  7.2 25.1 %copy-start = (bf16[2,256,64]{1,2,0:T(8,128)(2,1)S(1)}, bf16[2,256,64]{1,2,0:T(8,128)(2,1)}, u32[]{:S(2)}) copy-start(bf16[2,256,64]{1,2,0:T(8,128)(2,1)} %param.6) | copy-start | bytes 196612
  7.2 25.0 %all-to-all-start = ((bf16[8,256,256]{2,1,0:T(8,128)(2,1)}), bf16[8,256,256]{2,1,0:T(8,128)(2,1)S(1)}, u32[]{:S(2)}, u32[]{:S(2)}) async-start(bf16[8,256,256]{2,1,0:T(8,128)(2,1)} %param.9), calls=%async_computation | async-start | bytes 2097152 | tf_op jit(solution)/shard_map/all_to_all | solution.py:167
  11.5 72.8 %reduce-scatter.2.cloned.1.call-start = ((), (), s32[]{:S(2)}) async-start(), calls=%async_computation.3 | async-start | bytes 655360 | tf_op jit(solution)/shard_map/reduce_scatter | solution.py:175
  11.6 15.7 %collective-permute-start.3 = (bf16[2,128,256]{2,1,0:T(8,128)(2,1)S(1)}, bf16[2,128,256]{2,1,0:T(8,128)(2,1)S(1)}, u32[]{:S(2)}, u32[]{:S(2)}) collective-permute-start(bf16[2,128,256]{2,1,0:T(8,128)(2,1)S(1)} %pad_maximum_fusion), channel_id=1, source_target_pairs={{0,12},{1,0},{2,4},{3,8},{4,13},{5,1},{6,5},{7,9},{8,14},{9,2},{10... | collective-permute-start | bytes 393224 | tf_op jit(solution)/shard_map/ppermute | solution.py:164
  17.7 11.4 %collective-permute-start.2 = (bf16[2,128,256]{2,1,0:T(8,128)(2,1)S(1)}, bf16[2,128,256]{2,1,0:T(8,128)(2,1)S(1)}, u32[]{:S(2)}, u32[]{:S(2)}) collective-permute-start(bf16[2,128,256]{2,1,0:T(8,128)(2,1)S(1)} %pad_maximum_fusion), channel_id=1, source_target_pairs={{0,8},{1,12},{2,0},{3,4},{4,9},{5,13},{6,1},{7,5},{8,10},{9,14},{1... | collective-permute-start | bytes 393224 | tf_op jit(solution)/shard_map/ppermute | solution.py:164
  19.6 9.5 %collective-permute-start.1 = (bf16[2,128,256]{2,1,0:T(8,128)(2,1)S(1)}, bf16[2,128,256]{2,1,0:T(8,128)(2,1)S(1)}, u32[]{:S(2)}, u32[]{:S(2)}) collective-permute-start(bf16[2,128,256]{2,1,0:T(8,128)(2,1)S(1)} %pad_maximum_fusion), channel_id=1, source_target_pairs={{0,4},{1,8},{2,12},{3,0},{4,5},{5,9},{6,13},{7,1},{8,6},{9,10},{10... | collective-permute-start | bytes 393224 | tf_op jit(solution)/shard_map/ppermute | solution.py:164
  22.2 10.1 %collective-permute-start = (bf16[2,128,256]{2,1,0:T(8,128)(2,1)S(1)}, bf16[2,128,256]{2,1,0:T(8,128)(2,1)S(1)}, u32[]{:S(2)}, u32[]{:S(2)}) collective-permute-start(bf16[2,128,256]{2,1,0:T(8,128)(2,1)S(1)} %pad_maximum_fusion), channel_id=1, source_target_pairs={{0,0},{1,4},{2,8},{3,12},{4,1},{5,5},{6,9},{7,13},{8,2},{9,6},{10,... | collective-permute-start | bytes 393224 | tf_op jit(solution)/shard_map/ppermute | solution.py:164
  38.1 8.6 %collective-permute-start.4 = (bf16[16,64,256]{2,1,0:T(8,128)(2,1)S(1)}, bf16[16,64,256]{2,1,0:T(8,128)(2,1)S(1)}, u32[]{:S(2)}, u32[]{:S(2)}) collective-permute-start(bf16[16,64,256]{2,1,0:T(8,128)(2,1)S(1)} %get-tuple-element.14), channel_id=1, source_target_pairs={{0,16},{16,0},{1,17},{17,1},{2,18},{18,2},{3,19},{19,3},{4,20},{20... | collective-permute-start | bytes 1572872 | tf_op jit(solution)/shard_map/ppermute | solution.py:148
  63.2 16.5 %collective-permute-start.5 = (bf16[4,64,256]{2,1,0:T(8,128)(2,1)S(1)}, bf16[4,64,256]{2,1,0:T(8,128)(2,1)S(1)}, u32[]{:S(2)}, u32[]{:S(2)}) collective-permute-start(bf16[4,64,256]{2,1,0:T(8,128)(2,1)S(1)} %reduce_sum.12), channel_id=1, source_target_pairs={{0,128},{256,384},{128,0},{384,256},{1,129},{257,385},{129,1},{385... | collective-permute-start | bytes 393224 | tf_op jit(solution)/shard_map/ppermute | solution.py:148
  84.3 18.2 %collective-permute-start.6 = (bf16[4,64,256]{2,1,0:T(8,128)(2,1)S(1)}, bf16[4,64,256]{2,1,0:T(8,128)(2,1)S(1)}, u32[]{:S(2)}, u32[]{:S(2)}) collective-permute-start(bf16[4,64,256]{2,1,0:T(8,128)(2,1)S(1)} %add_convert_fusion.2), channel_id=1, source_target_pairs={{128,256},{384,0},{256,128},{0,384},{129,257},{385,1},{257,129},{1... | collective-permute-start | bytes 393224 | tf_op jit(solution)/shard_map/ppermute | solution.py:148
  88.8 28.3 %collective-permute-start.7 = (bf16[256,256]{1,0:T(8,128)(2,1)}, bf16[256,256]{1,0:T(8,128)(2,1)S(1)}, u32[]{:S(2)}, u32[]{:S(2)}) collective-permute-start(bf16[256,256]{1,0:T(8,128)(2,1)} %reduce-scatter.2.cloned.1.call-done), channel_id=1, source_target_pairs={{0,0},{1,4},{2,8},{3,12},{4,1},{5,5},{6,9},{7,13},{8,2},{9,6},{10,... | collective-permute-start | bytes 393224 | tf_op jit(solution)/shard_map/ppermute | solution.py:177
  117.0 7.7 %collective-permute-start.8 = (bf16[4,4,64,256]{3,2,1,0:T(8,128)(2,1)S(1)}, bf16[4,4,64,256]{3,2,1,0:T(8,128)(2,1)S(1)}, u32[]{:S(2)}, u32[]{:S(2)}) collective-permute-start(bf16[4,4,64,256]{3,2,1,0:T(8,128)(2,1)S(1)} %bitcast.15), channel_id=1, source_target_pairs={{0,16},{16,0},{1,17},{17,1},{2,18},{18,2},{3,19},{19,3},{4,20},{20... | collective-permute-start | bytes 1572872 | tf_op jit(solution)/shard_map/ppermute | solution.py:148
Sparse Core Ops, SparseCore 0:
  45.3 38.9 reduce-scatter.1

commit v8 on v4

v8 whole, which is shorter than its diff:
```python
import jax
import jax.numpy as jnp
from jax import lax
from jax.experimental import pallas as pl
from jax.experimental.pallas import tpu as pltpu
from jax.sharding import Mesh
from jax.sharding import PartitionSpec as P

HEAD = 32
SCALE = HEAD**-0.5
N = 4
ROWS = 256
KEYS = N * ROWS
LANES = 128
SEQS = 4
CHUNK = 32
UNROLL = 4
BF = jnp.bfloat16
F32 = jnp.float32
NT = (((1,), (1,)), ((), ()))
NN = (((1,), (0,)), ((), ()))


def attention_kernel(
    qgo_ref, kv0, kv1, kv2, kv3, bias,
    bias_grad, dq_ref, dkv_ref,
    stack, wide, raw, low, inner,
):
    ri, rj = lax.axis_index("ri"), lax.axis_index("rj")
    kvs = (kv0, kv1, kv2, kv3)
    blocks = [lax.rem(ri + N - t, N) for t in range(N)]
    channel = lax.broadcasted_iota(jnp.int32, (2 * HEAD, ROWS), 0) // HEAD

    for s in range(SEQS):
        for part in range(2):
            at = slice(part * ROWS, (part + 1) * ROWS)
            one = jnp.where(channel == part, qgo_ref[s, : 2 * HEAD], 0)
            wide[s, :, at] = one
            stack[s, at, :] = one.T
        dots = qgo_ref[s, HEAD : 2 * HEAD].astype(F32) * qgo_ref[s, 2 * HEAD :].astype(F32)
        sums = jnp.sum(dots, axis=0, keepdims=True)
        inner[s] = jnp.broadcast_to(sums, (LANES, ROWS)).T

    for s in range(SEQS):
        for t in range(N):
            at = slice(t * ROWS, (t + 1) * ROWS)
            raw[s, :, at] = lax.dot_general(stack[s], kvs[t][s], NN, preferred_element_type=F32)

    @pl.loop(0, ROWS // CHUNK, unroll=UNROLL)
    def _(i):
        r0 = pl.multiple_of(i * CHUNK, CHUNK)
        at_logits = pl.ds(r0, CHUNK)
        at_grads = pl.ds(pl.multiple_of(ROWS + r0, CHUNK), CHUNK)
        pair = jnp.concatenate([bias[b, at_logits, :] for b in blocks], axis=1).astype(F32)
        total = None
        for s in range(SEQS):
            logits = raw[s, at_logits, :] * SCALE + pair
            top = jnp.max(logits, axis=1, keepdims=True)
            weights = jnp.exp(logits - top)
            weights = weights * (1.0 / jnp.sum(weights, axis=1, keepdims=True))
            dots = jnp.concatenate([inner[s, at_logits, :]] * (KEYS // LANES), axis=1)
            grad = weights * (raw[s, at_grads, :] - dots)
            low[s, at_logits, :] = grad.astype(BF)
            low[s, at_grads, :] = weights.astype(BF)
            total = grad if total is None else total + grad
        total = total.astype(BF)
        quarter = i // (64 // CHUNK)
        within = pl.ds(pl.multiple_of(lax.rem(i, 64 // CHUNK) * CHUNK, CHUNK), CHUNK)
        for t, b in enumerate(blocks):
            bias_grad[quarter * N + b, within, :] = total[:, t * ROWS : (t + 1) * ROWS]

    for s in range(SEQS):
        query_grads = None
        for t, b in enumerate(blocks):
            at = slice(t * ROWS, (t + 1) * ROWS)
            grads = lax.dot_general(wide[s], low[s, :, at], NN, preferred_element_type=F32)
            grads = jnp.where(channel == 0, grads * SCALE, grads)
            dkv_ref[lax.rem(b + N - rj, N), s] = grads.astype(BF)
            term = lax.dot_general(low[s, :ROWS, at], kvs[t][s], NT, preferred_element_type=F32)
            query_grads = term if query_grads is None else query_grads + term
        dq_ref[s] = (query_grads.T[:HEAD] * SCALE).astype(BF)


def attention(qgo, kvs, bias):
    vmem = pl.BlockSpec(memory_space=pltpu.VMEM)
    return pl.pallas_call(
        attention_kernel,
        out_shape=(
            jax.ShapeDtypeStruct((N * N, 64, ROWS), BF),
            jax.ShapeDtypeStruct((SEQS, HEAD, ROWS), BF),
            jax.ShapeDtypeStruct((N, SEQS, 2 * HEAD, ROWS), BF),
        ),
        in_specs=[vmem] * 6,
        out_specs=(vmem,) * 3,
        scratch_shapes=[
            pltpu.VMEM((SEQS, 2 * ROWS, 2 * HEAD), BF),
            pltpu.VMEM((SEQS, 2 * HEAD, 2 * ROWS), BF),
            pltpu.VMEM((SEQS, 2 * ROWS, KEYS), F32),
            pltpu.VMEM((SEQS, 2 * ROWS, KEYS), BF),
            pltpu.VMEM((SEQS, ROWS, LANES), F32),
        ],
        compiler_params=pltpu.CompilerParams(vmem_limit_bytes=32 * 2**20),
        cost_estimate=pl.CostEstimate(
            flops=5 * 2 * 2**25, bytes_accessed=6 * 2**20, transcendentals=2**20
        ),
    )(qgo, *kvs, bias)


def split_kernel(after, x_ref, *outs):
    for t, out in enumerate(outs):
        out[...] = x_ref[t]


def choose_kernel(after, *refs):
    ri, rj = lax.axis_index("ri"), lax.axis_index("rj")
    for t, out in enumerate(refs[N:]):
        wanted = lax.rem(rj + 2 * N - ri - t, N)
        for source, x_ref in enumerate(refs[:N]):

            @pl.when(wanted == source)
            def _():
                out[...] = x_ref[...]


def hand_on(kernel, after, *args):
    anywhere, vmem = pl.BlockSpec(memory_space=pl.ANY), pl.BlockSpec(memory_space=pltpu.VMEM)
    return pl.pallas_call(
        kernel,
        out_shape=[jax.ShapeDtypeStruct(args[0].shape[-3:], BF)] * N,
        in_specs=[anywhere] + [vmem] * len(args),
        out_specs=[vmem] * N,
        compiler_params=pltpu.CompilerParams(vmem_limit_bytes=8 * 2**20),
        cost_estimate=pl.CostEstimate(flops=0, bytes_accessed=2**21, transcendentals=0),
    )(after, *args)


def place_kernel(first, x_ref, *refs):
    out_ref, wide, sem = refs[-3:]
    core = lax.axis_index("core")
    head = core if first else 1 - core
    copies = []
    for j in range(N):
        for x in range(N):
            at = (x * N + j) * 64
            wide[j, x * 64 : (x + 1) * 64, :] = x_ref[at : at + 64, :].astype(F32)
        copies.append(pltpu.make_async_copy(wide.at[j], out_ref.at[2 * j + head], sem.at[j]))
        copies[-1].start()
    for c in copies:
        c.wait()


def place(x, before=None):
    first = before is None
    anywhere, vmem = pl.BlockSpec(memory_space=pl.ANY), pl.BlockSpec(memory_space=pltpu.VMEM)
    return pl.pallas_call(
        lambda *refs: place_kernel(first, *refs),
        out_shape=jax.ShapeDtypeStruct((2 * N, ROWS, ROWS), F32),
        in_specs=[vmem] if first else [vmem, anywhere],
        out_specs=anywhere,
        scratch_shapes=[pltpu.VMEM((N, ROWS, ROWS), F32), pltpu.SemaphoreType.DMA((N,))],
        input_output_aliases={} if first else {1: 0},
        compiler_params=pltpu.CompilerParams(vmem_limit_bytes=8 * 2**20),
        cost_estimate=pl.CostEstimate(flops=2**18, bytes_accessed=3 * 2**19, transcendentals=0),
    )(*([x] if first else [x, before]))


def swap(x, axis, pairs):
    return lax.ppermute(x, axis, [(a, b) for a, b in pairs] + [(b, a) for a, b in pairs])


def add(a, b):
    return (a.astype(F32) + b.astype(F32)).astype(BF)


def body(query_proj, key_proj, value_proj, pair_bias, attn_output, output_grad):
    q, k, v, o, g = (
        jnp.swapaxes(x, 1, 2)
        for x in (query_proj, key_proj, value_proj, attn_output, output_grad)
    )
    grid = [(a, b) for a in range(N) for b in range(N)]

    core = lax.axis_index("core")

    def half(x, which):
        return jnp.where(which == 0, x[:, :HEAD], x[:, HEAD:])

    def halves(which):
        return jnp.concatenate([half(x, which) for x in (k, v, q, g, o)], axis=1)

    both = jnp.concatenate([halves(core), swap(halves(1 - core), "core", [(0, 1)])])
    kv, qgo = both[:, : 2 * HEAD], both[:, 2 * HEAD :]
    kvs = [
        lax.ppermute(kv, ("ri", "rj"), [(a * N + b, (b + t) % N * N + a) for a, b in grid])
        for t in range(N)
    ]
    bias = lax.dynamic_index_in_dim(pair_bias.reshape(N, 2, ROWS, ROWS), core, 1, False)
    bias = lax.all_to_all(bias, "rj", 0, 0, tiled=True)

    total, dq, dkv = attention(qgo, kvs, bias)

    def spread_out(parts, axis):
        return [parts[0]] + [
            lax.ppermute(parts[t], axis, [(a, (a + t) % N) for a in range(N)])
            for t in range(1, N)
        ]

    spread = lax.all_to_all(total, ("x", "rj"), 0, 0, tiled=True)
    total = jnp.sum(spread.reshape(N, N, 64, ROWS).astype(F32), axis=0).astype(BF)
    other = swap(total, "zh", [(0, 1), (2, 3)])
    parts = spread_out(hand_on(split_kernel, total, dkv), "rj")
    total = add(total, other)
    other = swap(total, "zh", [(1, 2), (3, 0)])
    parts = spread_out(hand_on(choose_kernel, total, *parts), "ri")
    total = add(total, other)
    mine = lax.all_gather(total, "x", axis=0, tiled=True).reshape(-1, ROWS)

    dkv = sum(x.astype(F32) for x in parts).astype(BF)
    grads = jnp.concatenate([dkv, dq], axis=1)
    own, others = grads[: SEQS // 2], grads[SEQS // 2 :]
    theirs = swap(jnp.concatenate([mine, others.reshape(-1, ROWS)]), "core", [(0, 1)])
    bias_grad = place(theirs, place(mine))
    heads = own, theirs[mine.shape[0] :].reshape(own.shape)
    first, second = (jnp.where(core == c, *heads) for c in range(2))

    def whole(part):
        at = slice(part * HEAD, (part + 1) * HEAD)
        return jnp.swapaxes(jnp.concatenate([first[:, at], second[:, at]], axis=1), 1, 2)

    return whole(2), whole(0), whole(1), bias_grad


def solution(mesh):
    split = Mesh(mesh.devices.reshape(N, N, 2, N, N), ("zh", "x", "core", "ri", "rj"))
    seq = ("zh", "x", "core")
    rows, keys, tile = P(seq, "ri", "rj"), P(seq, "rj", "ri"), P(None, "ri", "rj")
    return jax.shard_map(
        body,
        mesh=split,
        in_specs=(rows, keys, keys, tile, rows, rows),
        out_specs=(rows, keys, keys, tile),
        check_vma=False,
    )
```

time: 116 us -> 119 us (1.026)
  other arithmetic: 0.38 us -> 6.31 us
  waiting for transfers between devices: 9.34 us -> 4.37 us
  starting transfers between devices: 65 us -> 66.5 us
  blocking collectives: 31.3 us -> 32.6 us
    unnamed x0 -> x4, other arithmetic: none -> 3.27 us
    ppermute x4, waiting for transfers between devices: 5.46 us -> 2.23 us  [body(): lax.ppermute(kv, ('ri', 'rj'), [(a * N + b, (b + t) % N * N + a) for a, b...]
    ppermute x4, starting transfers between devices: 26.9 us -> 29.6 us  [swap(): lax.ppermute(x, axis, [(a, b) for a, b in pairs] + [(b, a) for a, b in pa...]
    transpose x0 -> x3, other arithmetic: none -> 1.9 us  [whole(): jnp.swapaxes(jnp.concatenate([first[:, at], second[:, at]], axis=1), 1, 2)]
    ppermute x4, waiting for transfers between devices: 3.85 us -> 2.12 us  [swap(): lax.ppermute(x, axis, [(a, b) for a, b in pairs] + [(b, a) for a, b in pa...]
    all_to_all x1, starting transfers between devices: 5.16 us -> 3.47 us  [body(): bias = lax.all_to_all(bias, 'rj', 0, 0, tiled=True)]
where the time goes in v8:
time: 119 us; the launch traced here: 118 us
  starting transfers between devices  66.5 us (56%)
  blocking collectives  32.6 us (27%)
  Pallas kernels  6.78 us (6%)
  other arithmetic  6.31 us (5%)
  waiting for transfers between devices  4.37 us (4%)
    ppermute x4, starting transfers between devices, swap(): lax.ppermute(x, axis, [(a, b) for a, b in pairs] + [(b, a) for a, b in pa...  29.6 us
    all_to_all x1, blocking collectives, body(): spread = lax.all_to_all(total, ('x', 'rj'), 0, 0, tiled=True)  21.2 us
    ppermute x6, starting transfers between devices, spread_out(): lax.ppermute(parts[t], axis, [(a, (a + t) % N) for a in range(N)])  20.1 us
    ppermute x4, starting transfers between devices, body(): lax.ppermute(kv, ('ri', 'rj'), [(a * N + b, (b + t) % N * N + a) for a, b...  13.3 us
    all_gather x1, blocking collectives, body(): mine = lax.all_gather(total, 'x', axis=0, tiled=True).reshape(-1, ROWS)  11.4 us
    pallas_call x1, Pallas kernels, attention(): pl.pallas_call(attention_kernel, out_shape=(jax.ShapeDtypeStruct((N * N,...  4.6 us
    all_to_all x1, starting transfers between devices, body(): bias = lax.all_to_all(bias, 'rj', 0, 0, tiled=True)  3.47 us
    unnamed x4, other arithmetic  3.27 us
  transfers between devices with their start and end apart: 15, of which 4 were waited for; matrix products, arithmetic and copies ran while one was open for 1% of the time, Pallas kernels for 1%

profile of v8, /device:TPU:1, one launch (start us, length us, event | category | flops | bytes accessed | tf_op | source)
XLA Modules:
  0.0 118.4 jit_solution(3160308091972977796)
XLA Ops:
  0.7 0.9 select_dynamic-update-slice_fusion.4
  1.5 0.8 select_dynamic-update-slice_fusion.3
  2.3 0.8 select_dynamic-update-slice_fusion.2
  3.1 0.8 select_dynamic-update-slice_fusion.1
  3.9 0.8 select_dynamic-update-slice_fusion
  4.7 8.8 %collective-permute-start = (bf16[2,160,256]{2,1,0:T(8,128)(2,1)S(1)}, bf16[2,160,256]{2,1,0:T(8,128)(2,1)S(1)}, u32[]{:S(2)}, u32[]{:S(2)}) collective-permute-start(bf16[2,160,256]{2,1,0:T(8,128)(2,1)S(1)} %get-tuple-element.34), channel_id=1, source_target_pairs={{0,16},{16,0},{1,17},{17,1},{2,18},{18,2},{3,19},{19,3},{4,20},{20... | collective-permute-start | bytes 491528 | tf_op jit(solution)/shard_map/ppermute | solution.py:168
  13.5 0.8 dynamic-slice_bitcast_fusion
  14.4 3.5 %all-to-all-start = ((bf16[4,256,256]{2,1,0:T(8,128)(2,1)}), bf16[4,256,256]{2,1,0:T(8,128)(2,1)S(1)}, u32[]{:S(2)}, u32[]{:S(2)}) async-start(bf16[4,256,256]{2,1,0:T(8,128)(2,1)} %dynamic-slice_bitcast_fusion), calls=%async_computation | async-start | bytes 1048576 | tf_op jit(solution)/shard_map/all_to_all | solution.py:197
  17.9 1.9 %collective-permute-start.3 = (bf16[4,64,256]{2,1,0:T(8,128)(2,1)S(1)}, bf16[4,64,256]{2,1,0:T(8,128)(2,1)S(1)}, u32[]{:S(2)}, u32[]{:S(2)}) collective-permute-start(bf16[4,64,256]{2,1,0:T(8,128)(2,1)S(1)} %pad_maximum_fusion.1), channel_id=1, source_target_pairs={{0,8},{1,12},{2,0},{3,4},{4,9},{5,13},{6,1},{7,5},{8,10},{9,14},{1... | collective-permute-start | bytes 393224 | tf_op jit(solution)/shard_map/ppermute | solution.py:193
  19.8 1.9 %collective-permute-start.2 = (bf16[4,64,256]{2,1,0:T(8,128)(2,1)S(1)}, bf16[4,64,256]{2,1,0:T(8,128)(2,1)S(1)}, u32[]{:S(2)}, u32[]{:S(2)}) collective-permute-start(bf16[4,64,256]{2,1,0:T(8,128)(2,1)S(1)} %pad_maximum_fusion.1), channel_id=1, source_target_pairs={{0,4},{1,8},{2,12},{3,0},{4,5},{5,9},{6,13},{7,1},{8,6},{9,10},{10... | collective-permute-start | bytes 393224 | tf_op jit(solution)/shard_map/ppermute | solution.py:193
  21.7 0.7 collective-permute-start.1
  22.4 8.8 %collective-permute-start.4 = (bf16[4,64,256]{2,1,0:T(8,128)(2,1)S(1)}, bf16[4,64,256]{2,1,0:T(8,128)(2,1)S(1)}, u32[]{:S(2)}, u32[]{:S(2)}) collective-permute-start(bf16[4,64,256]{2,1,0:T(8,128)(2,1)S(1)} %pad_maximum_fusion.1), channel_id=1, source_target_pairs={{0,12},{1,0},{2,4},{3,8},{4,13},{5,1},{6,5},{7,9},{8,14},{9,2},{10... | collective-permute-start | bytes 393224 | tf_op jit(solution)/shard_map/ppermute | solution.py:193
  31.2 1.9 %collective-permute-done.3.kv2 = bf16[4,64,256]{2,1,0:T(8,128)(2,1)S(1)} collective-permute-done((bf16[4,64,256]{2,1,0:T(8,128)(2,1)S(1)}, bf16[4,64,256]{2,1,0:T(8,128)(2,1)S(1)}, u32[]{:S(2)}, u32[]{:S(2)}) %collective-permute-start.3) | collective-permute-done | bytes 131104 | tf_op jit(solution)/shard_map/ppermute | solution.py:193
  33.5 4.6 %shard_map.93 = (bf16[16,64,256]{2,1,0:T(8,128)(2,1)S(1)}, bf16[4,32,256]{2,1,0:T(8,128)(2,1)S(1)}, bf16[4,4,64,256]{3,2,1,0:T(8,128)(2,1)S(1)}) custom-call(bf16[4,96,256]{2,1,0:T(8,128)(2,1)S(1)} %fusion.qgo_ref, bf16[4,64,256]{2,1,0:T(8,128)(2,1)S(1)} %collective-permute-done.1.kv0, bf16[4,64,256]{2,1,0:T(8,128)(2,1)S(1)} %collective-permute-done.2.kv1, ...), custom_call_target="tpu_custom_call" | custom-call | flops 335544320 | bytes 6291456 | tf_op jit(solution)/shard_map/pallas_call | solution.py:86
  38.1 21.2 %all_to_all.10 = bf16[16,64,256]{2,1,0:T(8,128)(2,1)S(1)} all-to-all(bf16[16,64,256]{2,1,0:T(8,128)(2,1)S(1)} %get-tuple-element.15), channel_id=1, replica_groups=mesh['zh'=4,'x'=4,'core'=2,'ri'=4,'rj'=4] {'x','rj'}, dimensions={0} | all-to-all | bytes 1048576 | tf_op jit(solution)/shard_map/all_to_all | solution.py:207
  59.3 8.8 %collective-permute-start.5 = (bf16[4,64,256]{2,1,0:T(8,128)(2,1)S(1)}, bf16[4,64,256]{2,1,0:T(8,128)(2,1)S(1)}, u32[]{:S(2)}, u32[]{:S(2)}) collective-permute-start(bf16[4,64,256]{2,1,0:T(8,128)(2,1)S(1)} %reduce_sum.12.after), channel_id=1, source_target_pairs={{0,128},{256,384},{128,0},{384,256},{1,129},{257,385},{129,1},{385... | collective-permute-start | bytes 393224 | tf_op jit(solution)/shard_map/ppermute | solution.py:168
  68.2 2.2 %collective-permute-start.6 = (bf16[4,64,256]{2,1,0:T(8,128)(2,1)S(1)}, bf16[4,64,256]{2,1,0:T(8,128)(2,1)S(1)}, u32[]{:S(2)}, u32[]{:S(2)}) collective-permute-start(bf16[4,64,256]{2,1,0:T(8,128)(2,1)S(1)} %get-tuple-element.18), channel_id=1, source_target_pairs={{0,1},{1,2},{2,3},{3,0},{4,5},{5,6},{6,7},{7,4},{8,9},{9,10},{10,1... | collective-permute-start | bytes 393224 | tf_op jit(solution)/shard_map/ppermute | solution.py:203
  70.4 3.3 %collective-permute-start.7 = (bf16[4,64,256]{2,1,0:T(8,128)(2,1)S(1)}, bf16[4,64,256]{2,1,0:T(8,128)(2,1)S(1)}, u32[]{:S(2)}, u32[]{:S(2)}) collective-permute-start(bf16[4,64,256]{2,1,0:T(8,128)(2,1)S(1)} %get-tuple-element.19), channel_id=1, source_target_pairs={{0,2},{1,3},{2,0},{3,1},{4,6},{5,7},{6,4},{7,5},{8,10},{9,11},{10,... | collective-permute-start | bytes 393224 | tf_op jit(solution)/shard_map/ppermute | solution.py:203
  73.7 3.4 %collective-permute-start.8 = (bf16[4,64,256]{2,1,0:T(8,128)(2,1)S(1)}, bf16[4,64,256]{2,1,0:T(8,128)(2,1)S(1)}, u32[]{:S(2)}, u32[]{:S(2)}) collective-permute-start(bf16[4,64,256]{2,1,0:T(8,128)(2,1)S(1)} %get-tuple-element.20), channel_id=1, source_target_pairs={{0,3},{1,0},{2,1},{3,2},{4,7},{5,4},{6,5},{7,6},{8,11},{9,8},{10,9... | collective-permute-start | bytes 393224 | tf_op jit(solution)/shard_map/ppermute | solution.py:203
  77.1 1.5 %collective-permute-done.5 = bf16[4,64,256]{2,1,0:T(8,128)(2,1)S(1)} collective-permute-done((bf16[4,64,256]{2,1,0:T(8,128)(2,1)S(1)}, bf16[4,64,256]{2,1,0:T(8,128)(2,1)S(1)}, u32[]{:S(2)}, u32[]{:S(2)}) %collective-permute-start.5) | collective-permute-done | bytes 131104 | tf_op jit(solution)/shard_map/ppermute | solution.py:168
  78.6 5.7 %collective-permute-start.12 = (bf16[4,64,256]{2,1,0:T(8,128)(2,1)S(1)}, bf16[4,64,256]{2,1,0:T(8,128)(2,1)S(1)}, u32[]{:S(2)}, u32[]{:S(2)}) collective-permute-start(bf16[4,64,256]{2,1,0:T(8,128)(2,1)S(1)} %add_convert_fusion.2.after), channel_id=1, source_target_pairs={{128,256},{384,0},{256,128},{0,384},{129,257},{385,1},{257,129},{1... | collective-permute-start | bytes 393224 | tf_op jit(solution)/shard_map/ppermute | solution.py:168
  84.5 1.9 %collective-permute-start.9 = (bf16[4,64,256]{2,1,0:T(8,128)(2,1)S(1)}, bf16[4,64,256]{2,1,0:T(8,128)(2,1)S(1)}, u32[]{:S(2)}, u32[]{:S(2)}) collective-permute-start(bf16[4,64,256]{2,1,0:T(8,128)(2,1)S(1)} %get-tuple-element.22), channel_id=1, source_target_pairs={{0,4},{4,8},{8,12},{12,0},{1,5},{5,9},{9,13},{13,1},{2,6},{6,10},{... | collective-permute-start | bytes 393224 | tf_op jit(solution)/shard_map/ppermute | solution.py:203
  86.4 7.4 %collective-permute-start.10 = (bf16[4,64,256]{2,1,0:T(8,128)(2,1)S(1)}, bf16[4,64,256]{2,1,0:T(8,128)(2,1)S(1)}, u32[]{:S(2)}, u32[]{:S(2)}) collective-permute-start(bf16[4,64,256]{2,1,0:T(8,128)(2,1)S(1)} %get-tuple-element.23), channel_id=1, source_target_pairs={{0,8},{4,12},{8,0},{12,4},{1,9},{5,13},{9,1},{13,5},{2,10},{6,14},... | collective-permute-start | bytes 393224 | tf_op jit(solution)/shard_map/ppermute | solution.py:203
  93.9 1.9 %collective-permute-start.11 = (bf16[4,64,256]{2,1,0:T(8,128)(2,1)S(1)}, bf16[4,64,256]{2,1,0:T(8,128)(2,1)S(1)}, u32[]{:S(2)}, u32[]{:S(2)}) collective-permute-start(bf16[4,64,256]{2,1,0:T(8,128)(2,1)S(1)} %get-tuple-element.24), channel_id=1, source_target_pairs={{0,12},{4,0},{8,4},{12,8},{1,13},{5,1},{9,5},{13,9},{2,14},{6,2},{... | collective-permute-start | bytes 393224 | tf_op jit(solution)/shard_map/ppermute | solution.py:203
  95.8 11.4 %all_gather.3 = bf16[16,64,256]{2,1,0:T(8,128)(2,1)S(1)} all-gather(bf16[4,64,256]{2,1,0:T(8,128)(2,1)S(1)} %add_convert_fusion), channel_id=1, replica_groups=mesh['zh'=4,'x'=4,'core'=2,'ri'=4,'rj'=4] {'x'}, dimensions={0}, use_global_device_ids=true | all-gather | bytes 655360 | tf_op jit(solution)/shard_map/all_gather | solution.py:215
  107.4 6.3 %collective-permute-start.13 = (bf16[1216,256]{1,0:T(8,128)(2,1)S(1)}, bf16[1216,256]{1,0:T(8,128)(2,1)S(1)}, u32[]{:S(2)}, u32[]{:S(2)}) collective-permute-start(bf16[1216,256]{1,0:T(8,128)(2,1)S(1)} %pad_maximum_fusion), channel_id=1, source_target_pairs={{0,16},{16,0},{1,17},{17,1},{2,18},{18,2},{3,19},{19,3},{4,20},{20... | collective-permute-start | bytes 1867784 | tf_op jit(solution)/shard_map/ppermute | solution.py:168
  113.7 1.0 shard_map.96.refs_1_
  114.8 0.6 collective-permute-done.13.refs_0_
  115.5 0.6 maximum_bitcast_fusion.2
  116.1 0.6 maximum_bitcast_fusion.1
  116.7 0.6 maximum_bitcast_fusion
  117.4 1.0 shard_map.97
  (27 shorter events, 0.9 us)
Async XLA Ops:
  0.6 12.9 %copy-start = (bf16[8,256,256]{2,1,0:T(8,128)(2,1)S(1)}, bf16[8,256,256]{2,1,0:T(8,128)(2,1)}, u32[]{:S(2)}) copy-start(bf16[8,256,256]{2,1,0:T(8,128)(2,1)} %param.9) | copy-start | bytes 3145732
  4.7 13.1 %collective-permute-start = (bf16[2,160,256]{2,1,0:T(8,128)(2,1)S(1)}, bf16[2,160,256]{2,1,0:T(8,128)(2,1)S(1)}, u32[]{:S(2)}, u32[]{:S(2)}) collective-permute-start(bf16[2,160,256]{2,1,0:T(8,128)(2,1)S(1)} %get-tuple-element.34), channel_id=1, source_target_pairs={{0,16},{16,0},{1,17},{17,1},{2,18},{18,2},{3,19},{19,3},{4,20},{20... | collective-permute-start | bytes 491528 | tf_op jit(solution)/shard_map/ppermute | solution.py:168
  14.4 19.1 %all-to-all-start = ((bf16[4,256,256]{2,1,0:T(8,128)(2,1)}), bf16[4,256,256]{2,1,0:T(8,128)(2,1)S(1)}, u32[]{:S(2)}, u32[]{:S(2)}) async-start(bf16[4,256,256]{2,1,0:T(8,128)(2,1)} %dynamic-slice_bitcast_fusion), calls=%async_computation | async-start | bytes 1048576 | tf_op jit(solution)/shard_map/all_to_all | solution.py:197
  17.9 15.2 %collective-permute-start.3 = (bf16[4,64,256]{2,1,0:T(8,128)(2,1)S(1)}, bf16[4,64,256]{2,1,0:T(8,128)(2,1)S(1)}, u32[]{:S(2)}, u32[]{:S(2)}) collective-permute-start(bf16[4,64,256]{2,1,0:T(8,128)(2,1)S(1)} %pad_maximum_fusion.1), channel_id=1, source_target_pairs={{0,8},{1,12},{2,0},{3,4},{4,9},{5,13},{6,1},{7,5},{8,10},{9,14},{1... | collective-permute-start | bytes 393224 | tf_op jit(solution)/shard_map/ppermute | solution.py:193
  19.8 13.3 %collective-permute-start.2 = (bf16[4,64,256]{2,1,0:T(8,128)(2,1)S(1)}, bf16[4,64,256]{2,1,0:T(8,128)(2,1)S(1)}, u32[]{:S(2)}, u32[]{:S(2)}) collective-permute-start(bf16[4,64,256]{2,1,0:T(8,128)(2,1)S(1)} %pad_maximum_fusion.1), channel_id=1, source_target_pairs={{0,4},{1,8},{2,12},{3,0},{4,5},{5,9},{6,13},{7,1},{8,6},{9,10},{10... | collective-permute-start | bytes 393224 | tf_op jit(solution)/shard_map/ppermute | solution.py:193
  21.7 11.4 %collective-permute-start.1 = (bf16[4,64,256]{2,1,0:T(8,128)(2,1)S(1)}, bf16[4,64,256]{2,1,0:T(8,128)(2,1)S(1)}, u32[]{:S(2)}, u32[]{:S(2)}) collective-permute-start(bf16[4,64,256]{2,1,0:T(8,128)(2,1)S(1)} %pad_maximum_fusion.1), channel_id=1, source_target_pairs={{0,0},{1,4},{2,8},{3,12},{4,1},{5,5},{6,9},{7,13},{8,2},{9,6},{10,... | collective-permute-start | bytes 393224 | tf_op jit(solution)/shard_map/ppermute | solution.py:193
  22.4 11.1 %collective-permute-start.4 = (bf16[4,64,256]{2,1,0:T(8,128)(2,1)S(1)}, bf16[4,64,256]{2,1,0:T(8,128)(2,1)S(1)}, u32[]{:S(2)}, u32[]{:S(2)}) collective-permute-start(bf16[4,64,256]{2,1,0:T(8,128)(2,1)S(1)} %pad_maximum_fusion.1), channel_id=1, source_target_pairs={{0,12},{1,0},{2,4},{3,8},{4,13},{5,1},{6,5},{7,9},{8,14},{9,2},{10... | collective-permute-start | bytes 393224 | tf_op jit(solution)/shard_map/ppermute | solution.py:193
  59.3 19.2 %collective-permute-start.5 = (bf16[4,64,256]{2,1,0:T(8,128)(2,1)S(1)}, bf16[4,64,256]{2,1,0:T(8,128)(2,1)S(1)}, u32[]{:S(2)}, u32[]{:S(2)}) collective-permute-start(bf16[4,64,256]{2,1,0:T(8,128)(2,1)S(1)} %reduce_sum.12.after), channel_id=1, source_target_pairs={{0,128},{256,384},{128,0},{384,256},{1,129},{257,385},{129,1},{385... | collective-permute-start | bytes 393224 | tf_op jit(solution)/shard_map/ppermute | solution.py:168
  68.2 16.1 %collective-permute-start.6 = (bf16[4,64,256]{2,1,0:T(8,128)(2,1)S(1)}, bf16[4,64,256]{2,1,0:T(8,128)(2,1)S(1)}, u32[]{:S(2)}, u32[]{:S(2)}) collective-permute-start(bf16[4,64,256]{2,1,0:T(8,128)(2,1)S(1)} %get-tuple-element.18), channel_id=1, source_target_pairs={{0,1},{1,2},{2,3},{3,0},{4,5},{5,6},{6,7},{7,4},{8,9},{9,10},{10,1... | collective-permute-start | bytes 393224 | tf_op jit(solution)/shard_map/ppermute | solution.py:203
  70.4 13.9 %collective-permute-start.7 = (bf16[4,64,256]{2,1,0:T(8,128)(2,1)S(1)}, bf16[4,64,256]{2,1,0:T(8,128)(2,1)S(1)}, u32[]{:S(2)}, u32[]{:S(2)}) collective-permute-start(bf16[4,64,256]{2,1,0:T(8,128)(2,1)S(1)} %get-tuple-element.19), channel_id=1, source_target_pairs={{0,2},{1,3},{2,0},{3,1},{4,6},{5,7},{6,4},{7,5},{8,10},{9,11},{10,... | collective-permute-start | bytes 393224 | tf_op jit(solution)/shard_map/ppermute | solution.py:203
  73.7 10.6 %collective-permute-start.8 = (bf16[4,64,256]{2,1,0:T(8,128)(2,1)S(1)}, bf16[4,64,256]{2,1,0:T(8,128)(2,1)S(1)}, u32[]{:S(2)}, u32[]{:S(2)}) collective-permute-start(bf16[4,64,256]{2,1,0:T(8,128)(2,1)S(1)} %get-tuple-element.20), channel_id=1, source_target_pairs={{0,3},{1,0},{2,1},{3,2},{4,7},{5,4},{6,5},{7,6},{8,11},{9,8},{10,9... | collective-permute-start | bytes 393224 | tf_op jit(solution)/shard_map/ppermute | solution.py:203
  78.6 17.2 %collective-permute-start.12 = (bf16[4,64,256]{2,1,0:T(8,128)(2,1)S(1)}, bf16[4,64,256]{2,1,0:T(8,128)(2,1)S(1)}, u32[]{:S(2)}, u32[]{:S(2)}) collective-permute-start(bf16[4,64,256]{2,1,0:T(8,128)(2,1)S(1)} %add_convert_fusion.2.after), channel_id=1, source_target_pairs={{128,256},{384,0},{256,128},{0,384},{129,257},{385,1},{257,129},{1... | collective-permute-start | bytes 393224 | tf_op jit(solution)/shard_map/ppermute | solution.py:168
  84.5 22.8 %collective-permute-start.9 = (bf16[4,64,256]{2,1,0:T(8,128)(2,1)S(1)}, bf16[4,64,256]{2,1,0:T(8,128)(2,1)S(1)}, u32[]{:S(2)}, u32[]{:S(2)}) collective-permute-start(bf16[4,64,256]{2,1,0:T(8,128)(2,1)S(1)} %get-tuple-element.22), channel_id=1, source_target_pairs={{0,4},{4,8},{8,12},{12,0},{1,5},{5,9},{9,13},{13,1},{2,6},{6,10},{... | collective-permute-start | bytes 393224 | tf_op jit(solution)/shard_map/ppermute | solution.py:203
  86.4 20.9 %collective-permute-start.10 = (bf16[4,64,256]{2,1,0:T(8,128)(2,1)S(1)}, bf16[4,64,256]{2,1,0:T(8,128)(2,1)S(1)}, u32[]{:S(2)}, u32[]{:S(2)}) collective-permute-start(bf16[4,64,256]{2,1,0:T(8,128)(2,1)S(1)} %get-tuple-element.23), channel_id=1, source_target_pairs={{0,8},{4,12},{8,0},{12,4},{1,9},{5,13},{9,1},{13,5},{2,10},{6,14},... | collective-permute-start | bytes 393224 | tf_op jit(solution)/shard_map/ppermute | solution.py:203
  93.9 13.4 %collective-permute-start.11 = (bf16[4,64,256]{2,1,0:T(8,128)(2,1)S(1)}, bf16[4,64,256]{2,1,0:T(8,128)(2,1)S(1)}, u32[]{:S(2)}, u32[]{:S(2)}) collective-permute-start(bf16[4,64,256]{2,1,0:T(8,128)(2,1)S(1)} %get-tuple-element.24), channel_id=1, source_target_pairs={{0,12},{4,0},{8,4},{12,8},{1,13},{5,1},{9,5},{13,9},{2,14},{6,2},{... | collective-permute-start | bytes 393224 | tf_op jit(solution)/shard_map/ppermute | solution.py:203
  107.4 8.0 %collective-permute-start.13 = (bf16[1216,256]{1,0:T(8,128)(2,1)S(1)}, bf16[1216,256]{1,0:T(8,128)(2,1)S(1)}, u32[]{:S(2)}, u32[]{:S(2)}) collective-permute-start(bf16[1216,256]{1,0:T(8,128)(2,1)S(1)} %pad_maximum_fusion), channel_id=1, source_target_pairs={{0,16},{16,0},{1,17},{17,1},{2,18},{18,2},{3,19},{19,3},{4,20},{20... | collective-permute-start | bytes 1867784 | tf_op jit(solution)/shard_map/ppermute | solution.py:168

commit v9 on v8

--- a/solution.py
+++ b/solution.py
@@ -19,6 +19,36 @@
 F32 = jnp.float32
 NT = (((1,), (1,)), ((), ()))
 NN = (((1,), (0,)), ((), ()))
+
+
+def pack_kernel(k_ref, v_ref, q_ref, g_ref, o_ref, bias_ref, keep, send, bias_out, sem):
+    core = lax.axis_index("core")
+    copies = []
+    for out, which in ((send, 1 - core), (keep, core)):
+        half = pl.ds(pl.multiple_of(which * HEAD, HEAD), HEAD)
+        for i, x_ref in enumerate((k_ref, v_ref, q_ref, g_ref, o_ref)):
+            copies.append((x_ref.at[:, half, :], out.at[:, i * HEAD : (i + 1) * HEAD, :]))
+    for j in range(N):
+        copies.append((bias_ref.at[2 * j + core], bias_out.at[j]))
+    copies = [pltpu.make_async_copy(*c, sem.at[i]) for i, c in enumerate(copies)]
+    for c in copies:
+        c.start()
+    for c in copies:
+        c.wait()
+
+
+def pack(*args):
+    hbm = pl.BlockSpec(memory_space=pltpu.HBM)
+    half = jax.ShapeDtypeStruct((SEQS // 2, 5 * HEAD, ROWS), BF)
+    return pl.pallas_call(
+        pack_kernel,
+        out_shape=(half, half, jax.ShapeDtypeStruct((N, ROWS, ROWS), BF)),
+        in_specs=[hbm] * 6,
+        out_specs=(hbm,) * 3,
+        scratch_shapes=[pltpu.SemaphoreType.DMA((10 + N,))],
+        compiler_params=pltpu.CompilerParams(vmem_limit_bytes=56 * 2**20),
+        cost_estimate=pl.CostEstimate(flops=0, bytes_accessed=2**21, transcendentals=0),
+    )(*args)
 
 
 def attention_kernel(
@@ -134,10 +164,7 @@
     )(after, *args)
 
 
-def place_kernel(first, x_ref, *refs):
-    out_ref, wide, sem = refs[-3:]
-    core = lax.axis_index("core")
-    head = core if first else 1 - core
+def place_heads(x_ref, out_ref, wide, sem, head):
     copies = []
     for j in range(N):
         for x in range(N):
@@ -145,23 +172,60 @@
             wide[j, x * 64 : (x + 1) * 64, :] = x_ref[at : at + 64, :].astype(F32)
         copies.append(pltpu.make_async_copy(wide.at[j], out_ref.at[2 * j + head], sem.at[j]))
         copies[-1].start()
+    return copies
+
+
+def place_kernel(x_ref, out_ref, wide, sem):
+    for c in place_heads(x_ref, out_ref, wide, sem, lax.axis_index("core")):
+        c.wait()
+
+
+def finish_kernel(x_ref, own_ref, before, out_ref, dk_ref, dv_ref, dq_ref, wide, both, sem):
+    core = lax.axis_index("core")
+    copies = place_heads(x_ref, out_ref, wide, sem, 1 - core)
+    mine = pl.ds(pl.multiple_of(core * HEAD, HEAD), HEAD)
+    theirs = pl.ds(pl.multiple_of((1 - core) * HEAD, HEAD), HEAD)
+    for i, grad_ref in enumerate((dk_ref, dv_ref, dq_ref)):
+        for s in range(SEQS // 2):
+            at = N * ROWS + (s * 3 + i) * HEAD
+            both[i, s, mine, :] = own_ref[s, i * HEAD : (i + 1) * HEAD, :]
+            both[i, s, theirs, :] = x_ref[at : at + HEAD, :]
+        copies.append(pltpu.make_async_copy(both.at[i], grad_ref, sem.at[N + i]))
+        copies[-1].start()
     for c in copies:
         c.wait()
 
 
-def place(x, before=None):
-    first = before is None
+def place(x):
     anywhere, vmem = pl.BlockSpec(memory_space=pl.ANY), pl.BlockSpec(memory_space=pltpu.VMEM)
     return pl.pallas_call(
-        lambda *refs: place_kernel(first, *refs),
+        place_kernel,
         out_shape=jax.ShapeDtypeStruct((2 * N, ROWS, ROWS), F32),
-        in_specs=[vmem] if first else [vmem, anywhere],
+        in_specs=[vmem],
         out_specs=anywhere,
         scratch_shapes=[pltpu.VMEM((N, ROWS, ROWS), F32), pltpu.SemaphoreType.DMA((N,))],
-        input_output_aliases={} if first else {1: 0},
         compiler_params=pltpu.CompilerParams(vmem_limit_bytes=8 * 2**20),
         cost_estimate=pl.CostEstimate(flops=2**18, bytes_accessed=3 * 2**19, transcendentals=0),
-    )(*([x] if first else [x, before]))
+    )(x)
+
+
+def finish(x, own, before):
+    anywhere, vmem = pl.BlockSpec(memory_space=pl.ANY), pl.BlockSpec(memory_space=pltpu.VMEM)
+    grad = jax.ShapeDtypeStruct((SEQS // 2, 2 * HEAD, ROWS), BF)
+    return pl.pallas_call(
+        finish_kernel,
+        out_shape=(jax.ShapeDtypeStruct(before.shape, F32), grad, grad, grad),
+        in_specs=[vmem, vmem, anywhere],
+        out_specs=(anywhere,) * 4,
+        scratch_shapes=[
+            pltpu.VMEM((N, ROWS, ROWS), F32),
+            pltpu.VMEM((3, *grad.shape), BF),
+            pltpu.SemaphoreType.DMA((N + 3,)),
+        ],
+        input_output_aliases={2: 0},
+        compiler_params=pltpu.CompilerParams(vmem_limit_bytes=8 * 2**20),
+        cost_estimate=pl.CostEstimate(flops=2**18, bytes_accessed=2**21, transcendentals=0),
+    )(x, own, before)
 
 
 def swap(x, axis, pairs):
@@ -179,21 +243,13 @@
     )
     grid = [(a, b) for a in range(N) for b in range(N)]
 
-    core = lax.axis_index("core")
-
-    def half(x, which):
-        return jnp.where(which == 0, x[:, :HEAD], x[:, HEAD:])
-
-    def halves(which):
-        return jnp.concatenate([half(x, which) for x in (k, v, q, g, o)], axis=1)
-
-    both = jnp.concatenate([halves(core), swap(halves(1 - core), "core", [(0, 1)])])
+    keep, send, bias = pack(k, v, q, g, o, pair_bias)
+    both = jnp.concatenate([keep, swap(send, "core", [(0, 1)])])
     kv, qgo = both[:, : 2 * HEAD], both[:, 2 * HEAD :]
     kvs = [
         lax.ppermute(kv, ("ri", "rj"), [(a * N + b, (b + t) % N * N + a) for a, b in grid])
         for t in range(N)
     ]
-    bias = lax.dynamic_index_in_dim(pair_bias.reshape(N, 2, ROWS, ROWS), core, 1, False)
     bias = lax.all_to_all(bias, "rj", 0, 0, tiled=True)
 
     total, dq, dkv = attention(qgo, kvs, bias)
@@ -218,15 +274,8 @@
     grads = jnp.concatenate([dkv, dq], axis=1)
     own, others = grads[: SEQS // 2], grads[SEQS // 2 :]
     theirs = swap(jnp.concatenate([mine, others.reshape(-1, ROWS)]), "core", [(0, 1)])
-    bias_grad = place(theirs, place(mine))
-    heads = own, theirs[mine.shape[0] :].reshape(own.shape)
-    first, second = (jnp.where(core == c, *heads) for c in range(2))
-
-    def whole(part):
-        at = slice(part * HEAD, (part + 1) * HEAD)
-        return jnp.swapaxes(jnp.concatenate([first[:, at], second[:, at]], axis=1), 1, 2)
-
-    return whole(2), whole(0), whole(1), bias_grad
+    bias_grad, dk, dv, dq = finish(theirs, own, place(mine))
+    return *(jnp.swapaxes(x, 1, 2) for x in (dq, dk, dv)), bias_grad
 
 
 def solution(mesh):

time: 119 us -> 140 us (1.18)
  Pallas kernels: 6.78 us -> 33.9 us
  other arithmetic: 6.31 us -> 0.28 us
    pallas_call x2 -> x3, Pallas kernels: 2.03 us -> 29.2 us  [the longest x1 27 us: pack(): pl.pallas_call(pack_kernel, out_shape=(half, half, jax.ShapeDtypeStruct((...]
    ppermute x4, starting transfers between devices: 29.6 us -> 33.4 us  [swap(): lax.ppermute(x, axis, [(a, b) for a, b in pairs] + [(b, a) for a, b in pa...]
    unnamed x4 -> x0, other arithmetic: 3.27 us -> none
    ppermute x6, starting transfers between devices: 20.1 us -> 17.8 us  [spread_out(): lax.ppermute(parts[t], axis, [(a, (a + t) % N) for a in range(N)])]
    ppermute x4, starting transfers between devices: 13.3 us -> 11.1 us  [body(): lax.ppermute(kv, ('ri', 'rj'), [(a * N + b, (b + t) % N * N + a) for a, b...]
    transpose x3 -> x0, other arithmetic: 1.9 us -> none  [whole(): jnp.swapaxes(jnp.concatenate([first[:, at], second[:, at]], axis=1), 1, 2)]
where the time goes in v9:
time: 140 us
  starting transfers between devices  65.7 us (47%)
  Pallas kernels  33.9 us (24%)
  blocking collectives  32.9 us (24%)
  waiting for transfers between devices  4.79 us (3%)
    ppermute x4, starting transfers between devices, swap(): lax.ppermute(x, axis, [(a, b) for a, b in pairs] + [(b, a) for a, b in pa...  33.4 us
    pallas_call x1, Pallas kernels, pack(): pl.pallas_call(pack_kernel, out_shape=(half, half, jax.ShapeDtypeStruct((...  27 us
    all_to_all x1, blocking collectives, body(): spread = lax.all_to_all(total, ('x', 'rj'), 0, 0, tiled=True)  22.4 us
    ppermute x6, starting transfers between devices, spread_out(): lax.ppermute(parts[t], axis, [(a, (a + t) % N) for a in range(N)])  17.8 us
    ppermute x4, starting transfers between devices, body(): lax.ppermute(kv, ('ri', 'rj'), [(a * N + b, (b + t) % N * N + a) for a, b...  11.1 us
    all_gather x1, blocking collectives, body(): mine = lax.all_gather(total, 'x', axis=0, tiled=True).reshape(-1, ROWS)  10.5 us
    pallas_call x1, Pallas kernels, attention(): pl.pallas_call(attention_kernel, out_shape=(jax.ShapeDtypeStruct((N * N,...  4.6 us
    all_to_all x1, starting transfers between devices, body(): bias = lax.all_to_all(bias, 'rj', 0, 0, tiled=True)  3.48 us
  transfers between devices with their start and end apart: 15, of which 4 were waited for; matrix products, arithmetic and copies ran while one was open for 1% of the time, Pallas kernels for 1%

profile of v9, /device:TPU:1, one launch (start us, length us, event | category | flops | bytes accessed | tf_op | source)
XLA Modules:
  0.0 139.5 jit_solution(4589966430477573047)
XLA Ops:
  0.6 27.0 %shard_map.93 = (bf16[2,160,256]{2,1,0:T(8,128)(2,1)}, bf16[2,160,256]{2,1,0:T(8,128)(2,1)}, bf16[4,256,256]{2,1,0:T(8,128)(2,1)}) custom-call(bf16[2,64,256]{2,1,0:T(8,128)(2,1)} %bitcast.15, bf16[2,64,256]{2,1,0:T(8,128)(2,1)} %bitcast.16, bf16[2,64,256]{2,1,0:T(8,128)(2,1)} %bitcast.17, bf16[2,64,256]{2,1,0:T(8,128)(2,1)} %bitcast.18, ...), custom_call_target="tpu_custom_call" | custom-call | bytes 2097152 | tf_op jit(solution)/shard_map/pallas_call | solution.py:43
  27.7 8.8 %collective-permute-start = (bf16[2,160,256]{2,1,0:T(8,128)(2,1)}, bf16[2,160,256]{2,1,0:T(8,128)(2,1)S(1)}, u32[]{:S(2)}, u32[]{:S(2)}) collective-permute-start(bf16[2,160,256]{2,1,0:T(8,128)(2,1)} %get-tuple-element.23), channel_id=1, source_target_pairs={{0,16},{16,0},{1,17},{17,1},{2,18},{18,2},{3,19},{19,3},{4,20},{20... | collective-permute-start | bytes 491528 | tf_op jit(solution)/shard_map/ppermute | solution.py:232
  36.5 3.5 %all-to-all-start = ((bf16[4,256,256]{2,1,0:T(8,128)(2,1)}), bf16[4,256,256]{2,1,0:T(8,128)(2,1)S(1)}, u32[]{:S(2)}, u32[]{:S(2)}) async-start(bf16[4,256,256]{2,1,0:T(8,128)(2,1)} %get-tuple-element.24), calls=%async_computation | async-start | bytes 1048576 | tf_op jit(solution)/shard_map/all_to_all | solution.py:253
  40.0 0.9 constant_dynamic-update-slice_fusion.1
  41.0 1.9 %collective-permute-start.4 = (bf16[4,64,256]{2,1,0:T(8,128)(2,1)S(1)}, bf16[4,64,256]{2,1,0:T(8,128)(2,1)S(1)}, u32[]{:S(2)}, u32[]{:S(2)}) collective-permute-start(bf16[4,64,256]{2,1,0:T(8,128)(2,1)S(1)} %slice.17), channel_id=1, source_target_pairs={{0,12},{1,0},{2,4},{3,8},{4,13},{5,1},{6,5},{7,9},{8,14},{9,2},{10... | collective-permute-start | bytes 393224 | tf_op jit(solution)/shard_map/ppermute | solution.py:250
  42.9 4.5 %collective-permute-start.3 = (bf16[4,64,256]{2,1,0:T(8,128)(2,1)S(1)}, bf16[4,64,256]{2,1,0:T(8,128)(2,1)S(1)}, u32[]{:S(2)}, u32[]{:S(2)}) collective-permute-start(bf16[4,64,256]{2,1,0:T(8,128)(2,1)S(1)} %slice.17), channel_id=1, source_target_pairs={{0,8},{1,12},{2,0},{3,4},{4,9},{5,13},{6,1},{7,5},{8,10},{9,14},{1... | collective-permute-start | bytes 393224 | tf_op jit(solution)/shard_map/ppermute | solution.py:250
  47.4 4.0 %collective-permute-start.2 = (bf16[4,64,256]{2,1,0:T(8,128)(2,1)S(1)}, bf16[4,64,256]{2,1,0:T(8,128)(2,1)S(1)}, u32[]{:S(2)}, u32[]{:S(2)}) collective-permute-start(bf16[4,64,256]{2,1,0:T(8,128)(2,1)S(1)} %slice.17), channel_id=1, source_target_pairs={{0,4},{1,8},{2,12},{3,0},{4,5},{5,9},{6,13},{7,1},{8,6},{9,10},{10... | collective-permute-start | bytes 393224 | tf_op jit(solution)/shard_map/ppermute | solution.py:250
  51.4 0.7 collective-permute-start.1
  52.1 1.6 %collective-permute-done.4.kv3 = bf16[4,64,256]{2,1,0:T(8,128)(2,1)S(1)} collective-permute-done((bf16[4,64,256]{2,1,0:T(8,128)(2,1)S(1)}, bf16[4,64,256]{2,1,0:T(8,128)(2,1)S(1)}, u32[]{:S(2)}, u32[]{:S(2)}) %collective-permute-start.4) | collective-permute-done | bytes 131104 | tf_op jit(solution)/shard_map/ppermute | solution.py:250
  53.7 0.0 collective-permute-done.3.kv2
  53.7 1.0 collective-permute-done.2.kv1
  54.6 0.0 collective-permute-done.1.kv0
  54.6 0.0 all-to-all-done.bias
  54.7 4.6 %shard_map.94 = (bf16[16,64,256]{2,1,0:T(8,128)(2,1)S(1)}, bf16[4,32,256]{2,1,0:T(8,128)(2,1)S(1)}, bf16[4,4,64,256]{3,2,1,0:T(8,128)(2,1)S(1)}) custom-call(bf16[4,96,256]{2,1,0:T(8,128)(2,1)S(1)} %slice.16.qgo_ref, bf16[4,64,256]{2,1,0:T(8,128)(2,1)S(1)} %collective-permute-done.1.kv0, bf16[4,64,256]{2,1,0:T(8,128)(2,1)S(1)} %collective-permute-done.2.kv1, ...), custom_call_target="tpu_custom_call" | custom-call | flops 335544320 | bytes 6291456 | tf_op jit(solution)/shard_map/pallas_call | solution.py:116
  59.3 22.4 %all_to_all.10 = bf16[16,64,256]{2,1,0:T(8,128)(2,1)S(1)} all-to-all(bf16[16,64,256]{2,1,0:T(8,128)(2,1)S(1)} %get-tuple-element.25), channel_id=1, replica_groups=mesh['zh'=4,'x'=4,'core'=2,'ri'=4,'rj'=4] {'x','rj'}, dimensions={0} | all-to-all | bytes 1048576 | tf_op jit(solution)/shard_map/all_to_all | solution.py:263
  81.7 0.1 reduce_sum.12.after
  81.8 8.8 %collective-permute-start.5 = (bf16[4,64,256]{2,1,0:T(8,128)(2,1)S(1)}, bf16[4,64,256]{2,1,0:T(8,128)(2,1)S(1)}, u32[]{:S(2)}, u32[]{:S(2)}) collective-permute-start(bf16[4,64,256]{2,1,0:T(8,128)(2,1)S(1)} %reduce_sum.12.after), channel_id=1, source_target_pairs={{0,128},{256,384},{128,0},{384,256},{1,129},{257,385},{129,1},{385... | collective-permute-start | bytes 393224 | tf_op jit(solution)/shard_map/ppermute | solution.py:232
  90.6 2.2 %collective-permute-start.7 = (bf16[4,64,256]{2,1,0:T(8,128)(2,1)S(1)}, bf16[4,64,256]{2,1,0:T(8,128)(2,1)S(1)}, u32[]{:S(2)}, u32[]{:S(2)}) collective-permute-start(bf16[4,64,256]{2,1,0:T(8,128)(2,1)S(1)} %get-tuple-element.28), channel_id=1, source_target_pairs={{0,1},{1,2},{2,3},{3,0},{4,5},{5,6},{6,7},{7,4},{8,9},{9,10},{10,1... | collective-permute-start | bytes 393224 | tf_op jit(solution)/shard_map/ppermute | solution.py:259
  92.9 3.3 %collective-permute-start.8 = (bf16[4,64,256]{2,1,0:T(8,128)(2,1)S(1)}, bf16[4,64,256]{2,1,0:T(8,128)(2,1)S(1)}, u32[]{:S(2)}, u32[]{:S(2)}) collective-permute-start(bf16[4,64,256]{2,1,0:T(8,128)(2,1)S(1)} %get-tuple-element.29), channel_id=1, source_target_pairs={{0,2},{1,3},{2,0},{3,1},{4,6},{5,7},{6,4},{7,5},{8,10},{9,11},{10,... | collective-permute-start | bytes 393224 | tf_op jit(solution)/shard_map/ppermute | solution.py:259
  96.1 3.3 %collective-permute-start.9 = (bf16[4,64,256]{2,1,0:T(8,128)(2,1)S(1)}, bf16[4,64,256]{2,1,0:T(8,128)(2,1)S(1)}, u32[]{:S(2)}, u32[]{:S(2)}) collective-permute-start(bf16[4,64,256]{2,1,0:T(8,128)(2,1)S(1)} %get-tuple-element.30), channel_id=1, source_target_pairs={{0,3},{1,0},{2,1},{3,2},{4,7},{5,4},{6,5},{7,6},{8,11},{9,8},{10,9... | collective-permute-start | bytes 393224 | tf_op jit(solution)/shard_map/ppermute | solution.py:259
  99.4 1.6 %collective-permute-done.5 = bf16[4,64,256]{2,1,0:T(8,128)(2,1)S(1)} collective-permute-done((bf16[4,64,256]{2,1,0:T(8,128)(2,1)S(1)}, bf16[4,64,256]{2,1,0:T(8,128)(2,1)S(1)}, u32[]{:S(2)}, u32[]{:S(2)}) %collective-permute-start.5) | collective-permute-done | bytes 131104 | tf_op jit(solution)/shard_map/ppermute | solution.py:232
  101.1 6.8 %collective-permute-start.6 = (bf16[4,64,256]{2,1,0:T(8,128)(2,1)S(1)}, bf16[4,64,256]{2,1,0:T(8,128)(2,1)S(1)}, u32[]{:S(2)}, u32[]{:S(2)}) collective-permute-start(bf16[4,64,256]{2,1,0:T(8,128)(2,1)S(1)} %add_convert_fusion.2.after), channel_id=1, source_target_pairs={{128,256},{384,0},{256,128},{0,384},{129,257},{385,1},{257,129},{1... | collective-permute-start | bytes 393224 | tf_op jit(solution)/shard_map/ppermute | solution.py:232
  107.9 0.1 shard_map.96
  108.1 1.9 %collective-permute-start.10 = (bf16[4,64,256]{2,1,0:T(8,128)(2,1)S(1)}, bf16[4,64,256]{2,1,0:T(8,128)(2,1)S(1)}, u32[]{:S(2)}, u32[]{:S(2)}) collective-permute-start(bf16[4,64,256]{2,1,0:T(8,128)(2,1)S(1)} %get-tuple-element.32), channel_id=1, source_target_pairs={{0,4},{4,8},{8,12},{12,0},{1,5},{5,9},{9,13},{13,1},{2,6},{6,10},{... | collective-permute-start | bytes 393224 | tf_op jit(solution)/shard_map/ppermute | solution.py:259
  110.0 1.9 %collective-permute-start.11 = (bf16[4,64,256]{2,1,0:T(8,128)(2,1)S(1)}, bf16[4,64,256]{2,1,0:T(8,128)(2,1)S(1)}, u32[]{:S(2)}, u32[]{:S(2)}) collective-permute-start(bf16[4,64,256]{2,1,0:T(8,128)(2,1)S(1)} %get-tuple-element.33), channel_id=1, source_target_pairs={{0,8},{4,12},{8,0},{12,4},{1,9},{5,13},{9,1},{13,5},{2,10},{6,14},... | collective-permute-start | bytes 393224 | tf_op jit(solution)/shard_map/ppermute | solution.py:259
  111.9 5.2 %collective-permute-start.12 = (bf16[4,64,256]{2,1,0:T(8,128)(2,1)S(1)}, bf16[4,64,256]{2,1,0:T(8,128)(2,1)S(1)}, u32[]{:S(2)}, u32[]{:S(2)}) collective-permute-start(bf16[4,64,256]{2,1,0:T(8,128)(2,1)S(1)} %get-tuple-element.34), channel_id=1, source_target_pairs={{0,12},{4,0},{8,4},{12,8},{1,13},{5,1},{9,5},{13,9},{2,14},{6,2},{... | collective-permute-start | bytes 393224 | tf_op jit(solution)/shard_map/ppermute | solution.py:259
  117.1 10.5 %all_gather.3 = bf16[16,64,256]{2,1,0:T(8,128)(2,1)S(1)} all-gather(bf16[4,64,256]{2,1,0:T(8,128)(2,1)S(1)} %add_convert_fusion.1), channel_id=1, replica_groups=mesh['zh'=4,'x'=4,'core'=2,'ri'=4,'rj'=4] {'x'}, dimensions={0}, use_global_device_ids=true | all-gather | bytes 655360 | tf_op jit(solution)/shard_map/all_gather | solution.py:271
  127.7 0.1 add_convert_fusion
  127.8 9.0 %collective-permute-start.13 = (bf16[1216,256]{1,0:T(8,128)(2,1)S(1)}, bf16[1216,256]{1,0:T(8,128)(2,1)S(1)}, u32[]{:S(2)}, u32[]{:S(2)}) collective-permute-start(bf16[1216,256]{1,0:T(8,128)(2,1)S(1)} %pad_maximum_fusion), channel_id=1, source_target_pairs={{0,16},{16,0},{1,17},{17,1},{2,18},{18,2},{3,19},{19,3},{4,20},{20... | collective-permute-start | bytes 1867784 | tf_op jit(solution)/shard_map/ppermute | solution.py:232
  136.8 1.0 shard_map.97.before
  137.8 0.6 collective-permute-done.13.x_ref
  138.4 1.1 shard_map.98
  (16 shorter events, 0.2 us)
Async XLA Ops:
  27.7 13.2 %collective-permute-start = (bf16[2,160,256]{2,1,0:T(8,128)(2,1)}, bf16[2,160,256]{2,1,0:T(8,128)(2,1)S(1)}, u32[]{:S(2)}, u32[]{:S(2)}) collective-permute-start(bf16[2,160,256]{2,1,0:T(8,128)(2,1)} %get-tuple-element.23), channel_id=1, source_target_pairs={{0,16},{16,0},{1,17},{17,1},{2,18},{18,2},{3,19},{19,3},{4,20},{20... | collective-permute-start | bytes 491528 | tf_op jit(solution)/shard_map/ppermute | solution.py:232
  36.5 18.2 %all-to-all-start = ((bf16[4,256,256]{2,1,0:T(8,128)(2,1)}), bf16[4,256,256]{2,1,0:T(8,128)(2,1)S(1)}, u32[]{:S(2)}, u32[]{:S(2)}) async-start(bf16[4,256,256]{2,1,0:T(8,128)(2,1)} %get-tuple-element.24), calls=%async_computation | async-start | bytes 1048576 | tf_op jit(solution)/shard_map/all_to_all | solution.py:253
  41.0 12.7 %collective-permute-start.4 = (bf16[4,64,256]{2,1,0:T(8,128)(2,1)S(1)}, bf16[4,64,256]{2,1,0:T(8,128)(2,1)S(1)}, u32[]{:S(2)}, u32[]{:S(2)}) collective-permute-start(bf16[4,64,256]{2,1,0:T(8,128)(2,1)S(1)} %slice.17), channel_id=1, source_target_pairs={{0,12},{1,0},{2,4},{3,8},{4,13},{5,1},{6,5},{7,9},{8,14},{9,2},{10... | collective-permute-start | bytes 393224 | tf_op jit(solution)/shard_map/ppermute | solution.py:250
  42.9 10.8 %collective-permute-start.3 = (bf16[4,64,256]{2,1,0:T(8,128)(2,1)S(1)}, bf16[4,64,256]{2,1,0:T(8,128)(2,1)S(1)}, u32[]{:S(2)}, u32[]{:S(2)}) collective-permute-start(bf16[4,64,256]{2,1,0:T(8,128)(2,1)S(1)} %slice.17), channel_id=1, source_target_pairs={{0,8},{1,12},{2,0},{3,4},{4,9},{5,13},{6,1},{7,5},{8,10},{9,14},{1... | collective-permute-start | bytes 393224 | tf_op jit(solution)/shard_map/ppermute | solution.py:250
  47.4 7.2 %collective-permute-start.2 = (bf16[4,64,256]{2,1,0:T(8,128)(2,1)S(1)}, bf16[4,64,256]{2,1,0:T(8,128)(2,1)S(1)}, u32[]{:S(2)}, u32[]{:S(2)}) collective-permute-start(bf16[4,64,256]{2,1,0:T(8,128)(2,1)S(1)} %slice.17), channel_id=1, source_target_pairs={{0,4},{1,8},{2,12},{3,0},{4,5},{5,9},{6,13},{7,1},{8,6},{9,10},{10... | collective-permute-start | bytes 393224 | tf_op jit(solution)/shard_map/ppermute | solution.py:250
  51.4 3.3 %collective-permute-start.1 = (bf16[4,64,256]{2,1,0:T(8,128)(2,1)S(1)}, bf16[4,64,256]{2,1,0:T(8,128)(2,1)S(1)}, u32[]{:S(2)}, u32[]{:S(2)}) collective-permute-start(bf16[4,64,256]{2,1,0:T(8,128)(2,1)S(1)} %slice.17), channel_id=1, source_target_pairs={{0,0},{1,4},{2,8},{3,12},{4,1},{5,5},{6,9},{7,13},{8,2},{9,6},{10,... | collective-permute-start | bytes 393224 | tf_op jit(solution)/shard_map/ppermute | solution.py:250
  81.8 19.2 %collective-permute-start.5 = (bf16[4,64,256]{2,1,0:T(8,128)(2,1)S(1)}, bf16[4,64,256]{2,1,0:T(8,128)(2,1)S(1)}, u32[]{:S(2)}, u32[]{:S(2)}) collective-permute-start(bf16[4,64,256]{2,1,0:T(8,128)(2,1)S(1)} %reduce_sum.12.after), channel_id=1, source_target_pairs={{0,128},{256,384},{128,0},{384,256},{1,129},{257,385},{129,1},{385... | collective-permute-start | bytes 393224 | tf_op jit(solution)/shard_map/ppermute | solution.py:232
  90.6 17.3 %collective-permute-start.7 = (bf16[4,64,256]{2,1,0:T(8,128)(2,1)S(1)}, bf16[4,64,256]{2,1,0:T(8,128)(2,1)S(1)}, u32[]{:S(2)}, u32[]{:S(2)}) collective-permute-start(bf16[4,64,256]{2,1,0:T(8,128)(2,1)S(1)} %get-tuple-element.28), channel_id=1, source_target_pairs={{0,1},{1,2},{2,3},{3,0},{4,5},{5,6},{6,7},{7,4},{8,9},{9,10},{10,1... | collective-permute-start | bytes 393224 | tf_op jit(solution)/shard_map/ppermute | solution.py:259
  92.9 15.1 %collective-permute-start.8 = (bf16[4,64,256]{2,1,0:T(8,128)(2,1)S(1)}, bf16[4,64,256]{2,1,0:T(8,128)(2,1)S(1)}, u32[]{:S(2)}, u32[]{:S(2)}) collective-permute-start(bf16[4,64,256]{2,1,0:T(8,128)(2,1)S(1)} %get-tuple-element.29), channel_id=1, source_target_pairs={{0,2},{1,3},{2,0},{3,1},{4,6},{5,7},{6,4},{7,5},{8,10},{9,11},{10,... | collective-permute-start | bytes 393224 | tf_op jit(solution)/shard_map/ppermute | solution.py:259
  96.1 11.8 %collective-permute-start.9 = (bf16[4,64,256]{2,1,0:T(8,128)(2,1)S(1)}, bf16[4,64,256]{2,1,0:T(8,128)(2,1)S(1)}, u32[]{:S(2)}, u32[]{:S(2)}) collective-permute-start(bf16[4,64,256]{2,1,0:T(8,128)(2,1)S(1)} %get-tuple-element.30), channel_id=1, source_target_pairs={{0,3},{1,0},{2,1},{3,2},{4,7},{5,4},{6,5},{7,6},{8,11},{9,8},{10,9... | collective-permute-start | bytes 393224 | tf_op jit(solution)/shard_map/ppermute | solution.py:259
  101.1 16.0 %collective-permute-start.6 = (bf16[4,64,256]{2,1,0:T(8,128)(2,1)S(1)}, bf16[4,64,256]{2,1,0:T(8,128)(2,1)S(1)}, u32[]{:S(2)}, u32[]{:S(2)}) collective-permute-start(bf16[4,64,256]{2,1,0:T(8,128)(2,1)S(1)} %add_convert_fusion.2.after), channel_id=1, source_target_pairs={{128,256},{384,0},{256,128},{0,384},{129,257},{385,1},{257,129},{1... | collective-permute-start | bytes 393224 | tf_op jit(solution)/shard_map/ppermute | solution.py:232
  108.1 19.6 %collective-permute-start.10 = (bf16[4,64,256]{2,1,0:T(8,128)(2,1)S(1)}, bf16[4,64,256]{2,1,0:T(8,128)(2,1)S(1)}, u32[]{:S(2)}, u32[]{:S(2)}) collective-permute-start(bf16[4,64,256]{2,1,0:T(8,128)(2,1)S(1)} %get-tuple-element.32), channel_id=1, source_target_pairs={{0,4},{4,8},{8,12},{12,0},{1,5},{5,9},{9,13},{13,1},{2,6},{6,10},{... | collective-permute-start | bytes 393224 | tf_op jit(solution)/shard_map/ppermute | solution.py:259
  110.0 17.7 %collective-permute-start.11 = (bf16[4,64,256]{2,1,0:T(8,128)(2,1)S(1)}, bf16[4,64,256]{2,1,0:T(8,128)(2,1)S(1)}, u32[]{:S(2)}, u32[]{:S(2)}) collective-permute-start(bf16[4,64,256]{2,1,0:T(8,128)(2,1)S(1)} %get-tuple-element.33), channel_id=1, source_target_pairs={{0,8},{4,12},{8,0},{12,4},{1,9},{5,13},{9,1},{13,5},{2,10},{6,14},... | collective-permute-start | bytes 393224 | tf_op jit(solution)/shard_map/ppermute | solution.py:259
  111.9 15.7 %collective-permute-start.12 = (bf16[4,64,256]{2,1,0:T(8,128)(2,1)S(1)}, bf16[4,64,256]{2,1,0:T(8,128)(2,1)S(1)}, u32[]{:S(2)}, u32[]{:S(2)}) collective-permute-start(bf16[4,64,256]{2,1,0:T(8,128)(2,1)S(1)} %get-tuple-element.34), channel_id=1, source_target_pairs={{0,12},{4,0},{8,4},{12,8},{1,13},{5,1},{9,5},{13,9},{2,14},{6,2},{... | collective-permute-start | bytes 393224 | tf_op jit(solution)/shard_map/ppermute | solution.py:259
  127.8 10.6 %collective-permute-start.13 = (bf16[1216,256]{1,0:T(8,128)(2,1)S(1)}, bf16[1216,256]{1,0:T(8,128)(2,1)S(1)}, u32[]{:S(2)}, u32[]{:S(2)}) collective-permute-start(bf16[1216,256]{1,0:T(8,128)(2,1)S(1)} %pad_maximum_fusion), channel_id=1, source_target_pairs={{0,16},{16,0},{1,17},{17,1},{2,18},{18,2},{3,19},{19,3},{4,20},{20... | collective-permute-start | bytes 1867784 | tf_op jit(solution)/shard_map/ppermute | solution.py:232

commit v10 on v9

--- a/solution.py
+++ b/solution.py
@@ -21,19 +21,33 @@
 NN = (((1,), (0,)), ((), ()))
 
 
-def pack_kernel(k_ref, v_ref, q_ref, g_ref, o_ref, bias_ref, keep, send, bias_out, sem):
+def pack_kernel(*refs):
+    inputs, bias_ref = refs[:5], refs[5]
+    keep, send, bias_out, held, bias_held, sem = refs[6:]
     core = lax.axis_index("core")
-    copies = []
-    for out, which in ((send, 1 - core), (keep, core)):
-        half = pl.ds(pl.multiple_of(which * HEAD, HEAD), HEAD)
-        for i, x_ref in enumerate((k_ref, v_ref, q_ref, g_ref, o_ref)):
-            copies.append((x_ref.at[:, half, :], out.at[:, i * HEAD : (i + 1) * HEAD, :]))
+    inward = [
+        pltpu.make_async_copy(x_ref, held.at[i], sem.at[i]) for i, x_ref in enumerate(inputs)
+    ]
     for j in range(N):
-        copies.append((bias_ref.at[2 * j + core], bias_out.at[j]))
-    copies = [pltpu.make_async_copy(*c, sem.at[i]) for i, c in enumerate(copies)]
-    for c in copies:
+        src = bias_ref.at[2 * j + core]
+        inward.append(pltpu.make_async_copy(src, bias_held.at[j], sem.at[5 + j]))
+    for c in inward:
         c.start()
-    for c in copies:
+    outward = []
+    for i in range(5):
+        inward[i].wait()
+        to = slice(i * HEAD, (i + 1) * HEAD)
+        for out, which in ((send, 1 - core), (keep, core)):
+            half = pl.ds(pl.multiple_of(which * HEAD, HEAD), HEAD)
+            here = sem.at[5 + N + len(outward)]
+            outward.append(pltpu.make_async_copy(held.at[i, :, half, :], out.at[:, to, :], here))
+            outward[-1].start()
+    for j in range(N):
+        inward[5 + j].wait()
+        here = sem.at[5 + N + len(outward)]
+        outward.append(pltpu.make_async_copy(bias_held.at[j], bias_out.at[j], here))
+        outward[-1].start()
+    for c in outward:
         c.wait()
 
 
@@ -45,7 +59,11 @@
         out_shape=(half, half, jax.ShapeDtypeStruct((N, ROWS, ROWS), BF)),
         in_specs=[hbm] * 6,
         out_specs=(hbm,) * 3,
-        scratch_shapes=[pltpu.SemaphoreType.DMA((10 + N,))],
+        scratch_shapes=[
+            pltpu.VMEM((5, *args[0].shape), BF),
+            pltpu.VMEM((N, ROWS, ROWS), BF),
+            pltpu.SemaphoreType.DMA((15 + 2 * N,)),
+        ],
         compiler_params=pltpu.CompilerParams(vmem_limit_bytes=56 * 2**20),
         cost_estimate=pl.CostEstimate(flops=0, bytes_accessed=2**21, transcendentals=0),
     )(*args)
@@ -58,7 +76,7 @@
 ):
     ri, rj = lax.axis_index("ri"), lax.axis_index("rj")
     kvs = (kv0, kv1, kv2, kv3)
-    blocks = [lax.rem(ri + N - t, N) for t in range(N)]
+    blocks = [lax.rem(ri + 2 * N - rj - t, N) for t in range(N)]
     channel = lax.broadcasted_iota(jnp.int32, (2 * HEAD, ROWS), 0) // HEAD
 
     for s in range(SEQS):
@@ -247,7 +265,7 @@
     both = jnp.concatenate([keep, swap(send, "core", [(0, 1)])])
     kv, qgo = both[:, : 2 * HEAD], both[:, 2 * HEAD :]
     kvs = [
-        lax.ppermute(kv, ("ri", "rj"), [(a * N + b, (b + t) % N * N + a) for a, b in grid])
+        lax.ppermute(kv, ("ri", "rj"), [(a * N + b, (a + b + t) % N * N + a) for a, b in grid])
         for t in range(N)
     ]
     bias = lax.all_to_all(bias, "rj", 0, 0, tiled=True)

time: 140 us -> 114 us (0.81)
  Pallas kernels: 33.9 us -> 8.97 us
  blocking collectives: 32.9 us -> 28.9 us
  waiting for transfers between devices: 4.79 us -> 7.45 us
    pallas_call x1, Pallas kernels: 27 us -> 2.1 us  [pack(): pl.pallas_call(pack_kernel, out_shape=(half, half, jax.ShapeDtypeStruct((...]
    ppermute x6, starting transfers between devices: 17.8 us -> 22.9 us  [spread_out(): lax.ppermute(parts[t], axis, [(a, (a + t) % N) for a in range(N)])]
    all_to_all x1, blocking collectives: 22.4 us -> 18 us  [body(): spread = lax.all_to_all(total, ('x', 'rj'), 0, 0, tiled=True)]
    ppermute x4, waiting for transfers between devices: 2.55 us -> 6.79 us  [body(): lax.ppermute(kv, ('ri', 'rj'), [(a * N + b, (a + b + t) % N * N + a) for...]
    ppermute x4, starting transfers between devices: 33.4 us -> 29.9 us  [swap(): lax.ppermute(x, axis, [(a, b) for a, b in pairs] + [(b, a) for a, b in pa...]
    ppermute x4, starting transfers between devices: 11.1 us -> 9.32 us  [body(): lax.ppermute(kv, ('ri', 'rj'), [(a * N + b, (a + b + t) % N * N + a) for...]
    ppermute x4, waiting for transfers between devices: 2.22 us -> 0.64 us  [swap(): lax.ppermute(x, axis, [(a, b) for a, b in pairs] + [(b, a) for a, b in pa...]
where the time goes in v10:
time: 114 us; the launch traced here: 113 us
  starting transfers between devices  65.6 us (58%)
  blocking collectives  28.9 us (25%)
  Pallas kernels  8.97 us (8%)
  waiting for transfers between devices  7.45 us (7%)
    ppermute x4, starting transfers between devices, swap(): lax.ppermute(x, axis, [(a, b) for a, b in pairs] + [(b, a) for a, b in pa...  29.9 us
    ppermute x6, starting transfers between devices, spread_out(): lax.ppermute(parts[t], axis, [(a, (a + t) % N) for a in range(N)])  22.9 us
    all_to_all x1, blocking collectives, body(): spread = lax.all_to_all(total, ('x', 'rj'), 0, 0, tiled=True)  18 us
    all_gather x1, blocking collectives, body(): mine = lax.all_gather(total, 'x', axis=0, tiled=True).reshape(-1, ROWS)  10.9 us
    ppermute x4, starting transfers between devices, body(): lax.ppermute(kv, ('ri', 'rj'), [(a * N + b, (a + b + t) % N * N + a) for...  9.32 us
    ppermute x4, waiting for transfers between devices, body(): lax.ppermute(kv, ('ri', 'rj'), [(a * N + b, (a + b + t) % N * N + a) for...  6.79 us
    pallas_call x1, Pallas kernels, attention(): pl.pallas_call(attention_kernel, out_shape=(jax.ShapeDtypeStruct((N * N,...  4.6 us
    all_to_all x1, starting transfers between devices, body(): bias = lax.all_to_all(bias, 'rj', 0, 0, tiled=True)  3.48 us
  transfers between devices with their start and end apart: 15, of which 4 were waited for; matrix products, arithmetic and copies ran while one was open for 1% of the time, Pallas kernels for 1%

profile of v10, /device:TPU:1, one launch (start us, length us, event | category | flops | bytes accessed | tf_op | source)
XLA Modules:
  0.0 113.1 jit_solution(10348427391069889142)
XLA Ops:
  0.6 2.1 %shard_map.93 = (bf16[2,160,256]{2,1,0:T(8,128)(2,1)}, bf16[2,160,256]{2,1,0:T(8,128)(2,1)}, bf16[4,256,256]{2,1,0:T(8,128)(2,1)}) custom-call(bf16[2,64,256]{2,1,0:T(8,128)(2,1)} %bitcast.15, bf16[2,64,256]{2,1,0:T(8,128)(2,1)} %bitcast.16, bf16[2,64,256]{2,1,0:T(8,128)(2,1)} %bitcast.17, bf16[2,64,256]{2,1,0:T(8,128)(2,1)} %bitcast.18, ...), custom_call_target="tpu_custom_call" | custom-call | bytes 2097152 | tf_op jit(solution)/shard_map/pallas_call | solution.py:57
  2.7 8.8 %collective-permute-start = (bf16[2,160,256]{2,1,0:T(8,128)(2,1)}, bf16[2,160,256]{2,1,0:T(8,128)(2,1)S(1)}, u32[]{:S(2)}, u32[]{:S(2)}) collective-permute-start(bf16[2,160,256]{2,1,0:T(8,128)(2,1)} %get-tuple-element.23), channel_id=1, source_target_pairs={{0,16},{16,0},{1,17},{17,1},{2,18},{18,2},{3,19},{19,3},{4,20},{20... | collective-permute-start | bytes 491528 | tf_op jit(solution)/shard_map/ppermute | solution.py:250
  11.5 3.5 %all-to-all-start = ((bf16[4,256,256]{2,1,0:T(8,128)(2,1)}), bf16[4,256,256]{2,1,0:T(8,128)(2,1)S(1)}, u32[]{:S(2)}, u32[]{:S(2)}) async-start(bf16[4,256,256]{2,1,0:T(8,128)(2,1)} %get-tuple-element.24), calls=%async_computation | async-start | bytes 1048576 | tf_op jit(solution)/shard_map/all_to_all | solution.py:271
  15.0 0.9 constant_dynamic-update-slice_fusion.1
  16.0 1.9 %collective-permute-start.4 = (bf16[4,64,256]{2,1,0:T(8,128)(2,1)S(1)}, bf16[4,64,256]{2,1,0:T(8,128)(2,1)S(1)}, u32[]{:S(2)}, u32[]{:S(2)}) collective-permute-start(bf16[4,64,256]{2,1,0:T(8,128)(2,1)S(1)} %slice.17), channel_id=1, source_target_pairs={{0,12},{1,0},{2,4},{3,8},{4,1},{5,5},{6,9},{7,13},{8,6},{9,10},{10... | collective-permute-start | bytes 393224 | tf_op jit(solution)/shard_map/ppermute | solution.py:268
  17.9 2.7 %collective-permute-start.3 = (bf16[4,64,256]{2,1,0:T(8,128)(2,1)S(1)}, bf16[4,64,256]{2,1,0:T(8,128)(2,1)S(1)}, u32[]{:S(2)}, u32[]{:S(2)}) collective-permute-start(bf16[4,64,256]{2,1,0:T(8,128)(2,1)S(1)} %slice.17), channel_id=1, source_target_pairs={{0,8},{1,12},{2,0},{3,4},{4,13},{5,1},{6,5},{7,9},{8,2},{9,6},{10,... | collective-permute-start | bytes 393224 | tf_op jit(solution)/shard_map/ppermute | solution.py:268
  20.7 4.0 %collective-permute-start.2 = (bf16[4,64,256]{2,1,0:T(8,128)(2,1)S(1)}, bf16[4,64,256]{2,1,0:T(8,128)(2,1)S(1)}, u32[]{:S(2)}, u32[]{:S(2)}) collective-permute-start(bf16[4,64,256]{2,1,0:T(8,128)(2,1)S(1)} %slice.17), channel_id=1, source_target_pairs={{0,4},{1,8},{2,12},{3,0},{4,9},{5,13},{6,1},{7,5},{8,14},{9,2},{10... | collective-permute-start | bytes 393224 | tf_op jit(solution)/shard_map/ppermute | solution.py:268
  24.7 0.7 collective-permute-start.1
  25.4 0.5 collective-permute-done.4.kv3
  25.9 4.4 %collective-permute-done.3.kv2 = bf16[4,64,256]{2,1,0:T(8,128)(2,1)S(1)} collective-permute-done((bf16[4,64,256]{2,1,0:T(8,128)(2,1)S(1)}, bf16[4,64,256]{2,1,0:T(8,128)(2,1)S(1)}, u32[]{:S(2)}, u32[]{:S(2)}) %collective-permute-start.3) | collective-permute-done | bytes 131104 | tf_op jit(solution)/shard_map/ppermute | solution.py:268
  30.3 1.9 %collective-permute-done.2.kv1 = bf16[4,64,256]{2,1,0:T(8,128)(2,1)S(1)} collective-permute-done((bf16[4,64,256]{2,1,0:T(8,128)(2,1)S(1)}, bf16[4,64,256]{2,1,0:T(8,128)(2,1)S(1)}, u32[]{:S(2)}, u32[]{:S(2)}) %collective-permute-start.2) | collective-permute-done | bytes 131104 | tf_op jit(solution)/shard_map/ppermute | solution.py:268
  32.2 4.6 %shard_map.94 = (bf16[16,64,256]{2,1,0:T(8,128)(2,1)S(1)}, bf16[4,32,256]{2,1,0:T(8,128)(2,1)S(1)}, bf16[4,4,64,256]{3,2,1,0:T(8,128)(2,1)S(1)}) custom-call(bf16[4,96,256]{2,1,0:T(8,128)(2,1)S(1)} %slice.16.qgo_ref, bf16[4,64,256]{2,1,0:T(8,128)(2,1)S(1)} %collective-permute-done.1.kv0, bf16[4,64,256]{2,1,0:T(8,128)(2,1)S(1)} %collective-permute-done.2.kv1, ...), custom_call_target="tpu_custom_call" | custom-call | flops 335544320 | bytes 6291456 | tf_op jit(solution)/shard_map/pallas_call | solution.py:134
  36.8 18.0 %all_to_all.10 = bf16[16,64,256]{2,1,0:T(8,128)(2,1)S(1)} all-to-all(bf16[16,64,256]{2,1,0:T(8,128)(2,1)S(1)} %get-tuple-element.25), channel_id=1, replica_groups=mesh['zh'=4,'x'=4,'core'=2,'ri'=4,'rj'=4] {'x','rj'}, dimensions={0} | all-to-all | bytes 1048576 | tf_op jit(solution)/shard_map/all_to_all | solution.py:281
  54.8 0.1 reduce_sum.12.after
  54.9 8.2 %collective-permute-start.5 = (bf16[4,64,256]{2,1,0:T(8,128)(2,1)S(1)}, bf16[4,64,256]{2,1,0:T(8,128)(2,1)S(1)}, u32[]{:S(2)}, u32[]{:S(2)}) collective-permute-start(bf16[4,64,256]{2,1,0:T(8,128)(2,1)S(1)} %reduce_sum.12.after), channel_id=1, source_target_pairs={{0,128},{256,384},{128,0},{384,256},{1,129},{257,385},{129,1},{385... | collective-permute-start | bytes 393224 | tf_op jit(solution)/shard_map/ppermute | solution.py:250
  63.1 2.3 %collective-permute-start.7 = (bf16[4,64,256]{2,1,0:T(8,128)(2,1)S(1)}, bf16[4,64,256]{2,1,0:T(8,128)(2,1)S(1)}, u32[]{:S(2)}, u32[]{:S(2)}) collective-permute-start(bf16[4,64,256]{2,1,0:T(8,128)(2,1)S(1)} %get-tuple-element.28), channel_id=1, source_target_pairs={{0,1},{1,2},{2,3},{3,0},{4,5},{5,6},{6,7},{7,4},{8,9},{9,10},{10,1... | collective-permute-start | bytes 393224 | tf_op jit(solution)/shard_map/ppermute | solution.py:277
  65.4 2.9 %collective-permute-start.8 = (bf16[4,64,256]{2,1,0:T(8,128)(2,1)S(1)}, bf16[4,64,256]{2,1,0:T(8,128)(2,1)S(1)}, u32[]{:S(2)}, u32[]{:S(2)}) collective-permute-start(bf16[4,64,256]{2,1,0:T(8,128)(2,1)S(1)} %get-tuple-element.29), channel_id=1, source_target_pairs={{0,2},{1,3},{2,0},{3,1},{4,6},{5,7},{6,4},{7,5},{8,10},{9,11},{10,... | collective-permute-start | bytes 393224 | tf_op jit(solution)/shard_map/ppermute | solution.py:277
  68.3 3.4 %collective-permute-start.9 = (bf16[4,64,256]{2,1,0:T(8,128)(2,1)S(1)}, bf16[4,64,256]{2,1,0:T(8,128)(2,1)S(1)}, u32[]{:S(2)}, u32[]{:S(2)}) collective-permute-start(bf16[4,64,256]{2,1,0:T(8,128)(2,1)S(1)} %get-tuple-element.30), channel_id=1, source_target_pairs={{0,3},{1,0},{2,1},{3,2},{4,7},{5,4},{6,5},{7,6},{8,11},{9,8},{10,9... | collective-permute-start | bytes 393224 | tf_op jit(solution)/shard_map/ppermute | solution.py:277
  71.7 0.0 collective-permute-done.5
  71.8 7.0 %collective-permute-start.6 = (bf16[4,64,256]{2,1,0:T(8,128)(2,1)S(1)}, bf16[4,64,256]{2,1,0:T(8,128)(2,1)S(1)}, u32[]{:S(2)}, u32[]{:S(2)}) collective-permute-start(bf16[4,64,256]{2,1,0:T(8,128)(2,1)S(1)} %add_convert_fusion.2.after), channel_id=1, source_target_pairs={{128,256},{384,0},{256,128},{0,384},{129,257},{385,1},{257,129},{1... | collective-permute-start | bytes 393224 | tf_op jit(solution)/shard_map/ppermute | solution.py:250
  78.8 0.0 collective-permute-done.7.refs_1_
  78.9 0.0 collective-permute-done.8.refs_2_
  78.9 0.1 shard_map.96
  79.0 5.4 %collective-permute-start.10 = (bf16[4,64,256]{2,1,0:T(8,128)(2,1)S(1)}, bf16[4,64,256]{2,1,0:T(8,128)(2,1)S(1)}, u32[]{:S(2)}, u32[]{:S(2)}) collective-permute-start(bf16[4,64,256]{2,1,0:T(8,128)(2,1)S(1)} %get-tuple-element.32), channel_id=1, source_target_pairs={{0,4},{4,8},{8,12},{12,0},{1,5},{5,9},{9,13},{13,1},{2,6},{6,10},{... | collective-permute-start | bytes 393224 | tf_op jit(solution)/shard_map/ppermute | solution.py:277
  84.4 7.1 %collective-permute-start.11 = (bf16[4,64,256]{2,1,0:T(8,128)(2,1)S(1)}, bf16[4,64,256]{2,1,0:T(8,128)(2,1)S(1)}, u32[]{:S(2)}, u32[]{:S(2)}) collective-permute-start(bf16[4,64,256]{2,1,0:T(8,128)(2,1)S(1)} %get-tuple-element.33), channel_id=1, source_target_pairs={{0,8},{4,12},{8,0},{12,4},{1,9},{5,13},{9,1},{13,5},{2,10},{6,14},... | collective-permute-start | bytes 393224 | tf_op jit(solution)/shard_map/ppermute | solution.py:277
  91.4 1.9 %collective-permute-start.12 = (bf16[4,64,256]{2,1,0:T(8,128)(2,1)S(1)}, bf16[4,64,256]{2,1,0:T(8,128)(2,1)S(1)}, u32[]{:S(2)}, u32[]{:S(2)}) collective-permute-start(bf16[4,64,256]{2,1,0:T(8,128)(2,1)S(1)} %get-tuple-element.34), channel_id=1, source_target_pairs={{0,12},{4,0},{8,4},{12,8},{1,13},{5,1},{9,5},{13,9},{2,14},{6,2},{... | collective-permute-start | bytes 393224 | tf_op jit(solution)/shard_map/ppermute | solution.py:277
  93.4 10.9 %all_gather.3 = bf16[16,64,256]{2,1,0:T(8,128)(2,1)S(1)} all-gather(bf16[4,64,256]{2,1,0:T(8,128)(2,1)S(1)} %add_convert_fusion.1), channel_id=1, replica_groups=mesh['zh'=4,'x'=4,'core'=2,'ri'=4,'rj'=4] {'x'}, dimensions={0}, use_global_device_ids=true | all-gather | bytes 655360 | tf_op jit(solution)/shard_map/all_gather | solution.py:289
  104.4 0.1 add_convert_fusion
  104.5 5.9 %collective-permute-start.13 = (bf16[1216,256]{1,0:T(8,128)(2,1)S(1)}, bf16[1216,256]{1,0:T(8,128)(2,1)S(1)}, u32[]{:S(2)}, u32[]{:S(2)}) collective-permute-start(bf16[1216,256]{1,0:T(8,128)(2,1)S(1)} %pad_maximum_fusion), channel_id=1, source_target_pairs={{0,16},{16,0},{1,17},{17,1},{2,18},{18,2},{3,19},{19,3},{4,20},{20... | collective-permute-start | bytes 1867784 | tf_op jit(solution)/shard_map/ppermute | solution.py:250
  110.4 1.0 shard_map.97.before
  111.4 0.6 collective-permute-done.13.x_ref
  112.1 1.1 shard_map.98
  (16 shorter events, 0.2 us)
Async XLA Ops:
  2.7 13.2 %collective-permute-start = (bf16[2,160,256]{2,1,0:T(8,128)(2,1)}, bf16[2,160,256]{2,1,0:T(8,128)(2,1)S(1)}, u32[]{:S(2)}, u32[]{:S(2)}) collective-permute-start(bf16[2,160,256]{2,1,0:T(8,128)(2,1)} %get-tuple-element.23), channel_id=1, source_target_pairs={{0,16},{16,0},{1,17},{17,1},{2,18},{18,2},{3,19},{19,3},{4,20},{20... | collective-permute-start | bytes 491528 | tf_op jit(solution)/shard_map/ppermute | solution.py:250
  11.5 20.6 %all-to-all-start = ((bf16[4,256,256]{2,1,0:T(8,128)(2,1)}), bf16[4,256,256]{2,1,0:T(8,128)(2,1)S(1)}, u32[]{:S(2)}, u32[]{:S(2)}) async-start(bf16[4,256,256]{2,1,0:T(8,128)(2,1)} %get-tuple-element.24), calls=%async_computation | async-start | bytes 1048576 | tf_op jit(solution)/shard_map/all_to_all | solution.py:271
  16.0 9.9 %collective-permute-start.4 = (bf16[4,64,256]{2,1,0:T(8,128)(2,1)S(1)}, bf16[4,64,256]{2,1,0:T(8,128)(2,1)S(1)}, u32[]{:S(2)}, u32[]{:S(2)}) collective-permute-start(bf16[4,64,256]{2,1,0:T(8,128)(2,1)S(1)} %slice.17), channel_id=1, source_target_pairs={{0,12},{1,0},{2,4},{3,8},{4,1},{5,5},{6,9},{7,13},{8,6},{9,10},{10... | collective-permute-start | bytes 393224 | tf_op jit(solution)/shard_map/ppermute | solution.py:268
  17.9 12.4 %collective-permute-start.3 = (bf16[4,64,256]{2,1,0:T(8,128)(2,1)S(1)}, bf16[4,64,256]{2,1,0:T(8,128)(2,1)S(1)}, u32[]{:S(2)}, u32[]{:S(2)}) collective-permute-start(bf16[4,64,256]{2,1,0:T(8,128)(2,1)S(1)} %slice.17), channel_id=1, source_target_pairs={{0,8},{1,12},{2,0},{3,4},{4,13},{5,1},{6,5},{7,9},{8,2},{9,6},{10,... | collective-permute-start | bytes 393224 | tf_op jit(solution)/shard_map/ppermute | solution.py:268
  20.7 11.5 %collective-permute-start.2 = (bf16[4,64,256]{2,1,0:T(8,128)(2,1)S(1)}, bf16[4,64,256]{2,1,0:T(8,128)(2,1)S(1)}, u32[]{:S(2)}, u32[]{:S(2)}) collective-permute-start(bf16[4,64,256]{2,1,0:T(8,128)(2,1)S(1)} %slice.17), channel_id=1, source_target_pairs={{0,4},{1,8},{2,12},{3,0},{4,9},{5,13},{6,1},{7,5},{8,14},{9,2},{10... | collective-permute-start | bytes 393224 | tf_op jit(solution)/shard_map/ppermute | solution.py:268
  24.7 7.5 %collective-permute-start.1 = (bf16[4,64,256]{2,1,0:T(8,128)(2,1)S(1)}, bf16[4,64,256]{2,1,0:T(8,128)(2,1)S(1)}, u32[]{:S(2)}, u32[]{:S(2)}) collective-permute-start(bf16[4,64,256]{2,1,0:T(8,128)(2,1)S(1)} %slice.17), channel_id=1, source_target_pairs={{0,0},{1,4},{2,8},{3,12},{4,5},{5,9},{6,13},{7,1},{8,10},{9,14},{1... | collective-permute-start | bytes 393224 | tf_op jit(solution)/shard_map/ppermute | solution.py:268
  54.9 16.9 %collective-permute-start.5 = (bf16[4,64,256]{2,1,0:T(8,128)(2,1)S(1)}, bf16[4,64,256]{2,1,0:T(8,128)(2,1)S(1)}, u32[]{:S(2)}, u32[]{:S(2)}) collective-permute-start(bf16[4,64,256]{2,1,0:T(8,128)(2,1)S(1)} %reduce_sum.12.after), channel_id=1, source_target_pairs={{0,128},{256,384},{128,0},{384,256},{1,129},{257,385},{129,1},{385... | collective-permute-start | bytes 393224 | tf_op jit(solution)/shard_map/ppermute | solution.py:250
  63.1 15.7 %collective-permute-start.7 = (bf16[4,64,256]{2,1,0:T(8,128)(2,1)S(1)}, bf16[4,64,256]{2,1,0:T(8,128)(2,1)S(1)}, u32[]{:S(2)}, u32[]{:S(2)}) collective-permute-start(bf16[4,64,256]{2,1,0:T(8,128)(2,1)S(1)} %get-tuple-element.28), channel_id=1, source_target_pairs={{0,1},{1,2},{2,3},{3,0},{4,5},{5,6},{6,7},{7,4},{8,9},{9,10},{10,1... | collective-permute-start | bytes 393224 | tf_op jit(solution)/shard_map/ppermute | solution.py:277
  65.4 13.4 %collective-permute-start.8 = (bf16[4,64,256]{2,1,0:T(8,128)(2,1)S(1)}, bf16[4,64,256]{2,1,0:T(8,128)(2,1)S(1)}, u32[]{:S(2)}, u32[]{:S(2)}) collective-permute-start(bf16[4,64,256]{2,1,0:T(8,128)(2,1)S(1)} %get-tuple-element.29), channel_id=1, source_target_pairs={{0,2},{1,3},{2,0},{3,1},{4,6},{5,7},{6,4},{7,5},{8,10},{9,11},{10,... | collective-permute-start | bytes 393224 | tf_op jit(solution)/shard_map/ppermute | solution.py:277
  68.3 10.5 %collective-permute-start.9 = (bf16[4,64,256]{2,1,0:T(8,128)(2,1)S(1)}, bf16[4,64,256]{2,1,0:T(8,128)(2,1)S(1)}, u32[]{:S(2)}, u32[]{:S(2)}) collective-permute-start(bf16[4,64,256]{2,1,0:T(8,128)(2,1)S(1)} %get-tuple-element.30), channel_id=1, source_target_pairs={{0,3},{1,0},{2,1},{3,2},{4,7},{5,4},{6,5},{7,6},{8,11},{9,8},{10,9... | collective-permute-start | bytes 393224 | tf_op jit(solution)/shard_map/ppermute | solution.py:277
  71.8 21.6 %collective-permute-start.6 = (bf16[4,64,256]{2,1,0:T(8,128)(2,1)S(1)}, bf16[4,64,256]{2,1,0:T(8,128)(2,1)S(1)}, u32[]{:S(2)}, u32[]{:S(2)}) collective-permute-start(bf16[4,64,256]{2,1,0:T(8,128)(2,1)S(1)} %add_convert_fusion.2.after), channel_id=1, source_target_pairs={{128,256},{384,0},{256,128},{0,384},{129,257},{385,1},{257,129},{1... | collective-permute-start | bytes 393224 | tf_op jit(solution)/shard_map/ppermute | solution.py:250
  79.0 25.3 %collective-permute-start.10 = (bf16[4,64,256]{2,1,0:T(8,128)(2,1)S(1)}, bf16[4,64,256]{2,1,0:T(8,128)(2,1)S(1)}, u32[]{:S(2)}, u32[]{:S(2)}) collective-permute-start(bf16[4,64,256]{2,1,0:T(8,128)(2,1)S(1)} %get-tuple-element.32), channel_id=1, source_target_pairs={{0,4},{4,8},{8,12},{12,0},{1,5},{5,9},{9,13},{13,1},{2,6},{6,10},{... | collective-permute-start | bytes 393224 | tf_op jit(solution)/shard_map/ppermute | solution.py:277
  84.4 20.0 %collective-permute-start.11 = (bf16[4,64,256]{2,1,0:T(8,128)(2,1)S(1)}, bf16[4,64,256]{2,1,0:T(8,128)(2,1)S(1)}, u32[]{:S(2)}, u32[]{:S(2)}) collective-permute-start(bf16[4,64,256]{2,1,0:T(8,128)(2,1)S(1)} %get-tuple-element.33), channel_id=1, source_target_pairs={{0,8},{4,12},{8,0},{12,4},{1,9},{5,13},{9,1},{13,5},{2,10},{6,14},... | collective-permute-start | bytes 393224 | tf_op jit(solution)/shard_map/ppermute | solution.py:277
  91.4 12.9 %collective-permute-start.12 = (bf16[4,64,256]{2,1,0:T(8,128)(2,1)S(1)}, bf16[4,64,256]{2,1,0:T(8,128)(2,1)S(1)}, u32[]{:S(2)}, u32[]{:S(2)}) collective-permute-start(bf16[4,64,256]{2,1,0:T(8,128)(2,1)S(1)} %get-tuple-element.34), channel_id=1, source_target_pairs={{0,12},{4,0},{8,4},{12,8},{1,13},{5,1},{9,5},{13,9},{2,14},{6,2},{... | collective-permute-start | bytes 393224 | tf_op jit(solution)/shard_map/ppermute | solution.py:277
  104.5 7.5 %collective-permute-start.13 = (bf16[1216,256]{1,0:T(8,128)(2,1)S(1)}, bf16[1216,256]{1,0:T(8,128)(2,1)S(1)}, u32[]{:S(2)}, u32[]{:S(2)}) collective-permute-start(bf16[1216,256]{1,0:T(8,128)(2,1)S(1)} %pad_maximum_fusion), channel_id=1, source_target_pairs={{0,16},{16,0},{1,17},{17,1},{2,18},{18,2},{3,19},{19,3},{4,20},{20... | collective-permute-start | bytes 1867784 | tf_op jit(solution)/shard_map/ppermute | solution.py:250

commit v11 on v10

--- a/solution.py
+++ b/solution.py
@@ -71,11 +71,11 @@
 
 def attention_kernel(
     qgo_ref, kv0, kv1, kv2, kv3, bias,
-    bias_grad, dq_ref, dkv_ref,
+    bias_grad, dq_ref, dkv0, dkv1, dkv2, dkv3,
     stack, wide, raw, low, inner,
 ):
     ri, rj = lax.axis_index("ri"), lax.axis_index("rj")
-    kvs = (kv0, kv1, kv2, kv3)
+    kvs, dkv_refs = (kv0, kv1, kv2, kv3), (dkv0, dkv1, dkv2, dkv3)
     blocks = [lax.rem(ri + 2 * N - rj - t, N) for t in range(N)]
     channel = lax.broadcasted_iota(jnp.int32, (2 * HEAD, ROWS), 0) // HEAD
 
@@ -119,14 +119,16 @@
 
     for s in range(SEQS):
         query_grads = None
-        for t, b in enumerate(blocks):
+        for t in range(N):
             at = slice(t * ROWS, (t + 1) * ROWS)
-            grads = lax.dot_general(wide[s], low[s, :, at], NN, preferred_element_type=F32)
-            grads = jnp.where(channel == 0, grads * SCALE, grads)
-            dkv_ref[lax.rem(b + N - rj, N), s] = grads.astype(BF)
             term = lax.dot_general(low[s, :ROWS, at], kvs[t][s], NT, preferred_element_type=F32)
             query_grads = term if query_grads is None else query_grads + term
         dq_ref[s] = (query_grads.T[:HEAD] * SCALE).astype(BF)
+        for u, dkv_ref in enumerate(dkv_refs):
+            t = lax.rem(ri + 3 * N - 2 * rj - u, N)
+            at = pl.ds(pl.multiple_of(t * ROWS, ROWS), ROWS)
+            grads = lax.dot_general(wide[s], low[s, :, at], NN, preferred_element_type=F32)
+            dkv_ref[s] = jnp.where(channel == 0, grads * SCALE, grads).astype(BF)
 
 
 def attention(qgo, kvs, bias):
@@ -136,10 +138,10 @@
         out_shape=(
             jax.ShapeDtypeStruct((N * N, 64, ROWS), BF),
             jax.ShapeDtypeStruct((SEQS, HEAD, ROWS), BF),
-            jax.ShapeDtypeStruct((N, SEQS, 2 * HEAD, ROWS), BF),
+            *[jax.ShapeDtypeStruct((SEQS, 2 * HEAD, ROWS), BF)] * N,
         ),
         in_specs=[vmem] * 6,
-        out_specs=(vmem,) * 3,
+        out_specs=(vmem,) * (N + 2),
         scratch_shapes=[
             pltpu.VMEM((SEQS, 2 * ROWS, 2 * HEAD), BF),
             pltpu.VMEM((SEQS, 2 * HEAD, 2 * ROWS), BF),
@@ -154,9 +156,9 @@
     )(qgo, *kvs, bias)
 
 
-def split_kernel(after, x_ref, *outs):
-    for t, out in enumerate(outs):
-        out[...] = x_ref[t]
+def copy_kernel(after, *refs):
+    for x_ref, out in zip(refs[: len(refs) // 2], refs[len(refs) // 2 :]):
+        out[...] = x_ref[...]
 
 
 def choose_kernel(after, *refs):
@@ -174,9 +176,9 @@
     anywhere, vmem = pl.BlockSpec(memory_space=pl.ANY), pl.BlockSpec(memory_space=pltpu.VMEM)
     return pl.pallas_call(
         kernel,
-        out_shape=[jax.ShapeDtypeStruct(args[0].shape[-3:], BF)] * N,
+        out_shape=[jax.ShapeDtypeStruct(x.shape, BF) for x in args],
         in_specs=[anywhere] + [vmem] * len(args),
-        out_specs=[vmem] * N,
+        out_specs=[vmem] * len(args),
         compiler_params=pltpu.CompilerParams(vmem_limit_bytes=8 * 2**20),
         cost_estimate=pl.CostEstimate(flops=0, bytes_accessed=2**21, transcendentals=0),
     )(after, *args)
@@ -270,21 +272,22 @@
     ]
     bias = lax.all_to_all(bias, "rj", 0, 0, tiled=True)
 
-    total, dq, dkv = attention(qgo, kvs, bias)
-
-    def spread_out(parts, axis):
-        return [parts[0]] + [
-            lax.ppermute(parts[t], axis, [(a, (a + t) % N) for a in range(N)])
-            for t in range(1, N)
-        ]
+    total, dq, *parts = attention(qgo, kvs, bias)
+
+    def onward(part, axis, t):
+        return lax.ppermute(part, axis, [(a, (a + t) % N) for a in range(N)])
 
     spread = lax.all_to_all(total, ("x", "rj"), 0, 0, tiled=True)
+    first = [onward(parts[t], "rj", t) for t in range(1, 2)]
+    spread, parts[0], *first = lax.optimization_barrier((spread, parts[0], *first))
     total = jnp.sum(spread.reshape(N, N, 64, ROWS).astype(F32), axis=0).astype(BF)
     other = swap(total, "zh", [(0, 1), (2, 3)])
-    parts = spread_out(hand_on(split_kernel, total, dkv), "rj")
+    rest = hand_on(copy_kernel, total, *parts[2:])
+    first += [onward(part, "rj", t) for t, part in enumerate(rest, 2)]
     total = add(total, other)
     other = swap(total, "zh", [(1, 2), (3, 0)])
-    parts = spread_out(hand_on(choose_kernel, total, *parts), "ri")
+    parts = hand_on(choose_kernel, total, parts[0], *first)
+    parts = [parts[0]] + [onward(parts[t], "ri", t) for t in range(1, N)]
     total = add(total, other)
     mine = lax.all_gather(total, "x", axis=0, tiled=True).reshape(-1, ROWS)
 

time: 114 us -> 118 us (1.035)
  blocking collectives: 28.9 us -> 11 us
  starting transfers between devices: 65.6 us -> 77.3 us
  waiting for transfers between devices: 7.45 us -> 17.2 us
    all_to_all x1 -> x0, blocking collectives: 18 us -> none  [body(): spread = lax.all_to_all(total, ('x', 'rj'), 0, 0, tiled=True)]
    ppermute x6, waiting for transfers between devices: 0.02 us -> 9.71 us  [onward(): return lax.ppermute(part, axis, [(a, (a + t) % N) for a in range(N)])]
    all_to_all x0 -> x1, starting transfers between devices: none -> 9 us  [body(): spread = lax.all_to_all(total, ('x', 'rj'), 0, 0, tiled=True)]
    ppermute x4, starting transfers between devices: 29.9 us -> 34.1 us  [swap(): lax.ppermute(x, axis, [(a, b) for a, b in pairs] + [(b, a) for a, b in pa...]
    ppermute x6, starting transfers between devices: 22.9 us -> 21.4 us  [onward(): return lax.ppermute(part, axis, [(a, (a + t) % N) for a in range(N)])]
  transfers between devices with their start and end apart: 15 -> 16, of which waited for: 4 -> 5; matrix products, arithmetic and copies ran while one was open for 1% -> 1% of each run, Pallas kernels for 1% -> 1%
where the time goes in v11:
time: 118 us; the launch traced here: 117 us
  starting transfers between devices  77.3 us (66%)
  waiting for transfers between devices  17.2 us (15%)
  blocking collectives  11 us (9%)
  Pallas kernels  9.55 us (8%)
    ppermute x4, starting transfers between devices, swap(): lax.ppermute(x, axis, [(a, b) for a, b in pairs] + [(b, a) for a, b in pa...  34.1 us
    ppermute x6, starting transfers between devices, onward(): return lax.ppermute(part, axis, [(a, (a + t) % N) for a in range(N)])  21.4 us
    all_gather x1, blocking collectives, body(): mine = lax.all_gather(total, 'x', axis=0, tiled=True).reshape(-1, ROWS)  11 us
    ppermute x6, waiting for transfers between devices, onward(): return lax.ppermute(part, axis, [(a, (a + t) % N) for a in range(N)])  9.71 us
    ppermute x4, starting transfers between devices, body(): lax.ppermute(kv, ('ri', 'rj'), [(a * N + b, (a + b + t) % N * N + a) for...  9.32 us
    all_to_all x1, starting transfers between devices, body(): spread = lax.all_to_all(total, ('x', 'rj'), 0, 0, tiled=True)  9 us
    ppermute x4, waiting for transfers between devices, body(): lax.ppermute(kv, ('ri', 'rj'), [(a * N + b, (a + b + t) % N * N + a) for...  6.79 us
    pallas_call x1, Pallas kernels, attention(): pl.pallas_call(attention_kernel, out_shape=(jax.ShapeDtypeStruct((N * N,...  5.2 us
  transfers between devices with their start and end apart: 16, of which 5 were waited for; matrix products, arithmetic and copies ran while one was open for 1% of the time, Pallas kernels for 1%

profile of v11, /device:TPU:1, one launch (start us, length us, event | category | flops | bytes accessed | tf_op | source)
XLA Modules:
  0.0 117.1 jit_solution(3793323991208400984)
XLA Ops:
  0.6 2.1 %shard_map.93 = (bf16[2,160,256]{2,1,0:T(8,128)(2,1)}, bf16[2,160,256]{2,1,0:T(8,128)(2,1)}, bf16[4,256,256]{2,1,0:T(8,128)(2,1)}) custom-call(bf16[2,64,256]{2,1,0:T(8,128)(2,1)} %bitcast.15, bf16[2,64,256]{2,1,0:T(8,128)(2,1)} %bitcast.16, bf16[2,64,256]{2,1,0:T(8,128)(2,1)} %bitcast.17, bf16[2,64,256]{2,1,0:T(8,128)(2,1)} %bitcast.18, ...), custom_call_target="tpu_custom_call" | custom-call | bytes 2097152 | tf_op jit(solution)/shard_map/pallas_call | solution.py:57
  2.7 8.8 %collective-permute-start = (bf16[2,160,256]{2,1,0:T(8,128)(2,1)}, bf16[2,160,256]{2,1,0:T(8,128)(2,1)S(1)}, u32[]{:S(2)}, u32[]{:S(2)}) collective-permute-start(bf16[2,160,256]{2,1,0:T(8,128)(2,1)} %get-tuple-element.27), channel_id=1, source_target_pairs={{0,16},{16,0},{1,17},{17,1},{2,18},{18,2},{3,19},{19,3},{4,20},{20... | collective-permute-start | bytes 491528 | tf_op jit(solution)/shard_map/ppermute | solution.py:252
  11.5 3.5 %all-to-all-start = ((bf16[4,256,256]{2,1,0:T(8,128)(2,1)}), bf16[4,256,256]{2,1,0:T(8,128)(2,1)S(1)}, u32[]{:S(2)}, u32[]{:S(2)}) async-start(bf16[4,256,256]{2,1,0:T(8,128)(2,1)} %get-tuple-element.28), calls=%async_computation | async-start | bytes 1048576 | tf_op jit(solution)/shard_map/all_to_all | solution.py:273
  15.0 0.9 constant_dynamic-update-slice_fusion.1
  16.0 1.9 %collective-permute-start.4 = (bf16[4,64,256]{2,1,0:T(8,128)(2,1)S(1)}, bf16[4,64,256]{2,1,0:T(8,128)(2,1)S(1)}, u32[]{:S(2)}, u32[]{:S(2)}) collective-permute-start(bf16[4,64,256]{2,1,0:T(8,128)(2,1)S(1)} %slice.17), channel_id=1, source_target_pairs={{0,12},{1,0},{2,4},{3,8},{4,1},{5,5},{6,9},{7,13},{8,6},{9,10},{10... | collective-permute-start | bytes 393224 | tf_op jit(solution)/shard_map/ppermute | solution.py:270
  17.9 2.7 %collective-permute-start.3 = (bf16[4,64,256]{2,1,0:T(8,128)(2,1)S(1)}, bf16[4,64,256]{2,1,0:T(8,128)(2,1)S(1)}, u32[]{:S(2)}, u32[]{:S(2)}) collective-permute-start(bf16[4,64,256]{2,1,0:T(8,128)(2,1)S(1)} %slice.17), channel_id=1, source_target_pairs={{0,8},{1,12},{2,0},{3,4},{4,13},{5,1},{6,5},{7,9},{8,2},{9,6},{10,... | collective-permute-start | bytes 393224 | tf_op jit(solution)/shard_map/ppermute | solution.py:270
  20.7 4.0 %collective-permute-start.2 = (bf16[4,64,256]{2,1,0:T(8,128)(2,1)S(1)}, bf16[4,64,256]{2,1,0:T(8,128)(2,1)S(1)}, u32[]{:S(2)}, u32[]{:S(2)}) collective-permute-start(bf16[4,64,256]{2,1,0:T(8,128)(2,1)S(1)} %slice.17), channel_id=1, source_target_pairs={{0,4},{1,8},{2,12},{3,0},{4,9},{5,13},{6,1},{7,5},{8,14},{9,2},{10... | collective-permute-start | bytes 393224 | tf_op jit(solution)/shard_map/ppermute | solution.py:270
  24.7 0.7 collective-permute-start.1
  25.4 0.5 collective-permute-done.4.kv3
  25.9 4.4 %collective-permute-done.3.kv2 = bf16[4,64,256]{2,1,0:T(8,128)(2,1)S(1)} collective-permute-done((bf16[4,64,256]{2,1,0:T(8,128)(2,1)S(1)}, bf16[4,64,256]{2,1,0:T(8,128)(2,1)S(1)}, u32[]{:S(2)}, u32[]{:S(2)}) %collective-permute-start.3) | collective-permute-done | bytes 131104 | tf_op jit(solution)/shard_map/ppermute | solution.py:270
  30.3 1.9 %collective-permute-done.2.kv1 = bf16[4,64,256]{2,1,0:T(8,128)(2,1)S(1)} collective-permute-done((bf16[4,64,256]{2,1,0:T(8,128)(2,1)S(1)}, bf16[4,64,256]{2,1,0:T(8,128)(2,1)S(1)}, u32[]{:S(2)}, u32[]{:S(2)}) %collective-permute-start.2) | collective-permute-done | bytes 131104 | tf_op jit(solution)/shard_map/ppermute | solution.py:270
  32.2 5.2 %shard_map.94 = (bf16[16,64,256]{2,1,0:T(8,128)(2,1)}, bf16[4,32,256]{2,1,0:T(8,128)(2,1)S(1)}, bf16[4,64,256]{2,1,0:T(8,128)(2,1)S(1)}, bf16[4,64,256]{2,1,0:T(...) custom-call(bf16[4,96,256]{2,1,0:T(8,128)(2,1)S(1)} %slice.16.qgo_ref, ...), custom_call_target="tpu_custom_call" | custom-call | flops 335544320 | bytes 6291456 | tf_op jit(solution)/shard_map/pallas_call | solution.py:136
  37.4 9.0 %all-to-all-start.1 = ((bf16[16,64,256]{2,1,0:T(8,128)(2,1)}), bf16[16,64,256]{2,1,0:T(8,128)(2,1)S(1)}, u32[]{:S(2)}, u32[]{:S(2)}) async-start(bf16[16,64,256]{2,1,0:T(8,128)(2,1)} %get-tuple-element.29), calls=%async_computation.1 | async-start | bytes 1048576 | tf_op jit(solution)/shard_map/all_to_all | solution.py:280
  46.4 3.3 %collective-permute-start.5 = (bf16[4,64,256]{2,1,0:T(8,128)(2,1)S(1)}, bf16[4,64,256]{2,1,0:T(8,128)(2,1)S(1)}, u32[]{:S(2)}, u32[]{:S(2)}) collective-permute-start(bf16[4,64,256]{2,1,0:T(8,128)(2,1)S(1)} %get-tuple-element.31), channel_id=1, source_target_pairs={{0,1},{1,2},{2,3},{3,0},{4,5},{5,6},{6,7},{7,4},{8,9},{9,10},{10,1... | collective-permute-start | bytes 393224 | tf_op jit(solution)/shard_map/ppermute | solution.py:278
  49.7 9.7 %collective-permute-done.5.refs_1_ = bf16[4,64,256]{2,1,0:T(8,128)(2,1)S(1)} collective-permute-done((bf16[4,64,256]{2,1,0:T(8,128)(2,1)S(1)}, bf16[4,64,256]{2,1,0:T(8,128)(2,1)S(1)}, u32[]{:S(2)}, u32[]{:S(2)}) %collective-permute-start.5) | collective-permute-done | bytes 131104 | tf_op jit(solution)/shard_map/ppermute | solution.py:278
  59.4 0.1 reduce_sum.12.after
  59.4 7.8 %collective-permute-start.6 = (bf16[4,64,256]{2,1,0:T(8,128)(2,1)S(1)}, bf16[4,64,256]{2,1,0:T(8,128)(2,1)S(1)}, u32[]{:S(2)}, u32[]{:S(2)}) collective-permute-start(bf16[4,64,256]{2,1,0:T(8,128)(2,1)S(1)} %reduce_sum.12.after), channel_id=1, source_target_pairs={{0,128},{256,384},{128,0},{384,256},{1,129},{257,385},{129,1},{385... | collective-permute-start | bytes 393224 | tf_op jit(solution)/shard_map/ppermute | solution.py:252
  67.3 3.0 %collective-permute-start.8 = (bf16[4,64,256]{2,1,0:T(8,128)(2,1)S(1)}, bf16[4,64,256]{2,1,0:T(8,128)(2,1)S(1)}, u32[]{:S(2)}, u32[]{:S(2)}) collective-permute-start(bf16[4,64,256]{2,1,0:T(8,128)(2,1)S(1)} %get-tuple-element.37), channel_id=1, source_target_pairs={{0,2},{1,3},{2,0},{3,1},{4,6},{5,7},{6,4},{7,5},{8,10},{9,11},{10,... | collective-permute-start | bytes 393224 | tf_op jit(solution)/shard_map/ppermute | solution.py:278
  70.3 2.8 %collective-permute-start.9 = (bf16[4,64,256]{2,1,0:T(8,128)(2,1)S(1)}, bf16[4,64,256]{2,1,0:T(8,128)(2,1)S(1)}, u32[]{:S(2)}, u32[]{:S(2)}) collective-permute-start(bf16[4,64,256]{2,1,0:T(8,128)(2,1)S(1)} %get-tuple-element.38), channel_id=1, source_target_pairs={{0,3},{1,0},{2,1},{3,2},{4,7},{5,4},{6,5},{7,6},{8,11},{9,8},{10,9... | collective-permute-start | bytes 393224 | tf_op jit(solution)/shard_map/ppermute | solution.py:278
  73.2 11.8 %collective-permute-start.7 = (bf16[4,64,256]{2,1,0:T(8,128)(2,1)S(1)}, bf16[4,64,256]{2,1,0:T(8,128)(2,1)S(1)}, u32[]{:S(2)}, u32[]{:S(2)}) collective-permute-start(bf16[4,64,256]{2,1,0:T(8,128)(2,1)S(1)} %add_convert_fusion.2.after), channel_id=1, source_target_pairs={{128,256},{384,0},{256,128},{0,384},{129,257},{385,1},{257,129},{1... | collective-permute-start | bytes 393224 | tf_op jit(solution)/shard_map/ppermute | solution.py:252
  85.0 0.0 collective-permute-done.9.refs_3_
  85.0 0.1 shard_map.96
  85.1 1.9 %collective-permute-start.10 = (bf16[4,64,256]{2,1,0:T(8,128)(2,1)S(1)}, bf16[4,64,256]{2,1,0:T(8,128)(2,1)S(1)}, u32[]{:S(2)}, u32[]{:S(2)}) collective-permute-start(bf16[4,64,256]{2,1,0:T(8,128)(2,1)S(1)} %get-tuple-element.40), channel_id=1, source_target_pairs={{0,4},{4,8},{8,12},{12,0},{1,5},{5,9},{9,13},{13,1},{2,6},{6,10},{... | collective-permute-start | bytes 393224 | tf_op jit(solution)/shard_map/ppermute | solution.py:278
  87.1 8.5 %collective-permute-start.11 = (bf16[4,64,256]{2,1,0:T(8,128)(2,1)S(1)}, bf16[4,64,256]{2,1,0:T(8,128)(2,1)S(1)}, u32[]{:S(2)}, u32[]{:S(2)}) collective-permute-start(bf16[4,64,256]{2,1,0:T(8,128)(2,1)S(1)} %get-tuple-element.41), channel_id=1, source_target_pairs={{0,8},{4,12},{8,0},{12,4},{1,9},{5,13},{9,1},{13,5},{2,10},{6,14},... | collective-permute-start | bytes 393224 | tf_op jit(solution)/shard_map/ppermute | solution.py:278
  95.5 1.9 %collective-permute-start.12 = (bf16[4,64,256]{2,1,0:T(8,128)(2,1)S(1)}, bf16[4,64,256]{2,1,0:T(8,128)(2,1)S(1)}, u32[]{:S(2)}, u32[]{:S(2)}) collective-permute-start(bf16[4,64,256]{2,1,0:T(8,128)(2,1)S(1)} %get-tuple-element.42), channel_id=1, source_target_pairs={{0,12},{4,0},{8,4},{12,8},{1,13},{5,1},{9,5},{13,9},{2,14},{6,2},{... | collective-permute-start | bytes 393224 | tf_op jit(solution)/shard_map/ppermute | solution.py:278
  97.5 11.0 %all_gather.3 = bf16[16,64,256]{2,1,0:T(8,128)(2,1)S(1)} all-gather(bf16[4,64,256]{2,1,0:T(8,128)(2,1)S(1)} %add_convert_fusion.1), channel_id=1, replica_groups=mesh['zh'=4,'x'=4,'core'=2,'ri'=4,'rj'=4] {'x'}, dimensions={0}, use_global_device_ids=true | all-gather | bytes 655360 | tf_op jit(solution)/shard_map/all_gather | solution.py:292
  108.5 0.0 collective-permute-done.10
  108.5 0.1 add_convert_fusion
  108.7 5.7 %collective-permute-start.13 = (bf16[1216,256]{1,0:T(8,128)(2,1)S(1)}, bf16[1216,256]{1,0:T(8,128)(2,1)S(1)}, u32[]{:S(2)}, u32[]{:S(2)}) collective-permute-start(bf16[1216,256]{1,0:T(8,128)(2,1)S(1)} %pad_maximum_fusion), channel_id=1, source_target_pairs={{0,16},{16,0},{1,17},{17,1},{2,18},{18,2},{3,19},{19,3},{4,20},{20... | collective-permute-start | bytes 1867784 | tf_op jit(solution)/shard_map/ppermute | solution.py:252
  114.4 1.0 shard_map.97.before
  115.4 0.6 collective-permute-done.13.x_ref
  116.0 1.1 shard_map.98
  (17 shorter events, 0.2 us)
Async XLA Ops:
  2.7 13.2 %collective-permute-start = (bf16[2,160,256]{2,1,0:T(8,128)(2,1)}, bf16[2,160,256]{2,1,0:T(8,128)(2,1)S(1)}, u32[]{:S(2)}, u32[]{:S(2)}) collective-permute-start(bf16[2,160,256]{2,1,0:T(8,128)(2,1)} %get-tuple-element.27), channel_id=1, source_target_pairs={{0,16},{16,0},{1,17},{17,1},{2,18},{18,2},{3,19},{19,3},{4,20},{20... | collective-permute-start | bytes 491528 | tf_op jit(solution)/shard_map/ppermute | solution.py:252
  11.5 20.6 %all-to-all-start = ((bf16[4,256,256]{2,1,0:T(8,128)(2,1)}), bf16[4,256,256]{2,1,0:T(8,128)(2,1)S(1)}, u32[]{:S(2)}, u32[]{:S(2)}) async-start(bf16[4,256,256]{2,1,0:T(8,128)(2,1)} %get-tuple-element.28), calls=%async_computation | async-start | bytes 1048576 | tf_op jit(solution)/shard_map/all_to_all | solution.py:273
  16.0 9.9 %collective-permute-start.4 = (bf16[4,64,256]{2,1,0:T(8,128)(2,1)S(1)}, bf16[4,64,256]{2,1,0:T(8,128)(2,1)S(1)}, u32[]{:S(2)}, u32[]{:S(2)}) collective-permute-start(bf16[4,64,256]{2,1,0:T(8,128)(2,1)S(1)} %slice.17), channel_id=1, source_target_pairs={{0,12},{1,0},{2,4},{3,8},{4,1},{5,5},{6,9},{7,13},{8,6},{9,10},{10... | collective-permute-start | bytes 393224 | tf_op jit(solution)/shard_map/ppermute | solution.py:270
  17.9 12.4 %collective-permute-start.3 = (bf16[4,64,256]{2,1,0:T(8,128)(2,1)S(1)}, bf16[4,64,256]{2,1,0:T(8,128)(2,1)S(1)}, u32[]{:S(2)}, u32[]{:S(2)}) collective-permute-start(bf16[4,64,256]{2,1,0:T(8,128)(2,1)S(1)} %slice.17), channel_id=1, source_target_pairs={{0,8},{1,12},{2,0},{3,4},{4,13},{5,1},{6,5},{7,9},{8,2},{9,6},{10,... | collective-permute-start | bytes 393224 | tf_op jit(solution)/shard_map/ppermute | solution.py:270
  20.7 11.5 %collective-permute-start.2 = (bf16[4,64,256]{2,1,0:T(8,128)(2,1)S(1)}, bf16[4,64,256]{2,1,0:T(8,128)(2,1)S(1)}, u32[]{:S(2)}, u32[]{:S(2)}) collective-permute-start(bf16[4,64,256]{2,1,0:T(8,128)(2,1)S(1)} %slice.17), channel_id=1, source_target_pairs={{0,4},{1,8},{2,12},{3,0},{4,9},{5,13},{6,1},{7,5},{8,14},{9,2},{10... | collective-permute-start | bytes 393224 | tf_op jit(solution)/shard_map/ppermute | solution.py:270
  24.7 7.5 %collective-permute-start.1 = (bf16[4,64,256]{2,1,0:T(8,128)(2,1)S(1)}, bf16[4,64,256]{2,1,0:T(8,128)(2,1)S(1)}, u32[]{:S(2)}, u32[]{:S(2)}) collective-permute-start(bf16[4,64,256]{2,1,0:T(8,128)(2,1)S(1)} %slice.17), channel_id=1, source_target_pairs={{0,0},{1,4},{2,8},{3,12},{4,5},{5,9},{6,13},{7,1},{8,10},{9,14},{1... | collective-permute-start | bytes 393224 | tf_op jit(solution)/shard_map/ppermute | solution.py:270
  37.4 22.0 %all-to-all-start.1 = ((bf16[16,64,256]{2,1,0:T(8,128)(2,1)}), bf16[16,64,256]{2,1,0:T(8,128)(2,1)S(1)}, u32[]{:S(2)}, u32[]{:S(2)}) async-start(bf16[16,64,256]{2,1,0:T(8,128)(2,1)} %get-tuple-element.29), calls=%async_computation.1 | async-start | bytes 1048576 | tf_op jit(solution)/shard_map/all_to_all | solution.py:280
  46.4 13.0 %collective-permute-start.5 = (bf16[4,64,256]{2,1,0:T(8,128)(2,1)S(1)}, bf16[4,64,256]{2,1,0:T(8,128)(2,1)S(1)}, u32[]{:S(2)}, u32[]{:S(2)}) collective-permute-start(bf16[4,64,256]{2,1,0:T(8,128)(2,1)S(1)} %get-tuple-element.31), channel_id=1, source_target_pairs={{0,1},{1,2},{2,3},{3,0},{4,5},{5,6},{6,7},{7,4},{8,9},{9,10},{10,1... | collective-permute-start | bytes 393224 | tf_op jit(solution)/shard_map/ppermute | solution.py:278
  59.4 13.7 %collective-permute-start.6 = (bf16[4,64,256]{2,1,0:T(8,128)(2,1)S(1)}, bf16[4,64,256]{2,1,0:T(8,128)(2,1)S(1)}, u32[]{:S(2)}, u32[]{:S(2)}) collective-permute-start(bf16[4,64,256]{2,1,0:T(8,128)(2,1)S(1)} %reduce_sum.12.after), channel_id=1, source_target_pairs={{0,128},{256,384},{128,0},{384,256},{1,129},{257,385},{129,1},{385... | collective-permute-start | bytes 393224 | tf_op jit(solution)/shard_map/ppermute | solution.py:252
  67.3 17.7 %collective-permute-start.8 = (bf16[4,64,256]{2,1,0:T(8,128)(2,1)S(1)}, bf16[4,64,256]{2,1,0:T(8,128)(2,1)S(1)}, u32[]{:S(2)}, u32[]{:S(2)}) collective-permute-start(bf16[4,64,256]{2,1,0:T(8,128)(2,1)S(1)} %get-tuple-element.37), channel_id=1, source_target_pairs={{0,2},{1,3},{2,0},{3,1},{4,6},{5,7},{6,4},{7,5},{8,10},{9,11},{10,... | collective-permute-start | bytes 393224 | tf_op jit(solution)/shard_map/ppermute | solution.py:278
  70.3 14.7 %collective-permute-start.9 = (bf16[4,64,256]{2,1,0:T(8,128)(2,1)S(1)}, bf16[4,64,256]{2,1,0:T(8,128)(2,1)S(1)}, u32[]{:S(2)}, u32[]{:S(2)}) collective-permute-start(bf16[4,64,256]{2,1,0:T(8,128)(2,1)S(1)} %get-tuple-element.38), channel_id=1, source_target_pairs={{0,3},{1,0},{2,1},{3,2},{4,7},{5,4},{6,5},{7,6},{8,11},{9,8},{10,9... | collective-permute-start | bytes 393224 | tf_op jit(solution)/shard_map/ppermute | solution.py:278
  73.2 24.2 %collective-permute-start.7 = (bf16[4,64,256]{2,1,0:T(8,128)(2,1)S(1)}, bf16[4,64,256]{2,1,0:T(8,128)(2,1)S(1)}, u32[]{:S(2)}, u32[]{:S(2)}) collective-permute-start(bf16[4,64,256]{2,1,0:T(8,128)(2,1)S(1)} %add_convert_fusion.2.after), channel_id=1, source_target_pairs={{128,256},{384,0},{256,128},{0,384},{129,257},{385,1},{257,129},{1... | collective-permute-start | bytes 393224 | tf_op jit(solution)/shard_map/ppermute | solution.py:252
  85.1 23.4 %collective-permute-start.10 = (bf16[4,64,256]{2,1,0:T(8,128)(2,1)S(1)}, bf16[4,64,256]{2,1,0:T(8,128)(2,1)S(1)}, u32[]{:S(2)}, u32[]{:S(2)}) collective-permute-start(bf16[4,64,256]{2,1,0:T(8,128)(2,1)S(1)} %get-tuple-element.40), channel_id=1, source_target_pairs={{0,4},{4,8},{8,12},{12,0},{1,5},{5,9},{9,13},{13,1},{2,6},{6,10},{... | collective-permute-start | bytes 393224 | tf_op jit(solution)/shard_map/ppermute | solution.py:278
  87.1 21.5 %collective-permute-start.11 = (bf16[4,64,256]{2,1,0:T(8,128)(2,1)S(1)}, bf16[4,64,256]{2,1,0:T(8,128)(2,1)S(1)}, u32[]{:S(2)}, u32[]{:S(2)}) collective-permute-start(bf16[4,64,256]{2,1,0:T(8,128)(2,1)S(1)} %get-tuple-element.41), channel_id=1, source_target_pairs={{0,8},{4,12},{8,0},{12,4},{1,9},{5,13},{9,1},{13,5},{2,10},{6,14},... | collective-permute-start | bytes 393224 | tf_op jit(solution)/shard_map/ppermute | solution.py:278
  95.5 13.0 %collective-permute-start.12 = (bf16[4,64,256]{2,1,0:T(8,128)(2,1)S(1)}, bf16[4,64,256]{2,1,0:T(8,128)(2,1)S(1)}, u32[]{:S(2)}, u32[]{:S(2)}) collective-permute-start(bf16[4,64,256]{2,1,0:T(8,128)(2,1)S(1)} %get-tuple-element.42), channel_id=1, source_target_pairs={{0,12},{4,0},{8,4},{12,8},{1,13},{5,1},{9,5},{13,9},{2,14},{6,2},{... | collective-permute-start | bytes 393224 | tf_op jit(solution)/shard_map/ppermute | solution.py:278
  108.7 7.3 %collective-permute-start.13 = (bf16[1216,256]{1,0:T(8,128)(2,1)S(1)}, bf16[1216,256]{1,0:T(8,128)(2,1)S(1)}, u32[]{:S(2)}, u32[]{:S(2)}) collective-permute-start(bf16[1216,256]{1,0:T(8,128)(2,1)S(1)} %pad_maximum_fusion), channel_id=1, source_target_pairs={{0,16},{16,0},{1,17},{17,1},{2,18},{18,2},{3,19},{19,3},{4,20},{20... | collective-permute-start | bytes 1867784 | tf_op jit(solution)/shard_map/ppermute | solution.py:252

commit v12 on v10

--- a/solution.py
+++ b/solution.py
@@ -14,7 +14,7 @@
 LANES = 128
 SEQS = 4
 CHUNK = 32
-UNROLL = 4
+UNROLL = 8
 BF = jnp.bfloat16
 F32 = jnp.float32
 NT = (((1,), (1,)), ((), ()))
@@ -28,32 +28,26 @@
     inward = [
         pltpu.make_async_copy(x_ref, held.at[i], sem.at[i]) for i, x_ref in enumerate(inputs)
     ]
-    for j in range(N):
-        src = bias_ref.at[2 * j + core]
-        inward.append(pltpu.make_async_copy(src, bias_held.at[j], sem.at[5 + j]))
+    bias_in = pltpu.make_async_copy(bias_ref.at[:, core], bias_held, sem.at[5])
+    for c in (*inward, bias_in):
+        c.start()
     for c in inward:
-        c.start()
+        c.wait()
     outward = []
-    for i in range(5):
-        inward[i].wait()
-        to = slice(i * HEAD, (i + 1) * HEAD)
-        for out, which in ((send, 1 - core), (keep, core)):
-            half = pl.ds(pl.multiple_of(which * HEAD, HEAD), HEAD)
-            here = sem.at[5 + N + len(outward)]
-            outward.append(pltpu.make_async_copy(held.at[i, :, half, :], out.at[:, to, :], here))
-            outward[-1].start()
-    for j in range(N):
-        inward[5 + j].wait()
-        here = sem.at[5 + N + len(outward)]
-        outward.append(pltpu.make_async_copy(bias_held.at[j], bias_out.at[j], here))
+    for i, (out, which) in enumerate(((send, 1 - core), (keep, core))):
+        half = pl.ds(pl.multiple_of(which * HEAD, HEAD), HEAD)
+        outward.append(pltpu.make_async_copy(held.at[:, :, half, :], out, sem.at[6 + i]))
         outward[-1].start()
+    bias_in.wait()
+    outward.append(pltpu.make_async_copy(bias_held, bias_out, sem.at[8]))
+    outward[-1].start()
     for c in outward:
         c.wait()
 
 
 def pack(*args):
     hbm = pl.BlockSpec(memory_space=pltpu.HBM)
-    half = jax.ShapeDtypeStruct((SEQS // 2, 5 * HEAD, ROWS), BF)
+    half = jax.ShapeDtypeStruct((5, SEQS // 2, HEAD, ROWS), BF)
     return pl.pallas_call(
         pack_kernel,
         out_shape=(half, half, jax.ShapeDtypeStruct((N, ROWS, ROWS), BF)),
@@ -62,7 +56,7 @@
         scratch_shapes=[
             pltpu.VMEM((5, *args[0].shape), BF),
             pltpu.VMEM((N, ROWS, ROWS), BF),
-            pltpu.SemaphoreType.DMA((15 + 2 * N,)),
+            pltpu.SemaphoreType.DMA((9,)),
         ],
         compiler_params=pltpu.CompilerParams(vmem_limit_bytes=56 * 2**20),
         cost_estimate=pl.CostEstimate(flops=0, bytes_accessed=2**21, transcendentals=0),
@@ -82,17 +76,18 @@
     for s in range(SEQS):
         for part in range(2):
             at = slice(part * ROWS, (part + 1) * ROWS)
-            one = jnp.where(channel == part, qgo_ref[s, : 2 * HEAD], 0)
+            one = jnp.where(channel == part, jnp.concatenate([qgo_ref[0, s], qgo_ref[1, s]]), 0)
             wide[s, :, at] = one
             stack[s, at, :] = one.T
-        dots = qgo_ref[s, HEAD : 2 * HEAD].astype(F32) * qgo_ref[s, 2 * HEAD :].astype(F32)
+        dots = qgo_ref[1, s].astype(F32) * qgo_ref[2, s].astype(F32)
         sums = jnp.sum(dots, axis=0, keepdims=True)
         inner[s] = jnp.broadcast_to(sums, (LANES, ROWS)).T
 
     for s in range(SEQS):
         for t in range(N):
             at = slice(t * ROWS, (t + 1) * ROWS)
-            raw[s, :, at] = lax.dot_general(stack[s], kvs[t][s], NN, preferred_element_type=F32)
+            kv = jnp.concatenate([kvs[t][0, s], kvs[t][1, s]])
+            raw[s, :, at] = lax.dot_general(stack[s], kv, NN, preferred_element_type=F32)
 
     @pl.loop(0, ROWS // CHUNK, unroll=UNROLL)
     def _(i):
@@ -124,9 +119,10 @@
             grads = lax.dot_general(wide[s], low[s, :, at], NN, preferred_element_type=F32)
             grads = jnp.where(channel == 0, grads * SCALE, grads)
             dkv_ref[lax.rem(b + N - rj, N), s] = grads.astype(BF)
-            term = lax.dot_general(low[s, :ROWS, at], kvs[t][s], NT, preferred_element_type=F32)
+            key = kvs[t][0, s]
+            term = lax.dot_general(low[s, :ROWS, at], key, NT, preferred_element_type=F32)
             query_grads = term if query_grads is None else query_grads + term
-        dq_ref[s] = (query_grads.T[:HEAD] * SCALE).astype(BF)
+        dq_ref[s] = (query_grads.T * SCALE).astype(BF)
 
 
 def attention(qgo, kvs, bias):
@@ -261,9 +257,9 @@
     )
     grid = [(a, b) for a in range(N) for b in range(N)]
 
-    keep, send, bias = pack(k, v, q, g, o, pair_bias)
-    both = jnp.concatenate([keep, swap(send, "core", [(0, 1)])])
-    kv, qgo = both[:, : 2 * HEAD], both[:, 2 * HEAD :]
+    keep, send, bias = pack(k, v, q, g, o, pair_bias.reshape(N, 2, ROWS, ROWS))
+    given = swap(send, "core", [(0, 1)])
+    kv, qgo = (jnp.concatenate([keep[at], given[at]], axis=1) for at in (slice(2), slice(2, 5)))
     kvs = [
         lax.ppermute(kv, ("ri", "rj"), [(a * N + b, (a + b + t) % N * N + a) for a, b in grid])
         for t in range(N)

time: 114 us -> 113 us (level)
  Pallas kernels: 8.97 us -> 7.71 us
    pallas_call x1, Pallas kernels: 4.6 us -> 3.36 us  [attention(): pl.pallas_call(attention_kernel, out_shape=(jax.ShapeDtypeStruct((N * N,...]
where the time goes in v12:
time: 113 us; the launch traced here: 112 us
  starting transfers between devices  65.8 us (58%)
  blocking collectives  28.8 us (25%)
  Pallas kernels  7.71 us (7%)
  waiting for transfers between devices  7.5 us (7%)
    ppermute x4, starting transfers between devices, swap(): lax.ppermute(x, axis, [(a, b) for a, b in pairs] + [(b, a) for a, b in pa...  30.1 us
    ppermute x6, starting transfers between devices, spread_out(): lax.ppermute(parts[t], axis, [(a, (a + t) % N) for a in range(N)])  22.9 us
    all_to_all x1, blocking collectives, body(): spread = lax.all_to_all(total, ('x', 'rj'), 0, 0, tiled=True)  17.9 us
    all_gather x1, blocking collectives, body(): mine = lax.all_gather(total, 'x', axis=0, tiled=True).reshape(-1, ROWS)  10.9 us
    ppermute x4, starting transfers between devices, body(): lax.ppermute(kv, ('ri', 'rj'), [(a * N + b, (a + b + t) % N * N + a) for...  9.32 us
    ppermute x4, waiting for transfers between devices, body(): lax.ppermute(kv, ('ri', 'rj'), [(a * N + b, (a + b + t) % N * N + a) for...  6.84 us
    all_to_all x1, starting transfers between devices, body(): bias = lax.all_to_all(bias, 'rj', 0, 0, tiled=True)  3.48 us
    pallas_call x1, Pallas kernels, attention(): pl.pallas_call(attention_kernel, out_shape=(jax.ShapeDtypeStruct((N * N,...  3.36 us
  transfers between devices with their start and end apart: 15, of which 4 were waited for; matrix products, arithmetic and copies ran while one was open for 1% of the time, Pallas kernels for 1%

profile of v12, /device:TPU:1, one launch (start us, length us, event | category | flops | bytes accessed | tf_op | source)
XLA Modules:
  0.0 111.9 jit_solution(11164036662341971430)
XLA Ops:
  0.6 2.1 %shard_map.93 = (bf16[5,2,32,256]{3,2,1,0:T(8,128)(2,1)}, bf16[5,2,32,256]{3,2,1,0:T(8,128)(2,1)}, bf16[4,256,256]{2,1,0:T(8,128)(2,1)}) custom-call(bf16[2,64,256]{2,1,0:T(8,128)(2,1)} %bitcast.17, bf16[2,64,256]{2,1,0:T(8,128)(2,1)} %bitcast.18, bf16[2,64,256]{2,1,0:T(8,128)(2,1)} %bitcast.19, bf16[2,64,256]{2,1,0:T(8,128)(2,1)} %bitcast.20, ...), custom_call_target="tpu_custom_call" | custom-call | bytes 2097152 | tf_op jit(solution)/shard_map/pallas_call | solution.py:51
  2.7 8.9 %collective-permute-start = (bf16[5,2,32,256]{3,2,1,0:T(8,128)(2,1)}, bf16[5,2,32,256]{3,2,1,0:T(8,128)(2,1)S(1)}, u32[]{:S(2)}, u32[]{:S(2)}) collective-permute-start(bf16[5,2,32,256]{3,2,1,0:T(8,128)(2,1)} %get-tuple-element.23), channel_id=1, source_target_pairs={{0,16},{16,0},{1,17},{17,1},{2,18},{18,2},{3,19},{19,3},{4,20},{20... | collective-permute-start | bytes 491528 | tf_op jit(solution)/shard_map/ppermute | solution.py:246
  11.7 3.5 %all-to-all-start = ((bf16[4,256,256]{2,1,0:T(8,128)(2,1)}), bf16[4,256,256]{2,1,0:T(8,128)(2,1)S(1)}, u32[]{:S(2)}, u32[]{:S(2)}) async-start(bf16[4,256,256]{2,1,0:T(8,128)(2,1)} %get-tuple-element.24), calls=%async_computation | async-start | bytes 1048576 | tf_op jit(solution)/shard_map/all_to_all | solution.py:267
  15.2 0.8 slice.20
  16.0 0.0 collective-permute-done
  16.0 1.9 %collective-permute-start.4 = (bf16[2,4,32,256]{3,2,1,0:T(8,128)(2,1)S(1)}, bf16[2,4,32,256]{3,2,1,0:T(8,128)(2,1)S(1)}, u32[]{:S(2)}, u32[]{:S(2)}) collective-permute-start(bf16[2,4,32,256]{3,2,1,0:T(8,128)(2,1)S(1)} %pad_maximum_fusion.2), channel_id=1, source_target_pairs={{0,12},{1,0},{2,4},{3,8},{4,1},{5,5},{6,9},{7,13},{8,6},{9,10},{10... | collective-permute-start | bytes 393224 | tf_op jit(solution)/shard_map/ppermute | solution.py:264
  18.0 2.7 %collective-permute-start.3 = (bf16[2,4,32,256]{3,2,1,0:T(8,128)(2,1)S(1)}, bf16[2,4,32,256]{3,2,1,0:T(8,128)(2,1)S(1)}, u32[]{:S(2)}, u32[]{:S(2)}) collective-permute-start(bf16[2,4,32,256]{3,2,1,0:T(8,128)(2,1)S(1)} %pad_maximum_fusion.2), channel_id=1, source_target_pairs={{0,8},{1,12},{2,0},{3,4},{4,13},{5,1},{6,5},{7,9},{8,2},{9,6},{10,... | collective-permute-start | bytes 393224 | tf_op jit(solution)/shard_map/ppermute | solution.py:264
  20.7 4.0 %collective-permute-start.2 = (bf16[2,4,32,256]{3,2,1,0:T(8,128)(2,1)S(1)}, bf16[2,4,32,256]{3,2,1,0:T(8,128)(2,1)S(1)}, u32[]{:S(2)}, u32[]{:S(2)}) collective-permute-start(bf16[2,4,32,256]{3,2,1,0:T(8,128)(2,1)S(1)} %pad_maximum_fusion.2), channel_id=1, source_target_pairs={{0,4},{1,8},{2,12},{3,0},{4,9},{5,13},{6,1},{7,5},{8,14},{9,2},{10... | collective-permute-start | bytes 393224 | tf_op jit(solution)/shard_map/ppermute | solution.py:264
  24.7 0.7 collective-permute-start.1
  25.5 0.6 collective-permute-done.4.kv3
  26.1 4.4 %collective-permute-done.3.kv2 = bf16[2,4,32,256]{3,2,1,0:T(8,128)(2,1)S(1)} collective-permute-done((bf16[2,4,32,256]{3,2,1,0:T(8,128)(2,1)S(1)}, bf16[2,4,32,256]{3,2,1,0:T(8,128)(2,1)S(1)}, u32[]{:S(2)}, u32[]{:S(2)}) %collective-permute-start.3) | collective-permute-done | bytes 131104 | tf_op jit(solution)/shard_map/ppermute | solution.py:264
  30.4 1.9 %collective-permute-done.2.kv1 = bf16[2,4,32,256]{3,2,1,0:T(8,128)(2,1)S(1)} collective-permute-done((bf16[2,4,32,256]{3,2,1,0:T(8,128)(2,1)S(1)}, bf16[2,4,32,256]{3,2,1,0:T(8,128)(2,1)S(1)}, u32[]{:S(2)}, u32[]{:S(2)}) %collective-permute-start.2) | collective-permute-done | bytes 131104 | tf_op jit(solution)/shard_map/ppermute | solution.py:264
  32.3 0.0 collective-permute-done.1.kv0
  32.3 0.0 all-to-all-done.bias
  32.3 3.4 %shard_map.94 = (bf16[16,64,256]{2,1,0:T(8,128)(2,1)S(1)}, bf16[4,32,256]{2,1,0:T(8,128)(2,1)S(1)}, bf16[4,4,64,256]{3,2,1,0:T(8,128)(2,1)S(1)}) custom-call(bf16[3,4,32,256]{3,2,1,0:T(8,128)(2,1)S(1)} %pad_maximum_fusion.1.qgo_ref, bf16[2,4,32,256]{3,2,1,0:T(8,128)(2,1)S(1)} %collective-permute-done.1.kv0, ...), custom_call_target="tpu_custom_call" | custom-call | flops 335544320 | bytes 6291456 | tf_op jit(solution)/shard_map/pallas_call | solution.py:130
  35.7 17.9 %all_to_all.10 = bf16[16,64,256]{2,1,0:T(8,128)(2,1)S(1)} all-to-all(bf16[16,64,256]{2,1,0:T(8,128)(2,1)S(1)} %get-tuple-element.25), channel_id=1, replica_groups=mesh['zh'=4,'x'=4,'core'=2,'ri'=4,'rj'=4] {'x','rj'}, dimensions={0} | all-to-all | bytes 1048576 | tf_op jit(solution)/shard_map/all_to_all | solution.py:277
  53.6 0.1 reduce_sum.12.after
  53.7 8.2 %collective-permute-start.5 = (bf16[4,64,256]{2,1,0:T(8,128)(2,1)S(1)}, bf16[4,64,256]{2,1,0:T(8,128)(2,1)S(1)}, u32[]{:S(2)}, u32[]{:S(2)}) collective-permute-start(bf16[4,64,256]{2,1,0:T(8,128)(2,1)S(1)} %reduce_sum.12.after), channel_id=1, source_target_pairs={{0,128},{256,384},{128,0},{384,256},{1,129},{257,385},{129,1},{385... | collective-permute-start | bytes 393224 | tf_op jit(solution)/shard_map/ppermute | solution.py:246
  61.9 2.3 %collective-permute-start.7 = (bf16[4,64,256]{2,1,0:T(8,128)(2,1)S(1)}, bf16[4,64,256]{2,1,0:T(8,128)(2,1)S(1)}, u32[]{:S(2)}, u32[]{:S(2)}) collective-permute-start(bf16[4,64,256]{2,1,0:T(8,128)(2,1)S(1)} %get-tuple-element.28), channel_id=1, source_target_pairs={{0,1},{1,2},{2,3},{3,0},{4,5},{5,6},{6,7},{7,4},{8,9},{9,10},{10,1... | collective-permute-start | bytes 393224 | tf_op jit(solution)/shard_map/ppermute | solution.py:273
  64.2 2.9 %collective-permute-start.8 = (bf16[4,64,256]{2,1,0:T(8,128)(2,1)S(1)}, bf16[4,64,256]{2,1,0:T(8,128)(2,1)S(1)}, u32[]{:S(2)}, u32[]{:S(2)}) collective-permute-start(bf16[4,64,256]{2,1,0:T(8,128)(2,1)S(1)} %get-tuple-element.29), channel_id=1, source_target_pairs={{0,2},{1,3},{2,0},{3,1},{4,6},{5,7},{6,4},{7,5},{8,10},{9,11},{10,... | collective-permute-start | bytes 393224 | tf_op jit(solution)/shard_map/ppermute | solution.py:273
  67.1 3.4 %collective-permute-start.9 = (bf16[4,64,256]{2,1,0:T(8,128)(2,1)S(1)}, bf16[4,64,256]{2,1,0:T(8,128)(2,1)S(1)}, u32[]{:S(2)}, u32[]{:S(2)}) collective-permute-start(bf16[4,64,256]{2,1,0:T(8,128)(2,1)S(1)} %get-tuple-element.30), channel_id=1, source_target_pairs={{0,3},{1,0},{2,1},{3,2},{4,7},{5,4},{6,5},{7,6},{8,11},{9,8},{10,9... | collective-permute-start | bytes 393224 | tf_op jit(solution)/shard_map/ppermute | solution.py:273
  70.6 7.0 %collective-permute-start.6 = (bf16[4,64,256]{2,1,0:T(8,128)(2,1)S(1)}, bf16[4,64,256]{2,1,0:T(8,128)(2,1)S(1)}, u32[]{:S(2)}, u32[]{:S(2)}) collective-permute-start(bf16[4,64,256]{2,1,0:T(8,128)(2,1)S(1)} %add_convert_fusion.2.after), channel_id=1, source_target_pairs={{128,256},{384,0},{256,128},{0,384},{129,257},{385,1},{257,129},{1... | collective-permute-start | bytes 393224 | tf_op jit(solution)/shard_map/ppermute | solution.py:246
  77.7 0.1 shard_map.96
  77.8 5.4 %collective-permute-start.10 = (bf16[4,64,256]{2,1,0:T(8,128)(2,1)S(1)}, bf16[4,64,256]{2,1,0:T(8,128)(2,1)S(1)}, u32[]{:S(2)}, u32[]{:S(2)}) collective-permute-start(bf16[4,64,256]{2,1,0:T(8,128)(2,1)S(1)} %get-tuple-element.32), channel_id=1, source_target_pairs={{0,4},{4,8},{8,12},{12,0},{1,5},{5,9},{9,13},{13,1},{2,6},{6,10},{... | collective-permute-start | bytes 393224 | tf_op jit(solution)/shard_map/ppermute | solution.py:273
  83.2 7.0 %collective-permute-start.11 = (bf16[4,64,256]{2,1,0:T(8,128)(2,1)S(1)}, bf16[4,64,256]{2,1,0:T(8,128)(2,1)S(1)}, u32[]{:S(2)}, u32[]{:S(2)}) collective-permute-start(bf16[4,64,256]{2,1,0:T(8,128)(2,1)S(1)} %get-tuple-element.33), channel_id=1, source_target_pairs={{0,8},{4,12},{8,0},{12,4},{1,9},{5,13},{9,1},{13,5},{2,10},{6,14},... | collective-permute-start | bytes 393224 | tf_op jit(solution)/shard_map/ppermute | solution.py:273
  90.2 1.9 %collective-permute-start.12 = (bf16[4,64,256]{2,1,0:T(8,128)(2,1)S(1)}, bf16[4,64,256]{2,1,0:T(8,128)(2,1)S(1)}, u32[]{:S(2)}, u32[]{:S(2)}) collective-permute-start(bf16[4,64,256]{2,1,0:T(8,128)(2,1)S(1)} %get-tuple-element.34), channel_id=1, source_target_pairs={{0,12},{4,0},{8,4},{12,8},{1,13},{5,1},{9,5},{13,9},{2,14},{6,2},{... | collective-permute-start | bytes 393224 | tf_op jit(solution)/shard_map/ppermute | solution.py:273
  92.2 10.9 %all_gather.3 = bf16[16,64,256]{2,1,0:T(8,128)(2,1)S(1)} all-gather(bf16[4,64,256]{2,1,0:T(8,128)(2,1)S(1)} %add_convert_fusion.1), channel_id=1, replica_groups=mesh['zh'=4,'x'=4,'core'=2,'ri'=4,'rj'=4] {'x'}, dimensions={0}, use_global_device_ids=true | all-gather | bytes 655360 | tf_op jit(solution)/shard_map/all_gather | solution.py:285
  103.1 0.1 add_convert_fusion
  103.3 5.9 %collective-permute-start.13 = (bf16[1216,256]{1,0:T(8,128)(2,1)S(1)}, bf16[1216,256]{1,0:T(8,128)(2,1)S(1)}, u32[]{:S(2)}, u32[]{:S(2)}) collective-permute-start(bf16[1216,256]{1,0:T(8,128)(2,1)S(1)} %pad_maximum_fusion), channel_id=1, source_target_pairs={{0,16},{16,0},{1,17},{17,1},{2,18},{18,2},{3,19},{19,3},{4,20},{20... | collective-permute-start | bytes 1867784 | tf_op jit(solution)/shard_map/ppermute | solution.py:246
  109.2 1.0 shard_map.97.before
  110.2 0.6 collective-permute-done.13.x_ref
  110.8 1.1 shard_map.98
  (20 shorter events, 0.3 us)
Async XLA Ops:
  2.7 22.7 %copy-start = (bf16[5,2,32,256]{3,2,1,0:T(8,128)(2,1)S(1)}, bf16[5,2,32,256]{3,2,1,0:T(8,128)(2,1)}, u32[]{:S(2)}) copy-start(bf16[5,2,32,256]{3,2,1,0:T(8,128)(2,1)} %get-tuple-element.22) | copy-start | bytes 491524
  2.7 13.3 %collective-permute-start = (bf16[5,2,32,256]{3,2,1,0:T(8,128)(2,1)}, bf16[5,2,32,256]{3,2,1,0:T(8,128)(2,1)S(1)}, u32[]{:S(2)}, u32[]{:S(2)}) collective-permute-start(bf16[5,2,32,256]{3,2,1,0:T(8,128)(2,1)} %get-tuple-element.23), channel_id=1, source_target_pairs={{0,16},{16,0},{1,17},{17,1},{2,18},{18,2},{3,19},{19,3},{4,20},{20... | collective-permute-start | bytes 491528 | tf_op jit(solution)/shard_map/ppermute | solution.py:246
  11.7 20.6 %all-to-all-start = ((bf16[4,256,256]{2,1,0:T(8,128)(2,1)}), bf16[4,256,256]{2,1,0:T(8,128)(2,1)S(1)}, u32[]{:S(2)}, u32[]{:S(2)}) async-start(bf16[4,256,256]{2,1,0:T(8,128)(2,1)} %get-tuple-element.24), calls=%async_computation | async-start | bytes 1048576 | tf_op jit(solution)/shard_map/all_to_all | solution.py:267
  16.0 10.0 %collective-permute-start.4 = (bf16[2,4,32,256]{3,2,1,0:T(8,128)(2,1)S(1)}, bf16[2,4,32,256]{3,2,1,0:T(8,128)(2,1)S(1)}, u32[]{:S(2)}, u32[]{:S(2)}) collective-permute-start(bf16[2,4,32,256]{3,2,1,0:T(8,128)(2,1)S(1)} %pad_maximum_fusion.2), channel_id=1, source_target_pairs={{0,12},{1,0},{2,4},{3,8},{4,1},{5,5},{6,9},{7,13},{8,6},{9,10},{10... | collective-permute-start | bytes 393224 | tf_op jit(solution)/shard_map/ppermute | solution.py:264
  18.0 12.5 %collective-permute-start.3 = (bf16[2,4,32,256]{3,2,1,0:T(8,128)(2,1)S(1)}, bf16[2,4,32,256]{3,2,1,0:T(8,128)(2,1)S(1)}, u32[]{:S(2)}, u32[]{:S(2)}) collective-permute-start(bf16[2,4,32,256]{3,2,1,0:T(8,128)(2,1)S(1)} %pad_maximum_fusion.2), channel_id=1, source_target_pairs={{0,8},{1,12},{2,0},{3,4},{4,13},{5,1},{6,5},{7,9},{8,2},{9,6},{10,... | collective-permute-start | bytes 393224 | tf_op jit(solution)/shard_map/ppermute | solution.py:264
  20.7 11.6 %collective-permute-start.2 = (bf16[2,4,32,256]{3,2,1,0:T(8,128)(2,1)S(1)}, bf16[2,4,32,256]{3,2,1,0:T(8,128)(2,1)S(1)}, u32[]{:S(2)}, u32[]{:S(2)}) collective-permute-start(bf16[2,4,32,256]{3,2,1,0:T(8,128)(2,1)S(1)} %pad_maximum_fusion.2), channel_id=1, source_target_pairs={{0,4},{1,8},{2,12},{3,0},{4,9},{5,13},{6,1},{7,5},{8,14},{9,2},{10... | collective-permute-start | bytes 393224 | tf_op jit(solution)/shard_map/ppermute | solution.py:264
  24.7 7.6 %collective-permute-start.1 = (bf16[2,4,32,256]{3,2,1,0:T(8,128)(2,1)S(1)}, bf16[2,4,32,256]{3,2,1,0:T(8,128)(2,1)S(1)}, u32[]{:S(2)}, u32[]{:S(2)}) collective-permute-start(bf16[2,4,32,256]{3,2,1,0:T(8,128)(2,1)S(1)} %pad_maximum_fusion.2), channel_id=1, source_target_pairs={{0,0},{1,4},{2,8},{3,12},{4,5},{5,9},{6,13},{7,1},{8,10},{9,14},{1... | collective-permute-start | bytes 393224 | tf_op jit(solution)/shard_map/ppermute | solution.py:264
  53.7 16.9 %collective-permute-start.5 = (bf16[4,64,256]{2,1,0:T(8,128)(2,1)S(1)}, bf16[4,64,256]{2,1,0:T(8,128)(2,1)S(1)}, u32[]{:S(2)}, u32[]{:S(2)}) collective-permute-start(bf16[4,64,256]{2,1,0:T(8,128)(2,1)S(1)} %reduce_sum.12.after), channel_id=1, source_target_pairs={{0,128},{256,384},{128,0},{384,256},{1,129},{257,385},{129,1},{385... | collective-permute-start | bytes 393224 | tf_op jit(solution)/shard_map/ppermute | solution.py:246
  61.9 15.7 %collective-permute-start.7 = (bf16[4,64,256]{2,1,0:T(8,128)(2,1)S(1)}, bf16[4,64,256]{2,1,0:T(8,128)(2,1)S(1)}, u32[]{:S(2)}, u32[]{:S(2)}) collective-permute-start(bf16[4,64,256]{2,1,0:T(8,128)(2,1)S(1)} %get-tuple-element.28), channel_id=1, source_target_pairs={{0,1},{1,2},{2,3},{3,0},{4,5},{5,6},{6,7},{7,4},{8,9},{9,10},{10,1... | collective-permute-start | bytes 393224 | tf_op jit(solution)/shard_map/ppermute | solution.py:273
  64.2 13.4 %collective-permute-start.8 = (bf16[4,64,256]{2,1,0:T(8,128)(2,1)S(1)}, bf16[4,64,256]{2,1,0:T(8,128)(2,1)S(1)}, u32[]{:S(2)}, u32[]{:S(2)}) collective-permute-start(bf16[4,64,256]{2,1,0:T(8,128)(2,1)S(1)} %get-tuple-element.29), channel_id=1, source_target_pairs={{0,2},{1,3},{2,0},{3,1},{4,6},{5,7},{6,4},{7,5},{8,10},{9,11},{10,... | collective-permute-start | bytes 393224 | tf_op jit(solution)/shard_map/ppermute | solution.py:273
  67.1 10.5 %collective-permute-start.9 = (bf16[4,64,256]{2,1,0:T(8,128)(2,1)S(1)}, bf16[4,64,256]{2,1,0:T(8,128)(2,1)S(1)}, u32[]{:S(2)}, u32[]{:S(2)}) collective-permute-start(bf16[4,64,256]{2,1,0:T(8,128)(2,1)S(1)} %get-tuple-element.30), channel_id=1, source_target_pairs={{0,3},{1,0},{2,1},{3,2},{4,7},{5,4},{6,5},{7,6},{8,11},{9,8},{10,9... | collective-permute-start | bytes 393224 | tf_op jit(solution)/shard_map/ppermute | solution.py:273
  70.6 21.5 %collective-permute-start.6 = (bf16[4,64,256]{2,1,0:T(8,128)(2,1)S(1)}, bf16[4,64,256]{2,1,0:T(8,128)(2,1)S(1)}, u32[]{:S(2)}, u32[]{:S(2)}) collective-permute-start(bf16[4,64,256]{2,1,0:T(8,128)(2,1)S(1)} %add_convert_fusion.2.after), channel_id=1, source_target_pairs={{128,256},{384,0},{256,128},{0,384},{129,257},{385,1},{257,129},{1... | collective-permute-start | bytes 393224 | tf_op jit(solution)/shard_map/ppermute | solution.py:246
  77.8 25.3 %collective-permute-start.10 = (bf16[4,64,256]{2,1,0:T(8,128)(2,1)S(1)}, bf16[4,64,256]{2,1,0:T(8,128)(2,1)S(1)}, u32[]{:S(2)}, u32[]{:S(2)}) collective-permute-start(bf16[4,64,256]{2,1,0:T(8,128)(2,1)S(1)} %get-tuple-element.32), channel_id=1, source_target_pairs={{0,4},{4,8},{8,12},{12,0},{1,5},{5,9},{9,13},{13,1},{2,6},{6,10},{... | collective-permute-start | bytes 393224 | tf_op jit(solution)/shard_map/ppermute | solution.py:273
  83.2 20.0 %collective-permute-start.11 = (bf16[4,64,256]{2,1,0:T(8,128)(2,1)S(1)}, bf16[4,64,256]{2,1,0:T(8,128)(2,1)S(1)}, u32[]{:S(2)}, u32[]{:S(2)}) collective-permute-start(bf16[4,64,256]{2,1,0:T(8,128)(2,1)S(1)} %get-tuple-element.33), channel_id=1, source_target_pairs={{0,8},{4,12},{8,0},{12,4},{1,9},{5,13},{9,1},{13,5},{2,10},{6,14},... | collective-permute-start | bytes 393224 | tf_op jit(solution)/shard_map/ppermute | solution.py:273
  90.2 12.9 %collective-permute-start.12 = (bf16[4,64,256]{2,1,0:T(8,128)(2,1)S(1)}, bf16[4,64,256]{2,1,0:T(8,128)(2,1)S(1)}, u32[]{:S(2)}, u32[]{:S(2)}) collective-permute-start(bf16[4,64,256]{2,1,0:T(8,128)(2,1)S(1)} %get-tuple-element.34), channel_id=1, source_target_pairs={{0,12},{4,0},{8,4},{12,8},{1,13},{5,1},{9,5},{13,9},{2,14},{6,2},{... | collective-permute-start | bytes 393224 | tf_op jit(solution)/shard_map/ppermute | solution.py:273
  103.3 7.5 %collective-permute-start.13 = (bf16[1216,256]{1,0:T(8,128)(2,1)S(1)}, bf16[1216,256]{1,0:T(8,128)(2,1)S(1)}, u32[]{:S(2)}, u32[]{:S(2)}) collective-permute-start(bf16[1216,256]{1,0:T(8,128)(2,1)S(1)} %pad_maximum_fusion), channel_id=1, source_target_pairs={{0,16},{16,0},{1,17},{17,1},{2,18},{18,2},{3,19},{19,3},{4,20},{20... | collective-permute-start | bytes 1867784 | tf_op jit(solution)/shard_map/ppermute | solution.py:246

commit v13 on v12

--- a/solution.py
+++ b/solution.py
@@ -179,11 +179,11 @@
 
 
 def place_heads(x_ref, out_ref, wide, sem, head):
-    copies = []
+    copies, place = [], lax.axis_index("x")
     for j in range(N):
-        for x in range(N):
-            at = (x * N + j) * 64
-            wide[j, x * 64 : (x + 1) * 64, :] = x_ref[at : at + 64, :].astype(F32)
+        for t in range(N):
+            at, rows = (t * N + j) * 64, lax.rem(place + N - t, N) * 64
+            wide[j, pl.ds(pl.multiple_of(rows, 64), 64), :] = x_ref[at : at + 64, :].astype(F32)
         copies.append(pltpu.make_async_copy(wide.at[j], out_ref.at[2 * j + head], sem.at[j]))
         copies[-1].start()
     return copies
@@ -282,7 +282,8 @@
     other = swap(total, "zh", [(1, 2), (3, 0)])
     parts = spread_out(hand_on(choose_kernel, total, *parts), "ri")
     total = add(total, other)
-    mine = lax.all_gather(total, "x", axis=0, tiled=True).reshape(-1, ROWS)
+    total, *parts = lax.optimization_barrier((total, *parts))
+    mine = jnp.concatenate(spread_out([total] * N, "x")).reshape(-1, ROWS)
 
     dkv = sum(x.astype(F32) for x in parts).astype(BF)
     grads = jnp.concatenate([dkv, dq], axis=1)

time: 113 us -> 120 us (1.062)
  waiting for transfers between devices: 7.5 us -> 21 us
  blocking collectives: 28.8 us -> 17.9 us
  starting transfers between devices: 65.8 us -> 70.8 us
    ppermute x6 -> x9, waiting for transfers between devices: 0.02 us -> 13.5 us  [spread_out(): lax.ppermute(parts[t], axis, [(a, (a + t) % N) for a in range(N)])]
    all_gather x1 -> x0, blocking collectives: 10.9 us -> none  [body(): mine = lax.all_gather(total, 'x', axis=0, tiled=True).reshape(-1, ROWS)]
    ppermute x6 -> x9, starting transfers between devices: 22.9 us -> 30.3 us  [spread_out(): lax.ppermute(parts[t], axis, [(a, (a + t) % N) for a in range(N)])]
    ppermute x4, starting transfers between devices: 30.1 us -> 27.7 us  [swap(): lax.ppermute(x, axis, [(a, b) for a, b in pairs] + [(b, a) for a, b in pa...]
  transfers between devices with their start and end apart: 15 -> 18, of which waited for: 4 -> 8; matrix products, arithmetic and copies ran while one was open for 1% -> 1% of each run, Pallas kernels for 1% -> 1%
where the time goes in v13:
time: 120 us
  starting transfers between devices  70.8 us (59%)
  waiting for transfers between devices  21 us (18%)
  blocking collectives  17.9 us (15%)
  Pallas kernels  7.74 us (6%)
    ppermute x9, starting transfers between devices, spread_out(): lax.ppermute(parts[t], axis, [(a, (a + t) % N) for a in range(N)])  30.3 us
    ppermute x4, starting transfers between devices, swap(): lax.ppermute(x, axis, [(a, b) for a, b in pairs] + [(b, a) for a, b in pa...  27.7 us
    all_to_all x1, blocking collectives, body(): spread = lax.all_to_all(total, ('x', 'rj'), 0, 0, tiled=True)  17.9 us
    ppermute x9, waiting for transfers between devices, spread_out(): lax.ppermute(parts[t], axis, [(a, (a + t) % N) for a in range(N)])  13.5 us
    ppermute x4, starting transfers between devices, body(): lax.ppermute(kv, ('ri', 'rj'), [(a * N + b, (a + b + t) % N * N + a) for...  9.32 us
    ppermute x4, waiting for transfers between devices, body(): lax.ppermute(kv, ('ri', 'rj'), [(a * N + b, (a + b + t) % N * N + a) for...  6.84 us
    all_to_all x1, starting transfers between devices, body(): bias = lax.all_to_all(bias, 'rj', 0, 0, tiled=True)  3.48 us
    pallas_call x1, Pallas kernels, attention(): pl.pallas_call(attention_kernel, out_shape=(jax.ShapeDtypeStruct((N * N,...  3.36 us
  transfers between devices with their start and end apart: 18, of which 8 were waited for; matrix products, arithmetic and copies ran while one was open for 1% of the time, Pallas kernels for 1%

profile of v13, /device:TPU:1, one launch (start us, length us, event | category | flops | bytes accessed | tf_op | source)
XLA Modules:
  0.0 119.6 jit_solution(13916887408144336102)
XLA Ops:
  0.6 2.1 %shard_map.93 = (bf16[5,2,32,256]{3,2,1,0:T(8,128)(2,1)}, bf16[5,2,32,256]{3,2,1,0:T(8,128)(2,1)}, bf16[4,256,256]{2,1,0:T(8,128)(2,1)}) custom-call(bf16[2,64,256]{2,1,0:T(8,128)(2,1)} %bitcast.17, bf16[2,64,256]{2,1,0:T(8,128)(2,1)} %bitcast.18, bf16[2,64,256]{2,1,0:T(8,128)(2,1)} %bitcast.19, bf16[2,64,256]{2,1,0:T(8,128)(2,1)} %bitcast.20, ...), custom_call_target="tpu_custom_call" | custom-call | bytes 2097152 | tf_op jit(solution)/shard_map/pallas_call | solution.py:51
  2.7 8.9 %collective-permute-start = (bf16[5,2,32,256]{3,2,1,0:T(8,128)(2,1)}, bf16[5,2,32,256]{3,2,1,0:T(8,128)(2,1)S(1)}, u32[]{:S(2)}, u32[]{:S(2)}) collective-permute-start(bf16[5,2,32,256]{3,2,1,0:T(8,128)(2,1)} %get-tuple-element.28), channel_id=1, source_target_pairs={{0,16},{16,0},{1,17},{17,1},{2,18},{18,2},{3,19},{19,3},{4,20},{20... | collective-permute-start | bytes 491528 | tf_op jit(solution)/shard_map/ppermute | solution.py:246
  11.7 3.5 %all-to-all-start = ((bf16[4,256,256]{2,1,0:T(8,128)(2,1)}), bf16[4,256,256]{2,1,0:T(8,128)(2,1)S(1)}, u32[]{:S(2)}, u32[]{:S(2)}) async-start(bf16[4,256,256]{2,1,0:T(8,128)(2,1)} %get-tuple-element.29), calls=%async_computation | async-start | bytes 1048576 | tf_op jit(solution)/shard_map/all_to_all | solution.py:267
  15.2 0.8 slice.20
  16.0 1.9 %collective-permute-start.4 = (bf16[2,4,32,256]{3,2,1,0:T(8,128)(2,1)S(1)}, bf16[2,4,32,256]{3,2,1,0:T(8,128)(2,1)S(1)}, u32[]{:S(2)}, u32[]{:S(2)}) collective-permute-start(bf16[2,4,32,256]{3,2,1,0:T(8,128)(2,1)S(1)} %pad_maximum_fusion.3), channel_id=1, source_target_pairs={{0,12},{1,0},{2,4},{3,8},{4,1},{5,5},{6,9},{7,13},{8,6},{9,10},{10... | collective-permute-start | bytes 393224 | tf_op jit(solution)/shard_map/ppermute | solution.py:264
  18.0 2.7 %collective-permute-start.3 = (bf16[2,4,32,256]{3,2,1,0:T(8,128)(2,1)S(1)}, bf16[2,4,32,256]{3,2,1,0:T(8,128)(2,1)S(1)}, u32[]{:S(2)}, u32[]{:S(2)}) collective-permute-start(bf16[2,4,32,256]{3,2,1,0:T(8,128)(2,1)S(1)} %pad_maximum_fusion.3), channel_id=1, source_target_pairs={{0,8},{1,12},{2,0},{3,4},{4,13},{5,1},{6,5},{7,9},{8,2},{9,6},{10,... | collective-permute-start | bytes 393224 | tf_op jit(solution)/shard_map/ppermute | solution.py:264
  20.7 4.0 %collective-permute-start.2 = (bf16[2,4,32,256]{3,2,1,0:T(8,128)(2,1)S(1)}, bf16[2,4,32,256]{3,2,1,0:T(8,128)(2,1)S(1)}, u32[]{:S(2)}, u32[]{:S(2)}) collective-permute-start(bf16[2,4,32,256]{3,2,1,0:T(8,128)(2,1)S(1)} %pad_maximum_fusion.3), channel_id=1, source_target_pairs={{0,4},{1,8},{2,12},{3,0},{4,9},{5,13},{6,1},{7,5},{8,14},{9,2},{10... | collective-permute-start | bytes 393224 | tf_op jit(solution)/shard_map/ppermute | solution.py:264
  24.7 0.7 collective-permute-start.1
  25.5 0.6 collective-permute-done.4.kv3
  26.1 4.4 %collective-permute-done.3.kv2 = bf16[2,4,32,256]{3,2,1,0:T(8,128)(2,1)S(1)} collective-permute-done((bf16[2,4,32,256]{3,2,1,0:T(8,128)(2,1)S(1)}, bf16[2,4,32,256]{3,2,1,0:T(8,128)(2,1)S(1)}, u32[]{:S(2)}, u32[]{:S(2)}) %collective-permute-start.3) | collective-permute-done | bytes 131104 | tf_op jit(solution)/shard_map/ppermute | solution.py:264
  30.4 1.9 %collective-permute-done.2.kv1 = bf16[2,4,32,256]{3,2,1,0:T(8,128)(2,1)S(1)} collective-permute-done((bf16[2,4,32,256]{3,2,1,0:T(8,128)(2,1)S(1)}, bf16[2,4,32,256]{3,2,1,0:T(8,128)(2,1)S(1)}, u32[]{:S(2)}, u32[]{:S(2)}) %collective-permute-start.2) | collective-permute-done | bytes 131104 | tf_op jit(solution)/shard_map/ppermute | solution.py:264
  32.3 3.4 %shard_map.94 = (bf16[16,64,256]{2,1,0:T(8,128)(2,1)S(1)}, bf16[4,32,256]{2,1,0:T(8,128)(2,1)S(1)}, bf16[4,4,64,256]{3,2,1,0:T(8,128)(2,1)S(1)}) custom-call(bf16[3,4,32,256]{3,2,1,0:T(8,128)(2,1)S(1)} %pad_maximum_fusion.2.qgo_ref, bf16[2,4,32,256]{3,2,1,0:T(8,128)(2,1)S(1)} %collective-permute-done.1.kv0, ...), custom_call_target="tpu_custom_call" | custom-call | flops 335544320 | bytes 6291456 | tf_op jit(solution)/shard_map/pallas_call | solution.py:130
  35.7 17.9 %all_to_all.10 = bf16[16,64,256]{2,1,0:T(8,128)(2,1)S(1)} all-to-all(bf16[16,64,256]{2,1,0:T(8,128)(2,1)S(1)} %get-tuple-element.30), channel_id=1, replica_groups=mesh['zh'=4,'x'=4,'core'=2,'ri'=4,'rj'=4] {'x','rj'}, dimensions={0} | all-to-all | bytes 1048576 | tf_op jit(solution)/shard_map/all_to_all | solution.py:277
  53.7 8.2 %collective-permute-start.5 = (bf16[4,64,256]{2,1,0:T(8,128)(2,1)S(1)}, bf16[4,64,256]{2,1,0:T(8,128)(2,1)S(1)}, u32[]{:S(2)}, u32[]{:S(2)}) collective-permute-start(bf16[4,64,256]{2,1,0:T(8,128)(2,1)S(1)} %reduce_sum.12.after), channel_id=1, source_target_pairs={{0,128},{256,384},{128,0},{384,256},{1,129},{257,385},{129,1},{385... | collective-permute-start | bytes 393224 | tf_op jit(solution)/shard_map/ppermute | solution.py:246
  61.9 2.3 %collective-permute-start.7 = (bf16[4,64,256]{2,1,0:T(8,128)(2,1)S(1)}, bf16[4,64,256]{2,1,0:T(8,128)(2,1)S(1)}, u32[]{:S(2)}, u32[]{:S(2)}) collective-permute-start(bf16[4,64,256]{2,1,0:T(8,128)(2,1)S(1)} %get-tuple-element.33), channel_id=1, source_target_pairs={{0,1},{1,2},{2,3},{3,0},{4,5},{5,6},{6,7},{7,4},{8,9},{9,10},{10,1... | collective-permute-start | bytes 393224 | tf_op jit(solution)/shard_map/ppermute | solution.py:273
  64.2 2.9 %collective-permute-start.8 = (bf16[4,64,256]{2,1,0:T(8,128)(2,1)S(1)}, bf16[4,64,256]{2,1,0:T(8,128)(2,1)S(1)}, u32[]{:S(2)}, u32[]{:S(2)}) collective-permute-start(bf16[4,64,256]{2,1,0:T(8,128)(2,1)S(1)} %get-tuple-element.34), channel_id=1, source_target_pairs={{0,2},{1,3},{2,0},{3,1},{4,6},{5,7},{6,4},{7,5},{8,10},{9,11},{10,... | collective-permute-start | bytes 393224 | tf_op jit(solution)/shard_map/ppermute | solution.py:273
  67.1 3.4 %collective-permute-start.9 = (bf16[4,64,256]{2,1,0:T(8,128)(2,1)S(1)}, bf16[4,64,256]{2,1,0:T(8,128)(2,1)S(1)}, u32[]{:S(2)}, u32[]{:S(2)}) collective-permute-start(bf16[4,64,256]{2,1,0:T(8,128)(2,1)S(1)} %get-tuple-element.35), channel_id=1, source_target_pairs={{0,3},{1,0},{2,1},{3,2},{4,7},{5,4},{6,5},{7,6},{8,11},{9,8},{10,9... | collective-permute-start | bytes 393224 | tf_op jit(solution)/shard_map/ppermute | solution.py:273
  70.6 7.0 %collective-permute-start.6 = (bf16[4,64,256]{2,1,0:T(8,128)(2,1)S(1)}, bf16[4,64,256]{2,1,0:T(8,128)(2,1)S(1)}, u32[]{:S(2)}, u32[]{:S(2)}) collective-permute-start(bf16[4,64,256]{2,1,0:T(8,128)(2,1)S(1)} %add_convert_fusion.2.after), channel_id=1, source_target_pairs={{128,256},{384,0},{256,128},{0,384},{129,257},{385,1},{257,129},{1... | collective-permute-start | bytes 393224 | tf_op jit(solution)/shard_map/ppermute | solution.py:246
  77.8 5.4 %collective-permute-start.10 = (bf16[4,64,256]{2,1,0:T(8,128)(2,1)S(1)}, bf16[4,64,256]{2,1,0:T(8,128)(2,1)S(1)}, u32[]{:S(2)}, u32[]{:S(2)}) collective-permute-start(bf16[4,64,256]{2,1,0:T(8,128)(2,1)S(1)} %get-tuple-element.37), channel_id=1, source_target_pairs={{0,4},{4,8},{8,12},{12,0},{1,5},{5,9},{9,13},{13,1},{2,6},{6,10},{... | collective-permute-start | bytes 393224 | tf_op jit(solution)/shard_map/ppermute | solution.py:273
  83.2 7.0 %collective-permute-start.11 = (bf16[4,64,256]{2,1,0:T(8,128)(2,1)S(1)}, bf16[4,64,256]{2,1,0:T(8,128)(2,1)S(1)}, u32[]{:S(2)}, u32[]{:S(2)}) collective-permute-start(bf16[4,64,256]{2,1,0:T(8,128)(2,1)S(1)} %get-tuple-element.38), channel_id=1, source_target_pairs={{0,8},{4,12},{8,0},{12,4},{1,9},{5,13},{9,1},{13,5},{2,10},{6,14},... | collective-permute-start | bytes 393224 | tf_op jit(solution)/shard_map/ppermute | solution.py:273
  90.2 1.9 %collective-permute-start.12 = (bf16[4,64,256]{2,1,0:T(8,128)(2,1)S(1)}, bf16[4,64,256]{2,1,0:T(8,128)(2,1)S(1)}, u32[]{:S(2)}, u32[]{:S(2)}) collective-permute-start(bf16[4,64,256]{2,1,0:T(8,128)(2,1)S(1)} %get-tuple-element.39), channel_id=1, source_target_pairs={{0,12},{4,0},{8,4},{12,8},{1,13},{5,1},{9,5},{13,9},{2,14},{6,2},{... | collective-permute-start | bytes 393224 | tf_op jit(solution)/shard_map/ppermute | solution.py:273
  92.2 6.2 %collective-permute-done.11 = bf16[4,64,256]{2,1,0:T(8,128)(2,1)S(1)} collective-permute-done((bf16[4,64,256]{2,1,0:T(8,128)(2,1)S(1)}, bf16[4,64,256]{2,1,0:T(8,128)(2,1)S(1)}, u32[]{:S(2)}, u32[]{:S(2)}) %collective-permute-start.11) | collective-permute-done | bytes 131104 | tf_op jit(solution)/shard_map/ppermute | solution.py:273
  98.4 0.8 collective-permute-done.12
  99.2 3.0 %collective-permute-start.15 = (bf16[4,64,256]{2,1,0:T(8,128)(2,1)S(1)}, bf16[4,64,256]{2,1,0:T(8,128)(2,1)S(1)}, u32[]{:S(2)}, u32[]{:S(2)}) collective-permute-start(bf16[4,64,256]{2,1,0:T(8,128)(2,1)S(1)} %add_convert_fusion.1), channel_id=1, source_target_pairs={{0,96},{32,0},{64,32},{96,64},{1,97},{33,1},{65,33},{97,65},{2,98}... | collective-permute-start | bytes 393224 | tf_op jit(solution)/shard_map/ppermute | solution.py:273
  102.2 2.2 %collective-permute-start.14 = (bf16[4,64,256]{2,1,0:T(8,128)(2,1)S(1)}, bf16[4,64,256]{2,1,0:T(8,128)(2,1)S(1)}, u32[]{:S(2)}, u32[]{:S(2)}) collective-permute-start(bf16[4,64,256]{2,1,0:T(8,128)(2,1)S(1)} %add_convert_fusion.1), channel_id=1, source_target_pairs={{0,64},{32,96},{64,0},{96,32},{1,65},{33,97},{65,1},{97,33},{2,66}... | collective-permute-start | bytes 393224 | tf_op jit(solution)/shard_map/ppermute | solution.py:273
  104.4 2.2 %collective-permute-start.13 = (bf16[4,64,256]{2,1,0:T(8,128)(2,1)S(1)}, bf16[4,64,256]{2,1,0:T(8,128)(2,1)S(1)}, u32[]{:S(2)}, u32[]{:S(2)}) collective-permute-start(bf16[4,64,256]{2,1,0:T(8,128)(2,1)S(1)} %add_convert_fusion.1), channel_id=1, source_target_pairs={{0,32},{32,64},{64,96},{96,0},{1,33},{33,65},{65,97},{97,1},{2,34}... | collective-permute-start | bytes 393224 | tf_op jit(solution)/shard_map/ppermute | solution.py:273
  106.7 2.7 %collective-permute-done.14 = bf16[4,64,256]{2,1,0:T(8,128)(2,1)S(1)} collective-permute-done((bf16[4,64,256]{2,1,0:T(8,128)(2,1)S(1)}, bf16[4,64,256]{2,1,0:T(8,128)(2,1)S(1)}, u32[]{:S(2)}, u32[]{:S(2)}) %collective-permute-start.14) | collective-permute-done | bytes 131104 | tf_op jit(solution)/shard_map/ppermute | solution.py:273
  109.4 3.8 %collective-permute-done.13 = bf16[4,64,256]{2,1,0:T(8,128)(2,1)S(1)} collective-permute-done((bf16[4,64,256]{2,1,0:T(8,128)(2,1)S(1)}, bf16[4,64,256]{2,1,0:T(8,128)(2,1)S(1)}, u32[]{:S(2)}, u32[]{:S(2)}) %collective-permute-start.13) | collective-permute-done | bytes 131104 | tf_op jit(solution)/shard_map/ppermute | solution.py:273
  113.3 3.5 %collective-permute-start.16 = (bf16[1216,256]{1,0:T(8,128)(2,1)S(1)}, bf16[1216,256]{1,0:T(8,128)(2,1)S(1)}, u32[]{:S(2)}, u32[]{:S(2)}) collective-permute-start(bf16[1216,256]{1,0:T(8,128)(2,1)S(1)} %pad_maximum_fusion), channel_id=1, source_target_pairs={{0,16},{16,0},{1,17},{17,1},{2,18},{18,2},{3,19},{19,3},{4,20},{20... | collective-permute-start | bytes 1867784 | tf_op jit(solution)/shard_map/ppermute | solution.py:246
  116.9 1.0 shard_map.97.before
  117.9 0.6 collective-permute-done.16.x_ref
  118.5 1.1 shard_map.98
  (26 shorter events, 0.6 us)
Async XLA Ops:
  2.7 22.7 %copy-start = (bf16[5,2,32,256]{3,2,1,0:T(8,128)(2,1)S(1)}, bf16[5,2,32,256]{3,2,1,0:T(8,128)(2,1)}, u32[]{:S(2)}) copy-start(bf16[5,2,32,256]{3,2,1,0:T(8,128)(2,1)} %get-tuple-element.27) | copy-start | bytes 491524
  2.7 13.3 %collective-permute-start = (bf16[5,2,32,256]{3,2,1,0:T(8,128)(2,1)}, bf16[5,2,32,256]{3,2,1,0:T(8,128)(2,1)S(1)}, u32[]{:S(2)}, u32[]{:S(2)}) collective-permute-start(bf16[5,2,32,256]{3,2,1,0:T(8,128)(2,1)} %get-tuple-element.28), channel_id=1, source_target_pairs={{0,16},{16,0},{1,17},{17,1},{2,18},{18,2},{3,19},{19,3},{4,20},{20... | collective-permute-start | bytes 491528 | tf_op jit(solution)/shard_map/ppermute | solution.py:246
  11.7 20.6 %all-to-all-start = ((bf16[4,256,256]{2,1,0:T(8,128)(2,1)}), bf16[4,256,256]{2,1,0:T(8,128)(2,1)S(1)}, u32[]{:S(2)}, u32[]{:S(2)}) async-start(bf16[4,256,256]{2,1,0:T(8,128)(2,1)} %get-tuple-element.29), calls=%async_computation | async-start | bytes 1048576 | tf_op jit(solution)/shard_map/all_to_all | solution.py:267
  16.0 10.0 %collective-permute-start.4 = (bf16[2,4,32,256]{3,2,1,0:T(8,128)(2,1)S(1)}, bf16[2,4,32,256]{3,2,1,0:T(8,128)(2,1)S(1)}, u32[]{:S(2)}, u32[]{:S(2)}) collective-permute-start(bf16[2,4,32,256]{3,2,1,0:T(8,128)(2,1)S(1)} %pad_maximum_fusion.3), channel_id=1, source_target_pairs={{0,12},{1,0},{2,4},{3,8},{4,1},{5,5},{6,9},{7,13},{8,6},{9,10},{10... | collective-permute-start | bytes 393224 | tf_op jit(solution)/shard_map/ppermute | solution.py:264
  18.0 12.5 %collective-permute-start.3 = (bf16[2,4,32,256]{3,2,1,0:T(8,128)(2,1)S(1)}, bf16[2,4,32,256]{3,2,1,0:T(8,128)(2,1)S(1)}, u32[]{:S(2)}, u32[]{:S(2)}) collective-permute-start(bf16[2,4,32,256]{3,2,1,0:T(8,128)(2,1)S(1)} %pad_maximum_fusion.3), channel_id=1, source_target_pairs={{0,8},{1,12},{2,0},{3,4},{4,13},{5,1},{6,5},{7,9},{8,2},{9,6},{10,... | collective-permute-start | bytes 393224 | tf_op jit(solution)/shard_map/ppermute | solution.py:264
  20.7 11.6 %collective-permute-start.2 = (bf16[2,4,32,256]{3,2,1,0:T(8,128)(2,1)S(1)}, bf16[2,4,32,256]{3,2,1,0:T(8,128)(2,1)S(1)}, u32[]{:S(2)}, u32[]{:S(2)}) collective-permute-start(bf16[2,4,32,256]{3,2,1,0:T(8,128)(2,1)S(1)} %pad_maximum_fusion.3), channel_id=1, source_target_pairs={{0,4},{1,8},{2,12},{3,0},{4,9},{5,13},{6,1},{7,5},{8,14},{9,2},{10... | collective-permute-start | bytes 393224 | tf_op jit(solution)/shard_map/ppermute | solution.py:264
  24.7 7.6 %collective-permute-start.1 = (bf16[2,4,32,256]{3,2,1,0:T(8,128)(2,1)S(1)}, bf16[2,4,32,256]{3,2,1,0:T(8,128)(2,1)S(1)}, u32[]{:S(2)}, u32[]{:S(2)}) collective-permute-start(bf16[2,4,32,256]{3,2,1,0:T(8,128)(2,1)S(1)} %pad_maximum_fusion.3), channel_id=1, source_target_pairs={{0,0},{1,4},{2,8},{3,12},{4,5},{5,9},{6,13},{7,1},{8,10},{9,14},{1... | collective-permute-start | bytes 393224 | tf_op jit(solution)/shard_map/ppermute | solution.py:264
  53.7 16.9 %collective-permute-start.5 = (bf16[4,64,256]{2,1,0:T(8,128)(2,1)S(1)}, bf16[4,64,256]{2,1,0:T(8,128)(2,1)S(1)}, u32[]{:S(2)}, u32[]{:S(2)}) collective-permute-start(bf16[4,64,256]{2,1,0:T(8,128)(2,1)S(1)} %reduce_sum.12.after), channel_id=1, source_target_pairs={{0,128},{256,384},{128,0},{384,256},{1,129},{257,385},{129,1},{385... | collective-permute-start | bytes 393224 | tf_op jit(solution)/shard_map/ppermute | solution.py:246
  61.9 15.7 %collective-permute-start.7 = (bf16[4,64,256]{2,1,0:T(8,128)(2,1)S(1)}, bf16[4,64,256]{2,1,0:T(8,128)(2,1)S(1)}, u32[]{:S(2)}, u32[]{:S(2)}) collective-permute-start(bf16[4,64,256]{2,1,0:T(8,128)(2,1)S(1)} %get-tuple-element.33), channel_id=1, source_target_pairs={{0,1},{1,2},{2,3},{3,0},{4,5},{5,6},{6,7},{7,4},{8,9},{9,10},{10,1... | collective-permute-start | bytes 393224 | tf_op jit(solution)/shard_map/ppermute | solution.py:273
  64.2 13.4 %collective-permute-start.8 = (bf16[4,64,256]{2,1,0:T(8,128)(2,1)S(1)}, bf16[4,64,256]{2,1,0:T(8,128)(2,1)S(1)}, u32[]{:S(2)}, u32[]{:S(2)}) collective-permute-start(bf16[4,64,256]{2,1,0:T(8,128)(2,1)S(1)} %get-tuple-element.34), channel_id=1, source_target_pairs={{0,2},{1,3},{2,0},{3,1},{4,6},{5,7},{6,4},{7,5},{8,10},{9,11},{10,... | collective-permute-start | bytes 393224 | tf_op jit(solution)/shard_map/ppermute | solution.py:273
  67.1 10.5 %collective-permute-start.9 = (bf16[4,64,256]{2,1,0:T(8,128)(2,1)S(1)}, bf16[4,64,256]{2,1,0:T(8,128)(2,1)S(1)}, u32[]{:S(2)}, u32[]{:S(2)}) collective-permute-start(bf16[4,64,256]{2,1,0:T(8,128)(2,1)S(1)} %get-tuple-element.35), channel_id=1, source_target_pairs={{0,3},{1,0},{2,1},{3,2},{4,7},{5,4},{6,5},{7,6},{8,11},{9,8},{10,9... | collective-permute-start | bytes 393224 | tf_op jit(solution)/shard_map/ppermute | solution.py:273
  70.6 21.5 %collective-permute-start.6 = (bf16[4,64,256]{2,1,0:T(8,128)(2,1)S(1)}, bf16[4,64,256]{2,1,0:T(8,128)(2,1)S(1)}, u32[]{:S(2)}, u32[]{:S(2)}) collective-permute-start(bf16[4,64,256]{2,1,0:T(8,128)(2,1)S(1)} %add_convert_fusion.2.after), channel_id=1, source_target_pairs={{128,256},{384,0},{256,128},{0,384},{129,257},{385,1},{257,129},{1... | collective-permute-start | bytes 393224 | tf_op jit(solution)/shard_map/ppermute | solution.py:246
  77.8 14.4 %collective-permute-start.10 = (bf16[4,64,256]{2,1,0:T(8,128)(2,1)S(1)}, bf16[4,64,256]{2,1,0:T(8,128)(2,1)S(1)}, u32[]{:S(2)}, u32[]{:S(2)}) collective-permute-start(bf16[4,64,256]{2,1,0:T(8,128)(2,1)S(1)} %get-tuple-element.37), channel_id=1, source_target_pairs={{0,4},{4,8},{8,12},{12,0},{1,5},{5,9},{9,13},{13,1},{2,6},{6,10},{... | collective-permute-start | bytes 393224 | tf_op jit(solution)/shard_map/ppermute | solution.py:273
  83.2 15.3 %collective-permute-start.11 = (bf16[4,64,256]{2,1,0:T(8,128)(2,1)S(1)}, bf16[4,64,256]{2,1,0:T(8,128)(2,1)S(1)}, u32[]{:S(2)}, u32[]{:S(2)}) collective-permute-start(bf16[4,64,256]{2,1,0:T(8,128)(2,1)S(1)} %get-tuple-element.38), channel_id=1, source_target_pairs={{0,8},{4,12},{8,0},{12,4},{1,9},{5,13},{9,1},{13,5},{2,10},{6,14},... | collective-permute-start | bytes 393224 | tf_op jit(solution)/shard_map/ppermute | solution.py:273
  90.2 9.0 %collective-permute-start.12 = (bf16[4,64,256]{2,1,0:T(8,128)(2,1)S(1)}, bf16[4,64,256]{2,1,0:T(8,128)(2,1)S(1)}, u32[]{:S(2)}, u32[]{:S(2)}) collective-permute-start(bf16[4,64,256]{2,1,0:T(8,128)(2,1)S(1)} %get-tuple-element.39), channel_id=1, source_target_pairs={{0,12},{4,0},{8,4},{12,8},{1,13},{5,1},{9,5},{13,9},{2,14},{6,2},{... | collective-permute-start | bytes 393224 | tf_op jit(solution)/shard_map/ppermute | solution.py:273
  99.2 7.5 %collective-permute-start.15 = (bf16[4,64,256]{2,1,0:T(8,128)(2,1)S(1)}, bf16[4,64,256]{2,1,0:T(8,128)(2,1)S(1)}, u32[]{:S(2)}, u32[]{:S(2)}) collective-permute-start(bf16[4,64,256]{2,1,0:T(8,128)(2,1)S(1)} %add_convert_fusion.1), channel_id=1, source_target_pairs={{0,96},{32,0},{64,32},{96,64},{1,97},{33,1},{65,33},{97,65},{2,98}... | collective-permute-start | bytes 393224 | tf_op jit(solution)/shard_map/ppermute | solution.py:273
  102.2 7.2 %collective-permute-start.14 = (bf16[4,64,256]{2,1,0:T(8,128)(2,1)S(1)}, bf16[4,64,256]{2,1,0:T(8,128)(2,1)S(1)}, u32[]{:S(2)}, u32[]{:S(2)}) collective-permute-start(bf16[4,64,256]{2,1,0:T(8,128)(2,1)S(1)} %add_convert_fusion.1), channel_id=1, source_target_pairs={{0,64},{32,96},{64,0},{96,32},{1,65},{33,97},{65,1},{97,33},{2,66}... | collective-permute-start | bytes 393224 | tf_op jit(solution)/shard_map/ppermute | solution.py:273
  104.4 8.8 %collective-permute-start.13 = (bf16[4,64,256]{2,1,0:T(8,128)(2,1)S(1)}, bf16[4,64,256]{2,1,0:T(8,128)(2,1)S(1)}, u32[]{:S(2)}, u32[]{:S(2)}) collective-permute-start(bf16[4,64,256]{2,1,0:T(8,128)(2,1)S(1)} %add_convert_fusion.1), channel_id=1, source_target_pairs={{0,32},{32,64},{64,96},{96,0},{1,33},{33,65},{65,97},{97,1},{2,34}... | collective-permute-start | bytes 393224 | tf_op jit(solution)/shard_map/ppermute | solution.py:273
  113.3 5.2 %collective-permute-start.16 = (bf16[1216,256]{1,0:T(8,128)(2,1)S(1)}, bf16[1216,256]{1,0:T(8,128)(2,1)S(1)}, u32[]{:S(2)}, u32[]{:S(2)}) collective-permute-start(bf16[1216,256]{1,0:T(8,128)(2,1)S(1)} %pad_maximum_fusion), channel_id=1, source_target_pairs={{0,16},{16,0},{1,17},{17,1},{2,18},{18,2},{3,19},{19,3},{4,20},{20... | collective-permute-start | bytes 1867784 | tf_op jit(solution)/shard_map/ppermute | solution.py:246

commit v14 on v9

--- a/solution.py
+++ b/solution.py
@@ -14,67 +14,82 @@
 LANES = 128
 SEQS = 4
 CHUNK = 32
-UNROLL = 4
+UNROLL = 8
 BF = jnp.bfloat16
 F32 = jnp.float32
 NT = (((1,), (1,)), ((), ()))
 NN = (((1,), (0,)), ((), ()))
 
 
-def pack_kernel(k_ref, v_ref, q_ref, g_ref, o_ref, bias_ref, keep, send, bias_out, sem):
-    core = lax.axis_index("core")
-    copies = []
-    for out, which in ((send, 1 - core), (keep, core)):
-        half = pl.ds(pl.multiple_of(which * HEAD, HEAD), HEAD)
-        for i, x_ref in enumerate((k_ref, v_ref, q_ref, g_ref, o_ref)):
-            copies.append((x_ref.at[:, half, :], out.at[:, i * HEAD : (i + 1) * HEAD, :]))
-    for j in range(N):
-        copies.append((bias_ref.at[2 * j + core], bias_out.at[j]))
-    copies = [pltpu.make_async_copy(*c, sem.at[i]) for i, c in enumerate(copies)]
-    for c in copies:
-        c.start()
-    for c in copies:
-        c.wait()
-
-
-def pack(*args):
-    hbm = pl.BlockSpec(memory_space=pltpu.HBM)
-    half = jax.ShapeDtypeStruct((SEQS // 2, 5 * HEAD, ROWS), BF)
-    return pl.pallas_call(
-        pack_kernel,
-        out_shape=(half, half, jax.ShapeDtypeStruct((N, ROWS, ROWS), BF)),
-        in_specs=[hbm] * 6,
-        out_specs=(hbm,) * 3,
-        scratch_shapes=[pltpu.SemaphoreType.DMA((10 + N,))],
-        compiler_params=pltpu.CompilerParams(vmem_limit_bytes=56 * 2**20),
-        cost_estimate=pl.CostEstimate(flops=0, bytes_accessed=2**21, transcendentals=0),
+def pick_kernel(q_ref, g_ref, o_ref, first, second, send):
+    other = 1 - lax.axis_index("core")
+    at = 0
+    half = pl.ds(pl.multiple_of(other * HEAD, HEAD), HEAD)
+    for x_ref in (q_ref, g_ref, o_ref):
+        for s in range(SEQS // 2):
+            send[at : at + HEAD, :] = x_ref[s, half, :]
+            at += HEAD
+    for x_ref in (first, second):
+        for s in range(SEQS):
+            for part in range(2):
+                half = pl.ds(pl.multiple_of((2 * part + other) * HEAD, HEAD), HEAD)
+                send[at : at + HEAD, :] = x_ref[s, half, :]
+                at += HEAD
+
+
+def pick(*args):
+    vmem = pl.BlockSpec(memory_space=pltpu.VMEM)
+    rows = (3 * (SEQS // 2) + 2 * SEQS * 2) * HEAD
+    return pl.pallas_call(
+        pick_kernel,
+        out_shape=jax.ShapeDtypeStruct((rows, ROWS), BF),
+        in_specs=[vmem] * 5,
+        out_specs=vmem,
+        compiler_params=pltpu.CompilerParams(vmem_limit_bytes=8 * 2**20),
+        cost_estimate=pl.CostEstimate(flops=0, bytes_accessed=2**20, transcendentals=0),
     )(*args)
 
 
 def attention_kernel(
-    qgo_ref, kv0, kv1, kv2, kv3, bias,
+    q_ref, g_ref, o_ref, first, second, given, bias,
     bias_grad, dq_ref, dkv_ref,
     stack, wide, raw, low, inner,
 ):
-    ri, rj = lax.axis_index("ri"), lax.axis_index("rj")
-    kvs = (kv0, kv1, kv2, kv3)
-    blocks = [lax.rem(ri + N - t, N) for t in range(N)]
+    ri, rj, core = (lax.axis_index(a) for a in ("ri", "rj", "core"))
+    own = pl.ds(pl.multiple_of(core * HEAD, HEAD), HEAD)
+    rounds = [2 * core, 2 * core + 1, 2 - 2 * core, 3 - 2 * core]
+    blocks = [lax.rem(ri + 2 * N - rj - t, N) for t in rounds]
+
+    def query_side(i, s):
+        if s < SEQS // 2:
+            return (q_ref, g_ref, o_ref)[i][s, own, :]
+        at = (i * (SEQS // 2) + s - SEQS // 2) * HEAD
+        return given[at : at + HEAD, :]
+
+    def key_side(part, t, s):
+        place = 2 * core + s if s < SEQS // 2 else 2 * (1 - core) + s - SEQS // 2
+        if t < 2:
+            half = pl.ds(pl.multiple_of((2 * part + core) * HEAD, HEAD), HEAD)
+            return (first, second)[t][place, half, :]
+        at = 3 * (SEQS // 2) + (((t - 2) * SEQS + place) * 2 + part)
+        return given[pl.ds(pl.multiple_of(at * HEAD, HEAD), HEAD), :]
     channel = lax.broadcasted_iota(jnp.int32, (2 * HEAD, ROWS), 0) // HEAD
 
     for s in range(SEQS):
         for part in range(2):
             at = slice(part * ROWS, (part + 1) * ROWS)
-            one = jnp.where(channel == part, qgo_ref[s, : 2 * HEAD], 0)
+            one = jnp.where(channel == part, jnp.concatenate([query_side(0, s), query_side(1, s)]), 0)
             wide[s, :, at] = one
             stack[s, at, :] = one.T
-        dots = qgo_ref[s, HEAD : 2 * HEAD].astype(F32) * qgo_ref[s, 2 * HEAD :].astype(F32)
+        dots = query_side(1, s).astype(F32) * query_side(2, s).astype(F32)
         sums = jnp.sum(dots, axis=0, keepdims=True)
         inner[s] = jnp.broadcast_to(sums, (LANES, ROWS)).T
 
     for s in range(SEQS):
         for t in range(N):
             at = slice(t * ROWS, (t + 1) * ROWS)
-            raw[s, :, at] = lax.dot_general(stack[s], kvs[t][s], NN, preferred_element_type=F32)
+            kv = jnp.concatenate([key_side(0, t, s), key_side(1, t, s)])
+            raw[s, :, at] = lax.dot_general(stack[s], kv, NN, preferred_element_type=F32)
 
     @pl.loop(0, ROWS // CHUNK, unroll=UNROLL)
     def _(i):
@@ -106,12 +121,13 @@
             grads = lax.dot_general(wide[s], low[s, :, at], NN, preferred_element_type=F32)
             grads = jnp.where(channel == 0, grads * SCALE, grads)
             dkv_ref[lax.rem(b + N - rj, N), s] = grads.astype(BF)
-            term = lax.dot_general(low[s, :ROWS, at], kvs[t][s], NT, preferred_element_type=F32)
+            key = key_side(0, t, s)
+            term = lax.dot_general(low[s, :ROWS, at], key, NT, preferred_element_type=F32)
             query_grads = term if query_grads is None else query_grads + term
-        dq_ref[s] = (query_grads.T[:HEAD] * SCALE).astype(BF)
-
-
-def attention(qgo, kvs, bias):
+        dq_ref[s] = (query_grads.T * SCALE).astype(BF)
+
+
+def attention(*args):
     vmem = pl.BlockSpec(memory_space=pltpu.VMEM)
     return pl.pallas_call(
         attention_kernel,
@@ -120,7 +136,7 @@
             jax.ShapeDtypeStruct((SEQS, HEAD, ROWS), BF),
             jax.ShapeDtypeStruct((N, SEQS, 2 * HEAD, ROWS), BF),
         ),
-        in_specs=[vmem] * 6,
+        in_specs=[vmem] * 7,
         out_specs=(vmem,) * 3,
         scratch_shapes=[
             pltpu.VMEM((SEQS, 2 * ROWS, 2 * HEAD), BF),
@@ -133,7 +149,7 @@
         cost_estimate=pl.CostEstimate(
             flops=5 * 2 * 2**25, bytes_accessed=6 * 2**20, transcendentals=2**20
         ),
-    )(qgo, *kvs, bias)
+    )(*args)
 
 
 def split_kernel(after, x_ref, *outs):
@@ -243,16 +259,23 @@
     )
     grid = [(a, b) for a in range(N) for b in range(N)]
 
-    keep, send, bias = pack(k, v, q, g, o, pair_bias)
-    both = jnp.concatenate([keep, swap(send, "core", [(0, 1)])])
-    kv, qgo = both[:, : 2 * HEAD], both[:, 2 * HEAD :]
-    kvs = [
-        lax.ppermute(kv, ("ri", "rj"), [(a * N + b, (b + t) % N * N + a) for a, b in grid])
-        for t in range(N)
-    ]
+    core = lax.axis_index("core")
+    held = jnp.concatenate([k, v], axis=1)
+    theirs = swap(held, "core", [(0, 1)])
+    kv = jnp.concatenate([jnp.where(core == c, held, theirs) for c in range(2)])
+    spread = []
+    for i in range(2):
+        steps = []
+        for c in range(2):
+            for a, b in grid:
+                target = (a + b + 2 * c + i) % N * N + a
+                steps.append((c * N * N + a * N + b, c * N * N + target))
+        spread.append(lax.ppermute(kv, ("core", "ri", "rj"), steps))
+    bias = lax.dynamic_index_in_dim(pair_bias.reshape(N, 2, ROWS, ROWS), core, 1, False)
     bias = lax.all_to_all(bias, "rj", 0, 0, tiled=True)
-
-    total, dq, dkv = attention(qgo, kvs, bias)
+    given = swap(pick(q, g, o, *spread), "core", [(0, 1)])
+
+    total, dq, dkv = attention(q, g, o, *spread, given, bias)
 
     def spread_out(parts, axis):
         return [parts[0]] + [

time: 140 us -> 109 us (0.78)
  Pallas kernels: 33.9 us -> 5.64 us
  blocking collectives: 32.9 us -> 27.8 us
  waiting for transfers between devices: 4.79 us -> 9.65 us
  starting transfers between devices: 65.7 us -> 61 us
  other arithmetic: 0.28 us -> 2.2 us
    pallas_call x1, Pallas kernels: 27 us -> 0.04 us  [pick(): pl.pallas_call(pick_kernel, out_shape=jax.ShapeDtypeStruct((rows, ROWS),...]
    ppermute x4 -> x2, starting transfers between devices: 11.1 us -> 4.02 us  [body(): spread.append(lax.ppermute(kv, ('core', 'ri', 'rj'), steps))]
    all_to_all x1, blocking collectives: 22.4 us -> 16.8 us  [body(): spread = lax.all_to_all(total, ('x', 'rj'), 0, 0, tiled=True)]
    all_to_all x1, waiting for transfers between devices: 0.01 us -> 2.73 us  [body(): bias = lax.all_to_all(bias, 'rj', 0, 0, tiled=True)]
    ppermute x4 -> x5, waiting for transfers between devices: 2.22 us -> 4.66 us  [swap(): lax.ppermute(x, axis, [(a, b) for a, b in pairs] + [(b, a) for a, b in pa...]
    ppermute x6, starting transfers between devices: 17.8 us -> 19.6 us  [spread_out(): lax.ppermute(parts[t], axis, [(a, (a + t) % N) for a in range(N)])]
    ppermute x4 -> x5, starting transfers between devices: 33.4 us -> 33.2 us  [swap(): lax.ppermute(x, axis, [(a, b) for a, b in pairs] + [(b, a) for a, b in pa...]
  transfers between devices with their start and end apart: 15 -> 14, of which waited for: 4 -> 5; matrix products, arithmetic and copies ran while one was open for 1% -> 1% of each run, Pallas kernels for 1% -> 1%
where the time goes in v14:
time: 109 us; the launch traced here: 108 us
  starting transfers between devices  61 us (56%)
  blocking collectives  27.8 us (26%)
  waiting for transfers between devices  9.65 us (9%)
  Pallas kernels  5.64 us (5%)
  other arithmetic  2.2 us (2%)
    ppermute x5, starting transfers between devices, swap(): lax.ppermute(x, axis, [(a, b) for a, b in pairs] + [(b, a) for a, b in pa...  33.2 us
    ppermute x6, starting transfers between devices, spread_out(): lax.ppermute(parts[t], axis, [(a, (a + t) % N) for a in range(N)])  19.6 us
    all_to_all x1, blocking collectives, body(): spread = lax.all_to_all(total, ('x', 'rj'), 0, 0, tiled=True)  16.8 us
    all_gather x1, blocking collectives, body(): mine = lax.all_gather(total, 'x', axis=0, tiled=True).reshape(-1, ROWS)  11 us
    ppermute x5, waiting for transfers between devices, swap(): lax.ppermute(x, axis, [(a, b) for a, b in pairs] + [(b, a) for a, b in pa...  4.66 us
    all_to_all x1, starting transfers between devices, body(): bias = lax.all_to_all(bias, 'rj', 0, 0, tiled=True)  4.17 us
    ppermute x2, starting transfers between devices, body(): spread.append(lax.ppermute(kv, ('core', 'ri', 'rj'), steps))  4.02 us
    pallas_call x1, Pallas kernels, attention(): pl.pallas_call(attention_kernel, out_shape=(jax.ShapeDtypeStruct((N * N,...  3.34 us
  transfers between devices with their start and end apart: 14, of which 5 were waited for; matrix products, arithmetic and copies ran while one was open for 1% of the time, Pallas kernels for 1%

profile of v14, /device:TPU:1, one launch (start us, length us, event | category | flops | bytes accessed | tf_op | source)
XLA Modules:
  0.0 108.0 jit_solution(8157288974034646311)
XLA Ops:
  0.6 0.0 copy-start
  0.6 1.0 pad_maximum_fusion.2
  1.6 8.8 %collective-permute-start = (bf16[2,128,256]{2,1,0:T(8,128)(2,1)S(1)}, bf16[2,128,256]{2,1,0:T(8,128)(2,1)S(1)}, u32[]{:S(2)}, u32[]{:S(2)}) collective-permute-start(bf16[2,128,256]{2,1,0:T(8,128)(2,1)S(1)} %pad_maximum_fusion.2), channel_id=1, source_target_pairs={{0,16},{16,0},{1,17},{17,1},{2,18},{18,2},{3,19},{19,3},{4,20},{20... | collective-permute-start | bytes 393224 | tf_op jit(solution)/shard_map/ppermute | solution.py:248
  10.4 1.0 collective-permute-done
  11.4 0.9 broadcast_select_fusion.1
  12.3 0.0 copy-start.1
  12.4 2.1 %collective-permute-start.2 = (bf16[4,128,256]{2,1,0:T(8,128)(2,1)S(1)}, bf16[4,128,256]{2,1,0:T(8,128)(2,1)S(1)}, u32[]{:S(2)}, u32[]{:S(2)}) collective-permute-start(bf16[4,128,256]{2,1,0:T(8,128)(2,1)S(1)} %pad_maximum_fusion.1), channel_id=1, source_target_pairs={{0,4},{1,8},{2,12},{3,0},{4,9},{5,13},{6,1},{7,5},{8,14},{9,2},{10... | collective-permute-start | bytes 786440 | tf_op jit(solution)/shard_map/ppermute | solution.py:273
  14.4 2.0 %collective-permute-start.1 = (bf16[4,128,256]{2,1,0:T(8,128)(2,1)S(1)}, bf16[4,128,256]{2,1,0:T(8,128)(2,1)S(1)}, u32[]{:S(2)}, u32[]{:S(2)}) collective-permute-start(bf16[4,128,256]{2,1,0:T(8,128)(2,1)S(1)} %pad_maximum_fusion.1), channel_id=1, source_target_pairs={{0,0},{1,4},{2,8},{3,12},{4,5},{5,9},{6,13},{7,1},{8,10},{9,14},{1... | collective-permute-start | bytes 786440 | tf_op jit(solution)/shard_map/ppermute | solution.py:273
  16.4 0.8 dynamic-slice_bitcast_fusion
  17.3 4.2 %all-to-all-start = ((bf16[4,256,256]{2,1,0:T(8,128)(2,1)}), bf16[4,256,256]{2,1,0:T(8,128)(2,1)S(1)}, u32[]{:S(2)}, u32[]{:S(2)}) async-start(bf16[4,256,256]{2,1,0:T(8,128)(2,1)} %dynamic-slice_bitcast_fusion), calls=%async_computation | async-start | bytes 1048576 | tf_op jit(solution)/shard_map/all_to_all | solution.py:275
  21.4 2.2 %collective-permute-done.1.first = bf16[4,128,256]{2,1,0:T(8,128)(2,1)S(1)} collective-permute-done((bf16[4,128,256]{2,1,0:T(8,128)(2,1)S(1)}, bf16[4,128,256]{2,1,0:T(8,128)(2,1)S(1)}, u32[]{:S(2)}, u32[]{:S(2)}) %collective-permute-start.1) | collective-permute-done | bytes 262176 | tf_op jit(solution)/shard_map/ppermute | solution.py:273
  23.7 3.4 %collective-permute-start.3 = (bf16[704,256]{1,0:T(8,128)(2,1)S(1)}, bf16[704,256]{1,0:T(8,128)(2,1)S(1)}, u32[]{:S(2)}, u32[]{:S(2)}) collective-permute-start(bf16[704,256]{1,0:T(8,128)(2,1)S(1)} %shard_map.93), channel_id=1, source_target_pairs={{0,16},{16,0},{1,17},{17,1},{2,18},{18,2},{3,19},{19,3},{4,20},{20... | collective-permute-start | bytes 1081352 | tf_op jit(solution)/shard_map/ppermute | solution.py:248
  27.1 2.7 %all-to-all-done.bias = bf16[4,256,256]{2,1,0:T(8,128)(2,1)S(1)} async-done(((bf16[4,256,256]{2,1,0:T(8,128)(2,1)}), bf16[4,256,256]{2,1,0:T(8,128)(2,1)S(1)}, u32[]{:S(2)}, u32[]{:S(2)}) %all-to-all-start) | async-done | bytes 524320 | tf_op jit(solution)/shard_map/all_to_all | solution.py:275
  29.9 3.3 %shard_map.94 = (bf16[16,64,256]{2,1,0:T(8,128)(2,1)S(1)}, bf16[4,32,256]{2,1,0:T(8,128)(2,1)S(1)}, bf16[4,4,64,256]{3,2,1,0:T(8,128)(2,1)S(1)}) custom-call(bf16[2,64,256]{2,1,0:T(8,128)(2,1)S(1)} %bitcast.20, bf16[2,64,256]{2,1,0:T(8,128)(2,1)S(1)} %bitcast.22, bf16[2,64,256]{2,1,0:T(8,128)(2,1)S(1)} %bitcast.24, ...), custom_call_target="tpu_custom_call" | custom-call | flops 335544320 | bytes 6291456 | tf_op jit(solution)/shard_map/pallas_call | solution.py:132
  33.2 16.8 %all_to_all.10 = bf16[16,64,256]{2,1,0:T(8,128)(2,1)S(1)} all-to-all(bf16[16,64,256]{2,1,0:T(8,128)(2,1)S(1)} %get-tuple-element.19), channel_id=1, replica_groups=mesh['zh'=4,'x'=4,'core'=2,'ri'=4,'rj'=4] {'x','rj'}, dimensions={0} | all-to-all | bytes 1048576 | tf_op jit(solution)/shard_map/all_to_all | solution.py:286
  50.0 0.1 reduce_sum.12.after
  50.1 8.8 %collective-permute-start.4 = (bf16[4,64,256]{2,1,0:T(8,128)(2,1)S(1)}, bf16[4,64,256]{2,1,0:T(8,128)(2,1)S(1)}, u32[]{:S(2)}, u32[]{:S(2)}) collective-permute-start(bf16[4,64,256]{2,1,0:T(8,128)(2,1)S(1)} %reduce_sum.12.after), channel_id=1, source_target_pairs={{0,128},{256,384},{128,0},{384,256},{1,129},{257,385},{129,1},{385... | collective-permute-start | bytes 393224 | tf_op jit(solution)/shard_map/ppermute | solution.py:248
  59.0 2.4 %collective-permute-start.6 = (bf16[4,64,256]{2,1,0:T(8,128)(2,1)S(1)}, bf16[4,64,256]{2,1,0:T(8,128)(2,1)S(1)}, u32[]{:S(2)}, u32[]{:S(2)}) collective-permute-start(bf16[4,64,256]{2,1,0:T(8,128)(2,1)S(1)} %get-tuple-element.22), channel_id=1, source_target_pairs={{0,1},{1,2},{2,3},{3,0},{4,5},{5,6},{6,7},{7,4},{8,9},{9,10},{10,1... | collective-permute-start | bytes 393224 | tf_op jit(solution)/shard_map/ppermute | solution.py:282
  61.4 3.3 %collective-permute-start.7 = (bf16[4,64,256]{2,1,0:T(8,128)(2,1)S(1)}, bf16[4,64,256]{2,1,0:T(8,128)(2,1)S(1)}, u32[]{:S(2)}, u32[]{:S(2)}) collective-permute-start(bf16[4,64,256]{2,1,0:T(8,128)(2,1)S(1)} %get-tuple-element.23), channel_id=1, source_target_pairs={{0,2},{1,3},{2,0},{3,1},{4,6},{5,7},{6,4},{7,5},{8,10},{9,11},{10,... | collective-permute-start | bytes 393224 | tf_op jit(solution)/shard_map/ppermute | solution.py:282
  64.7 3.0 %collective-permute-start.8 = (bf16[4,64,256]{2,1,0:T(8,128)(2,1)S(1)}, bf16[4,64,256]{2,1,0:T(8,128)(2,1)S(1)}, u32[]{:S(2)}, u32[]{:S(2)}) collective-permute-start(bf16[4,64,256]{2,1,0:T(8,128)(2,1)S(1)} %get-tuple-element.24), channel_id=1, source_target_pairs={{0,3},{1,0},{2,1},{3,2},{4,7},{5,4},{6,5},{7,6},{8,11},{9,8},{10,9... | collective-permute-start | bytes 393224 | tf_op jit(solution)/shard_map/ppermute | solution.py:282
  67.7 3.1 %collective-permute-done.4 = bf16[4,64,256]{2,1,0:T(8,128)(2,1)S(1)} collective-permute-done((bf16[4,64,256]{2,1,0:T(8,128)(2,1)S(1)}, bf16[4,64,256]{2,1,0:T(8,128)(2,1)S(1)}, u32[]{:S(2)}, u32[]{:S(2)}) %collective-permute-start.4) | collective-permute-done | bytes 131104 | tf_op jit(solution)/shard_map/ppermute | solution.py:248
  70.8 6.6 %collective-permute-start.5 = (bf16[4,64,256]{2,1,0:T(8,128)(2,1)S(1)}, bf16[4,64,256]{2,1,0:T(8,128)(2,1)S(1)}, u32[]{:S(2)}, u32[]{:S(2)}) collective-permute-start(bf16[4,64,256]{2,1,0:T(8,128)(2,1)S(1)} %add_convert_fusion.2.after), channel_id=1, source_target_pairs={{128,256},{384,0},{256,128},{0,384},{129,257},{385,1},{257,129},{1... | collective-permute-start | bytes 393224 | tf_op jit(solution)/shard_map/ppermute | solution.py:248
  77.4 0.1 shard_map.96
  77.6 1.9 %collective-permute-start.9 = (bf16[4,64,256]{2,1,0:T(8,128)(2,1)S(1)}, bf16[4,64,256]{2,1,0:T(8,128)(2,1)S(1)}, u32[]{:S(2)}, u32[]{:S(2)}) collective-permute-start(bf16[4,64,256]{2,1,0:T(8,128)(2,1)S(1)} %get-tuple-element.26), channel_id=1, source_target_pairs={{0,4},{4,8},{8,12},{12,0},{1,5},{5,9},{9,13},{13,1},{2,6},{6,10},{... | collective-permute-start | bytes 393224 | tf_op jit(solution)/shard_map/ppermute | solution.py:282
  79.5 7.0 %collective-permute-start.10 = (bf16[4,64,256]{2,1,0:T(8,128)(2,1)S(1)}, bf16[4,64,256]{2,1,0:T(8,128)(2,1)S(1)}, u32[]{:S(2)}, u32[]{:S(2)}) collective-permute-start(bf16[4,64,256]{2,1,0:T(8,128)(2,1)S(1)} %get-tuple-element.27), channel_id=1, source_target_pairs={{0,8},{4,12},{8,0},{12,4},{1,9},{5,13},{9,1},{13,5},{2,10},{6,14},... | collective-permute-start | bytes 393224 | tf_op jit(solution)/shard_map/ppermute | solution.py:282
  86.5 1.9 %collective-permute-start.11 = (bf16[4,64,256]{2,1,0:T(8,128)(2,1)S(1)}, bf16[4,64,256]{2,1,0:T(8,128)(2,1)S(1)}, u32[]{:S(2)}, u32[]{:S(2)}) collective-permute-start(bf16[4,64,256]{2,1,0:T(8,128)(2,1)S(1)} %get-tuple-element.28), channel_id=1, source_target_pairs={{0,12},{4,0},{8,4},{12,8},{1,13},{5,1},{9,5},{13,9},{2,14},{6,2},{... | collective-permute-start | bytes 393224 | tf_op jit(solution)/shard_map/ppermute | solution.py:282
  88.5 11.0 %all_gather.3 = bf16[16,64,256]{2,1,0:T(8,128)(2,1)S(1)} all-gather(bf16[4,64,256]{2,1,0:T(8,128)(2,1)S(1)} %add_convert_fusion.1), channel_id=1, replica_groups=mesh['zh'=4,'x'=4,'core'=2,'ri'=4,'rj'=4] {'x'}, dimensions={0}, use_global_device_ids=true | all-gather | bytes 655360 | tf_op jit(solution)/shard_map/all_gather | solution.py:294
  99.5 0.1 add_convert_fusion
  99.6 5.6 %collective-permute-start.12 = (bf16[1216,256]{1,0:T(8,128)(2,1)S(1)}, bf16[1216,256]{1,0:T(8,128)(2,1)S(1)}, u32[]{:S(2)}, u32[]{:S(2)}) collective-permute-start(bf16[1216,256]{1,0:T(8,128)(2,1)S(1)} %pad_maximum_fusion), channel_id=1, source_target_pairs={{0,16},{16,0},{1,17},{17,1},{2,18},{18,2},{3,19},{19,3},{4,20},{20... | collective-permute-start | bytes 1867784 | tf_op jit(solution)/shard_map/ppermute | solution.py:248
  105.3 1.0 shard_map.97.before
  106.3 0.6 collective-permute-done.12.x_ref
  106.9 1.1 %shard_map.98 = (f32[8,256,256]{2,1,0:T(8,128)}, bf16[2,64,256]{2,1,0:T(8,128)(2,1)}, bf16[2,64,256]{2,1,0:T(8,128)(2,1)}, bf16[2,64,256]{2,1,0:T(8,128)(2,1)}) custom-call(bf16[1216,256]{1,0:T(8,128)(2,1)S(1)} %collective-permute-done.12.x_ref, bf16[2,96,256]{2,1,0:T(8,128)(2,1)S(1)} %get-tuple-element.36.own_ref, ...), custom_call_target="tpu_custom_call", output_to_operand_aliasing={{0}: (2, {})} | custom-call | flops 262144 | bytes 2097152 | tf_op jit(solution)/shard_map/pallas_call | solution.py:231
  (22 shorter events, 0.3 us)
Async XLA Ops:
  0.6 15.8 %copy-start = (bf16[8,256,256]{2,1,0:T(8,128)(2,1)S(1)}, bf16[8,256,256]{2,1,0:T(8,128)(2,1)}, u32[]{:S(2)}) copy-start(bf16[8,256,256]{2,1,0:T(8,128)(2,1)} %param.9) | copy-start | bytes 3145732
  1.6 9.8 %collective-permute-start = (bf16[2,128,256]{2,1,0:T(8,128)(2,1)S(1)}, bf16[2,128,256]{2,1,0:T(8,128)(2,1)S(1)}, u32[]{:S(2)}, u32[]{:S(2)}) collective-permute-start(bf16[2,128,256]{2,1,0:T(8,128)(2,1)S(1)} %pad_maximum_fusion.2), channel_id=1, source_target_pairs={{0,16},{16,0},{1,17},{17,1},{2,18},{18,2},{3,19},{19,3},{4,20},{20... | collective-permute-start | bytes 393224 | tf_op jit(solution)/shard_map/ppermute | solution.py:248
  12.3 11.4 %copy-start.1 = (bf16[2,256,64]{1,2,0:T(8,128)(2,1)S(1)}, bf16[2,256,64]{1,2,0:T(8,128)(2,1)}, u32[]{:S(2)}) copy-start(bf16[2,256,64]{1,2,0:T(8,128)(2,1)} %param.6) | copy-start | bytes 196612
  12.3 11.4 %copy-start.2 = (bf16[2,256,64]{1,2,0:T(8,128)(2,1)S(1)}, bf16[2,256,64]{1,2,0:T(8,128)(2,1)}, u32[]{:S(2)}) copy-start(bf16[2,256,64]{1,2,0:T(8,128)(2,1)} %param.11) | copy-start | bytes 196612
  12.3 11.4 %copy-start.3 = (bf16[2,256,64]{1,2,0:T(8,128)(2,1)S(1)}, bf16[2,256,64]{1,2,0:T(8,128)(2,1)}, u32[]{:S(2)}) copy-start(bf16[2,256,64]{1,2,0:T(8,128)(2,1)} %param.10) | copy-start | bytes 196612
  12.4 9.1 %collective-permute-start.2 = (bf16[4,128,256]{2,1,0:T(8,128)(2,1)S(1)}, bf16[4,128,256]{2,1,0:T(8,128)(2,1)S(1)}, u32[]{:S(2)}, u32[]{:S(2)}) collective-permute-start(bf16[4,128,256]{2,1,0:T(8,128)(2,1)S(1)} %pad_maximum_fusion.1), channel_id=1, source_target_pairs={{0,4},{1,8},{2,12},{3,0},{4,9},{5,13},{6,1},{7,5},{8,14},{9,2},{10... | collective-permute-start | bytes 786440 | tf_op jit(solution)/shard_map/ppermute | solution.py:273
  14.4 9.2 %collective-permute-start.1 = (bf16[4,128,256]{2,1,0:T(8,128)(2,1)S(1)}, bf16[4,128,256]{2,1,0:T(8,128)(2,1)S(1)}, u32[]{:S(2)}, u32[]{:S(2)}) collective-permute-start(bf16[4,128,256]{2,1,0:T(8,128)(2,1)S(1)} %pad_maximum_fusion.1), channel_id=1, source_target_pairs={{0,0},{1,4},{2,8},{3,12},{4,5},{5,9},{6,13},{7,1},{8,10},{9,14},{1... | collective-permute-start | bytes 786440 | tf_op jit(solution)/shard_map/ppermute | solution.py:273
  17.3 12.6 %all-to-all-start = ((bf16[4,256,256]{2,1,0:T(8,128)(2,1)}), bf16[4,256,256]{2,1,0:T(8,128)(2,1)S(1)}, u32[]{:S(2)}, u32[]{:S(2)}) async-start(bf16[4,256,256]{2,1,0:T(8,128)(2,1)} %dynamic-slice_bitcast_fusion), calls=%async_computation | async-start | bytes 1048576 | tf_op jit(solution)/shard_map/all_to_all | solution.py:275
  23.7 6.1 %collective-permute-start.3 = (bf16[704,256]{1,0:T(8,128)(2,1)S(1)}, bf16[704,256]{1,0:T(8,128)(2,1)S(1)}, u32[]{:S(2)}, u32[]{:S(2)}) collective-permute-start(bf16[704,256]{1,0:T(8,128)(2,1)S(1)} %shard_map.93), channel_id=1, source_target_pairs={{0,16},{16,0},{1,17},{17,1},{2,18},{18,2},{3,19},{19,3},{4,20},{20... | collective-permute-start | bytes 1081352 | tf_op jit(solution)/shard_map/ppermute | solution.py:248
  50.1 20.7 %collective-permute-start.4 = (bf16[4,64,256]{2,1,0:T(8,128)(2,1)S(1)}, bf16[4,64,256]{2,1,0:T(8,128)(2,1)S(1)}, u32[]{:S(2)}, u32[]{:S(2)}) collective-permute-start(bf16[4,64,256]{2,1,0:T(8,128)(2,1)S(1)} %reduce_sum.12.after), channel_id=1, source_target_pairs={{0,128},{256,384},{128,0},{384,256},{1,129},{257,385},{129,1},{385... | collective-permute-start | bytes 393224 | tf_op jit(solution)/shard_map/ppermute | solution.py:248
  59.0 18.4 %collective-permute-start.6 = (bf16[4,64,256]{2,1,0:T(8,128)(2,1)S(1)}, bf16[4,64,256]{2,1,0:T(8,128)(2,1)S(1)}, u32[]{:S(2)}, u32[]{:S(2)}) collective-permute-start(bf16[4,64,256]{2,1,0:T(8,128)(2,1)S(1)} %get-tuple-element.22), channel_id=1, source_target_pairs={{0,1},{1,2},{2,3},{3,0},{4,5},{5,6},{6,7},{7,4},{8,9},{9,10},{10,1... | collective-permute-start | bytes 393224 | tf_op jit(solution)/shard_map/ppermute | solution.py:282
  61.4 16.0 %collective-permute-start.7 = (bf16[4,64,256]{2,1,0:T(8,128)(2,1)S(1)}, bf16[4,64,256]{2,1,0:T(8,128)(2,1)S(1)}, u32[]{:S(2)}, u32[]{:S(2)}) collective-permute-start(bf16[4,64,256]{2,1,0:T(8,128)(2,1)S(1)} %get-tuple-element.23), channel_id=1, source_target_pairs={{0,2},{1,3},{2,0},{3,1},{4,6},{5,7},{6,4},{7,5},{8,10},{9,11},{10,... | collective-permute-start | bytes 393224 | tf_op jit(solution)/shard_map/ppermute | solution.py:282
  64.7 12.7 %collective-permute-start.8 = (bf16[4,64,256]{2,1,0:T(8,128)(2,1)S(1)}, bf16[4,64,256]{2,1,0:T(8,128)(2,1)S(1)}, u32[]{:S(2)}, u32[]{:S(2)}) collective-permute-start(bf16[4,64,256]{2,1,0:T(8,128)(2,1)S(1)} %get-tuple-element.24), channel_id=1, source_target_pairs={{0,3},{1,0},{2,1},{3,2},{4,7},{5,4},{6,5},{7,6},{8,11},{9,8},{10,9... | collective-permute-start | bytes 393224 | tf_op jit(solution)/shard_map/ppermute | solution.py:282
  70.8 17.6 %collective-permute-start.5 = (bf16[4,64,256]{2,1,0:T(8,128)(2,1)S(1)}, bf16[4,64,256]{2,1,0:T(8,128)(2,1)S(1)}, u32[]{:S(2)}, u32[]{:S(2)}) collective-permute-start(bf16[4,64,256]{2,1,0:T(8,128)(2,1)S(1)} %add_convert_fusion.2.after), channel_id=1, source_target_pairs={{128,256},{384,0},{256,128},{0,384},{129,257},{385,1},{257,129},{1... | collective-permute-start | bytes 393224 | tf_op jit(solution)/shard_map/ppermute | solution.py:248
  77.6 21.9 %collective-permute-start.9 = (bf16[4,64,256]{2,1,0:T(8,128)(2,1)S(1)}, bf16[4,64,256]{2,1,0:T(8,128)(2,1)S(1)}, u32[]{:S(2)}, u32[]{:S(2)}) collective-permute-start(bf16[4,64,256]{2,1,0:T(8,128)(2,1)S(1)} %get-tuple-element.26), channel_id=1, source_target_pairs={{0,4},{4,8},{8,12},{12,0},{1,5},{5,9},{9,13},{13,1},{2,6},{6,10},{... | collective-permute-start | bytes 393224 | tf_op jit(solution)/shard_map/ppermute | solution.py:282
  79.5 20.0 %collective-permute-start.10 = (bf16[4,64,256]{2,1,0:T(8,128)(2,1)S(1)}, bf16[4,64,256]{2,1,0:T(8,128)(2,1)S(1)}, u32[]{:S(2)}, u32[]{:S(2)}) collective-permute-start(bf16[4,64,256]{2,1,0:T(8,128)(2,1)S(1)} %get-tuple-element.27), channel_id=1, source_target_pairs={{0,8},{4,12},{8,0},{12,4},{1,9},{5,13},{9,1},{13,5},{2,10},{6,14},... | collective-permute-start | bytes 393224 | tf_op jit(solution)/shard_map/ppermute | solution.py:282
  86.5 12.9 %collective-permute-start.11 = (bf16[4,64,256]{2,1,0:T(8,128)(2,1)S(1)}, bf16[4,64,256]{2,1,0:T(8,128)(2,1)S(1)}, u32[]{:S(2)}, u32[]{:S(2)}) collective-permute-start(bf16[4,64,256]{2,1,0:T(8,128)(2,1)S(1)} %get-tuple-element.28), channel_id=1, source_target_pairs={{0,12},{4,0},{8,4},{12,8},{1,13},{5,1},{9,5},{13,9},{2,14},{6,2},{... | collective-permute-start | bytes 393224 | tf_op jit(solution)/shard_map/ppermute | solution.py:282
  99.6 7.3 %collective-permute-start.12 = (bf16[1216,256]{1,0:T(8,128)(2,1)S(1)}, bf16[1216,256]{1,0:T(8,128)(2,1)S(1)}, u32[]{:S(2)}, u32[]{:S(2)}) collective-permute-start(bf16[1216,256]{1,0:T(8,128)(2,1)S(1)} %pad_maximum_fusion), channel_id=1, source_target_pairs={{0,16},{16,0},{1,17},{17,1},{2,18},{18,2},{3,19},{19,3},{4,20},{20... | collective-permute-start | bytes 1867784 | tf_op jit(solution)/shard_map/ppermute | solution.py:248

commit v15 on v14

--- a/solution.py
+++ b/solution.py
@@ -67,12 +67,13 @@
         return given[at : at + HEAD, :]
 
     def key_side(part, t, s):
-        place = 2 * core + s if s < SEQS // 2 else 2 * (1 - core) + s - SEQS // 2
         if t < 2:
             half = pl.ds(pl.multiple_of((2 * part + core) * HEAD, HEAD), HEAD)
-            return (first, second)[t][place, half, :]
-        at = 3 * (SEQS // 2) + (((t - 2) * SEQS + place) * 2 + part)
-        return given[pl.ds(pl.multiple_of(at * HEAD, HEAD), HEAD), :]
+            return (first, second)[t][s, half, :]
+        there = (s + SEQS // 2) % SEQS
+        at = (3 * (SEQS // 2) + ((t - 2) * SEQS + there) * 2 + part) * HEAD
+        return given[at : at + HEAD, :]
+
     channel = lax.broadcasted_iota(jnp.int32, (2 * HEAD, ROWS), 0) // HEAD
 
     for s in range(SEQS):
@@ -261,8 +262,9 @@
 
     core = lax.axis_index("core")
     held = jnp.concatenate([k, v], axis=1)
-    theirs = swap(held, "core", [(0, 1)])
-    kv = jnp.concatenate([jnp.where(core == c, held, theirs) for c in range(2)])
+    bias = lax.dynamic_index_in_dim(pair_bias.reshape(N, 2, ROWS, ROWS), core, 1, False)
+    theirs, bias = lax.optimization_barrier((swap(held, "core", [(0, 1)]), bias))
+    kv = jnp.concatenate([held, theirs])
     spread = []
     for i in range(2):
         steps = []
@@ -271,7 +273,6 @@
                 target = (a + b + 2 * c + i) % N * N + a
                 steps.append((c * N * N + a * N + b, c * N * N + target))
         spread.append(lax.ppermute(kv, ("core", "ri", "rj"), steps))
-    bias = lax.dynamic_index_in_dim(pair_bias.reshape(N, 2, ROWS, ROWS), core, 1, False)
     bias = lax.all_to_all(bias, "rj", 0, 0, tiled=True)
     given = swap(pick(q, g, o, *spread), "core", [(0, 1)])
 

time: 109 us -> 107 us (0.982)
  blocking collectives: 27.8 us -> 30 us
  starting transfers between devices: 61 us -> 59.2 us
  waiting for transfers between devices: 9.65 us -> 8.26 us
    all_to_all x1, blocking collectives: 16.8 us -> 18.7 us  [body(): spread = lax.all_to_all(total, ('x', 'rj'), 0, 0, tiled=True)]
    all_to_all x1, waiting for transfers between devices: 2.73 us -> 1.09 us  [body(): bias = lax.all_to_all(bias, 'rj', 0, 0, tiled=True)]
    ppermute x6, starting transfers between devices: 19.6 us -> 18.1 us  [spread_out(): lax.ppermute(parts[t], axis, [(a, (a + t) % N) for a in range(N)])]
  transfers between devices with their start and end apart: 14 -> 14, of which waited for: 5 -> 6; matrix products, arithmetic and copies ran while one was open for 1% -> 1% of each run, Pallas kernels for 1% -> 1%
where the time goes in v15:
time: 107 us; the launch traced here: 106 us
  starting transfers between devices  59.2 us (55%)
  blocking collectives  30 us (28%)
  waiting for transfers between devices  8.26 us (8%)
  Pallas kernels  5.66 us (5%)
  other arithmetic  1.28 us (1%)
    ppermute x5, starting transfers between devices, swap(): lax.ppermute(x, axis, [(a, b) for a, b in pairs] + [(b, a) for a, b in pa...  33.1 us
    all_to_all x1, blocking collectives, body(): spread = lax.all_to_all(total, ('x', 'rj'), 0, 0, tiled=True)  18.7 us
    ppermute x6, starting transfers between devices, spread_out(): lax.ppermute(parts[t], axis, [(a, (a + t) % N) for a in range(N)])  18.1 us
    all_gather x1, blocking collectives, body(): mine = lax.all_gather(total, 'x', axis=0, tiled=True).reshape(-1, ROWS)  11.4 us
    all_to_all x1, starting transfers between devices, body(): bias = lax.all_to_all(bias, 'rj', 0, 0, tiled=True)  4.19 us
    ppermute x5, waiting for transfers between devices, swap(): lax.ppermute(x, axis, [(a, b) for a, b in pairs] + [(b, a) for a, b in pa...  4.09 us
    ppermute x2, starting transfers between devices, body(): spread.append(lax.ppermute(kv, ('core', 'ri', 'rj'), steps))  3.89 us
    pallas_call x1, Pallas kernels, attention(): pl.pallas_call(attention_kernel, out_shape=(jax.ShapeDtypeStruct((N * N,...  3.36 us
  transfers between devices with their start and end apart: 14, of which 6 were waited for; matrix products, arithmetic and copies ran while one was open for 1% of the time, Pallas kernels for 1%

profile of v15, /device:TPU:1, one launch (start us, length us, event | category | flops | bytes accessed | tf_op | source)
XLA Modules:
  0.0 106.2 jit_solution(1189651490302936485)
XLA Ops:
  0.6 0.0 copy-start
  0.7 1.0 pad_maximum_fusion.2
  1.6 8.8 %collective-permute-start = (bf16[2,128,256]{2,1,0:T(8,128)(2,1)S(1)}, bf16[2,128,256]{2,1,0:T(8,128)(2,1)S(1)}, u32[]{:S(2)}, u32[]{:S(2)}) collective-permute-start(bf16[2,128,256]{2,1,0:T(8,128)(2,1)S(1)} %pad_maximum_fusion.2), channel_id=1, source_target_pairs={{0,16},{16,0},{1,17},{17,1},{2,18},{18,2},{3,19},{19,3},{4,20},{20... | collective-permute-start | bytes 393224 | tf_op jit(solution)/shard_map/ppermute | solution.py:249
  10.5 0.0 copy-start.1
  10.5 0.8 dynamic-slice_bitcast_fusion
  11.3 0.1 collective-permute-done
  11.4 1.9 %collective-permute-start.2 = (bf16[4,128,256]{2,1,0:T(8,128)(2,1)S(1)}, bf16[4,128,256]{2,1,0:T(8,128)(2,1)S(1)}, u32[]{:S(2)}, u32[]{:S(2)}) collective-permute-start(bf16[4,128,256]{2,1,0:T(8,128)(2,1)S(1)} %pad_maximum_fusion.1), channel_id=1, source_target_pairs={{0,4},{1,8},{2,12},{3,0},{4,9},{5,13},{6,1},{7,5},{8,14},{9,2},{10... | collective-permute-start | bytes 786440 | tf_op jit(solution)/shard_map/ppermute | solution.py:275
  13.4 2.0 %collective-permute-start.1 = (bf16[4,128,256]{2,1,0:T(8,128)(2,1)S(1)}, bf16[4,128,256]{2,1,0:T(8,128)(2,1)S(1)}, u32[]{:S(2)}, u32[]{:S(2)}) collective-permute-start(bf16[4,128,256]{2,1,0:T(8,128)(2,1)S(1)} %pad_maximum_fusion.1), channel_id=1, source_target_pairs={{0,0},{1,4},{2,8},{3,12},{4,5},{5,9},{6,13},{7,1},{8,10},{9,14},{1... | collective-permute-start | bytes 786440 | tf_op jit(solution)/shard_map/ppermute | solution.py:275
  15.3 4.2 %all-to-all-start = ((bf16[4,256,256]{2,1,0:T(8,128)(2,1)}), bf16[4,256,256]{2,1,0:T(8,128)(2,1)S(1)}, u32[]{:S(2)}, u32[]{:S(2)}) async-start(bf16[4,256,256]{2,1,0:T(8,128)(2,1)} %dynamic-slice_bitcast_fusion), calls=%async_computation | async-start | bytes 1048576 | tf_op jit(solution)/shard_map/all_to_all | solution.py:276
  19.5 3.1 %collective-permute-done.1.first = bf16[4,128,256]{2,1,0:T(8,128)(2,1)S(1)} collective-permute-done((bf16[4,128,256]{2,1,0:T(8,128)(2,1)S(1)}, bf16[4,128,256]{2,1,0:T(8,128)(2,1)S(1)}, u32[]{:S(2)}, u32[]{:S(2)}) %collective-permute-start.1) | collective-permute-done | bytes 262176 | tf_op jit(solution)/shard_map/ppermute | solution.py:275
  22.7 3.4 %collective-permute-start.3 = (bf16[704,256]{1,0:T(8,128)(2,1)S(1)}, bf16[704,256]{1,0:T(8,128)(2,1)S(1)}, u32[]{:S(2)}, u32[]{:S(2)}) collective-permute-start(bf16[704,256]{1,0:T(8,128)(2,1)S(1)} %shard_map.93), channel_id=1, source_target_pairs={{0,16},{16,0},{1,17},{17,1},{2,18},{18,2},{3,19},{19,3},{4,20},{20... | collective-permute-start | bytes 1081352 | tf_op jit(solution)/shard_map/ppermute | solution.py:249
  26.1 1.1 %all-to-all-done.bias = bf16[4,256,256]{2,1,0:T(8,128)(2,1)S(1)} async-done(((bf16[4,256,256]{2,1,0:T(8,128)(2,1)}), bf16[4,256,256]{2,1,0:T(8,128)(2,1)S(1)}, u32[]{:S(2)}, u32[]{:S(2)}) %all-to-all-start) | async-done | bytes 524320 | tf_op jit(solution)/shard_map/all_to_all | solution.py:276
  27.1 0.2 collective-permute-done.3.given
  27.3 3.4 %shard_map.94 = (bf16[16,64,256]{2,1,0:T(8,128)(2,1)S(1)}, bf16[4,32,256]{2,1,0:T(8,128)(2,1)S(1)}, bf16[4,4,64,256]{3,2,1,0:T(8,128)(2,1)S(1)}) custom-call(bf16[2,64,256]{2,1,0:T(8,128)(2,1)S(1)} %bitcast.20, bf16[2,64,256]{2,1,0:T(8,128)(2,1)S(1)} %bitcast.22, bf16[2,64,256]{2,1,0:T(8,128)(2,1)S(1)} %bitcast.24, ...), custom_call_target="tpu_custom_call" | custom-call | flops 335544320 | bytes 6291456 | tf_op jit(solution)/shard_map/pallas_call | solution.py:133
  30.7 18.7 %all_to_all.10 = bf16[16,64,256]{2,1,0:T(8,128)(2,1)S(1)} all-to-all(bf16[16,64,256]{2,1,0:T(8,128)(2,1)S(1)} %get-tuple-element.23), channel_id=1, replica_groups=mesh['zh'=4,'x'=4,'core'=2,'ri'=4,'rj'=4] {'x','rj'}, dimensions={0} | all-to-all | bytes 1048576 | tf_op jit(solution)/shard_map/all_to_all | solution.py:287
  49.4 0.1 reduce_sum.12.after
  49.4 8.8 %collective-permute-start.4 = (bf16[4,64,256]{2,1,0:T(8,128)(2,1)S(1)}, bf16[4,64,256]{2,1,0:T(8,128)(2,1)S(1)}, u32[]{:S(2)}, u32[]{:S(2)}) collective-permute-start(bf16[4,64,256]{2,1,0:T(8,128)(2,1)S(1)} %reduce_sum.12.after), channel_id=1, source_target_pairs={{0,128},{256,384},{128,0},{384,256},{1,129},{257,385},{129,1},{385... | collective-permute-start | bytes 393224 | tf_op jit(solution)/shard_map/ppermute | solution.py:249
  58.3 2.4 %collective-permute-start.6 = (bf16[4,64,256]{2,1,0:T(8,128)(2,1)S(1)}, bf16[4,64,256]{2,1,0:T(8,128)(2,1)S(1)}, u32[]{:S(2)}, u32[]{:S(2)}) collective-permute-start(bf16[4,64,256]{2,1,0:T(8,128)(2,1)S(1)} %get-tuple-element.26), channel_id=1, source_target_pairs={{0,1},{1,2},{2,3},{3,0},{4,5},{5,6},{6,7},{7,4},{8,9},{9,10},{10,1... | collective-permute-start | bytes 393224 | tf_op jit(solution)/shard_map/ppermute | solution.py:283
  60.7 3.3 %collective-permute-start.7 = (bf16[4,64,256]{2,1,0:T(8,128)(2,1)S(1)}, bf16[4,64,256]{2,1,0:T(8,128)(2,1)S(1)}, u32[]{:S(2)}, u32[]{:S(2)}) collective-permute-start(bf16[4,64,256]{2,1,0:T(8,128)(2,1)S(1)} %get-tuple-element.27), channel_id=1, source_target_pairs={{0,2},{1,3},{2,0},{3,1},{4,6},{5,7},{6,4},{7,5},{8,10},{9,11},{10,... | collective-permute-start | bytes 393224 | tf_op jit(solution)/shard_map/ppermute | solution.py:283
  64.1 3.2 %collective-permute-start.8 = (bf16[4,64,256]{2,1,0:T(8,128)(2,1)S(1)}, bf16[4,64,256]{2,1,0:T(8,128)(2,1)S(1)}, u32[]{:S(2)}, u32[]{:S(2)}) collective-permute-start(bf16[4,64,256]{2,1,0:T(8,128)(2,1)S(1)} %get-tuple-element.28), channel_id=1, source_target_pairs={{0,3},{1,0},{2,1},{3,2},{4,7},{5,4},{6,5},{7,6},{8,11},{9,8},{10,9... | collective-permute-start | bytes 393224 | tf_op jit(solution)/shard_map/ppermute | solution.py:283
  67.3 3.2 %collective-permute-done.4 = bf16[4,64,256]{2,1,0:T(8,128)(2,1)S(1)} collective-permute-done((bf16[4,64,256]{2,1,0:T(8,128)(2,1)S(1)}, bf16[4,64,256]{2,1,0:T(8,128)(2,1)S(1)}, u32[]{:S(2)}, u32[]{:S(2)}) %collective-permute-start.4) | collective-permute-done | bytes 131104 | tf_op jit(solution)/shard_map/ppermute | solution.py:249
  70.5 6.3 %collective-permute-start.5 = (bf16[4,64,256]{2,1,0:T(8,128)(2,1)S(1)}, bf16[4,64,256]{2,1,0:T(8,128)(2,1)S(1)}, u32[]{:S(2)}, u32[]{:S(2)}) collective-permute-start(bf16[4,64,256]{2,1,0:T(8,128)(2,1)S(1)} %add_convert_fusion.2.after), channel_id=1, source_target_pairs={{128,256},{384,0},{256,128},{0,384},{129,257},{385,1},{257,129},{1... | collective-permute-start | bytes 393224 | tf_op jit(solution)/shard_map/ppermute | solution.py:249
  76.8 0.1 shard_map.96
  77.0 1.9 %collective-permute-start.9 = (bf16[4,64,256]{2,1,0:T(8,128)(2,1)S(1)}, bf16[4,64,256]{2,1,0:T(8,128)(2,1)S(1)}, u32[]{:S(2)}, u32[]{:S(2)}) collective-permute-start(bf16[4,64,256]{2,1,0:T(8,128)(2,1)S(1)} %get-tuple-element.30), channel_id=1, source_target_pairs={{0,4},{4,8},{8,12},{12,0},{1,5},{5,9},{9,13},{13,1},{2,6},{6,10},{... | collective-permute-start | bytes 393224 | tf_op jit(solution)/shard_map/ppermute | solution.py:283
  78.9 5.3 %collective-permute-start.10 = (bf16[4,64,256]{2,1,0:T(8,128)(2,1)S(1)}, bf16[4,64,256]{2,1,0:T(8,128)(2,1)S(1)}, u32[]{:S(2)}, u32[]{:S(2)}) collective-permute-start(bf16[4,64,256]{2,1,0:T(8,128)(2,1)S(1)} %get-tuple-element.31), channel_id=1, source_target_pairs={{0,8},{4,12},{8,0},{12,4},{1,9},{5,13},{9,1},{13,5},{2,10},{6,14},... | collective-permute-start | bytes 393224 | tf_op jit(solution)/shard_map/ppermute | solution.py:283
  84.2 1.9 %collective-permute-start.11 = (bf16[4,64,256]{2,1,0:T(8,128)(2,1)S(1)}, bf16[4,64,256]{2,1,0:T(8,128)(2,1)S(1)}, u32[]{:S(2)}, u32[]{:S(2)}) collective-permute-start(bf16[4,64,256]{2,1,0:T(8,128)(2,1)S(1)} %get-tuple-element.32), channel_id=1, source_target_pairs={{0,12},{4,0},{8,4},{12,8},{1,13},{5,1},{9,5},{13,9},{2,14},{6,2},{... | collective-permute-start | bytes 393224 | tf_op jit(solution)/shard_map/ppermute | solution.py:283
  86.1 11.4 %all_gather.3 = bf16[16,64,256]{2,1,0:T(8,128)(2,1)S(1)} all-gather(bf16[4,64,256]{2,1,0:T(8,128)(2,1)S(1)} %add_convert_fusion.1), channel_id=1, replica_groups=mesh['zh'=4,'x'=4,'core'=2,'ri'=4,'rj'=4] {'x'}, dimensions={0}, use_global_device_ids=true | all-gather | bytes 655360 | tf_op jit(solution)/shard_map/all_gather | solution.py:295
  97.5 0.1 add_convert_fusion
  97.7 5.8 %collective-permute-start.12 = (bf16[1216,256]{1,0:T(8,128)(2,1)S(1)}, bf16[1216,256]{1,0:T(8,128)(2,1)S(1)}, u32[]{:S(2)}, u32[]{:S(2)}) collective-permute-start(bf16[1216,256]{1,0:T(8,128)(2,1)S(1)} %pad_maximum_fusion), channel_id=1, source_target_pairs={{0,16},{16,0},{1,17},{17,1},{2,18},{18,2},{3,19},{19,3},{4,20},{20... | collective-permute-start | bytes 1867784 | tf_op jit(solution)/shard_map/ppermute | solution.py:249
  103.5 1.0 shard_map.97.before
  104.5 0.6 collective-permute-done.12.x_ref
  105.1 1.1 %shard_map.98 = (f32[8,256,256]{2,1,0:T(8,128)}, bf16[2,64,256]{2,1,0:T(8,128)(2,1)}, bf16[2,64,256]{2,1,0:T(8,128)(2,1)}, bf16[2,64,256]{2,1,0:T(8,128)(2,1)}) custom-call(bf16[1216,256]{1,0:T(8,128)(2,1)S(1)} %collective-permute-done.12.x_ref, bf16[2,96,256]{2,1,0:T(8,128)(2,1)S(1)} %get-tuple-element.38.own_ref, ...), custom_call_target="tpu_custom_call", output_to_operand_aliasing={{0}: (2, {})} | custom-call | flops 262144 | bytes 2097152 | tf_op jit(solution)/shard_map/pallas_call | solution.py:232
  (25 shorter events, 0.3 us)
Async XLA Ops:
  0.6 9.8 %copy-start = (bf16[8,256,256]{2,1,0:T(8,128)(2,1)S(1)}, bf16[8,256,256]{2,1,0:T(8,128)(2,1)}, u32[]{:S(2)}) copy-start(bf16[8,256,256]{2,1,0:T(8,128)(2,1)} %param.9) | copy-start | bytes 3145732
  0.6 10.8 %copy-start.4 = (bf16[2,256,64]{1,2,0:T(8,128)(2,1)S(1)}, bf16[2,256,64]{1,2,0:T(8,128)(2,1)}, u32[]{:S(2)}) copy-start(bf16[2,256,64]{1,2,0:T(8,128)(2,1)} %param.8) | copy-start | bytes 196612
  0.7 10.8 %copy-start.5 = (bf16[2,256,64]{1,2,0:T(8,128)(2,1)S(1)}, bf16[2,256,64]{1,2,0:T(8,128)(2,1)}, u32[]{:S(2)}) copy-start(bf16[2,256,64]{1,2,0:T(8,128)(2,1)} %param.7) | copy-start | bytes 196612
  1.6 9.8 %collective-permute-start = (bf16[2,128,256]{2,1,0:T(8,128)(2,1)S(1)}, bf16[2,128,256]{2,1,0:T(8,128)(2,1)S(1)}, u32[]{:S(2)}, u32[]{:S(2)}) collective-permute-start(bf16[2,128,256]{2,1,0:T(8,128)(2,1)S(1)} %pad_maximum_fusion.2), channel_id=1, source_target_pairs={{0,16},{16,0},{1,17},{17,1},{2,18},{18,2},{3,19},{19,3},{4,20},{20... | collective-permute-start | bytes 393224 | tf_op jit(solution)/shard_map/ppermute | solution.py:249
  10.5 12.1 %copy-start.1 = (bf16[2,256,64]{1,2,0:T(8,128)(2,1)S(1)}, bf16[2,256,64]{1,2,0:T(8,128)(2,1)}, u32[]{:S(2)}) copy-start(bf16[2,256,64]{1,2,0:T(8,128)(2,1)} %param.6) | copy-start | bytes 196612
  10.5 12.1 %copy-start.2 = (bf16[2,256,64]{1,2,0:T(8,128)(2,1)S(1)}, bf16[2,256,64]{1,2,0:T(8,128)(2,1)}, u32[]{:S(2)}) copy-start(bf16[2,256,64]{1,2,0:T(8,128)(2,1)} %param.11) | copy-start | bytes 196612
  10.5 12.1 %copy-start.3 = (bf16[2,256,64]{1,2,0:T(8,128)(2,1)S(1)}, bf16[2,256,64]{1,2,0:T(8,128)(2,1)}, u32[]{:S(2)}) copy-start(bf16[2,256,64]{1,2,0:T(8,128)(2,1)} %param.10) | copy-start | bytes 196612
  11.4 8.1 %collective-permute-start.2 = (bf16[4,128,256]{2,1,0:T(8,128)(2,1)S(1)}, bf16[4,128,256]{2,1,0:T(8,128)(2,1)S(1)}, u32[]{:S(2)}, u32[]{:S(2)}) collective-permute-start(bf16[4,128,256]{2,1,0:T(8,128)(2,1)S(1)} %pad_maximum_fusion.1), channel_id=1, source_target_pairs={{0,4},{1,8},{2,12},{3,0},{4,9},{5,13},{6,1},{7,5},{8,14},{9,2},{10... | collective-permute-start | bytes 786440 | tf_op jit(solution)/shard_map/ppermute | solution.py:275
  13.4 9.2 %collective-permute-start.1 = (bf16[4,128,256]{2,1,0:T(8,128)(2,1)S(1)}, bf16[4,128,256]{2,1,0:T(8,128)(2,1)S(1)}, u32[]{:S(2)}, u32[]{:S(2)}) collective-permute-start(bf16[4,128,256]{2,1,0:T(8,128)(2,1)S(1)} %pad_maximum_fusion.1), channel_id=1, source_target_pairs={{0,0},{1,4},{2,8},{3,12},{4,5},{5,9},{6,13},{7,1},{8,10},{9,14},{1... | collective-permute-start | bytes 786440 | tf_op jit(solution)/shard_map/ppermute | solution.py:275
  15.3 11.8 %all-to-all-start = ((bf16[4,256,256]{2,1,0:T(8,128)(2,1)}), bf16[4,256,256]{2,1,0:T(8,128)(2,1)S(1)}, u32[]{:S(2)}, u32[]{:S(2)}) async-start(bf16[4,256,256]{2,1,0:T(8,128)(2,1)} %dynamic-slice_bitcast_fusion), calls=%async_computation | async-start | bytes 1048576 | tf_op jit(solution)/shard_map/all_to_all | solution.py:276
  22.7 4.7 %collective-permute-start.3 = (bf16[704,256]{1,0:T(8,128)(2,1)S(1)}, bf16[704,256]{1,0:T(8,128)(2,1)S(1)}, u32[]{:S(2)}, u32[]{:S(2)}) collective-permute-start(bf16[704,256]{1,0:T(8,128)(2,1)S(1)} %shard_map.93), channel_id=1, source_target_pairs={{0,16},{16,0},{1,17},{17,1},{2,18},{18,2},{3,19},{19,3},{4,20},{20... | collective-permute-start | bytes 1081352 | tf_op jit(solution)/shard_map/ppermute | solution.py:249
  49.4 21.0 %collective-permute-start.4 = (bf16[4,64,256]{2,1,0:T(8,128)(2,1)S(1)}, bf16[4,64,256]{2,1,0:T(8,128)(2,1)S(1)}, u32[]{:S(2)}, u32[]{:S(2)}) collective-permute-start(bf16[4,64,256]{2,1,0:T(8,128)(2,1)S(1)} %reduce_sum.12.after), channel_id=1, source_target_pairs={{0,128},{256,384},{128,0},{384,256},{1,129},{257,385},{129,1},{385... | collective-permute-start | bytes 393224 | tf_op jit(solution)/shard_map/ppermute | solution.py:249
  58.3 18.5 %collective-permute-start.6 = (bf16[4,64,256]{2,1,0:T(8,128)(2,1)S(1)}, bf16[4,64,256]{2,1,0:T(8,128)(2,1)S(1)}, u32[]{:S(2)}, u32[]{:S(2)}) collective-permute-start(bf16[4,64,256]{2,1,0:T(8,128)(2,1)S(1)} %get-tuple-element.26), channel_id=1, source_target_pairs={{0,1},{1,2},{2,3},{3,0},{4,5},{5,6},{6,7},{7,4},{8,9},{9,10},{10,1... | collective-permute-start | bytes 393224 | tf_op jit(solution)/shard_map/ppermute | solution.py:283
  60.7 16.1 %collective-permute-start.7 = (bf16[4,64,256]{2,1,0:T(8,128)(2,1)S(1)}, bf16[4,64,256]{2,1,0:T(8,128)(2,1)S(1)}, u32[]{:S(2)}, u32[]{:S(2)}) collective-permute-start(bf16[4,64,256]{2,1,0:T(8,128)(2,1)S(1)} %get-tuple-element.27), channel_id=1, source_target_pairs={{0,2},{1,3},{2,0},{3,1},{4,6},{5,7},{6,4},{7,5},{8,10},{9,11},{10,... | collective-permute-start | bytes 393224 | tf_op jit(solution)/shard_map/ppermute | solution.py:283
  64.1 12.7 %collective-permute-start.8 = (bf16[4,64,256]{2,1,0:T(8,128)(2,1)S(1)}, bf16[4,64,256]{2,1,0:T(8,128)(2,1)S(1)}, u32[]{:S(2)}, u32[]{:S(2)}) collective-permute-start(bf16[4,64,256]{2,1,0:T(8,128)(2,1)S(1)} %get-tuple-element.28), channel_id=1, source_target_pairs={{0,3},{1,0},{2,1},{3,2},{4,7},{5,4},{6,5},{7,6},{8,11},{9,8},{10,9... | collective-permute-start | bytes 393224 | tf_op jit(solution)/shard_map/ppermute | solution.py:283
  70.5 15.6 %collective-permute-start.5 = (bf16[4,64,256]{2,1,0:T(8,128)(2,1)S(1)}, bf16[4,64,256]{2,1,0:T(8,128)(2,1)S(1)}, u32[]{:S(2)}, u32[]{:S(2)}) collective-permute-start(bf16[4,64,256]{2,1,0:T(8,128)(2,1)S(1)} %add_convert_fusion.2.after), channel_id=1, source_target_pairs={{128,256},{384,0},{256,128},{0,384},{129,257},{385,1},{257,129},{1... | collective-permute-start | bytes 393224 | tf_op jit(solution)/shard_map/ppermute | solution.py:249
  77.0 20.6 %collective-permute-start.9 = (bf16[4,64,256]{2,1,0:T(8,128)(2,1)S(1)}, bf16[4,64,256]{2,1,0:T(8,128)(2,1)S(1)}, u32[]{:S(2)}, u32[]{:S(2)}) collective-permute-start(bf16[4,64,256]{2,1,0:T(8,128)(2,1)S(1)} %get-tuple-element.30), channel_id=1, source_target_pairs={{0,4},{4,8},{8,12},{12,0},{1,5},{5,9},{9,13},{13,1},{2,6},{6,10},{... | collective-permute-start | bytes 393224 | tf_op jit(solution)/shard_map/ppermute | solution.py:283
  78.9 18.6 %collective-permute-start.10 = (bf16[4,64,256]{2,1,0:T(8,128)(2,1)S(1)}, bf16[4,64,256]{2,1,0:T(8,128)(2,1)S(1)}, u32[]{:S(2)}, u32[]{:S(2)}) collective-permute-start(bf16[4,64,256]{2,1,0:T(8,128)(2,1)S(1)} %get-tuple-element.31), channel_id=1, source_target_pairs={{0,8},{4,12},{8,0},{12,4},{1,9},{5,13},{9,1},{13,5},{2,10},{6,14},... | collective-permute-start | bytes 393224 | tf_op jit(solution)/shard_map/ppermute | solution.py:283
  84.2 13.4 %collective-permute-start.11 = (bf16[4,64,256]{2,1,0:T(8,128)(2,1)S(1)}, bf16[4,64,256]{2,1,0:T(8,128)(2,1)S(1)}, u32[]{:S(2)}, u32[]{:S(2)}) collective-permute-start(bf16[4,64,256]{2,1,0:T(8,128)(2,1)S(1)} %get-tuple-element.32), channel_id=1, source_target_pairs={{0,12},{4,0},{8,4},{12,8},{1,13},{5,1},{9,5},{13,9},{2,14},{6,2},{... | collective-permute-start | bytes 393224 | tf_op jit(solution)/shard_map/ppermute | solution.py:283
  97.7 7.5 %collective-permute-start.12 = (bf16[1216,256]{1,0:T(8,128)(2,1)S(1)}, bf16[1216,256]{1,0:T(8,128)(2,1)S(1)}, u32[]{:S(2)}, u32[]{:S(2)}) collective-permute-start(bf16[1216,256]{1,0:T(8,128)(2,1)S(1)} %pad_maximum_fusion), channel_id=1, source_target_pairs={{0,16},{16,0},{1,17},{17,1},{2,18},{18,2},{3,19},{19,3},{4,20},{20... | collective-permute-start | bytes 1867784 | tf_op jit(solution)/shard_map/ppermute | solution.py:249

commit v16 on v15

--- a/solution.py
+++ b/solution.py
@@ -21,7 +21,7 @@
 NN = (((1,), (0,)), ((), ()))
 
 
-def pick_kernel(q_ref, g_ref, o_ref, first, second, send):
+def pick_kernel(q_ref, g_ref, o_ref, first, second, bias, send):
     other = 1 - lax.axis_index("core")
     at = 0
     half = pl.ds(pl.multiple_of(other * HEAD, HEAD), HEAD)
@@ -35,15 +35,16 @@
                 half = pl.ds(pl.multiple_of((2 * part + other) * HEAD, HEAD), HEAD)
                 send[at : at + HEAD, :] = x_ref[s, half, :]
                 at += HEAD
+    send[at : at + ROWS, :] = bias[other]
 
 
 def pick(*args):
     vmem = pl.BlockSpec(memory_space=pltpu.VMEM)
-    rows = (3 * (SEQS // 2) + 2 * SEQS * 2) * HEAD
+    rows = (3 * (SEQS // 2) + 2 * SEQS * 2) * HEAD + ROWS
     return pl.pallas_call(
         pick_kernel,
         out_shape=jax.ShapeDtypeStruct((rows, ROWS), BF),
-        in_specs=[vmem] * 5,
+        in_specs=[vmem] * 6,
         out_specs=vmem,
         compiler_params=pltpu.CompilerParams(vmem_limit_bytes=8 * 2**20),
         cost_estimate=pl.CostEstimate(flops=0, bytes_accessed=2**20, transcendentals=0),
@@ -51,9 +52,9 @@
 
 
 def attention_kernel(
-    q_ref, g_ref, o_ref, first, second, given, bias,
+    q_ref, g_ref, o_ref, first, second, given, bias_own, bias_near, bias_far,
     bias_grad, dq_ref, dkv_ref,
-    stack, wide, raw, low, inner,
+    stack, wide, raw, low, inner, bias,
 ):
     ri, rj, core = (lax.axis_index(a) for a in ("ri", "rj", "core"))
     own = pl.ds(pl.multiple_of(core * HEAD, HEAD), HEAD)
@@ -75,6 +76,11 @@
         return given[at : at + HEAD, :]
 
     channel = lax.broadcasted_iota(jnp.int32, (2 * HEAD, ROWS), 0) // HEAD
+
+    bias[rj] = bias_own[...]
+    bias[lax.rem(rj + N - 1 - 2 * core, N)] = bias_near[core]
+    bias[lax.rem(rj + 1 + 2 * core, N)] = given[given.shape[0] - ROWS :, :]
+    bias[lax.rem(rj + 2, N)] = bias_far[...]
 
     for s in range(SEQS):
         for part in range(2):
@@ -137,7 +143,7 @@
             jax.ShapeDtypeStruct((SEQS, HEAD, ROWS), BF),
             jax.ShapeDtypeStruct((N, SEQS, 2 * HEAD, ROWS), BF),
         ),
-        in_specs=[vmem] * 7,
+        in_specs=[vmem] * 9,
         out_specs=(vmem,) * 3,
         scratch_shapes=[
             pltpu.VMEM((SEQS, 2 * ROWS, 2 * HEAD), BF),
@@ -145,6 +151,7 @@
             pltpu.VMEM((SEQS, 2 * ROWS, KEYS), F32),
             pltpu.VMEM((SEQS, 2 * ROWS, KEYS), BF),
             pltpu.VMEM((SEQS, ROWS, LANES), F32),
+            pltpu.VMEM((N, ROWS, ROWS), BF),
         ],
         compiler_params=pltpu.CompilerParams(vmem_limit_bytes=32 * 2**20),
         cost_estimate=pl.CostEstimate(
@@ -262,8 +269,14 @@
 
     core = lax.axis_index("core")
     held = jnp.concatenate([k, v], axis=1)
-    bias = lax.dynamic_index_in_dim(pair_bias.reshape(N, 2, ROWS, ROWS), core, 1, False)
-    theirs, bias = lax.optimization_barrier((swap(held, "core", [(0, 1)]), bias))
+    rj = lax.axis_index("rj")
+    heads = pair_bias.reshape(N, 2, ROWS, ROWS)
+    near = lax.dynamic_index_in_dim(heads, lax.rem(rj + 1 + 2 * core, N), 0, False)
+    far = lax.dynamic_index_in_dim(pair_bias, 2 * lax.rem(rj + 2, N) + core, 0, False)
+    bias_own = lax.dynamic_index_in_dim(pair_bias, 2 * rj + core, 0, False)
+    theirs, near, far, bias_own = lax.optimization_barrier(
+        (swap(held, "core", [(0, 1)]), near, far, bias_own)
+    )
     kv = jnp.concatenate([held, theirs])
     spread = []
     for i in range(2):
@@ -273,10 +286,13 @@
                 target = (a + b + 2 * c + i) % N * N + a
                 steps.append((c * N * N + a * N + b, c * N * N + target))
         spread.append(lax.ppermute(kv, ("core", "ri", "rj"), steps))
-    bias = lax.all_to_all(bias, "rj", 0, 0, tiled=True)
-    given = swap(pick(q, g, o, *spread), "core", [(0, 1)])
-
-    total, dq, dkv = attention(q, g, o, *spread, given, bias)
+    steps = [(c * N + a, c * N + (a + 1 + 2 * c) % N) for c in range(2) for a in range(N)]
+    near = lax.ppermute(near, ("core", "rj"), steps)
+    far = lax.ppermute(far, "rj", [(a, (a + 2) % N) for a in range(N)])
+    near, far, *spread = lax.optimization_barrier((near, far, *spread))
+    given = swap(pick(q, g, o, *spread, near), "core", [(0, 1)])
+
+    total, dq, dkv = attention(q, g, o, *spread, given, bias_own, near, far)
 
     def spread_out(parts, axis):
         return [parts[0]] + [

time: 107 us -> 112 us (1.047)
  starting transfers between devices: 59.2 us -> 65.2 us
    ppermute x0 -> x2, starting transfers between devices: none -> 7.96 us  [the longest x1 6.04 us: body(): far = lax.ppermute(far, 'rj', [(a, (a + 2) % N) for a in range(N)])]
    all_to_all x1 -> x0, starting transfers between devices: 4.19 us -> none  [body(): bias = lax.all_to_all(bias, 'rj', 0, 0, tiled=True)]
    ppermute x0 -> x2, waiting for transfers between devices: none -> 4.11 us  [the longest x1 4.11 us: body(): far = lax.ppermute(far, 'rj', [(a, (a + 2) % N) for a in range(N)])]
    ppermute x2, waiting for transfers between devices: 3.07 us -> 0.01 us  [body(): spread.append(lax.ppermute(kv, ('core', 'ri', 'rj'), steps))]
    ppermute x5, starting transfers between devices: 33.1 us -> 34.5 us  [swap(): lax.ppermute(x, axis, [(a, b) for a, b in pairs] + [(b, a) for a, b in pa...]
    squeeze x1 -> x2, local copies, waits for them, and re-layouts: 0.83 us -> 1.96 us  [the longest x1 0.99 us: body(): bias_own = lax.dynamic_index_in_dim(pair_bias, 2 * rj + core, 0, False)]
  transfers between devices with their start and end apart: 14 -> 15, of which waited for: 6 -> 4; matrix products, arithmetic and copies ran while one was open for 1% -> 2% of each run, Pallas kernels for 1% -> 1%
where the time goes in v16:
time: 112 us
  starting transfers between devices  65.2 us (58%)
  blocking collectives  28.9 us (26%)
  waiting for transfers between devices  7.71 us (7%)
  Pallas kernels  5.68 us (5%)
  local copies, waits for them, and re-layouts  1.98 us (2%)
  other arithmetic  1.26 us (1%)
    ppermute x5, starting transfers between devices, swap(): lax.ppermute(x, axis, [(a, b) for a, b in pairs] + [(b, a) for a, b in pa...  34.5 us
    ppermute x6, starting transfers between devices, spread_out(): lax.ppermute(parts[t], axis, [(a, (a + t) % N) for a in range(N)])  18.9 us
    all_to_all x1, blocking collectives, body(): spread = lax.all_to_all(total, ('x', 'rj'), 0, 0, tiled=True)  17.7 us
    all_gather x1, blocking collectives, body(): mine = lax.all_gather(total, 'x', axis=0, tiled=True).reshape(-1, ROWS)  11.2 us
    ppermute x1, starting transfers between devices, body(): far = lax.ppermute(far, 'rj', [(a, (a + 2) % N) for a in range(N)])  6.04 us
    ppermute x1, waiting for transfers between devices, body(): far = lax.ppermute(far, 'rj', [(a, (a + 2) % N) for a in range(N)])  4.11 us
    ppermute x2, starting transfers between devices, body(): spread.append(lax.ppermute(kv, ('core', 'ri', 'rj'), steps))  3.89 us
    ppermute x5, waiting for transfers between devices, swap(): lax.ppermute(x, axis, [(a, b) for a, b in pairs] + [(b, a) for a, b in pa...  3.58 us
  transfers between devices with their start and end apart: 15, of which 4 were waited for; matrix products, arithmetic and copies ran while one was open for 2% of the time, Pallas kernels for 1%

profile of v16, /device:TPU:1, one launch (start us, length us, event | category | flops | bytes accessed | tf_op | source)
XLA Modules:
  0.0 111.8 jit_solution(3001123029408050823)
XLA Ops:
  0.7 1.0 pad_maximum_fusion.2
  1.6 8.8 %collective-permute-start = (bf16[2,128,256]{2,1,0:T(8,128)(2,1)S(1)}, bf16[2,128,256]{2,1,0:T(8,128)(2,1)S(1)}, u32[]{:S(2)}, u32[]{:S(2)}) collective-permute-start(bf16[2,128,256]{2,1,0:T(8,128)(2,1)S(1)} %pad_maximum_fusion.2), channel_id=1, source_target_pairs={{0,16},{16,0},{1,17},{17,1},{2,18},{18,2},{3,19},{19,3},{4,20},{20... | collective-permute-start | bytes 393224 | tf_op jit(solution)/shard_map/ppermute | solution.py:256
  10.5 1.0 dynamic-slice_bitcast_fusion.1
  11.5 1.0 dynamic-slice_bitcast_fusion
  12.4 0.0 collective-permute-done
  12.5 1.9 %collective-permute-start.4 = (bf16[4,128,256]{2,1,0:T(8,128)(2,1)S(1)}, bf16[4,128,256]{2,1,0:T(8,128)(2,1)S(1)}, u32[]{:S(2)}, u32[]{:S(2)}) collective-permute-start(bf16[4,128,256]{2,1,0:T(8,128)(2,1)S(1)} %pad_maximum_fusion.1), channel_id=1, source_target_pairs={{0,4},{1,8},{2,12},{3,0},{4,9},{5,13},{6,1},{7,5},{8,14},{9,2},{10... | collective-permute-start | bytes 786440 | tf_op jit(solution)/shard_map/ppermute | solution.py:288
  14.4 2.0 %collective-permute-start.3 = (bf16[4,128,256]{2,1,0:T(8,128)(2,1)S(1)}, bf16[4,128,256]{2,1,0:T(8,128)(2,1)S(1)}, u32[]{:S(2)}, u32[]{:S(2)}) collective-permute-start(bf16[4,128,256]{2,1,0:T(8,128)(2,1)S(1)} %pad_maximum_fusion.1), channel_id=1, source_target_pairs={{0,0},{1,4},{2,8},{3,12},{4,5},{5,9},{6,13},{7,1},{8,10},{9,14},{1... | collective-permute-start | bytes 786440 | tf_op jit(solution)/shard_map/ppermute | solution.py:288
  16.4 1.9 %collective-permute-start.1 = (bf16[2,256,256]{2,1,0:T(8,128)(2,1)S(1)}, bf16[2,256,256]{2,1,0:T(8,128)(2,1)S(1)}, u32[]{:S(2)}, u32[]{:S(2)}) collective-permute-start(bf16[2,256,256]{2,1,0:T(8,128)(2,1)S(1)} %dynamic-slice_bitcast_fusion), channel_id=1, source_target_pairs={{0,1},{1,2},{2,3},{3,0},{16,19},{17,16},{18,17},{19,18},{4,5},{5,6... | collective-permute-start | bytes 786440 | tf_op jit(solution)/shard_map/ppermute | solution.py:290
  18.3 6.0 %collective-permute-start.2 = (bf16[256,256]{1,0:T(8,128)(2,1)S(1)}, bf16[256,256]{1,0:T(8,128)(2,1)S(1)}, u32[]{:S(2)}, u32[]{:S(2)}) collective-permute-start(bf16[256,256]{1,0:T(8,128)(2,1)S(1)} %get-tuple-element.28), channel_id=1, source_target_pairs={{0,2},{1,3},{2,0},{3,1},{4,6},{5,7},{6,4},{7,5},{8,10},{9,11},{10,... | collective-permute-start | bytes 393224 | tf_op jit(solution)/shard_map/ppermute | solution.py:291
  24.4 4.1 %collective-permute-done.2.bias_far = bf16[256,256]{1,0:T(8,128)(2,1)S(1)} collective-permute-done((bf16[256,256]{1,0:T(8,128)(2,1)S(1)}, bf16[256,256]{1,0:T(8,128)(2,1)S(1)}, u32[]{:S(2)}, u32[]{:S(2)}) %collective-permute-start.2) | collective-permute-done | bytes 131104 | tf_op jit(solution)/shard_map/ppermute | solution.py:291
  28.5 0.0 collective-permute-done.4.second
  28.6 4.2 %collective-permute-start.5 = (bf16[960,256]{1,0:T(8,128)(2,1)S(1)}, bf16[960,256]{1,0:T(8,128)(2,1)S(1)}, u32[]{:S(2)}, u32[]{:S(2)}) collective-permute-start(bf16[960,256]{1,0:T(8,128)(2,1)S(1)} %shard_map.93), channel_id=1, source_target_pairs={{0,16},{16,0},{1,17},{17,1},{2,18},{18,2},{3,19},{19,3},{4,20},{20... | collective-permute-start | bytes 1474568 | tf_op jit(solution)/shard_map/ppermute | solution.py:256
  32.8 1.5 %collective-permute-done.5.given = bf16[960,256]{1,0:T(8,128)(2,1)S(1)} collective-permute-done((bf16[960,256]{1,0:T(8,128)(2,1)S(1)}, bf16[960,256]{1,0:T(8,128)(2,1)S(1)}, u32[]{:S(2)}, u32[]{:S(2)}) %collective-permute-start.5) | collective-permute-done | bytes 491552 | tf_op jit(solution)/shard_map/ppermute | solution.py:256
  34.3 3.4 %shard_map.94 = (bf16[16,64,256]{2,1,0:T(8,128)(2,1)S(1)}, bf16[4,32,256]{2,1,0:T(8,128)(2,1)S(1)}, bf16[4,4,64,256]{3,2,1,0:T(8,128)(2,1)S(1)}) custom-call(bf16[2,64,256]{2,1,0:T(8,128)(2,1)S(1)} %bitcast.21, bf16[2,64,256]{2,1,0:T(8,128)(2,1)S(1)} %bitcast.23, bf16[2,64,256]{2,1,0:T(8,128)(2,1)S(1)} %bitcast.25, ...), custom_call_target="tpu_custom_call" | custom-call | flops 335544320 | bytes 6291456 | tf_op jit(solution)/shard_map/pallas_call | solution.py:139
  37.7 17.7 %all_to_all.5 = bf16[16,64,256]{2,1,0:T(8,128)(2,1)S(1)} all-to-all(bf16[16,64,256]{2,1,0:T(8,128)(2,1)S(1)} %get-tuple-element.35), channel_id=1, replica_groups=mesh['zh'=4,'x'=4,'core'=2,'ri'=4,'rj'=4] {'x','rj'}, dimensions={0} | all-to-all | bytes 1048576 | tf_op jit(solution)/shard_map/all_to_all | solution.py:303
  55.4 0.1 reduce_sum.12.after
  55.5 8.8 %collective-permute-start.6 = (bf16[4,64,256]{2,1,0:T(8,128)(2,1)S(1)}, bf16[4,64,256]{2,1,0:T(8,128)(2,1)S(1)}, u32[]{:S(2)}, u32[]{:S(2)}) collective-permute-start(bf16[4,64,256]{2,1,0:T(8,128)(2,1)S(1)} %reduce_sum.12.after), channel_id=1, source_target_pairs={{0,128},{256,384},{128,0},{384,256},{1,129},{257,385},{129,1},{385... | collective-permute-start | bytes 393224 | tf_op jit(solution)/shard_map/ppermute | solution.py:256
  64.3 2.3 %collective-permute-start.8 = (bf16[4,64,256]{2,1,0:T(8,128)(2,1)S(1)}, bf16[4,64,256]{2,1,0:T(8,128)(2,1)S(1)}, u32[]{:S(2)}, u32[]{:S(2)}) collective-permute-start(bf16[4,64,256]{2,1,0:T(8,128)(2,1)S(1)} %get-tuple-element.38), channel_id=1, source_target_pairs={{0,1},{1,2},{2,3},{3,0},{4,5},{5,6},{6,7},{7,4},{8,9},{9,10},{10,1... | collective-permute-start | bytes 393224 | tf_op jit(solution)/shard_map/ppermute | solution.py:299
  66.7 3.6 %collective-permute-start.9 = (bf16[4,64,256]{2,1,0:T(8,128)(2,1)S(1)}, bf16[4,64,256]{2,1,0:T(8,128)(2,1)S(1)}, u32[]{:S(2)}, u32[]{:S(2)}) collective-permute-start(bf16[4,64,256]{2,1,0:T(8,128)(2,1)S(1)} %get-tuple-element.39), channel_id=1, source_target_pairs={{0,2},{1,3},{2,0},{3,1},{4,6},{5,7},{6,4},{7,5},{8,10},{9,11},{10,... | collective-permute-start | bytes 393224 | tf_op jit(solution)/shard_map/ppermute | solution.py:299
  70.2 3.1 %collective-permute-start.10 = (bf16[4,64,256]{2,1,0:T(8,128)(2,1)S(1)}, bf16[4,64,256]{2,1,0:T(8,128)(2,1)S(1)}, u32[]{:S(2)}, u32[]{:S(2)}) collective-permute-start(bf16[4,64,256]{2,1,0:T(8,128)(2,1)S(1)} %get-tuple-element.40), channel_id=1, source_target_pairs={{0,3},{1,0},{2,1},{3,2},{4,7},{5,4},{6,5},{7,6},{8,11},{9,8},{10,9... | collective-permute-start | bytes 393224 | tf_op jit(solution)/shard_map/ppermute | solution.py:299
  73.4 1.5 %collective-permute-done.6 = bf16[4,64,256]{2,1,0:T(8,128)(2,1)S(1)} collective-permute-done((bf16[4,64,256]{2,1,0:T(8,128)(2,1)S(1)}, bf16[4,64,256]{2,1,0:T(8,128)(2,1)S(1)}, u32[]{:S(2)}, u32[]{:S(2)}) %collective-permute-start.6) | collective-permute-done | bytes 131104 | tf_op jit(solution)/shard_map/ppermute | solution.py:256
  74.9 6.5 %collective-permute-start.7 = (bf16[4,64,256]{2,1,0:T(8,128)(2,1)S(1)}, bf16[4,64,256]{2,1,0:T(8,128)(2,1)S(1)}, u32[]{:S(2)}, u32[]{:S(2)}) collective-permute-start(bf16[4,64,256]{2,1,0:T(8,128)(2,1)S(1)} %add_convert_fusion.2.after), channel_id=1, source_target_pairs={{128,256},{384,0},{256,128},{0,384},{129,257},{385,1},{257,129},{1... | collective-permute-start | bytes 393224 | tf_op jit(solution)/shard_map/ppermute | solution.py:256
  81.4 0.1 shard_map.96
  81.6 1.9 %collective-permute-start.11 = (bf16[4,64,256]{2,1,0:T(8,128)(2,1)S(1)}, bf16[4,64,256]{2,1,0:T(8,128)(2,1)S(1)}, u32[]{:S(2)}, u32[]{:S(2)}) collective-permute-start(bf16[4,64,256]{2,1,0:T(8,128)(2,1)S(1)} %get-tuple-element.42), channel_id=1, source_target_pairs={{0,4},{4,8},{8,12},{12,0},{1,5},{5,9},{9,13},{13,1},{2,6},{6,10},{... | collective-permute-start | bytes 393224 | tf_op jit(solution)/shard_map/ppermute | solution.py:299
  83.5 6.0 %collective-permute-start.12 = (bf16[4,64,256]{2,1,0:T(8,128)(2,1)S(1)}, bf16[4,64,256]{2,1,0:T(8,128)(2,1)S(1)}, u32[]{:S(2)}, u32[]{:S(2)}) collective-permute-start(bf16[4,64,256]{2,1,0:T(8,128)(2,1)S(1)} %get-tuple-element.43), channel_id=1, source_target_pairs={{0,8},{4,12},{8,0},{12,4},{1,9},{5,13},{9,1},{13,5},{2,10},{6,14},... | collective-permute-start | bytes 393224 | tf_op jit(solution)/shard_map/ppermute | solution.py:299
  89.5 1.9 %collective-permute-start.13 = (bf16[4,64,256]{2,1,0:T(8,128)(2,1)S(1)}, bf16[4,64,256]{2,1,0:T(8,128)(2,1)S(1)}, u32[]{:S(2)}, u32[]{:S(2)}) collective-permute-start(bf16[4,64,256]{2,1,0:T(8,128)(2,1)S(1)} %get-tuple-element.44), channel_id=1, source_target_pairs={{0,12},{4,0},{8,4},{12,8},{1,13},{5,1},{9,5},{13,9},{2,14},{6,2},{... | collective-permute-start | bytes 393224 | tf_op jit(solution)/shard_map/ppermute | solution.py:299
  91.5 11.2 %all_gather.3 = bf16[16,64,256]{2,1,0:T(8,128)(2,1)S(1)} all-gather(bf16[4,64,256]{2,1,0:T(8,128)(2,1)S(1)} %add_convert_fusion.1), channel_id=1, replica_groups=mesh['zh'=4,'x'=4,'core'=2,'ri'=4,'rj'=4] {'x'}, dimensions={0}, use_global_device_ids=true | all-gather | bytes 655360 | tf_op jit(solution)/shard_map/all_gather | solution.py:311
  102.7 0.1 add_convert_fusion
  102.9 6.2 %collective-permute-start.14 = (bf16[1216,256]{1,0:T(8,128)(2,1)S(1)}, bf16[1216,256]{1,0:T(8,128)(2,1)S(1)}, u32[]{:S(2)}, u32[]{:S(2)}) collective-permute-start(bf16[1216,256]{1,0:T(8,128)(2,1)S(1)} %pad_maximum_fusion), channel_id=1, source_target_pairs={{0,16},{16,0},{1,17},{17,1},{2,18},{18,2},{3,19},{19,3},{4,20},{20... | collective-permute-start | bytes 1867784 | tf_op jit(solution)/shard_map/ppermute | solution.py:256
  109.0 1.0 shard_map.97.before
  110.0 0.6 collective-permute-done.14.x_ref
  110.7 1.1 shard_map.98
  (26 shorter events, 0.3 us)
Async XLA Ops:
  0.6 11.8 %copy-start.3 = (bf16[2,256,64]{1,2,0:T(8,128)(2,1)S(1)}, bf16[2,256,64]{1,2,0:T(8,128)(2,1)}, u32[]{:S(2)}) copy-start(bf16[2,256,64]{1,2,0:T(8,128)(2,1)} %param.8) | copy-start | bytes 196612
  0.6 11.8 %copy-start.4 = (bf16[2,256,64]{1,2,0:T(8,128)(2,1)S(1)}, bf16[2,256,64]{1,2,0:T(8,128)(2,1)}, u32[]{:S(2)}) copy-start(bf16[2,256,64]{1,2,0:T(8,128)(2,1)} %param.7) | copy-start | bytes 196612
  0.7 27.9 %copy-start.1 = (bf16[2,256,64]{1,2,0:T(8,128)(2,1)S(1)}, bf16[2,256,64]{1,2,0:T(8,128)(2,1)}, u32[]{:S(2)}) copy-start(bf16[2,256,64]{1,2,0:T(8,128)(2,1)} %param.11) | copy-start | bytes 196612
  0.7 27.9 %copy-start.2 = (bf16[2,256,64]{1,2,0:T(8,128)(2,1)S(1)}, bf16[2,256,64]{1,2,0:T(8,128)(2,1)}, u32[]{:S(2)}) copy-start(bf16[2,256,64]{1,2,0:T(8,128)(2,1)} %param.10) | copy-start | bytes 196612
  0.7 27.9 %copy-start = (bf16[2,256,64]{1,2,0:T(8,128)(2,1)S(1)}, bf16[2,256,64]{1,2,0:T(8,128)(2,1)}, u32[]{:S(2)}) copy-start(bf16[2,256,64]{1,2,0:T(8,128)(2,1)} %param.6) | copy-start | bytes 196612
  1.6 10.8 %collective-permute-start = (bf16[2,128,256]{2,1,0:T(8,128)(2,1)S(1)}, bf16[2,128,256]{2,1,0:T(8,128)(2,1)S(1)}, u32[]{:S(2)}, u32[]{:S(2)}) collective-permute-start(bf16[2,128,256]{2,1,0:T(8,128)(2,1)S(1)} %pad_maximum_fusion.2), channel_id=1, source_target_pairs={{0,16},{16,0},{1,17},{17,1},{2,18},{18,2},{3,19},{19,3},{4,20},{20... | collective-permute-start | bytes 393224 | tf_op jit(solution)/shard_map/ppermute | solution.py:256
  12.5 16.0 %collective-permute-start.4 = (bf16[4,128,256]{2,1,0:T(8,128)(2,1)S(1)}, bf16[4,128,256]{2,1,0:T(8,128)(2,1)S(1)}, u32[]{:S(2)}, u32[]{:S(2)}) collective-permute-start(bf16[4,128,256]{2,1,0:T(8,128)(2,1)S(1)} %pad_maximum_fusion.1), channel_id=1, source_target_pairs={{0,4},{1,8},{2,12},{3,0},{4,9},{5,13},{6,1},{7,5},{8,14},{9,2},{10... | collective-permute-start | bytes 786440 | tf_op jit(solution)/shard_map/ppermute | solution.py:288
  14.4 14.1 %collective-permute-start.3 = (bf16[4,128,256]{2,1,0:T(8,128)(2,1)S(1)}, bf16[4,128,256]{2,1,0:T(8,128)(2,1)S(1)}, u32[]{:S(2)}, u32[]{:S(2)}) collective-permute-start(bf16[4,128,256]{2,1,0:T(8,128)(2,1)S(1)} %pad_maximum_fusion.1), channel_id=1, source_target_pairs={{0,0},{1,4},{2,8},{3,12},{4,5},{5,9},{6,13},{7,1},{8,10},{9,14},{1... | collective-permute-start | bytes 786440 | tf_op jit(solution)/shard_map/ppermute | solution.py:288
  16.4 12.1 %collective-permute-start.1 = (bf16[2,256,256]{2,1,0:T(8,128)(2,1)S(1)}, bf16[2,256,256]{2,1,0:T(8,128)(2,1)S(1)}, u32[]{:S(2)}, u32[]{:S(2)}) collective-permute-start(bf16[2,256,256]{2,1,0:T(8,128)(2,1)S(1)} %dynamic-slice_bitcast_fusion), channel_id=1, source_target_pairs={{0,1},{1,2},{2,3},{3,0},{16,19},{17,16},{18,17},{19,18},{4,5},{5,6... | collective-permute-start | bytes 786440 | tf_op jit(solution)/shard_map/ppermute | solution.py:290
  18.3 10.2 %collective-permute-start.2 = (bf16[256,256]{1,0:T(8,128)(2,1)S(1)}, bf16[256,256]{1,0:T(8,128)(2,1)S(1)}, u32[]{:S(2)}, u32[]{:S(2)}) collective-permute-start(bf16[256,256]{1,0:T(8,128)(2,1)S(1)} %get-tuple-element.28), channel_id=1, source_target_pairs={{0,2},{1,3},{2,0},{3,1},{4,6},{5,7},{6,4},{7,5},{8,10},{9,11},{10,... | collective-permute-start | bytes 393224 | tf_op jit(solution)/shard_map/ppermute | solution.py:291
  28.6 5.7 %collective-permute-start.5 = (bf16[960,256]{1,0:T(8,128)(2,1)S(1)}, bf16[960,256]{1,0:T(8,128)(2,1)S(1)}, u32[]{:S(2)}, u32[]{:S(2)}) collective-permute-start(bf16[960,256]{1,0:T(8,128)(2,1)S(1)} %shard_map.93), channel_id=1, source_target_pairs={{0,16},{16,0},{1,17},{17,1},{2,18},{18,2},{3,19},{19,3},{4,20},{20... | collective-permute-start | bytes 1474568 | tf_op jit(solution)/shard_map/ppermute | solution.py:256
  55.5 19.4 %collective-permute-start.6 = (bf16[4,64,256]{2,1,0:T(8,128)(2,1)S(1)}, bf16[4,64,256]{2,1,0:T(8,128)(2,1)S(1)}, u32[]{:S(2)}, u32[]{:S(2)}) collective-permute-start(bf16[4,64,256]{2,1,0:T(8,128)(2,1)S(1)} %reduce_sum.12.after), channel_id=1, source_target_pairs={{0,128},{256,384},{128,0},{384,256},{1,129},{257,385},{129,1},{385... | collective-permute-start | bytes 393224 | tf_op jit(solution)/shard_map/ppermute | solution.py:256
  64.3 17.1 %collective-permute-start.8 = (bf16[4,64,256]{2,1,0:T(8,128)(2,1)S(1)}, bf16[4,64,256]{2,1,0:T(8,128)(2,1)S(1)}, u32[]{:S(2)}, u32[]{:S(2)}) collective-permute-start(bf16[4,64,256]{2,1,0:T(8,128)(2,1)S(1)} %get-tuple-element.38), channel_id=1, source_target_pairs={{0,1},{1,2},{2,3},{3,0},{4,5},{5,6},{6,7},{7,4},{8,9},{9,10},{10,1... | collective-permute-start | bytes 393224 | tf_op jit(solution)/shard_map/ppermute | solution.py:299
  66.7 14.7 %collective-permute-start.9 = (bf16[4,64,256]{2,1,0:T(8,128)(2,1)S(1)}, bf16[4,64,256]{2,1,0:T(8,128)(2,1)S(1)}, u32[]{:S(2)}, u32[]{:S(2)}) collective-permute-start(bf16[4,64,256]{2,1,0:T(8,128)(2,1)S(1)} %get-tuple-element.39), channel_id=1, source_target_pairs={{0,2},{1,3},{2,0},{3,1},{4,6},{5,7},{6,4},{7,5},{8,10},{9,11},{10,... | collective-permute-start | bytes 393224 | tf_op jit(solution)/shard_map/ppermute | solution.py:299
  70.2 11.2 %collective-permute-start.10 = (bf16[4,64,256]{2,1,0:T(8,128)(2,1)S(1)}, bf16[4,64,256]{2,1,0:T(8,128)(2,1)S(1)}, u32[]{:S(2)}, u32[]{:S(2)}) collective-permute-start(bf16[4,64,256]{2,1,0:T(8,128)(2,1)S(1)} %get-tuple-element.40), channel_id=1, source_target_pairs={{0,3},{1,0},{2,1},{3,2},{4,7},{5,4},{6,5},{7,6},{8,11},{9,8},{10,9... | collective-permute-start | bytes 393224 | tf_op jit(solution)/shard_map/ppermute | solution.py:299
  74.9 16.6 %collective-permute-start.7 = (bf16[4,64,256]{2,1,0:T(8,128)(2,1)S(1)}, bf16[4,64,256]{2,1,0:T(8,128)(2,1)S(1)}, u32[]{:S(2)}, u32[]{:S(2)}) collective-permute-start(bf16[4,64,256]{2,1,0:T(8,128)(2,1)S(1)} %add_convert_fusion.2.after), channel_id=1, source_target_pairs={{128,256},{384,0},{256,128},{0,384},{129,257},{385,1},{257,129},{1... | collective-permute-start | bytes 393224 | tf_op jit(solution)/shard_map/ppermute | solution.py:256
  81.6 21.1 %collective-permute-start.11 = (bf16[4,64,256]{2,1,0:T(8,128)(2,1)S(1)}, bf16[4,64,256]{2,1,0:T(8,128)(2,1)S(1)}, u32[]{:S(2)}, u32[]{:S(2)}) collective-permute-start(bf16[4,64,256]{2,1,0:T(8,128)(2,1)S(1)} %get-tuple-element.42), channel_id=1, source_target_pairs={{0,4},{4,8},{8,12},{12,0},{1,5},{5,9},{9,13},{13,1},{2,6},{6,10},{... | collective-permute-start | bytes 393224 | tf_op jit(solution)/shard_map/ppermute | solution.py:299
  83.5 19.2 %collective-permute-start.12 = (bf16[4,64,256]{2,1,0:T(8,128)(2,1)S(1)}, bf16[4,64,256]{2,1,0:T(8,128)(2,1)S(1)}, u32[]{:S(2)}, u32[]{:S(2)}) collective-permute-start(bf16[4,64,256]{2,1,0:T(8,128)(2,1)S(1)} %get-tuple-element.43), channel_id=1, source_target_pairs={{0,8},{4,12},{8,0},{12,4},{1,9},{5,13},{9,1},{13,5},{2,10},{6,14},... | collective-permute-start | bytes 393224 | tf_op jit(solution)/shard_map/ppermute | solution.py:299
  89.5 13.2 %collective-permute-start.13 = (bf16[4,64,256]{2,1,0:T(8,128)(2,1)S(1)}, bf16[4,64,256]{2,1,0:T(8,128)(2,1)S(1)}, u32[]{:S(2)}, u32[]{:S(2)}) collective-permute-start(bf16[4,64,256]{2,1,0:T(8,128)(2,1)S(1)} %get-tuple-element.44), channel_id=1, source_target_pairs={{0,12},{4,0},{8,4},{12,8},{1,13},{5,1},{9,5},{13,9},{2,14},{6,2},{... | collective-permute-start | bytes 393224 | tf_op jit(solution)/shard_map/ppermute | solution.py:299
  102.9 7.8 %collective-permute-start.14 = (bf16[1216,256]{1,0:T(8,128)(2,1)S(1)}, bf16[1216,256]{1,0:T(8,128)(2,1)S(1)}, u32[]{:S(2)}, u32[]{:S(2)}) collective-permute-start(bf16[1216,256]{1,0:T(8,128)(2,1)S(1)} %pad_maximum_fusion), channel_id=1, source_target_pairs={{0,16},{16,0},{1,17},{17,1},{2,18},{18,2},{3,19},{19,3},{4,20},{20... | collective-permute-start | bytes 1867784 | tf_op jit(solution)/shard_map/ppermute | solution.py:256

commit v17 on v15

--- a/solution.py
+++ b/solution.py
@@ -253,6 +253,15 @@
     return (a.astype(F32) + b.astype(F32)).astype(BF)
 
 
+def beside_ring(x, step):
+    pairs = []
+    for core in range(2):
+        for zh in range(N):
+            up = (zh + step + core) % 2 == 0
+            pairs.append((zh * 2 + core, (zh + (1 if up else -1)) % N * 2 + core))
+    return lax.ppermute(x, ("zh", "core"), pairs)
+
+
 def body(query_proj, key_proj, value_proj, pair_bias, attn_output, output_grad):
     q, k, v, o, g = (
         jnp.swapaxes(x, 1, 2)
@@ -286,10 +295,10 @@
 
     spread = lax.all_to_all(total, ("x", "rj"), 0, 0, tiled=True)
     total = jnp.sum(spread.reshape(N, N, 64, ROWS).astype(F32), axis=0).astype(BF)
-    other = swap(total, "zh", [(0, 1), (2, 3)])
+    other = beside_ring(total, 0)
     parts = spread_out(hand_on(split_kernel, total, dkv), "rj")
     total = add(total, other)
-    other = swap(total, "zh", [(1, 2), (3, 0)])
+    other = beside_ring(total, 1)
     parts = spread_out(hand_on(choose_kernel, total, *parts), "ri")
     total = add(total, other)
     mine = lax.all_gather(total, "x", axis=0, tiled=True).reshape(-1, ROWS)

time: 107 us -> 107 us (level)
  starting transfers between devices: 59.2 us -> 63.6 us
  waiting for transfers between devices: 8.26 us -> 5.09 us
  blocking collectives: 30 us -> 28.8 us
    ppermute x0 -> x2, starting transfers between devices: none -> 17.1 us  [beside_ring(): return lax.ppermute(x, ('zh', 'core'), pairs)]
    ppermute x5 -> x3, starting transfers between devices: 33.1 us -> 20.4 us  [swap(): lax.ppermute(x, axis, [(a, b) for a, b in pairs] + [(b, a) for a, b in pa...]
    ppermute x5 -> x3, waiting for transfers between devices: 4.09 us -> 0.91 us  [swap(): lax.ppermute(x, axis, [(a, b) for a, b in pairs] + [(b, a) for a, b in pa...]
    all_gather x1, blocking collectives: 11.4 us -> 10.2 us  [body(): mine = lax.all_gather(total, 'x', axis=0, tiled=True).reshape(-1, ROWS)]
  transfers between devices with their start and end apart: 14 -> 14, of which waited for: 6 -> 5; matrix products, arithmetic and copies ran while one was open for 1% -> 1% of each run, Pallas kernels for 1% -> 1%
where the time goes in v17:
time: 107 us; the launch traced here: 106 us
  starting transfers between devices  63.6 us (59%)
  blocking collectives  28.8 us (27%)
  Pallas kernels  5.66 us (5%)
  waiting for transfers between devices  5.09 us (5%)
  other arithmetic  1.28 us (1%)
    ppermute x3, starting transfers between devices, swap(): lax.ppermute(x, axis, [(a, b) for a, b in pairs] + [(b, a) for a, b in pa...  20.4 us
    all_to_all x1, blocking collectives, body(): spread = lax.all_to_all(total, ('x', 'rj'), 0, 0, tiled=True)  18.7 us
    ppermute x6, starting transfers between devices, spread_out(): lax.ppermute(parts[t], axis, [(a, (a + t) % N) for a in range(N)])  18 us
    ppermute x2, starting transfers between devices, beside_ring(): return lax.ppermute(x, ('zh', 'core'), pairs)  17.1 us
    all_gather x1, blocking collectives, body(): mine = lax.all_gather(total, 'x', axis=0, tiled=True).reshape(-1, ROWS)  10.2 us
    all_to_all x1, starting transfers between devices, body(): bias = lax.all_to_all(bias, 'rj', 0, 0, tiled=True)  4.19 us
    ppermute x2, starting transfers between devices, body(): spread.append(lax.ppermute(kv, ('core', 'ri', 'rj'), steps))  3.89 us
    pallas_call x1, Pallas kernels, attention(): pl.pallas_call(attention_kernel, out_shape=(jax.ShapeDtypeStruct((N * N,...  3.36 us
  transfers between devices with their start and end apart: 14, of which 5 were waited for; matrix products, arithmetic and copies ran while one was open for 1% of the time, Pallas kernels for 1%

profile of v17, /device:TPU:1, one launch (start us, length us, event | category | flops | bytes accessed | tf_op | source)
XLA Modules:
  0.0 106.2 jit_solution(5630509777911279054)
XLA Ops:
  0.6 0.0 copy-start
  0.7 1.0 pad_maximum_fusion.2
  1.6 8.8 %collective-permute-start = (bf16[2,128,256]{2,1,0:T(8,128)(2,1)S(1)}, bf16[2,128,256]{2,1,0:T(8,128)(2,1)S(1)}, u32[]{:S(2)}, u32[]{:S(2)}) collective-permute-start(bf16[2,128,256]{2,1,0:T(8,128)(2,1)S(1)} %pad_maximum_fusion.2), channel_id=1, source_target_pairs={{0,16},{16,0},{1,17},{17,1},{2,18},{18,2},{3,19},{19,3},{4,20},{20... | collective-permute-start | bytes 393224 | tf_op jit(solution)/shard_map/ppermute | solution.py:249
  10.5 0.0 copy-start.1
  10.5 0.0 copy-start.2
  10.5 0.8 dynamic-slice_bitcast_fusion
  11.3 0.1 collective-permute-done
  11.4 1.9 %collective-permute-start.2 = (bf16[4,128,256]{2,1,0:T(8,128)(2,1)S(1)}, bf16[4,128,256]{2,1,0:T(8,128)(2,1)S(1)}, u32[]{:S(2)}, u32[]{:S(2)}) collective-permute-start(bf16[4,128,256]{2,1,0:T(8,128)(2,1)S(1)} %pad_maximum_fusion.1), channel_id=1, source_target_pairs={{0,4},{1,8},{2,12},{3,0},{4,9},{5,13},{6,1},{7,5},{8,14},{9,2},{10... | collective-permute-start | bytes 786440 | tf_op jit(solution)/shard_map/ppermute | solution.py:284
  13.4 2.0 %collective-permute-start.1 = (bf16[4,128,256]{2,1,0:T(8,128)(2,1)S(1)}, bf16[4,128,256]{2,1,0:T(8,128)(2,1)S(1)}, u32[]{:S(2)}, u32[]{:S(2)}) collective-permute-start(bf16[4,128,256]{2,1,0:T(8,128)(2,1)S(1)} %pad_maximum_fusion.1), channel_id=1, source_target_pairs={{0,0},{1,4},{2,8},{3,12},{4,5},{5,9},{6,13},{7,1},{8,10},{9,14},{1... | collective-permute-start | bytes 786440 | tf_op jit(solution)/shard_map/ppermute | solution.py:284
  15.3 4.2 %all-to-all-start = ((bf16[4,256,256]{2,1,0:T(8,128)(2,1)}), bf16[4,256,256]{2,1,0:T(8,128)(2,1)S(1)}, u32[]{:S(2)}, u32[]{:S(2)}) async-start(bf16[4,256,256]{2,1,0:T(8,128)(2,1)} %dynamic-slice_bitcast_fusion), calls=%async_computation | async-start | bytes 1048576 | tf_op jit(solution)/shard_map/all_to_all | solution.py:285
  19.5 3.1 %collective-permute-done.1.first = bf16[4,128,256]{2,1,0:T(8,128)(2,1)S(1)} collective-permute-done((bf16[4,128,256]{2,1,0:T(8,128)(2,1)S(1)}, bf16[4,128,256]{2,1,0:T(8,128)(2,1)S(1)}, u32[]{:S(2)}, u32[]{:S(2)}) %collective-permute-start.1) | collective-permute-done | bytes 262176 | tf_op jit(solution)/shard_map/ppermute | solution.py:284
  22.7 3.4 %collective-permute-start.3 = (bf16[704,256]{1,0:T(8,128)(2,1)S(1)}, bf16[704,256]{1,0:T(8,128)(2,1)S(1)}, u32[]{:S(2)}, u32[]{:S(2)}) collective-permute-start(bf16[704,256]{1,0:T(8,128)(2,1)S(1)} %shard_map.93), channel_id=1, source_target_pairs={{0,16},{16,0},{1,17},{17,1},{2,18},{18,2},{3,19},{19,3},{4,20},{20... | collective-permute-start | bytes 1081352 | tf_op jit(solution)/shard_map/ppermute | solution.py:249
  26.1 1.1 %all-to-all-done.bias = bf16[4,256,256]{2,1,0:T(8,128)(2,1)S(1)} async-done(((bf16[4,256,256]{2,1,0:T(8,128)(2,1)}), bf16[4,256,256]{2,1,0:T(8,128)(2,1)S(1)}, u32[]{:S(2)}, u32[]{:S(2)}) %all-to-all-start) | async-done | bytes 524320 | tf_op jit(solution)/shard_map/all_to_all | solution.py:285
  27.1 0.2 collective-permute-done.3.given
  27.3 3.4 %shard_map.94 = (bf16[16,64,256]{2,1,0:T(8,128)(2,1)S(1)}, bf16[4,32,256]{2,1,0:T(8,128)(2,1)S(1)}, bf16[4,4,64,256]{3,2,1,0:T(8,128)(2,1)S(1)}) custom-call(bf16[2,64,256]{2,1,0:T(8,128)(2,1)S(1)} %bitcast.20, bf16[2,64,256]{2,1,0:T(8,128)(2,1)S(1)} %bitcast.22, bf16[2,64,256]{2,1,0:T(8,128)(2,1)S(1)} %bitcast.24, ...), custom_call_target="tpu_custom_call" | custom-call | flops 335544320 | bytes 6291456 | tf_op jit(solution)/shard_map/pallas_call | solution.py:133
  30.7 18.7 %all_to_all.10 = bf16[16,64,256]{2,1,0:T(8,128)(2,1)S(1)} all-to-all(bf16[16,64,256]{2,1,0:T(8,128)(2,1)S(1)} %get-tuple-element.23), channel_id=1, replica_groups=mesh['zh'=4,'x'=4,'core'=2,'ri'=4,'rj'=4] {'x','rj'}, dimensions={0} | all-to-all | bytes 1048576 | tf_op jit(solution)/shard_map/all_to_all | solution.py:296
  49.4 0.1 reduce_sum.12.after
  49.4 11.9 %collective-permute-start.4 = (bf16[4,64,256]{2,1,0:T(8,128)(2,1)S(1)}, bf16[4,64,256]{2,1,0:T(8,128)(2,1)S(1)}, u32[]{:S(2)}, u32[]{:S(2)}) collective-permute-start(bf16[4,64,256]{2,1,0:T(8,128)(2,1)S(1)} %reduce_sum.12.after), channel_id=1, source_target_pairs={{0,128},{128,0},{256,384},{384,256},{16,400},{144,272},{272,144},{... | collective-permute-start | bytes 393224 | tf_op jit(solution)/shard_map/ppermute | solution.py:262
  61.4 2.3 %collective-permute-start.6 = (bf16[4,64,256]{2,1,0:T(8,128)(2,1)S(1)}, bf16[4,64,256]{2,1,0:T(8,128)(2,1)S(1)}, u32[]{:S(2)}, u32[]{:S(2)}) collective-permute-start(bf16[4,64,256]{2,1,0:T(8,128)(2,1)S(1)} %get-tuple-element.26), channel_id=1, source_target_pairs={{0,1},{1,2},{2,3},{3,0},{4,5},{5,6},{6,7},{7,4},{8,9},{9,10},{10,1... | collective-permute-start | bytes 393224 | tf_op jit(solution)/shard_map/ppermute | solution.py:292
  63.8 3.6 %collective-permute-start.7 = (bf16[4,64,256]{2,1,0:T(8,128)(2,1)S(1)}, bf16[4,64,256]{2,1,0:T(8,128)(2,1)S(1)}, u32[]{:S(2)}, u32[]{:S(2)}) collective-permute-start(bf16[4,64,256]{2,1,0:T(8,128)(2,1)S(1)} %get-tuple-element.27), channel_id=1, source_target_pairs={{0,2},{1,3},{2,0},{3,1},{4,6},{5,7},{6,4},{7,5},{8,10},{9,11},{10,... | collective-permute-start | bytes 393224 | tf_op jit(solution)/shard_map/ppermute | solution.py:292
  67.4 3.1 %collective-permute-start.8 = (bf16[4,64,256]{2,1,0:T(8,128)(2,1)S(1)}, bf16[4,64,256]{2,1,0:T(8,128)(2,1)S(1)}, u32[]{:S(2)}, u32[]{:S(2)}) collective-permute-start(bf16[4,64,256]{2,1,0:T(8,128)(2,1)S(1)} %get-tuple-element.28), channel_id=1, source_target_pairs={{0,3},{1,0},{2,1},{3,2},{4,7},{5,4},{6,5},{7,6},{8,11},{9,8},{10,9... | collective-permute-start | bytes 393224 | tf_op jit(solution)/shard_map/ppermute | solution.py:292
  70.5 5.2 %collective-permute-start.5 = (bf16[4,64,256]{2,1,0:T(8,128)(2,1)S(1)}, bf16[4,64,256]{2,1,0:T(8,128)(2,1)S(1)}, u32[]{:S(2)}, u32[]{:S(2)}) collective-permute-start(bf16[4,64,256]{2,1,0:T(8,128)(2,1)S(1)} %add_convert_fusion.2.after), channel_id=1, source_target_pairs={{0,384},{128,256},{256,128},{384,0},{16,144},{144,16},{272,400},{4... | collective-permute-start | bytes 393224 | tf_op jit(solution)/shard_map/ppermute | solution.py:262
  75.8 0.1 shard_map.96
  75.9 2.4 %collective-permute-start.9 = (bf16[4,64,256]{2,1,0:T(8,128)(2,1)S(1)}, bf16[4,64,256]{2,1,0:T(8,128)(2,1)S(1)}, u32[]{:S(2)}, u32[]{:S(2)}) collective-permute-start(bf16[4,64,256]{2,1,0:T(8,128)(2,1)S(1)} %get-tuple-element.30), channel_id=1, source_target_pairs={{0,4},{4,8},{8,12},{12,0},{1,5},{5,9},{9,13},{13,1},{2,6},{6,10},{... | collective-permute-start | bytes 393224 | tf_op jit(solution)/shard_map/ppermute | solution.py:292
  78.3 2.6 %collective-permute-start.10 = (bf16[4,64,256]{2,1,0:T(8,128)(2,1)S(1)}, bf16[4,64,256]{2,1,0:T(8,128)(2,1)S(1)}, u32[]{:S(2)}, u32[]{:S(2)}) collective-permute-start(bf16[4,64,256]{2,1,0:T(8,128)(2,1)S(1)} %get-tuple-element.31), channel_id=1, source_target_pairs={{0,8},{4,12},{8,0},{12,4},{1,9},{5,13},{9,1},{13,5},{2,10},{6,14},... | collective-permute-start | bytes 393224 | tf_op jit(solution)/shard_map/ppermute | solution.py:292
  80.8 4.1 %collective-permute-start.11 = (bf16[4,64,256]{2,1,0:T(8,128)(2,1)S(1)}, bf16[4,64,256]{2,1,0:T(8,128)(2,1)S(1)}, u32[]{:S(2)}, u32[]{:S(2)}) collective-permute-start(bf16[4,64,256]{2,1,0:T(8,128)(2,1)S(1)} %get-tuple-element.32), channel_id=1, source_target_pairs={{0,12},{4,0},{8,4},{12,8},{1,13},{5,1},{9,5},{13,9},{2,14},{6,2},{... | collective-permute-start | bytes 393224 | tf_op jit(solution)/shard_map/ppermute | solution.py:292
  85.0 10.2 %all_gather.3 = bf16[16,64,256]{2,1,0:T(8,128)(2,1)S(1)} all-gather(bf16[4,64,256]{2,1,0:T(8,128)(2,1)S(1)} %add_convert_fusion.1), channel_id=1, replica_groups=mesh['zh'=4,'x'=4,'core'=2,'ri'=4,'rj'=4] {'x'}, dimensions={0}, use_global_device_ids=true | all-gather | bytes 655360 | tf_op jit(solution)/shard_map/all_gather | solution.py:304
  95.2 0.1 add_convert_fusion
  95.3 8.2 %collective-permute-start.12 = (bf16[1216,256]{1,0:T(8,128)(2,1)S(1)}, bf16[1216,256]{1,0:T(8,128)(2,1)S(1)}, u32[]{:S(2)}, u32[]{:S(2)}) collective-permute-start(bf16[1216,256]{1,0:T(8,128)(2,1)S(1)} %pad_maximum_fusion), channel_id=1, source_target_pairs={{0,16},{16,0},{1,17},{17,1},{2,18},{18,2},{3,19},{19,3},{4,20},{20... | collective-permute-start | bytes 1867784 | tf_op jit(solution)/shard_map/ppermute | solution.py:249
  103.5 1.0 shard_map.97.before
  104.5 0.6 collective-permute-done.12.x_ref
  105.1 1.1 %shard_map.98 = (f32[8,256,256]{2,1,0:T(8,128)}, bf16[2,64,256]{2,1,0:T(8,128)(2,1)}, bf16[2,64,256]{2,1,0:T(8,128)(2,1)}, bf16[2,64,256]{2,1,0:T(8,128)(2,1)}) custom-call(bf16[1216,256]{1,0:T(8,128)(2,1)S(1)} %collective-permute-done.12.x_ref, bf16[2,96,256]{2,1,0:T(8,128)(2,1)S(1)} %get-tuple-element.38.own_ref, ...), custom_call_target="tpu_custom_call", output_to_operand_aliasing={{0}: (2, {})} | custom-call | flops 262144 | bytes 2097152 | tf_op jit(solution)/shard_map/pallas_call | solution.py:232
  (25 shorter events, 0.3 us)
Async XLA Ops:
  0.6 9.8 %copy-start = (bf16[8,256,256]{2,1,0:T(8,128)(2,1)S(1)}, bf16[8,256,256]{2,1,0:T(8,128)(2,1)}, u32[]{:S(2)}) copy-start(bf16[8,256,256]{2,1,0:T(8,128)(2,1)} %param.9) | copy-start | bytes 3145732
  0.6 10.8 %copy-start.4 = (bf16[2,256,64]{1,2,0:T(8,128)(2,1)S(1)}, bf16[2,256,64]{1,2,0:T(8,128)(2,1)}, u32[]{:S(2)}) copy-start(bf16[2,256,64]{1,2,0:T(8,128)(2,1)} %param.8) | copy-start | bytes 196612
  0.7 10.8 %copy-start.5 = (bf16[2,256,64]{1,2,0:T(8,128)(2,1)S(1)}, bf16[2,256,64]{1,2,0:T(8,128)(2,1)}, u32[]{:S(2)}) copy-start(bf16[2,256,64]{1,2,0:T(8,128)(2,1)} %param.7) | copy-start | bytes 196612
  1.6 9.8 %collective-permute-start = (bf16[2,128,256]{2,1,0:T(8,128)(2,1)S(1)}, bf16[2,128,256]{2,1,0:T(8,128)(2,1)S(1)}, u32[]{:S(2)}, u32[]{:S(2)}) collective-permute-start(bf16[2,128,256]{2,1,0:T(8,128)(2,1)S(1)} %pad_maximum_fusion.2), channel_id=1, source_target_pairs={{0,16},{16,0},{1,17},{17,1},{2,18},{18,2},{3,19},{19,3},{4,20},{20... | collective-permute-start | bytes 393224 | tf_op jit(solution)/shard_map/ppermute | solution.py:249
  10.5 12.1 %copy-start.1 = (bf16[2,256,64]{1,2,0:T(8,128)(2,1)S(1)}, bf16[2,256,64]{1,2,0:T(8,128)(2,1)}, u32[]{:S(2)}) copy-start(bf16[2,256,64]{1,2,0:T(8,128)(2,1)} %param.6) | copy-start | bytes 196612
  10.5 12.1 %copy-start.2 = (bf16[2,256,64]{1,2,0:T(8,128)(2,1)S(1)}, bf16[2,256,64]{1,2,0:T(8,128)(2,1)}, u32[]{:S(2)}) copy-start(bf16[2,256,64]{1,2,0:T(8,128)(2,1)} %param.11) | copy-start | bytes 196612
  10.5 12.1 %copy-start.3 = (bf16[2,256,64]{1,2,0:T(8,128)(2,1)S(1)}, bf16[2,256,64]{1,2,0:T(8,128)(2,1)}, u32[]{:S(2)}) copy-start(bf16[2,256,64]{1,2,0:T(8,128)(2,1)} %param.10) | copy-start | bytes 196612
  11.4 8.1 %collective-permute-start.2 = (bf16[4,128,256]{2,1,0:T(8,128)(2,1)S(1)}, bf16[4,128,256]{2,1,0:T(8,128)(2,1)S(1)}, u32[]{:S(2)}, u32[]{:S(2)}) collective-permute-start(bf16[4,128,256]{2,1,0:T(8,128)(2,1)S(1)} %pad_maximum_fusion.1), channel_id=1, source_target_pairs={{0,4},{1,8},{2,12},{3,0},{4,9},{5,13},{6,1},{7,5},{8,14},{9,2},{10... | collective-permute-start | bytes 786440 | tf_op jit(solution)/shard_map/ppermute | solution.py:284
  13.4 9.2 %collective-permute-start.1 = (bf16[4,128,256]{2,1,0:T(8,128)(2,1)S(1)}, bf16[4,128,256]{2,1,0:T(8,128)(2,1)S(1)}, u32[]{:S(2)}, u32[]{:S(2)}) collective-permute-start(bf16[4,128,256]{2,1,0:T(8,128)(2,1)S(1)} %pad_maximum_fusion.1), channel_id=1, source_target_pairs={{0,0},{1,4},{2,8},{3,12},{4,5},{5,9},{6,13},{7,1},{8,10},{9,14},{1... | collective-permute-start | bytes 786440 | tf_op jit(solution)/shard_map/ppermute | solution.py:284
  15.3 11.8 %all-to-all-start = ((bf16[4,256,256]{2,1,0:T(8,128)(2,1)}), bf16[4,256,256]{2,1,0:T(8,128)(2,1)S(1)}, u32[]{:S(2)}, u32[]{:S(2)}) async-start(bf16[4,256,256]{2,1,0:T(8,128)(2,1)} %dynamic-slice_bitcast_fusion), calls=%async_computation | async-start | bytes 1048576 | tf_op jit(solution)/shard_map/all_to_all | solution.py:285
  22.7 4.7 %collective-permute-start.3 = (bf16[704,256]{1,0:T(8,128)(2,1)S(1)}, bf16[704,256]{1,0:T(8,128)(2,1)S(1)}, u32[]{:S(2)}, u32[]{:S(2)}) collective-permute-start(bf16[704,256]{1,0:T(8,128)(2,1)S(1)} %shard_map.93), channel_id=1, source_target_pairs={{0,16},{16,0},{1,17},{17,1},{2,18},{18,2},{3,19},{19,3},{4,20},{20... | collective-permute-start | bytes 1081352 | tf_op jit(solution)/shard_map/ppermute | solution.py:249
  49.4 21.0 %collective-permute-start.4 = (bf16[4,64,256]{2,1,0:T(8,128)(2,1)S(1)}, bf16[4,64,256]{2,1,0:T(8,128)(2,1)S(1)}, u32[]{:S(2)}, u32[]{:S(2)}) collective-permute-start(bf16[4,64,256]{2,1,0:T(8,128)(2,1)S(1)} %reduce_sum.12.after), channel_id=1, source_target_pairs={{0,128},{128,0},{256,384},{384,256},{16,400},{144,272},{272,144},{... | collective-permute-start | bytes 393224 | tf_op jit(solution)/shard_map/ppermute | solution.py:262
  61.4 14.3 %collective-permute-start.6 = (bf16[4,64,256]{2,1,0:T(8,128)(2,1)S(1)}, bf16[4,64,256]{2,1,0:T(8,128)(2,1)S(1)}, u32[]{:S(2)}, u32[]{:S(2)}) collective-permute-start(bf16[4,64,256]{2,1,0:T(8,128)(2,1)S(1)} %get-tuple-element.26), channel_id=1, source_target_pairs={{0,1},{1,2},{2,3},{3,0},{4,5},{5,6},{6,7},{7,4},{8,9},{9,10},{10,1... | collective-permute-start | bytes 393224 | tf_op jit(solution)/shard_map/ppermute | solution.py:292
  63.8 12.0 %collective-permute-start.7 = (bf16[4,64,256]{2,1,0:T(8,128)(2,1)S(1)}, bf16[4,64,256]{2,1,0:T(8,128)(2,1)S(1)}, u32[]{:S(2)}, u32[]{:S(2)}) collective-permute-start(bf16[4,64,256]{2,1,0:T(8,128)(2,1)S(1)} %get-tuple-element.27), channel_id=1, source_target_pairs={{0,2},{1,3},{2,0},{3,1},{4,6},{5,7},{6,4},{7,5},{8,10},{9,11},{10,... | collective-permute-start | bytes 393224 | tf_op jit(solution)/shard_map/ppermute | solution.py:292
  67.4 8.4 %collective-permute-start.8 = (bf16[4,64,256]{2,1,0:T(8,128)(2,1)S(1)}, bf16[4,64,256]{2,1,0:T(8,128)(2,1)S(1)}, u32[]{:S(2)}, u32[]{:S(2)}) collective-permute-start(bf16[4,64,256]{2,1,0:T(8,128)(2,1)S(1)} %get-tuple-element.28), channel_id=1, source_target_pairs={{0,3},{1,0},{2,1},{3,2},{4,7},{5,4},{6,5},{7,6},{8,11},{9,8},{10,9... | collective-permute-start | bytes 393224 | tf_op jit(solution)/shard_map/ppermute | solution.py:292
  70.5 14.4 %collective-permute-start.5 = (bf16[4,64,256]{2,1,0:T(8,128)(2,1)S(1)}, bf16[4,64,256]{2,1,0:T(8,128)(2,1)S(1)}, u32[]{:S(2)}, u32[]{:S(2)}) collective-permute-start(bf16[4,64,256]{2,1,0:T(8,128)(2,1)S(1)} %add_convert_fusion.2.after), channel_id=1, source_target_pairs={{0,384},{128,256},{256,128},{384,0},{16,144},{144,16},{272,400},{4... | collective-permute-start | bytes 393224 | tf_op jit(solution)/shard_map/ppermute | solution.py:262
  75.9 19.3 %collective-permute-start.9 = (bf16[4,64,256]{2,1,0:T(8,128)(2,1)S(1)}, bf16[4,64,256]{2,1,0:T(8,128)(2,1)S(1)}, u32[]{:S(2)}, u32[]{:S(2)}) collective-permute-start(bf16[4,64,256]{2,1,0:T(8,128)(2,1)S(1)} %get-tuple-element.30), channel_id=1, source_target_pairs={{0,4},{4,8},{8,12},{12,0},{1,5},{5,9},{9,13},{13,1},{2,6},{6,10},{... | collective-permute-start | bytes 393224 | tf_op jit(solution)/shard_map/ppermute | solution.py:292
  78.3 16.9 %collective-permute-start.10 = (bf16[4,64,256]{2,1,0:T(8,128)(2,1)S(1)}, bf16[4,64,256]{2,1,0:T(8,128)(2,1)S(1)}, u32[]{:S(2)}, u32[]{:S(2)}) collective-permute-start(bf16[4,64,256]{2,1,0:T(8,128)(2,1)S(1)} %get-tuple-element.31), channel_id=1, source_target_pairs={{0,8},{4,12},{8,0},{12,4},{1,9},{5,13},{9,1},{13,5},{2,10},{6,14},... | collective-permute-start | bytes 393224 | tf_op jit(solution)/shard_map/ppermute | solution.py:292
  80.8 14.3 %collective-permute-start.11 = (bf16[4,64,256]{2,1,0:T(8,128)(2,1)S(1)}, bf16[4,64,256]{2,1,0:T(8,128)(2,1)S(1)}, u32[]{:S(2)}, u32[]{:S(2)}) collective-permute-start(bf16[4,64,256]{2,1,0:T(8,128)(2,1)S(1)} %get-tuple-element.32), channel_id=1, source_target_pairs={{0,12},{4,0},{8,4},{12,8},{1,13},{5,1},{9,5},{13,9},{2,14},{6,2},{... | collective-permute-start | bytes 393224 | tf_op jit(solution)/shard_map/ppermute | solution.py:292
  95.3 9.8 %collective-permute-start.12 = (bf16[1216,256]{1,0:T(8,128)(2,1)S(1)}, bf16[1216,256]{1,0:T(8,128)(2,1)S(1)}, u32[]{:S(2)}, u32[]{:S(2)}) collective-permute-start(bf16[1216,256]{1,0:T(8,128)(2,1)S(1)} %pad_maximum_fusion), channel_id=1, source_target_pairs={{0,16},{16,0},{1,17},{17,1},{2,18},{18,2},{3,19},{19,3},{4,20},{20... | collective-permute-start | bytes 1867784 | tf_op jit(solution)/shard_map/ppermute | solution.py:249

commit v18 on v17

--- a/solution.py
+++ b/solution.py
@@ -257,7 +257,7 @@
     pairs = []
     for core in range(2):
         for zh in range(N):
-            up = (zh + step + core) % 2 == 0
+            up = (zh + step + core) % 2 == 1
             pairs.append((zh * 2 + core, (zh + (1 if up else -1)) % N * 2 + core))
     return lax.ppermute(x, ("zh", "core"), pairs)
 

time: 107 us -> 107 us (level)
  no operation moved by 1% of the time
where the time goes in v18:
time: 107 us; the launch traced here: 106 us
  starting transfers between devices  63.4 us (59%)
  blocking collectives  29 us (27%)
  Pallas kernels  5.66 us (5%)
  waiting for transfers between devices  5.09 us (5%)
  other arithmetic  1.28 us (1%)
    ppermute x3, starting transfers between devices, swap(): lax.ppermute(x, axis, [(a, b) for a, b in pairs] + [(b, a) for a, b in pa...  20.2 us
    all_to_all x1, blocking collectives, body(): spread = lax.all_to_all(total, ('x', 'rj'), 0, 0, tiled=True)  18.7 us
    ppermute x6, starting transfers between devices, spread_out(): lax.ppermute(parts[t], axis, [(a, (a + t) % N) for a in range(N)])  18 us
    ppermute x2, starting transfers between devices, beside_ring(): return lax.ppermute(x, ('zh', 'core'), pairs)  17.2 us
    all_gather x1, blocking collectives, body(): mine = lax.all_gather(total, 'x', axis=0, tiled=True).reshape(-1, ROWS)  10.3 us
    all_to_all x1, starting transfers between devices, body(): bias = lax.all_to_all(bias, 'rj', 0, 0, tiled=True)  4.19 us
    ppermute x2, starting transfers between devices, body(): spread.append(lax.ppermute(kv, ('core', 'ri', 'rj'), steps))  3.89 us
    pallas_call x1, Pallas kernels, attention(): pl.pallas_call(attention_kernel, out_shape=(jax.ShapeDtypeStruct((N * N,...  3.36 us
  transfers between devices with their start and end apart: 14, of which 5 were waited for; matrix products, arithmetic and copies ran while one was open for 1% of the time, Pallas kernels for 1%

profile of v18, /device:TPU:1, one launch (start us, length us, event | category | flops | bytes accessed | tf_op | source)
XLA Modules:
  0.0 106.2 jit_solution(13991665038867746103)
XLA Ops:
  0.6 0.0 copy-start
  0.7 1.0 pad_maximum_fusion.2
  1.6 8.8 %collective-permute-start = (bf16[2,128,256]{2,1,0:T(8,128)(2,1)S(1)}, bf16[2,128,256]{2,1,0:T(8,128)(2,1)S(1)}, u32[]{:S(2)}, u32[]{:S(2)}) collective-permute-start(bf16[2,128,256]{2,1,0:T(8,128)(2,1)S(1)} %pad_maximum_fusion.2), channel_id=1, source_target_pairs={{0,16},{16,0},{1,17},{17,1},{2,18},{18,2},{3,19},{19,3},{4,20},{20... | collective-permute-start | bytes 393224 | tf_op jit(solution)/shard_map/ppermute | solution.py:249
  10.5 0.0 copy-start.1
  10.5 0.0 copy-start.2
  10.5 0.8 dynamic-slice_bitcast_fusion
  11.3 0.1 collective-permute-done
  11.4 1.9 %collective-permute-start.2 = (bf16[4,128,256]{2,1,0:T(8,128)(2,1)S(1)}, bf16[4,128,256]{2,1,0:T(8,128)(2,1)S(1)}, u32[]{:S(2)}, u32[]{:S(2)}) collective-permute-start(bf16[4,128,256]{2,1,0:T(8,128)(2,1)S(1)} %pad_maximum_fusion.1), channel_id=1, source_target_pairs={{0,4},{1,8},{2,12},{3,0},{4,9},{5,13},{6,1},{7,5},{8,14},{9,2},{10... | collective-permute-start | bytes 786440 | tf_op jit(solution)/shard_map/ppermute | solution.py:284
  13.4 2.0 %collective-permute-start.1 = (bf16[4,128,256]{2,1,0:T(8,128)(2,1)S(1)}, bf16[4,128,256]{2,1,0:T(8,128)(2,1)S(1)}, u32[]{:S(2)}, u32[]{:S(2)}) collective-permute-start(bf16[4,128,256]{2,1,0:T(8,128)(2,1)S(1)} %pad_maximum_fusion.1), channel_id=1, source_target_pairs={{0,0},{1,4},{2,8},{3,12},{4,5},{5,9},{6,13},{7,1},{8,10},{9,14},{1... | collective-permute-start | bytes 786440 | tf_op jit(solution)/shard_map/ppermute | solution.py:284
  15.3 4.2 %all-to-all-start = ((bf16[4,256,256]{2,1,0:T(8,128)(2,1)}), bf16[4,256,256]{2,1,0:T(8,128)(2,1)S(1)}, u32[]{:S(2)}, u32[]{:S(2)}) async-start(bf16[4,256,256]{2,1,0:T(8,128)(2,1)} %dynamic-slice_bitcast_fusion), calls=%async_computation | async-start | bytes 1048576 | tf_op jit(solution)/shard_map/all_to_all | solution.py:285
  19.5 3.1 %collective-permute-done.1.first = bf16[4,128,256]{2,1,0:T(8,128)(2,1)S(1)} collective-permute-done((bf16[4,128,256]{2,1,0:T(8,128)(2,1)S(1)}, bf16[4,128,256]{2,1,0:T(8,128)(2,1)S(1)}, u32[]{:S(2)}, u32[]{:S(2)}) %collective-permute-start.1) | collective-permute-done | bytes 262176 | tf_op jit(solution)/shard_map/ppermute | solution.py:284
  22.7 3.4 %collective-permute-start.3 = (bf16[704,256]{1,0:T(8,128)(2,1)S(1)}, bf16[704,256]{1,0:T(8,128)(2,1)S(1)}, u32[]{:S(2)}, u32[]{:S(2)}) collective-permute-start(bf16[704,256]{1,0:T(8,128)(2,1)S(1)} %shard_map.93), channel_id=1, source_target_pairs={{0,16},{16,0},{1,17},{17,1},{2,18},{18,2},{3,19},{19,3},{4,20},{20... | collective-permute-start | bytes 1081352 | tf_op jit(solution)/shard_map/ppermute | solution.py:249
  26.1 1.1 %all-to-all-done.bias = bf16[4,256,256]{2,1,0:T(8,128)(2,1)S(1)} async-done(((bf16[4,256,256]{2,1,0:T(8,128)(2,1)}), bf16[4,256,256]{2,1,0:T(8,128)(2,1)S(1)}, u32[]{:S(2)}, u32[]{:S(2)}) %all-to-all-start) | async-done | bytes 524320 | tf_op jit(solution)/shard_map/all_to_all | solution.py:285
  27.1 0.2 collective-permute-done.3.given
  27.3 3.4 %shard_map.94 = (bf16[16,64,256]{2,1,0:T(8,128)(2,1)S(1)}, bf16[4,32,256]{2,1,0:T(8,128)(2,1)S(1)}, bf16[4,4,64,256]{3,2,1,0:T(8,128)(2,1)S(1)}) custom-call(bf16[2,64,256]{2,1,0:T(8,128)(2,1)S(1)} %bitcast.20, bf16[2,64,256]{2,1,0:T(8,128)(2,1)S(1)} %bitcast.22, bf16[2,64,256]{2,1,0:T(8,128)(2,1)S(1)} %bitcast.24, ...), custom_call_target="tpu_custom_call" | custom-call | flops 335544320 | bytes 6291456 | tf_op jit(solution)/shard_map/pallas_call | solution.py:133
  30.7 18.7 %all_to_all.10 = bf16[16,64,256]{2,1,0:T(8,128)(2,1)S(1)} all-to-all(bf16[16,64,256]{2,1,0:T(8,128)(2,1)S(1)} %get-tuple-element.23), channel_id=1, replica_groups=mesh['zh'=4,'x'=4,'core'=2,'ri'=4,'rj'=4] {'x','rj'}, dimensions={0} | all-to-all | bytes 1048576 | tf_op jit(solution)/shard_map/all_to_all | solution.py:296
  49.4 0.1 reduce_sum.12.after
  49.4 8.8 %collective-permute-start.4 = (bf16[4,64,256]{2,1,0:T(8,128)(2,1)S(1)}, bf16[4,64,256]{2,1,0:T(8,128)(2,1)S(1)}, u32[]{:S(2)}, u32[]{:S(2)}) collective-permute-start(bf16[4,64,256]{2,1,0:T(8,128)(2,1)S(1)} %reduce_sum.12.after), channel_id=1, source_target_pairs={{0,384},{128,256},{256,128},{384,0},{16,144},{144,16},{272,400},{4... | collective-permute-start | bytes 393224 | tf_op jit(solution)/shard_map/ppermute | solution.py:262
  58.3 2.4 %collective-permute-start.6 = (bf16[4,64,256]{2,1,0:T(8,128)(2,1)S(1)}, bf16[4,64,256]{2,1,0:T(8,128)(2,1)S(1)}, u32[]{:S(2)}, u32[]{:S(2)}) collective-permute-start(bf16[4,64,256]{2,1,0:T(8,128)(2,1)S(1)} %get-tuple-element.26), channel_id=1, source_target_pairs={{0,1},{1,2},{2,3},{3,0},{4,5},{5,6},{6,7},{7,4},{8,9},{9,10},{10,1... | collective-permute-start | bytes 393224 | tf_op jit(solution)/shard_map/ppermute | solution.py:292
  60.7 3.3 %collective-permute-start.7 = (bf16[4,64,256]{2,1,0:T(8,128)(2,1)S(1)}, bf16[4,64,256]{2,1,0:T(8,128)(2,1)S(1)}, u32[]{:S(2)}, u32[]{:S(2)}) collective-permute-start(bf16[4,64,256]{2,1,0:T(8,128)(2,1)S(1)} %get-tuple-element.27), channel_id=1, source_target_pairs={{0,2},{1,3},{2,0},{3,1},{4,6},{5,7},{6,4},{7,5},{8,10},{9,11},{10,... | collective-permute-start | bytes 393224 | tf_op jit(solution)/shard_map/ppermute | solution.py:292
  64.1 3.2 %collective-permute-start.8 = (bf16[4,64,256]{2,1,0:T(8,128)(2,1)S(1)}, bf16[4,64,256]{2,1,0:T(8,128)(2,1)S(1)}, u32[]{:S(2)}, u32[]{:S(2)}) collective-permute-start(bf16[4,64,256]{2,1,0:T(8,128)(2,1)S(1)} %get-tuple-element.28), channel_id=1, source_target_pairs={{0,3},{1,0},{2,1},{3,2},{4,7},{5,4},{6,5},{7,6},{8,11},{9,8},{10,9... | collective-permute-start | bytes 393224 | tf_op jit(solution)/shard_map/ppermute | solution.py:292
  67.4 8.4 %collective-permute-start.5 = (bf16[4,64,256]{2,1,0:T(8,128)(2,1)S(1)}, bf16[4,64,256]{2,1,0:T(8,128)(2,1)S(1)}, u32[]{:S(2)}, u32[]{:S(2)}) collective-permute-start(bf16[4,64,256]{2,1,0:T(8,128)(2,1)S(1)} %add_convert_fusion.2.after), channel_id=1, source_target_pairs={{0,128},{128,0},{256,384},{384,256},{16,400},{144,272},{272,144},{... | collective-permute-start | bytes 393224 | tf_op jit(solution)/shard_map/ppermute | solution.py:262
  75.8 0.1 shard_map.96
  75.9 2.4 %collective-permute-start.9 = (bf16[4,64,256]{2,1,0:T(8,128)(2,1)S(1)}, bf16[4,64,256]{2,1,0:T(8,128)(2,1)S(1)}, u32[]{:S(2)}, u32[]{:S(2)}) collective-permute-start(bf16[4,64,256]{2,1,0:T(8,128)(2,1)S(1)} %get-tuple-element.30), channel_id=1, source_target_pairs={{0,4},{4,8},{8,12},{12,0},{1,5},{5,9},{9,13},{13,1},{2,6},{6,10},{... | collective-permute-start | bytes 393224 | tf_op jit(solution)/shard_map/ppermute | solution.py:292
  78.3 2.6 %collective-permute-start.10 = (bf16[4,64,256]{2,1,0:T(8,128)(2,1)S(1)}, bf16[4,64,256]{2,1,0:T(8,128)(2,1)S(1)}, u32[]{:S(2)}, u32[]{:S(2)}) collective-permute-start(bf16[4,64,256]{2,1,0:T(8,128)(2,1)S(1)} %get-tuple-element.31), channel_id=1, source_target_pairs={{0,8},{4,12},{8,0},{12,4},{1,9},{5,13},{9,1},{13,5},{2,10},{6,14},... | collective-permute-start | bytes 393224 | tf_op jit(solution)/shard_map/ppermute | solution.py:292
  80.8 4.1 %collective-permute-start.11 = (bf16[4,64,256]{2,1,0:T(8,128)(2,1)S(1)}, bf16[4,64,256]{2,1,0:T(8,128)(2,1)S(1)}, u32[]{:S(2)}, u32[]{:S(2)}) collective-permute-start(bf16[4,64,256]{2,1,0:T(8,128)(2,1)S(1)} %get-tuple-element.32), channel_id=1, source_target_pairs={{0,12},{4,0},{8,4},{12,8},{1,13},{5,1},{9,5},{13,9},{2,14},{6,2},{... | collective-permute-start | bytes 393224 | tf_op jit(solution)/shard_map/ppermute | solution.py:292
  85.0 10.3 %all_gather.3 = bf16[16,64,256]{2,1,0:T(8,128)(2,1)S(1)} all-gather(bf16[4,64,256]{2,1,0:T(8,128)(2,1)S(1)} %add_convert_fusion.1), channel_id=1, replica_groups=mesh['zh'=4,'x'=4,'core'=2,'ri'=4,'rj'=4] {'x'}, dimensions={0}, use_global_device_ids=true | all-gather | bytes 655360 | tf_op jit(solution)/shard_map/all_gather | solution.py:304
  95.3 0.1 add_convert_fusion
  95.5 8.0 %collective-permute-start.12 = (bf16[1216,256]{1,0:T(8,128)(2,1)S(1)}, bf16[1216,256]{1,0:T(8,128)(2,1)S(1)}, u32[]{:S(2)}, u32[]{:S(2)}) collective-permute-start(bf16[1216,256]{1,0:T(8,128)(2,1)S(1)} %pad_maximum_fusion), channel_id=1, source_target_pairs={{0,16},{16,0},{1,17},{17,1},{2,18},{18,2},{3,19},{19,3},{4,20},{20... | collective-permute-start | bytes 1867784 | tf_op jit(solution)/shard_map/ppermute | solution.py:249
  103.5 1.0 shard_map.97.before
  104.5 0.6 collective-permute-done.12.x_ref
  105.1 1.1 %shard_map.98 = (f32[8,256,256]{2,1,0:T(8,128)}, bf16[2,64,256]{2,1,0:T(8,128)(2,1)}, bf16[2,64,256]{2,1,0:T(8,128)(2,1)}, bf16[2,64,256]{2,1,0:T(8,128)(2,1)}) custom-call(bf16[1216,256]{1,0:T(8,128)(2,1)S(1)} %collective-permute-done.12.x_ref, bf16[2,96,256]{2,1,0:T(8,128)(2,1)S(1)} %get-tuple-element.38.own_ref, ...), custom_call_target="tpu_custom_call", output_to_operand_aliasing={{0}: (2, {})} | custom-call | flops 262144 | bytes 2097152 | tf_op jit(solution)/shard_map/pallas_call | solution.py:232
  (25 shorter events, 0.3 us)
Async XLA Ops:
  0.6 9.8 %copy-start = (bf16[8,256,256]{2,1,0:T(8,128)(2,1)S(1)}, bf16[8,256,256]{2,1,0:T(8,128)(2,1)}, u32[]{:S(2)}) copy-start(bf16[8,256,256]{2,1,0:T(8,128)(2,1)} %param.9) | copy-start | bytes 3145732
  0.6 10.8 %copy-start.4 = (bf16[2,256,64]{1,2,0:T(8,128)(2,1)S(1)}, bf16[2,256,64]{1,2,0:T(8,128)(2,1)}, u32[]{:S(2)}) copy-start(bf16[2,256,64]{1,2,0:T(8,128)(2,1)} %param.8) | copy-start | bytes 196612
  0.7 10.8 %copy-start.5 = (bf16[2,256,64]{1,2,0:T(8,128)(2,1)S(1)}, bf16[2,256,64]{1,2,0:T(8,128)(2,1)}, u32[]{:S(2)}) copy-start(bf16[2,256,64]{1,2,0:T(8,128)(2,1)} %param.7) | copy-start | bytes 196612
  1.6 9.8 %collective-permute-start = (bf16[2,128,256]{2,1,0:T(8,128)(2,1)S(1)}, bf16[2,128,256]{2,1,0:T(8,128)(2,1)S(1)}, u32[]{:S(2)}, u32[]{:S(2)}) collective-permute-start(bf16[2,128,256]{2,1,0:T(8,128)(2,1)S(1)} %pad_maximum_fusion.2), channel_id=1, source_target_pairs={{0,16},{16,0},{1,17},{17,1},{2,18},{18,2},{3,19},{19,3},{4,20},{20... | collective-permute-start | bytes 393224 | tf_op jit(solution)/shard_map/ppermute | solution.py:249
  10.5 12.1 %copy-start.1 = (bf16[2,256,64]{1,2,0:T(8,128)(2,1)S(1)}, bf16[2,256,64]{1,2,0:T(8,128)(2,1)}, u32[]{:S(2)}) copy-start(bf16[2,256,64]{1,2,0:T(8,128)(2,1)} %param.6) | copy-start | bytes 196612
  10.5 12.1 %copy-start.2 = (bf16[2,256,64]{1,2,0:T(8,128)(2,1)S(1)}, bf16[2,256,64]{1,2,0:T(8,128)(2,1)}, u32[]{:S(2)}) copy-start(bf16[2,256,64]{1,2,0:T(8,128)(2,1)} %param.11) | copy-start | bytes 196612
  10.5 12.1 %copy-start.3 = (bf16[2,256,64]{1,2,0:T(8,128)(2,1)S(1)}, bf16[2,256,64]{1,2,0:T(8,128)(2,1)}, u32[]{:S(2)}) copy-start(bf16[2,256,64]{1,2,0:T(8,128)(2,1)} %param.10) | copy-start | bytes 196612
  11.4 8.1 %collective-permute-start.2 = (bf16[4,128,256]{2,1,0:T(8,128)(2,1)S(1)}, bf16[4,128,256]{2,1,0:T(8,128)(2,1)S(1)}, u32[]{:S(2)}, u32[]{:S(2)}) collective-permute-start(bf16[4,128,256]{2,1,0:T(8,128)(2,1)S(1)} %pad_maximum_fusion.1), channel_id=1, source_target_pairs={{0,4},{1,8},{2,12},{3,0},{4,9},{5,13},{6,1},{7,5},{8,14},{9,2},{10... | collective-permute-start | bytes 786440 | tf_op jit(solution)/shard_map/ppermute | solution.py:284
  13.4 9.2 %collective-permute-start.1 = (bf16[4,128,256]{2,1,0:T(8,128)(2,1)S(1)}, bf16[4,128,256]{2,1,0:T(8,128)(2,1)S(1)}, u32[]{:S(2)}, u32[]{:S(2)}) collective-permute-start(bf16[4,128,256]{2,1,0:T(8,128)(2,1)S(1)} %pad_maximum_fusion.1), channel_id=1, source_target_pairs={{0,0},{1,4},{2,8},{3,12},{4,5},{5,9},{6,13},{7,1},{8,10},{9,14},{1... | collective-permute-start | bytes 786440 | tf_op jit(solution)/shard_map/ppermute | solution.py:284
  15.3 11.8 %all-to-all-start = ((bf16[4,256,256]{2,1,0:T(8,128)(2,1)}), bf16[4,256,256]{2,1,0:T(8,128)(2,1)S(1)}, u32[]{:S(2)}, u32[]{:S(2)}) async-start(bf16[4,256,256]{2,1,0:T(8,128)(2,1)} %dynamic-slice_bitcast_fusion), calls=%async_computation | async-start | bytes 1048576 | tf_op jit(solution)/shard_map/all_to_all | solution.py:285
  22.7 4.7 %collective-permute-start.3 = (bf16[704,256]{1,0:T(8,128)(2,1)S(1)}, bf16[704,256]{1,0:T(8,128)(2,1)S(1)}, u32[]{:S(2)}, u32[]{:S(2)}) collective-permute-start(bf16[704,256]{1,0:T(8,128)(2,1)S(1)} %shard_map.93), channel_id=1, source_target_pairs={{0,16},{16,0},{1,17},{17,1},{2,18},{18,2},{3,19},{19,3},{4,20},{20... | collective-permute-start | bytes 1081352 | tf_op jit(solution)/shard_map/ppermute | solution.py:249
  49.4 17.9 %collective-permute-start.4 = (bf16[4,64,256]{2,1,0:T(8,128)(2,1)S(1)}, bf16[4,64,256]{2,1,0:T(8,128)(2,1)S(1)}, u32[]{:S(2)}, u32[]{:S(2)}) collective-permute-start(bf16[4,64,256]{2,1,0:T(8,128)(2,1)S(1)} %reduce_sum.12.after), channel_id=1, source_target_pairs={{0,384},{128,256},{256,128},{384,0},{16,144},{144,16},{272,400},{4... | collective-permute-start | bytes 393224 | tf_op jit(solution)/shard_map/ppermute | solution.py:262
  58.3 17.4 %collective-permute-start.6 = (bf16[4,64,256]{2,1,0:T(8,128)(2,1)S(1)}, bf16[4,64,256]{2,1,0:T(8,128)(2,1)S(1)}, u32[]{:S(2)}, u32[]{:S(2)}) collective-permute-start(bf16[4,64,256]{2,1,0:T(8,128)(2,1)S(1)} %get-tuple-element.26), channel_id=1, source_target_pairs={{0,1},{1,2},{2,3},{3,0},{4,5},{5,6},{6,7},{7,4},{8,9},{9,10},{10,1... | collective-permute-start | bytes 393224 | tf_op jit(solution)/shard_map/ppermute | solution.py:292
  60.7 15.0 %collective-permute-start.7 = (bf16[4,64,256]{2,1,0:T(8,128)(2,1)S(1)}, bf16[4,64,256]{2,1,0:T(8,128)(2,1)S(1)}, u32[]{:S(2)}, u32[]{:S(2)}) collective-permute-start(bf16[4,64,256]{2,1,0:T(8,128)(2,1)S(1)} %get-tuple-element.27), channel_id=1, source_target_pairs={{0,2},{1,3},{2,0},{3,1},{4,6},{5,7},{6,4},{7,5},{8,10},{9,11},{10,... | collective-permute-start | bytes 393224 | tf_op jit(solution)/shard_map/ppermute | solution.py:292
  64.1 11.7 %collective-permute-start.8 = (bf16[4,64,256]{2,1,0:T(8,128)(2,1)S(1)}, bf16[4,64,256]{2,1,0:T(8,128)(2,1)S(1)}, u32[]{:S(2)}, u32[]{:S(2)}) collective-permute-start(bf16[4,64,256]{2,1,0:T(8,128)(2,1)S(1)} %get-tuple-element.28), channel_id=1, source_target_pairs={{0,3},{1,0},{2,1},{3,2},{4,7},{5,4},{6,5},{7,6},{8,11},{9,8},{10,9... | collective-permute-start | bytes 393224 | tf_op jit(solution)/shard_map/ppermute | solution.py:292
  67.4 17.6 %collective-permute-start.5 = (bf16[4,64,256]{2,1,0:T(8,128)(2,1)S(1)}, bf16[4,64,256]{2,1,0:T(8,128)(2,1)S(1)}, u32[]{:S(2)}, u32[]{:S(2)}) collective-permute-start(bf16[4,64,256]{2,1,0:T(8,128)(2,1)S(1)} %add_convert_fusion.2.after), channel_id=1, source_target_pairs={{0,128},{128,0},{256,384},{384,256},{16,400},{144,272},{272,144},{... | collective-permute-start | bytes 393224 | tf_op jit(solution)/shard_map/ppermute | solution.py:262
  75.9 19.4 %collective-permute-start.9 = (bf16[4,64,256]{2,1,0:T(8,128)(2,1)S(1)}, bf16[4,64,256]{2,1,0:T(8,128)(2,1)S(1)}, u32[]{:S(2)}, u32[]{:S(2)}) collective-permute-start(bf16[4,64,256]{2,1,0:T(8,128)(2,1)S(1)} %get-tuple-element.30), channel_id=1, source_target_pairs={{0,4},{4,8},{8,12},{12,0},{1,5},{5,9},{9,13},{13,1},{2,6},{6,10},{... | collective-permute-start | bytes 393224 | tf_op jit(solution)/shard_map/ppermute | solution.py:292
  78.3 17.0 %collective-permute-start.10 = (bf16[4,64,256]{2,1,0:T(8,128)(2,1)S(1)}, bf16[4,64,256]{2,1,0:T(8,128)(2,1)S(1)}, u32[]{:S(2)}, u32[]{:S(2)}) collective-permute-start(bf16[4,64,256]{2,1,0:T(8,128)(2,1)S(1)} %get-tuple-element.31), channel_id=1, source_target_pairs={{0,8},{4,12},{8,0},{12,4},{1,9},{5,13},{9,1},{13,5},{2,10},{6,14},... | collective-permute-start | bytes 393224 | tf_op jit(solution)/shard_map/ppermute | solution.py:292
  80.8 14.5 %collective-permute-start.11 = (bf16[4,64,256]{2,1,0:T(8,128)(2,1)S(1)}, bf16[4,64,256]{2,1,0:T(8,128)(2,1)S(1)}, u32[]{:S(2)}, u32[]{:S(2)}) collective-permute-start(bf16[4,64,256]{2,1,0:T(8,128)(2,1)S(1)} %get-tuple-element.32), channel_id=1, source_target_pairs={{0,12},{4,0},{8,4},{12,8},{1,13},{5,1},{9,5},{13,9},{2,14},{6,2},{... | collective-permute-start | bytes 393224 | tf_op jit(solution)/shard_map/ppermute | solution.py:292
  95.5 9.7 %collective-permute-start.12 = (bf16[1216,256]{1,0:T(8,128)(2,1)S(1)}, bf16[1216,256]{1,0:T(8,128)(2,1)S(1)}, u32[]{:S(2)}, u32[]{:S(2)}) collective-permute-start(bf16[1216,256]{1,0:T(8,128)(2,1)S(1)} %pad_maximum_fusion), channel_id=1, source_target_pairs={{0,16},{16,0},{1,17},{17,1},{2,18},{18,2},{3,19},{19,3},{4,20},{20... | collective-permute-start | bytes 1867784 | tf_op jit(solution)/shard_map/ppermute | solution.py:249

commit v19 on v17

--- a/solution.py
+++ b/solution.py
@@ -121,7 +121,7 @@
             at = slice(t * ROWS, (t + 1) * ROWS)
             grads = lax.dot_general(wide[s], low[s, :, at], NN, preferred_element_type=F32)
             grads = jnp.where(channel == 0, grads * SCALE, grads)
-            dkv_ref[lax.rem(b + N - rj, N), s] = grads.astype(BF)
+            dkv_ref[b, s] = grads.astype(BF)
             key = key_side(0, t, s)
             term = lax.dot_general(low[s, :ROWS, at], key, NT, preferred_element_type=F32)
             query_grads = term if query_grads is None else query_grads + term
@@ -153,34 +153,6 @@
     )(*args)
 
 
-def split_kernel(after, x_ref, *outs):
-    for t, out in enumerate(outs):
-        out[...] = x_ref[t]
-
-
-def choose_kernel(after, *refs):
-    ri, rj = lax.axis_index("ri"), lax.axis_index("rj")
-    for t, out in enumerate(refs[N:]):
-        wanted = lax.rem(rj + 2 * N - ri - t, N)
-        for source, x_ref in enumerate(refs[:N]):
-
-            @pl.when(wanted == source)
-            def _():
-                out[...] = x_ref[...]
-
-
-def hand_on(kernel, after, *args):
-    anywhere, vmem = pl.BlockSpec(memory_space=pl.ANY), pl.BlockSpec(memory_space=pltpu.VMEM)
-    return pl.pallas_call(
-        kernel,
-        out_shape=[jax.ShapeDtypeStruct(args[0].shape[-3:], BF)] * N,
-        in_specs=[anywhere] + [vmem] * len(args),
-        out_specs=[vmem] * N,
-        compiler_params=pltpu.CompilerParams(vmem_limit_bytes=8 * 2**20),
-        cost_estimate=pl.CostEstimate(flops=0, bytes_accessed=2**21, transcendentals=0),
-    )(after, *args)
-
-
 def place_heads(x_ref, out_ref, wide, sem, head):
     copies = []
     for j in range(N):
@@ -287,24 +259,17 @@
 
     total, dq, dkv = attention(q, g, o, *spread, given, bias)
 
-    def spread_out(parts, axis):
-        return [parts[0]] + [
-            lax.ppermute(parts[t], axis, [(a, (a + t) % N) for a in range(N)])
-            for t in range(1, N)
-        ]
-
     spread = lax.all_to_all(total, ("x", "rj"), 0, 0, tiled=True)
+    back = lax.psum_scatter(dkv.reshape(-1, ROWS), "ri", scatter_dimension=0, tiled=True)
     total = jnp.sum(spread.reshape(N, N, 64, ROWS).astype(F32), axis=0).astype(BF)
-    other = beside_ring(total, 0)
-    parts = spread_out(hand_on(split_kernel, total, dkv), "rj")
-    total = add(total, other)
-    other = beside_ring(total, 1)
-    parts = spread_out(hand_on(choose_kernel, total, *parts), "ri")
-    total = add(total, other)
-    mine = lax.all_gather(total, "x", axis=0, tiled=True).reshape(-1, ROWS)
-
-    dkv = sum(x.astype(F32) for x in parts).astype(BF)
-    grads = jnp.concatenate([dkv, dq], axis=1)
+    total = add(total, beside_ring(total, 0))
+    total = add(total, beside_ring(total, 1))
+    total, back = lax.optimization_barrier((total, back))
+    back = lax.ppermute(back, ("ri", "rj"), [(a * N + b, b * N + a) for a, b in grid])
+    mine, back = lax.optimization_barrier((lax.all_gather(total, "x", axis=0, tiled=True), back))
+    mine = mine.reshape(-1, ROWS)
+
+    grads = jnp.concatenate([back.reshape(dkv.shape[1:]), dq], axis=1)
     own, others = grads[: SEQS // 2], grads[SEQS // 2 :]
     theirs = swap(jnp.concatenate([mine, others.reshape(-1, ROWS)]), "core", [(0, 1)])
     bias_grad, dk, dv, dq = finish(theirs, own, place(mine))

time: 107 us -> 122 us (1.14)
  the two profiles are of different devices: /device:TPU:1 before, /device:TPU:17 now
where the time goes in v19:
time: 122 us
  starting transfers between devices  56.5 us (46%)
  waiting for transfers between devices  32.3 us (26%)
  between operations  14.2 us (12%)
  blocking collectives  10.2 us (8%)
  Pallas kernels  6.29 us (5%)
    ppermute x2, starting transfers between devices, beside_ring(): return lax.ppermute(x, ('zh', 'core'), pairs)  18 us
    ppermute x3, starting transfers between devices, swap(): lax.ppermute(x, axis, [(a, b) for a, b in pairs] + [(b, a) for a, b in pa...  15.3 us
    ppermute x2, waiting for transfers between devices, beside_ring(): return lax.ppermute(x, ('zh', 'core'), pairs)  11.7 us
    all_gather x1, blocking collectives, body(): lax.all_gather(total, 'x', axis=0, tiled=True)  10.2 us
    ppermute x2, starting transfers between devices, body(): spread.append(lax.ppermute(kv, ('core', 'ri', 'rj'), steps))  9.26 us
    all_to_all x1, waiting for transfers between devices, body(): spread = lax.all_to_all(total, ('x', 'rj'), 0, 0, tiled=True)  7.88 us
    all_to_all x1, starting transfers between devices, body(): spread = lax.all_to_all(total, ('x', 'rj'), 0, 0, tiled=True)  6.71 us
    ppermute x2, waiting for transfers between devices, body(): spread.append(lax.ppermute(kv, ('core', 'ri', 'rj'), steps))  5.93 us
  transfers between devices with their start and end apart: 11, of which 9 were waited for; matrix products, arithmetic and copies ran while one was open for 1% of the time, Pallas kernels for 1%

profile of v19, /device:TPU:17, one launch (start us, length us, event | category | flops | bytes accessed | tf_op | source)
XLA Modules:
  0.0 121.6 jit_solution(3955797491797543875)
XLA Ops:
  7.2 0.0 copy-start
  7.2 1.0 pad_maximum_fusion.2
  8.2 2.6 %collective-permute-start = (bf16[2,128,256]{2,1,0:T(8,128)(2,1)S(1)}, bf16[2,128,256]{2,1,0:T(8,128)(2,1)S(1)}, u32[]{:S(2)}, u32[]{:S(2)}) collective-permute-start(bf16[2,128,256]{2,1,0:T(8,128)(2,1)S(1)} %pad_maximum_fusion.2), channel_id=1, source_target_pairs={{0,16},{16,0},{1,17},{17,1},{2,18},{18,2},{3,19},{19,3},{4,20},{20... | collective-permute-start | bytes 393224 | tf_op jit(solution)/shard_map/ppermute | solution.py:221
  10.8 0.0 copy-start.1
  10.8 0.0 copy-start.2
  10.8 0.0 copy-start.3
  10.8 0.8 dynamic-slice_bitcast_fusion
  11.7 0.1 collective-permute-done
  11.8 3.3 %collective-permute-start.2 = (bf16[4,128,256]{2,1,0:T(8,128)(2,1)S(1)}, bf16[4,128,256]{2,1,0:T(8,128)(2,1)S(1)}, u32[]{:S(2)}, u32[]{:S(2)}) collective-permute-start(bf16[4,128,256]{2,1,0:T(8,128)(2,1)S(1)} %pad_maximum_fusion.1), channel_id=1, source_target_pairs={{0,4},{1,8},{2,12},{3,0},{4,9},{5,13},{6,1},{7,5},{8,14},{9,2},{10... | collective-permute-start | bytes 786440 | tf_op jit(solution)/shard_map/ppermute | solution.py:256
  15.1 5.9 %collective-permute-start.1 = (bf16[4,128,256]{2,1,0:T(8,128)(2,1)S(1)}, bf16[4,128,256]{2,1,0:T(8,128)(2,1)S(1)}, u32[]{:S(2)}, u32[]{:S(2)}) collective-permute-start(bf16[4,128,256]{2,1,0:T(8,128)(2,1)S(1)} %pad_maximum_fusion.1), channel_id=1, source_target_pairs={{0,0},{1,4},{2,8},{3,12},{4,5},{5,9},{6,13},{7,1},{8,10},{9,14},{1... | collective-permute-start | bytes 786440 | tf_op jit(solution)/shard_map/ppermute | solution.py:256
  21.0 4.2 %all-to-all-start = ((bf16[4,256,256]{2,1,0:T(8,128)(2,1)}), bf16[4,256,256]{2,1,0:T(8,128)(2,1)S(1)}, u32[]{:S(2)}, u32[]{:S(2)}) async-start(bf16[4,256,256]{2,1,0:T(8,128)(2,1)} %dynamic-slice_bitcast_fusion), calls=%async_computation | async-start | bytes 1048576 | tf_op jit(solution)/shard_map/all_to_all | solution.py:257
  25.3 2.0 %collective-permute-done.2.second = bf16[4,128,256]{2,1,0:T(8,128)(2,1)S(1)} collective-permute-done((bf16[4,128,256]{2,1,0:T(8,128)(2,1)S(1)}, bf16[4,128,256]{2,1,0:T(8,128)(2,1)S(1)}, u32[]{:S(2)}, u32[]{:S(2)}) %collective-permute-start.2) | collective-permute-done | bytes 262176 | tf_op jit(solution)/shard_map/ppermute | solution.py:256
  27.3 3.9 %collective-permute-done.1.first = bf16[4,128,256]{2,1,0:T(8,128)(2,1)S(1)} collective-permute-done((bf16[4,128,256]{2,1,0:T(8,128)(2,1)S(1)}, bf16[4,128,256]{2,1,0:T(8,128)(2,1)S(1)}, u32[]{:S(2)}, u32[]{:S(2)}) %collective-permute-start.1) | collective-permute-done | bytes 262176 | tf_op jit(solution)/shard_map/ppermute | solution.py:256
  31.3 1.9 %collective-permute-start.3 = (bf16[704,256]{1,0:T(8,128)(2,1)S(1)}, bf16[704,256]{1,0:T(8,128)(2,1)S(1)}, u32[]{:S(2)}, u32[]{:S(2)}) collective-permute-start(bf16[704,256]{1,0:T(8,128)(2,1)S(1)} %shard_map.93), channel_id=1, source_target_pairs={{0,16},{16,0},{1,17},{17,1},{2,18},{18,2},{3,19},{19,3},{4,20},{20... | collective-permute-start | bytes 1081352 | tf_op jit(solution)/shard_map/ppermute | solution.py:221
  33.2 1.6 %collective-permute-done.3.given = bf16[704,256]{1,0:T(8,128)(2,1)S(1)} collective-permute-done((bf16[704,256]{1,0:T(8,128)(2,1)S(1)}, bf16[704,256]{1,0:T(8,128)(2,1)S(1)}, u32[]{:S(2)}, u32[]{:S(2)}) %collective-permute-start.3) | collective-permute-done | bytes 360480 | tf_op jit(solution)/shard_map/ppermute | solution.py:221
  34.8 4.1 %shard_map.94 = (bf16[16,64,256]{2,1,0:T(8,128)(2,1)}, bf16[4,32,256]{2,1,0:T(8,128)(2,1)S(1)}, bf16[4,4,64,256]{3,2,1,0:T(8,128)(2,1)}) custom-call(bf16[2,64,256]{2,1,0:T(8,128)(2,1)S(1)} %bitcast.22, bf16[2,64,256]{2,1,0:T(8,128)(2,1)S(1)} %bitcast.24, bf16[2,64,256]{2,1,0:T(8,128)(2,1)S(1)} %bitcast.26, ...), custom_call_target="tpu_custom_call" | custom-call | flops 335544320 | bytes 6291456 | tf_op jit(solution)/shard_map/pallas_call | solution.py:133
  39.0 6.7 %all-to-all-start.1 = ((bf16[16,64,256]{2,1,0:T(8,128)(2,1)}), bf16[16,64,256]{2,1,0:T(8,128)(2,1)S(1)}, u32[]{:S(2)}, u32[]{:S(2)}) async-start(bf16[16,64,256]{2,1,0:T(8,128)(2,1)} %get-tuple-element.19), calls=%async_computation.1 | async-start | bytes 1048576 | tf_op jit(solution)/shard_map/all_to_all | solution.py:262
  45.7 0.0 reduce-scatter.2.cloned.1.call-start
  45.7 0.7 reduce-scatter.2.cloned.1.call-update
  46.4 7.9 %all-to-all-done.1 = bf16[16,64,256]{2,1,0:T(8,128)(2,1)S(1)} async-done(((bf16[16,64,256]{2,1,0:T(8,128)(2,1)}), bf16[16,64,256]{2,1,0:T(8,128)(2,1)S(1)}, u32[]{:S(2)}, u32[]{:S(2)}) %all-to-all-start.1) | async-done | bytes 524320 | tf_op jit(solution)/shard_map/all_to_all | solution.py:262
  54.3 0.1 reduce_sum.12
  54.4 12.0 %collective-permute-start.4 = (bf16[4,64,256]{2,1,0:T(8,128)(2,1)S(1)}, bf16[4,64,256]{2,1,0:T(8,128)(2,1)S(1)}, u32[]{:S(2)}, u32[]{:S(2)}) collective-permute-start(bf16[4,64,256]{2,1,0:T(8,128)(2,1)S(1)} %reduce_sum.12), channel_id=1, source_target_pairs={{0,128},{128,0},{256,384},{384,256},{16,400},{144,272},{272,144},{... | collective-permute-start | bytes 393224 | tf_op jit(solution)/shard_map/ppermute | solution.py:234
  66.4 4.9 %collective-permute-done.4 = bf16[4,64,256]{2,1,0:T(8,128)(2,1)S(1)} collective-permute-done((bf16[4,64,256]{2,1,0:T(8,128)(2,1)S(1)}, bf16[4,64,256]{2,1,0:T(8,128)(2,1)S(1)}, u32[]{:S(2)}, u32[]{:S(2)}) %collective-permute-start.4) | collective-permute-done | bytes 131104 | tf_op jit(solution)/shard_map/ppermute | solution.py:234
  71.3 6.0 %collective-permute-start.5 = (bf16[4,64,256]{2,1,0:T(8,128)(2,1)S(1)}, bf16[4,64,256]{2,1,0:T(8,128)(2,1)S(1)}, u32[]{:S(2)}, u32[]{:S(2)}) collective-permute-start(bf16[4,64,256]{2,1,0:T(8,128)(2,1)S(1)} %add_convert_fusion.1), channel_id=1, source_target_pairs={{0,384},{128,256},{256,128},{384,0},{16,144},{144,16},{272,400},{4... | collective-permute-start | bytes 393224 | tf_op jit(solution)/shard_map/ppermute | solution.py:234
  77.4 6.8 %collective-permute-done.5 = bf16[4,64,256]{2,1,0:T(8,128)(2,1)S(1)} collective-permute-done((bf16[4,64,256]{2,1,0:T(8,128)(2,1)S(1)}, bf16[4,64,256]{2,1,0:T(8,128)(2,1)S(1)}, u32[]{:S(2)}, u32[]{:S(2)}) %collective-permute-start.5) | collective-permute-done | bytes 131104 | tf_op jit(solution)/shard_map/ppermute | solution.py:234
  84.2 3.8 %reduce-scatter.2.cloned.1.call-done = bf16[256,256]{1,0:T(8,128)(2,1)} async-done(((bf16[1024,256]{1,0:T(8,128)(2,1)}), bf16[256,256]{1,0:T(8,128)(2,1)}) %reduce-scatter.2.cloned.1.call-update) | async-done | bytes 131088 | tf_op jit(solution)/shard_map/reduce_scatter | solution.py:263
  88.0 2.8 %collective-permute-start.6 = (bf16[256,256]{1,0:T(8,128)(2,1)}, bf16[256,256]{1,0:T(8,128)(2,1)S(1)}, u32[]{:S(2)}, u32[]{:S(2)}) collective-permute-start(bf16[256,256]{1,0:T(8,128)(2,1)} %reduce-scatter.2.cloned.1.call-done), channel_id=1, source_target_pairs={{0,0},{1,4},{2,8},{3,12},{4,1},{5,5},{6,9},{7,13},{8,2},{9,6},{10,... | collective-permute-start | bytes 393224 | tf_op jit(solution)/shard_map/ppermute | solution.py:268
  90.9 10.2 %all_gather.3 = bf16[16,64,256]{2,1,0:T(8,128)(2,1)S(1)} all-gather(bf16[4,64,256]{2,1,0:T(8,128)(2,1)S(1)} %add_convert_fusion), channel_id=1, replica_groups=mesh['zh'=4,'x'=4,'core'=2,'ri'=4,'rj'=4] {'x'}, dimensions={0}, use_global_device_ids=true | all-gather | bytes 655360 | tf_op jit(solution)/shard_map/all_gather | solution.py:269
  101.1 10.8 %collective-permute-start.7 = (bf16[1216,256]{1,0:T(8,128)(2,1)S(1)}, bf16[1216,256]{1,0:T(8,128)(2,1)S(1)}, u32[]{:S(2)}, u32[]{:S(2)}) collective-permute-start(bf16[1216,256]{1,0:T(8,128)(2,1)S(1)} %pad_maximum_fusion), channel_id=1, source_target_pairs={{0,16},{16,0},{1,17},{17,1},{2,18},{18,2},{3,19},{19,3},{4,20},{20... | collective-permute-start | bytes 1867784 | tf_op jit(solution)/shard_map/ppermute | solution.py:221
  112.0 1.0 shard_map.95.before
  113.0 0.6 collective-permute-done.7.x_ref
  113.6 1.1 shard_map.96
  (16 shorter events, 0.2 us)
Async XLA Ops:
  7.2 3.6 %copy-start = (bf16[8,256,256]{2,1,0:T(8,128)(2,1)S(1)}, bf16[8,256,256]{2,1,0:T(8,128)(2,1)}, u32[]{:S(2)}) copy-start(bf16[8,256,256]{2,1,0:T(8,128)(2,1)} %param.9) | copy-start | bytes 3145732
  7.2 4.6 %copy-start.4 = (bf16[2,256,64]{1,2,0:T(8,128)(2,1)S(1)}, bf16[2,256,64]{1,2,0:T(8,128)(2,1)}, u32[]{:S(2)}) copy-start(bf16[2,256,64]{1,2,0:T(8,128)(2,1)} %param.8) | copy-start | bytes 196612
  7.2 4.5 %copy-start.5 = (bf16[2,256,64]{1,2,0:T(8,128)(2,1)S(1)}, bf16[2,256,64]{1,2,0:T(8,128)(2,1)}, u32[]{:S(2)}) copy-start(bf16[2,256,64]{1,2,0:T(8,128)(2,1)} %param.7) | copy-start | bytes 196612
  8.2 3.6 %collective-permute-start = (bf16[2,128,256]{2,1,0:T(8,128)(2,1)S(1)}, bf16[2,128,256]{2,1,0:T(8,128)(2,1)S(1)}, u32[]{:S(2)}, u32[]{:S(2)}) collective-permute-start(bf16[2,128,256]{2,1,0:T(8,128)(2,1)S(1)} %pad_maximum_fusion.2), channel_id=1, source_target_pairs={{0,16},{16,0},{1,17},{17,1},{2,18},{18,2},{3,19},{19,3},{4,20},{20... | collective-permute-start | bytes 393224 | tf_op jit(solution)/shard_map/ppermute | solution.py:221
  10.8 20.4 %copy-start.1 = (bf16[2,256,64]{1,2,0:T(8,128)(2,1)S(1)}, bf16[2,256,64]{1,2,0:T(8,128)(2,1)}, u32[]{:S(2)}) copy-start(bf16[2,256,64]{1,2,0:T(8,128)(2,1)} %param.6) | copy-start | bytes 196612
  10.8 20.4 %copy-start.2 = (bf16[2,256,64]{1,2,0:T(8,128)(2,1)S(1)}, bf16[2,256,64]{1,2,0:T(8,128)(2,1)}, u32[]{:S(2)}) copy-start(bf16[2,256,64]{1,2,0:T(8,128)(2,1)} %param.11) | copy-start | bytes 196612
  10.8 20.4 %copy-start.3 = (bf16[2,256,64]{1,2,0:T(8,128)(2,1)S(1)}, bf16[2,256,64]{1,2,0:T(8,128)(2,1)}, u32[]{:S(2)}) copy-start(bf16[2,256,64]{1,2,0:T(8,128)(2,1)} %param.10) | copy-start | bytes 196612
  11.8 15.6 %collective-permute-start.2 = (bf16[4,128,256]{2,1,0:T(8,128)(2,1)S(1)}, bf16[4,128,256]{2,1,0:T(8,128)(2,1)S(1)}, u32[]{:S(2)}, u32[]{:S(2)}) collective-permute-start(bf16[4,128,256]{2,1,0:T(8,128)(2,1)S(1)} %pad_maximum_fusion.1), channel_id=1, source_target_pairs={{0,4},{1,8},{2,12},{3,0},{4,9},{5,13},{6,1},{7,5},{8,14},{9,2},{10... | collective-permute-start | bytes 786440 | tf_op jit(solution)/shard_map/ppermute | solution.py:256
  15.1 16.1 %collective-permute-start.1 = (bf16[4,128,256]{2,1,0:T(8,128)(2,1)S(1)}, bf16[4,128,256]{2,1,0:T(8,128)(2,1)S(1)}, u32[]{:S(2)}, u32[]{:S(2)}) collective-permute-start(bf16[4,128,256]{2,1,0:T(8,128)(2,1)S(1)} %pad_maximum_fusion.1), channel_id=1, source_target_pairs={{0,0},{1,4},{2,8},{3,12},{4,5},{5,9},{6,13},{7,1},{8,10},{9,14},{1... | collective-permute-start | bytes 786440 | tf_op jit(solution)/shard_map/ppermute | solution.py:256
  21.0 12.2 %all-to-all-start = ((bf16[4,256,256]{2,1,0:T(8,128)(2,1)}), bf16[4,256,256]{2,1,0:T(8,128)(2,1)S(1)}, u32[]{:S(2)}, u32[]{:S(2)}) async-start(bf16[4,256,256]{2,1,0:T(8,128)(2,1)} %dynamic-slice_bitcast_fusion), calls=%async_computation | async-start | bytes 1048576 | tf_op jit(solution)/shard_map/all_to_all | solution.py:257
  31.3 3.6 %collective-permute-start.3 = (bf16[704,256]{1,0:T(8,128)(2,1)S(1)}, bf16[704,256]{1,0:T(8,128)(2,1)S(1)}, u32[]{:S(2)}, u32[]{:S(2)}) collective-permute-start(bf16[704,256]{1,0:T(8,128)(2,1)S(1)} %shard_map.93), channel_id=1, source_target_pairs={{0,16},{16,0},{1,17},{17,1},{2,18},{18,2},{3,19},{19,3},{4,20},{20... | collective-permute-start | bytes 1081352 | tf_op jit(solution)/shard_map/ppermute | solution.py:221
  39.0 15.3 %all-to-all-start.1 = ((bf16[16,64,256]{2,1,0:T(8,128)(2,1)}), bf16[16,64,256]{2,1,0:T(8,128)(2,1)S(1)}, u32[]{:S(2)}, u32[]{:S(2)}) async-start(bf16[16,64,256]{2,1,0:T(8,128)(2,1)} %get-tuple-element.19), calls=%async_computation.1 | async-start | bytes 1048576 | tf_op jit(solution)/shard_map/all_to_all | solution.py:262
  45.7 42.3 %reduce-scatter.2.cloned.1.call-start = ((), (), s32[]{:S(2)}) async-start(), calls=%async_computation.3 | async-start | bytes 655360 | tf_op jit(solution)/shard_map/reduce_scatter | solution.py:263
  54.4 16.9 %collective-permute-start.4 = (bf16[4,64,256]{2,1,0:T(8,128)(2,1)S(1)}, bf16[4,64,256]{2,1,0:T(8,128)(2,1)S(1)}, u32[]{:S(2)}, u32[]{:S(2)}) collective-permute-start(bf16[4,64,256]{2,1,0:T(8,128)(2,1)S(1)} %reduce_sum.12), channel_id=1, source_target_pairs={{0,128},{128,0},{256,384},{384,256},{16,400},{144,272},{272,144},{... | collective-permute-start | bytes 393224 | tf_op jit(solution)/shard_map/ppermute | solution.py:234
  71.3 12.8 %collective-permute-start.5 = (bf16[4,64,256]{2,1,0:T(8,128)(2,1)S(1)}, bf16[4,64,256]{2,1,0:T(8,128)(2,1)S(1)}, u32[]{:S(2)}, u32[]{:S(2)}) collective-permute-start(bf16[4,64,256]{2,1,0:T(8,128)(2,1)S(1)} %add_convert_fusion.1), channel_id=1, source_target_pairs={{0,384},{128,256},{256,128},{384,0},{16,144},{144,16},{272,400},{4... | collective-permute-start | bytes 393224 | tf_op jit(solution)/shard_map/ppermute | solution.py:234
  88.0 13.0 %collective-permute-start.6 = (bf16[256,256]{1,0:T(8,128)(2,1)}, bf16[256,256]{1,0:T(8,128)(2,1)S(1)}, u32[]{:S(2)}, u32[]{:S(2)}) collective-permute-start(bf16[256,256]{1,0:T(8,128)(2,1)} %reduce-scatter.2.cloned.1.call-done), channel_id=1, source_target_pairs={{0,0},{1,4},{2,8},{3,12},{4,1},{5,5},{6,9},{7,13},{8,2},{9,6},{10,... | collective-permute-start | bytes 393224 | tf_op jit(solution)/shard_map/ppermute | solution.py:268
  101.1 12.5 %collective-permute-start.7 = (bf16[1216,256]{1,0:T(8,128)(2,1)S(1)}, bf16[1216,256]{1,0:T(8,128)(2,1)S(1)}, u32[]{:S(2)}, u32[]{:S(2)}) collective-permute-start(bf16[1216,256]{1,0:T(8,128)(2,1)S(1)} %pad_maximum_fusion), channel_id=1, source_target_pairs={{0,16},{16,0},{1,17},{17,1},{2,18},{18,2},{3,19},{19,3},{4,20},{20... | collective-permute-start | bytes 1867784 | tf_op jit(solution)/shard_map/ppermute | solution.py:221
Sparse Core Ops, SparseCore 0:
  49.4 38.6 reduce-scatter.1

commit v20 on v17

--- a/solution.py
+++ b/solution.py
@@ -57,7 +57,7 @@
 ):
     ri, rj, core = (lax.axis_index(a) for a in ("ri", "rj", "core"))
     own = pl.ds(pl.multiple_of(core * HEAD, HEAD), HEAD)
-    rounds = [2 * core, 2 * core + 1, 2 - 2 * core, 3 - 2 * core]
+    rounds = [core, core + 2, 1 - core, 3 - core]
     blocks = [lax.rem(ri + 2 * N - rj - t, N) for t in rounds]
 
     def query_side(i, s):
@@ -279,7 +279,7 @@
         steps = []
         for c in range(2):
             for a, b in grid:
-                target = (a + b + 2 * c + i) % N * N + a
+                target = (a + b + c + 2 * i) % N * N + a
                 steps.append((c * N * N + a * N + b, c * N * N + target))
         spread.append(lax.ppermute(kv, ("core", "ri", "rj"), steps))
     bias = lax.all_to_all(bias, "rj", 0, 0, tiled=True)

time: 107 us -> 108 us (level)
  waiting for transfers between devices: 5.09 us -> 8.76 us
  blocking collectives: 28.8 us -> 27.3 us
  starting transfers between devices: 63.6 us -> 62.5 us
    all_to_all x1, waiting for transfers between devices: 1.09 us -> 4.19 us  [body(): bias = lax.all_to_all(bias, 'rj', 0, 0, tiled=True)]
    all_to_all x1, blocking collectives: 18.7 us -> 17.3 us  [body(): spread = lax.all_to_all(total, ('x', 'rj'), 0, 0, tiled=True)]
    ppermute x3, starting transfers between devices: 20.4 us -> 19 us  [swap(): lax.ppermute(x, axis, [(a, b) for a, b in pairs] + [(b, a) for a, b in pa...]
  transfers between devices with their start and end apart: 14 -> 14, of which waited for: 5 -> 4; matrix products, arithmetic and copies ran while one was open for 1% -> 1% of each run, Pallas kernels for 1% -> 1%
where the time goes in v20:
time: 108 us; the launch traced here: 107 us
  starting transfers between devices  62.5 us (58%)
  blocking collectives  27.3 us (25%)
  waiting for transfers between devices  8.76 us (8%)
  Pallas kernels  5.66 us (5%)
  other arithmetic  1.28 us (1%)
    ppermute x3, starting transfers between devices, swap(): lax.ppermute(x, axis, [(a, b) for a, b in pairs] + [(b, a) for a, b in pa...  19 us
    ppermute x6, starting transfers between devices, spread_out(): lax.ppermute(parts[t], axis, [(a, (a + t) % N) for a in range(N)])  18 us
    all_to_all x1, blocking collectives, body(): spread = lax.all_to_all(total, ('x', 'rj'), 0, 0, tiled=True)  17.3 us
    ppermute x2, starting transfers between devices, beside_ring(): return lax.ppermute(x, ('zh', 'core'), pairs)  16.4 us
    all_gather x1, blocking collectives, body(): mine = lax.all_gather(total, 'x', axis=0, tiled=True).reshape(-1, ROWS)  10 us
    all_to_all x1, starting transfers between devices, body(): bias = lax.all_to_all(bias, 'rj', 0, 0, tiled=True)  5.19 us
    all_to_all x1, waiting for transfers between devices, body(): bias = lax.all_to_all(bias, 'rj', 0, 0, tiled=True)  4.19 us
    ppermute x2, starting transfers between devices, body(): spread.append(lax.ppermute(kv, ('core', 'ri', 'rj'), steps))  3.84 us
  transfers between devices with their start and end apart: 14, of which 4 were waited for; matrix products, arithmetic and copies ran while one was open for 1% of the time, Pallas kernels for 1%

profile of v20, /device:TPU:1, one launch (start us, length us, event | category | flops | bytes accessed | tf_op | source)
XLA Modules:
  0.0 107.3 jit_solution(18048073931764517755)
XLA Ops:
  0.6 0.0 copy-start
  0.7 1.0 pad_maximum_fusion.2
  1.6 8.8 %collective-permute-start = (bf16[2,128,256]{2,1,0:T(8,128)(2,1)S(1)}, bf16[2,128,256]{2,1,0:T(8,128)(2,1)S(1)}, u32[]{:S(2)}, u32[]{:S(2)}) collective-permute-start(bf16[2,128,256]{2,1,0:T(8,128)(2,1)S(1)} %pad_maximum_fusion.2), channel_id=1, source_target_pairs={{0,16},{16,0},{1,17},{17,1},{2,18},{18,2},{3,19},{19,3},{4,20},{20... | collective-permute-start | bytes 393224 | tf_op jit(solution)/shard_map/ppermute | solution.py:249
  10.5 0.0 copy-start.1
  10.5 0.0 copy-start.2
  10.5 0.0 copy-start.3
  10.5 0.8 dynamic-slice_bitcast_fusion
  11.3 0.1 collective-permute-done
  11.4 1.9 %collective-permute-start.2 = (bf16[4,128,256]{2,1,0:T(8,128)(2,1)S(1)}, bf16[4,128,256]{2,1,0:T(8,128)(2,1)S(1)}, u32[]{:S(2)}, u32[]{:S(2)}) collective-permute-start(bf16[4,128,256]{2,1,0:T(8,128)(2,1)S(1)} %pad_maximum_fusion.1), channel_id=1, source_target_pairs={{0,8},{1,12},{2,0},{3,4},{4,13},{5,1},{6,5},{7,9},{8,2},{9,6},{10,... | collective-permute-start | bytes 786440 | tf_op jit(solution)/shard_map/ppermute | solution.py:284
  13.4 1.9 %collective-permute-start.1 = (bf16[4,128,256]{2,1,0:T(8,128)(2,1)S(1)}, bf16[4,128,256]{2,1,0:T(8,128)(2,1)S(1)}, u32[]{:S(2)}, u32[]{:S(2)}) collective-permute-start(bf16[4,128,256]{2,1,0:T(8,128)(2,1)S(1)} %pad_maximum_fusion.1), channel_id=1, source_target_pairs={{0,0},{1,4},{2,8},{3,12},{4,5},{5,9},{6,13},{7,1},{8,10},{9,14},{1... | collective-permute-start | bytes 786440 | tf_op jit(solution)/shard_map/ppermute | solution.py:284
  15.3 5.2 %all-to-all-start = ((bf16[4,256,256]{2,1,0:T(8,128)(2,1)}), bf16[4,256,256]{2,1,0:T(8,128)(2,1)S(1)}, u32[]{:S(2)}, u32[]{:S(2)}) async-start(bf16[4,256,256]{2,1,0:T(8,128)(2,1)} %dynamic-slice_bitcast_fusion), calls=%async_computation | async-start | bytes 1048576 | tf_op jit(solution)/shard_map/all_to_all | solution.py:285
  20.5 3.8 %collective-permute-done.1.first = bf16[4,128,256]{2,1,0:T(8,128)(2,1)S(1)} collective-permute-done((bf16[4,128,256]{2,1,0:T(8,128)(2,1)S(1)}, bf16[4,128,256]{2,1,0:T(8,128)(2,1)S(1)}, u32[]{:S(2)}, u32[]{:S(2)}) %collective-permute-start.1) | collective-permute-done | bytes 262176 | tf_op jit(solution)/shard_map/ppermute | solution.py:284
  24.4 1.9 %collective-permute-start.3 = (bf16[704,256]{1,0:T(8,128)(2,1)S(1)}, bf16[704,256]{1,0:T(8,128)(2,1)S(1)}, u32[]{:S(2)}, u32[]{:S(2)}) collective-permute-start(bf16[704,256]{1,0:T(8,128)(2,1)S(1)} %shard_map.93), channel_id=1, source_target_pairs={{0,16},{16,0},{1,17},{17,1},{2,18},{18,2},{3,19},{19,3},{4,20},{20... | collective-permute-start | bytes 1081352 | tf_op jit(solution)/shard_map/ppermute | solution.py:249
  26.3 4.2 %all-to-all-done.bias = bf16[4,256,256]{2,1,0:T(8,128)(2,1)S(1)} async-done(((bf16[4,256,256]{2,1,0:T(8,128)(2,1)}), bf16[4,256,256]{2,1,0:T(8,128)(2,1)S(1)}, u32[]{:S(2)}, u32[]{:S(2)}) %all-to-all-start) | async-done | bytes 524320 | tf_op jit(solution)/shard_map/all_to_all | solution.py:285
  30.5 3.4 %shard_map.94 = (bf16[16,64,256]{2,1,0:T(8,128)(2,1)S(1)}, bf16[4,32,256]{2,1,0:T(8,128)(2,1)S(1)}, bf16[4,4,64,256]{3,2,1,0:T(8,128)(2,1)S(1)}) custom-call(bf16[2,64,256]{2,1,0:T(8,128)(2,1)S(1)} %bitcast.20, bf16[2,64,256]{2,1,0:T(8,128)(2,1)S(1)} %bitcast.22, bf16[2,64,256]{2,1,0:T(8,128)(2,1)S(1)} %bitcast.24, ...), custom_call_target="tpu_custom_call" | custom-call | flops 335544320 | bytes 6291456 | tf_op jit(solution)/shard_map/pallas_call | solution.py:133
  33.9 17.3 %all_to_all.10 = bf16[16,64,256]{2,1,0:T(8,128)(2,1)S(1)} all-to-all(bf16[16,64,256]{2,1,0:T(8,128)(2,1)S(1)} %get-tuple-element.23), channel_id=1, replica_groups=mesh['zh'=4,'x'=4,'core'=2,'ri'=4,'rj'=4] {'x','rj'}, dimensions={0} | all-to-all | bytes 1048576 | tf_op jit(solution)/shard_map/all_to_all | solution.py:296
  51.1 0.1 reduce_sum.12.after
  51.2 11.2 %collective-permute-start.4 = (bf16[4,64,256]{2,1,0:T(8,128)(2,1)S(1)}, bf16[4,64,256]{2,1,0:T(8,128)(2,1)S(1)}, u32[]{:S(2)}, u32[]{:S(2)}) collective-permute-start(bf16[4,64,256]{2,1,0:T(8,128)(2,1)S(1)} %reduce_sum.12.after), channel_id=1, source_target_pairs={{0,128},{128,0},{256,384},{384,256},{16,400},{144,272},{272,144},{... | collective-permute-start | bytes 393224 | tf_op jit(solution)/shard_map/ppermute | solution.py:262
  62.5 2.3 %collective-permute-start.6 = (bf16[4,64,256]{2,1,0:T(8,128)(2,1)S(1)}, bf16[4,64,256]{2,1,0:T(8,128)(2,1)S(1)}, u32[]{:S(2)}, u32[]{:S(2)}) collective-permute-start(bf16[4,64,256]{2,1,0:T(8,128)(2,1)S(1)} %get-tuple-element.26), channel_id=1, source_target_pairs={{0,1},{1,2},{2,3},{3,0},{4,5},{5,6},{6,7},{7,4},{8,9},{9,10},{10,1... | collective-permute-start | bytes 393224 | tf_op jit(solution)/shard_map/ppermute | solution.py:292
  64.8 3.6 %collective-permute-start.7 = (bf16[4,64,256]{2,1,0:T(8,128)(2,1)S(1)}, bf16[4,64,256]{2,1,0:T(8,128)(2,1)S(1)}, u32[]{:S(2)}, u32[]{:S(2)}) collective-permute-start(bf16[4,64,256]{2,1,0:T(8,128)(2,1)S(1)} %get-tuple-element.27), channel_id=1, source_target_pairs={{0,2},{1,3},{2,0},{3,1},{4,6},{5,7},{6,4},{7,5},{8,10},{9,11},{10,... | collective-permute-start | bytes 393224 | tf_op jit(solution)/shard_map/ppermute | solution.py:292
  68.4 3.1 %collective-permute-start.8 = (bf16[4,64,256]{2,1,0:T(8,128)(2,1)S(1)}, bf16[4,64,256]{2,1,0:T(8,128)(2,1)S(1)}, u32[]{:S(2)}, u32[]{:S(2)}) collective-permute-start(bf16[4,64,256]{2,1,0:T(8,128)(2,1)S(1)} %get-tuple-element.28), channel_id=1, source_target_pairs={{0,3},{1,0},{2,1},{3,2},{4,7},{5,4},{6,5},{7,6},{8,11},{9,8},{10,9... | collective-permute-start | bytes 393224 | tf_op jit(solution)/shard_map/ppermute | solution.py:292
  71.6 5.2 %collective-permute-start.5 = (bf16[4,64,256]{2,1,0:T(8,128)(2,1)S(1)}, bf16[4,64,256]{2,1,0:T(8,128)(2,1)S(1)}, u32[]{:S(2)}, u32[]{:S(2)}) collective-permute-start(bf16[4,64,256]{2,1,0:T(8,128)(2,1)S(1)} %add_convert_fusion.2.after), channel_id=1, source_target_pairs={{0,384},{128,256},{256,128},{384,0},{16,144},{144,16},{272,400},{4... | collective-permute-start | bytes 393224 | tf_op jit(solution)/shard_map/ppermute | solution.py:262
  76.8 0.1 shard_map.96
  76.9 1.9 %collective-permute-start.9 = (bf16[4,64,256]{2,1,0:T(8,128)(2,1)S(1)}, bf16[4,64,256]{2,1,0:T(8,128)(2,1)S(1)}, u32[]{:S(2)}, u32[]{:S(2)}) collective-permute-start(bf16[4,64,256]{2,1,0:T(8,128)(2,1)S(1)} %get-tuple-element.30), channel_id=1, source_target_pairs={{0,4},{4,8},{8,12},{12,0},{1,5},{5,9},{9,13},{13,1},{2,6},{6,10},{... | collective-permute-start | bytes 393224 | tf_op jit(solution)/shard_map/ppermute | solution.py:292
  78.8 4.4 %collective-permute-start.10 = (bf16[4,64,256]{2,1,0:T(8,128)(2,1)S(1)}, bf16[4,64,256]{2,1,0:T(8,128)(2,1)S(1)}, u32[]{:S(2)}, u32[]{:S(2)}) collective-permute-start(bf16[4,64,256]{2,1,0:T(8,128)(2,1)S(1)} %get-tuple-element.31), channel_id=1, source_target_pairs={{0,8},{4,12},{8,0},{12,4},{1,9},{5,13},{9,1},{13,5},{2,10},{6,14},... | collective-permute-start | bytes 393224 | tf_op jit(solution)/shard_map/ppermute | solution.py:292
  83.2 2.7 %collective-permute-start.11 = (bf16[4,64,256]{2,1,0:T(8,128)(2,1)S(1)}, bf16[4,64,256]{2,1,0:T(8,128)(2,1)S(1)}, u32[]{:S(2)}, u32[]{:S(2)}) collective-permute-start(bf16[4,64,256]{2,1,0:T(8,128)(2,1)S(1)} %get-tuple-element.32), channel_id=1, source_target_pairs={{0,12},{4,0},{8,4},{12,8},{1,13},{5,1},{9,5},{13,9},{2,14},{6,2},{... | collective-permute-start | bytes 393224 | tf_op jit(solution)/shard_map/ppermute | solution.py:292
  86.0 10.0 %all_gather.3 = bf16[16,64,256]{2,1,0:T(8,128)(2,1)S(1)} all-gather(bf16[4,64,256]{2,1,0:T(8,128)(2,1)S(1)} %add_convert_fusion.1), channel_id=1, replica_groups=mesh['zh'=4,'x'=4,'core'=2,'ri'=4,'rj'=4] {'x'}, dimensions={0}, use_global_device_ids=true | all-gather | bytes 655360 | tf_op jit(solution)/shard_map/all_gather | solution.py:304
  96.0 0.1 add_convert_fusion
  96.2 8.3 %collective-permute-start.12 = (bf16[1216,256]{1,0:T(8,128)(2,1)S(1)}, bf16[1216,256]{1,0:T(8,128)(2,1)S(1)}, u32[]{:S(2)}, u32[]{:S(2)}) collective-permute-start(bf16[1216,256]{1,0:T(8,128)(2,1)S(1)} %pad_maximum_fusion), channel_id=1, source_target_pairs={{0,16},{16,0},{1,17},{17,1},{2,18},{18,2},{3,19},{19,3},{4,20},{20... | collective-permute-start | bytes 1867784 | tf_op jit(solution)/shard_map/ppermute | solution.py:249
  104.5 1.0 shard_map.97.before
  105.5 0.6 collective-permute-done.12.x_ref
  106.2 1.1 %shard_map.98 = (f32[8,256,256]{2,1,0:T(8,128)}, bf16[2,64,256]{2,1,0:T(8,128)(2,1)}, bf16[2,64,256]{2,1,0:T(8,128)(2,1)}, bf16[2,64,256]{2,1,0:T(8,128)(2,1)}) custom-call(bf16[1216,256]{1,0:T(8,128)(2,1)S(1)} %collective-permute-done.12.x_ref, bf16[2,96,256]{2,1,0:T(8,128)(2,1)S(1)} %get-tuple-element.38.own_ref, ...), custom_call_target="tpu_custom_call", output_to_operand_aliasing={{0}: (2, {})} | custom-call | flops 262144 | bytes 2097152 | tf_op jit(solution)/shard_map/pallas_call | solution.py:232
  (25 shorter events, 0.3 us)
Async XLA Ops:
  0.6 9.8 %copy-start = (bf16[8,256,256]{2,1,0:T(8,128)(2,1)S(1)}, bf16[8,256,256]{2,1,0:T(8,128)(2,1)}, u32[]{:S(2)}) copy-start(bf16[8,256,256]{2,1,0:T(8,128)(2,1)} %param.9) | copy-start | bytes 3145732
  0.6 10.8 %copy-start.4 = (bf16[2,256,64]{1,2,0:T(8,128)(2,1)S(1)}, bf16[2,256,64]{1,2,0:T(8,128)(2,1)}, u32[]{:S(2)}) copy-start(bf16[2,256,64]{1,2,0:T(8,128)(2,1)} %param.8) | copy-start | bytes 196612
  0.7 10.8 %copy-start.5 = (bf16[2,256,64]{1,2,0:T(8,128)(2,1)S(1)}, bf16[2,256,64]{1,2,0:T(8,128)(2,1)}, u32[]{:S(2)}) copy-start(bf16[2,256,64]{1,2,0:T(8,128)(2,1)} %param.7) | copy-start | bytes 196612
  1.6 9.8 %collective-permute-start = (bf16[2,128,256]{2,1,0:T(8,128)(2,1)S(1)}, bf16[2,128,256]{2,1,0:T(8,128)(2,1)S(1)}, u32[]{:S(2)}, u32[]{:S(2)}) collective-permute-start(bf16[2,128,256]{2,1,0:T(8,128)(2,1)S(1)} %pad_maximum_fusion.2), channel_id=1, source_target_pairs={{0,16},{16,0},{1,17},{17,1},{2,18},{18,2},{3,19},{19,3},{4,20},{20... | collective-permute-start | bytes 393224 | tf_op jit(solution)/shard_map/ppermute | solution.py:249
  10.5 13.9 %copy-start.1 = (bf16[2,256,64]{1,2,0:T(8,128)(2,1)S(1)}, bf16[2,256,64]{1,2,0:T(8,128)(2,1)}, u32[]{:S(2)}) copy-start(bf16[2,256,64]{1,2,0:T(8,128)(2,1)} %param.6) | copy-start | bytes 196612
  10.5 13.9 %copy-start.2 = (bf16[2,256,64]{1,2,0:T(8,128)(2,1)S(1)}, bf16[2,256,64]{1,2,0:T(8,128)(2,1)}, u32[]{:S(2)}) copy-start(bf16[2,256,64]{1,2,0:T(8,128)(2,1)} %param.11) | copy-start | bytes 196612
  10.5 13.8 %copy-start.3 = (bf16[2,256,64]{1,2,0:T(8,128)(2,1)S(1)}, bf16[2,256,64]{1,2,0:T(8,128)(2,1)}, u32[]{:S(2)}) copy-start(bf16[2,256,64]{1,2,0:T(8,128)(2,1)} %param.10) | copy-start | bytes 196612
  11.4 9.1 %collective-permute-start.2 = (bf16[4,128,256]{2,1,0:T(8,128)(2,1)S(1)}, bf16[4,128,256]{2,1,0:T(8,128)(2,1)S(1)}, u32[]{:S(2)}, u32[]{:S(2)}) collective-permute-start(bf16[4,128,256]{2,1,0:T(8,128)(2,1)S(1)} %pad_maximum_fusion.1), channel_id=1, source_target_pairs={{0,8},{1,12},{2,0},{3,4},{4,13},{5,1},{6,5},{7,9},{8,2},{9,6},{10,... | collective-permute-start | bytes 786440 | tf_op jit(solution)/shard_map/ppermute | solution.py:284
  13.4 11.0 %collective-permute-start.1 = (bf16[4,128,256]{2,1,0:T(8,128)(2,1)S(1)}, bf16[4,128,256]{2,1,0:T(8,128)(2,1)S(1)}, u32[]{:S(2)}, u32[]{:S(2)}) collective-permute-start(bf16[4,128,256]{2,1,0:T(8,128)(2,1)S(1)} %pad_maximum_fusion.1), channel_id=1, source_target_pairs={{0,0},{1,4},{2,8},{3,12},{4,5},{5,9},{6,13},{7,1},{8,10},{9,14},{1... | collective-permute-start | bytes 786440 | tf_op jit(solution)/shard_map/ppermute | solution.py:284
  15.3 15.2 %all-to-all-start = ((bf16[4,256,256]{2,1,0:T(8,128)(2,1)}), bf16[4,256,256]{2,1,0:T(8,128)(2,1)S(1)}, u32[]{:S(2)}, u32[]{:S(2)}) async-start(bf16[4,256,256]{2,1,0:T(8,128)(2,1)} %dynamic-slice_bitcast_fusion), calls=%async_computation | async-start | bytes 1048576 | tf_op jit(solution)/shard_map/all_to_all | solution.py:285
  24.4 6.1 %collective-permute-start.3 = (bf16[704,256]{1,0:T(8,128)(2,1)S(1)}, bf16[704,256]{1,0:T(8,128)(2,1)S(1)}, u32[]{:S(2)}, u32[]{:S(2)}) collective-permute-start(bf16[704,256]{1,0:T(8,128)(2,1)S(1)} %shard_map.93), channel_id=1, source_target_pairs={{0,16},{16,0},{1,17},{17,1},{2,18},{18,2},{3,19},{19,3},{4,20},{20... | collective-permute-start | bytes 1081352 | tf_op jit(solution)/shard_map/ppermute | solution.py:249
  51.2 20.3 %collective-permute-start.4 = (bf16[4,64,256]{2,1,0:T(8,128)(2,1)S(1)}, bf16[4,64,256]{2,1,0:T(8,128)(2,1)S(1)}, u32[]{:S(2)}, u32[]{:S(2)}) collective-permute-start(bf16[4,64,256]{2,1,0:T(8,128)(2,1)S(1)} %reduce_sum.12.after), channel_id=1, source_target_pairs={{0,128},{128,0},{256,384},{384,256},{16,400},{144,272},{272,144},{... | collective-permute-start | bytes 393224 | tf_op jit(solution)/shard_map/ppermute | solution.py:262
  62.5 14.3 %collective-permute-start.6 = (bf16[4,64,256]{2,1,0:T(8,128)(2,1)S(1)}, bf16[4,64,256]{2,1,0:T(8,128)(2,1)S(1)}, u32[]{:S(2)}, u32[]{:S(2)}) collective-permute-start(bf16[4,64,256]{2,1,0:T(8,128)(2,1)S(1)} %get-tuple-element.26), channel_id=1, source_target_pairs={{0,1},{1,2},{2,3},{3,0},{4,5},{5,6},{6,7},{7,4},{8,9},{9,10},{10,1... | collective-permute-start | bytes 393224 | tf_op jit(solution)/shard_map/ppermute | solution.py:292
  64.8 11.9 %collective-permute-start.7 = (bf16[4,64,256]{2,1,0:T(8,128)(2,1)S(1)}, bf16[4,64,256]{2,1,0:T(8,128)(2,1)S(1)}, u32[]{:S(2)}, u32[]{:S(2)}) collective-permute-start(bf16[4,64,256]{2,1,0:T(8,128)(2,1)S(1)} %get-tuple-element.27), channel_id=1, source_target_pairs={{0,2},{1,3},{2,0},{3,1},{4,6},{5,7},{6,4},{7,5},{8,10},{9,11},{10,... | collective-permute-start | bytes 393224 | tf_op jit(solution)/shard_map/ppermute | solution.py:292
  68.4 8.4 %collective-permute-start.8 = (bf16[4,64,256]{2,1,0:T(8,128)(2,1)S(1)}, bf16[4,64,256]{2,1,0:T(8,128)(2,1)S(1)}, u32[]{:S(2)}, u32[]{:S(2)}) collective-permute-start(bf16[4,64,256]{2,1,0:T(8,128)(2,1)S(1)} %get-tuple-element.28), channel_id=1, source_target_pairs={{0,3},{1,0},{2,1},{3,2},{4,7},{5,4},{6,5},{7,6},{8,11},{9,8},{10,9... | collective-permute-start | bytes 393224 | tf_op jit(solution)/shard_map/ppermute | solution.py:292
  71.6 14.4 %collective-permute-start.5 = (bf16[4,64,256]{2,1,0:T(8,128)(2,1)S(1)}, bf16[4,64,256]{2,1,0:T(8,128)(2,1)S(1)}, u32[]{:S(2)}, u32[]{:S(2)}) collective-permute-start(bf16[4,64,256]{2,1,0:T(8,128)(2,1)S(1)} %add_convert_fusion.2.after), channel_id=1, source_target_pairs={{0,384},{128,256},{256,128},{384,0},{16,144},{144,16},{272,400},{4... | collective-permute-start | bytes 393224 | tf_op jit(solution)/shard_map/ppermute | solution.py:262
  76.9 19.1 %collective-permute-start.9 = (bf16[4,64,256]{2,1,0:T(8,128)(2,1)S(1)}, bf16[4,64,256]{2,1,0:T(8,128)(2,1)S(1)}, u32[]{:S(2)}, u32[]{:S(2)}) collective-permute-start(bf16[4,64,256]{2,1,0:T(8,128)(2,1)S(1)} %get-tuple-element.30), channel_id=1, source_target_pairs={{0,4},{4,8},{8,12},{12,0},{1,5},{5,9},{9,13},{13,1},{2,6},{6,10},{... | collective-permute-start | bytes 393224 | tf_op jit(solution)/shard_map/ppermute | solution.py:292
  78.8 17.2 %collective-permute-start.10 = (bf16[4,64,256]{2,1,0:T(8,128)(2,1)S(1)}, bf16[4,64,256]{2,1,0:T(8,128)(2,1)S(1)}, u32[]{:S(2)}, u32[]{:S(2)}) collective-permute-start(bf16[4,64,256]{2,1,0:T(8,128)(2,1)S(1)} %get-tuple-element.31), channel_id=1, source_target_pairs={{0,8},{4,12},{8,0},{12,4},{1,9},{5,13},{9,1},{13,5},{2,10},{6,14},... | collective-permute-start | bytes 393224 | tf_op jit(solution)/shard_map/ppermute | solution.py:292
  83.2 12.8 %collective-permute-start.11 = (bf16[4,64,256]{2,1,0:T(8,128)(2,1)S(1)}, bf16[4,64,256]{2,1,0:T(8,128)(2,1)S(1)}, u32[]{:S(2)}, u32[]{:S(2)}) collective-permute-start(bf16[4,64,256]{2,1,0:T(8,128)(2,1)S(1)} %get-tuple-element.32), channel_id=1, source_target_pairs={{0,12},{4,0},{8,4},{12,8},{1,13},{5,1},{9,5},{13,9},{2,14},{6,2},{... | collective-permute-start | bytes 393224 | tf_op jit(solution)/shard_map/ppermute | solution.py:292
  96.2 10.0 %collective-permute-start.12 = (bf16[1216,256]{1,0:T(8,128)(2,1)S(1)}, bf16[1216,256]{1,0:T(8,128)(2,1)S(1)}, u32[]{:S(2)}, u32[]{:S(2)}) collective-permute-start(bf16[1216,256]{1,0:T(8,128)(2,1)S(1)} %pad_maximum_fusion), channel_id=1, source_target_pairs={{0,16},{16,0},{1,17},{17,1},{2,18},{18,2},{3,19},{19,3},{4,20},{20... | collective-permute-start | bytes 1867784 | tf_op jit(solution)/shard_map/ppermute | solution.py:249

commit v21 on v17

--- a/solution.py
+++ b/solution.py
@@ -301,7 +301,8 @@
     other = beside_ring(total, 1)
     parts = spread_out(hand_on(choose_kernel, total, *parts), "ri")
     total = add(total, other)
-    mine = lax.all_gather(total, "x", axis=0, tiled=True).reshape(-1, ROWS)
+    copies = jnp.broadcast_to(total, (N, *total.shape))
+    mine = lax.all_to_all(copies, "x", 0, 0, tiled=True).reshape(-1, ROWS)
 
     dkv = sum(x.astype(F32) for x in parts).astype(BF)
     grads = jnp.concatenate([dkv, dq], axis=1)

time: 107 us -> 106 us (level)
  blocking collectives: 28.8 us -> 18.7 us
  waiting for transfers between devices: 5.09 us -> 11.9 us
  starting transfers between devices: 63.6 us -> 65.6 us
    all_gather x1 -> x0, blocking collectives: 10.2 us -> none  [body(): mine = lax.all_gather(total, 'x', axis=0, tiled=True).reshape(-1, ROWS)]
    ppermute x6, waiting for transfers between devices: 0.02 us -> 3.77 us  [spread_out(): lax.ppermute(parts[t], axis, [(a, (a + t) % N) for a in range(N)])]
    all_to_all x0 -> x1, starting transfers between devices: none -> 3.47 us  [body(): mine = lax.all_to_all(copies, 'x', 0, 0, tiled=True).reshape(-1, ROWS)]
    all_to_all x0 -> x1, waiting for transfers between devices: none -> 3.03 us  [body(): mine = lax.all_to_all(copies, 'x', 0, 0, tiled=True).reshape(-1, ROWS)]
    ppermute x3, starting transfers between devices: 20.4 us -> 18.9 us  [swap(): lax.ppermute(x, axis, [(a, b) for a, b in pairs] + [(b, a) for a, b in pa...]
  transfers between devices with their start and end apart: 14 -> 15, of which waited for: 5 -> 7; matrix products, arithmetic and copies ran while one was open for 1% -> 2% of each run, Pallas kernels for 1% -> 1%
where the time goes in v21:
time: 106 us
  starting transfers between devices  65.6 us (62%)
  blocking collectives  18.7 us (18%)
  waiting for transfers between devices  11.9 us (11%)
  Pallas kernels  5.66 us (5%)
  local copies, waits for them, and re-layouts  1.72 us (2%)
  other arithmetic  1.27 us (1%)
    ppermute x3, starting transfers between devices, swap(): lax.ppermute(x, axis, [(a, b) for a, b in pairs] + [(b, a) for a, b in pa...  18.9 us
    all_to_all x1, blocking collectives, body(): spread = lax.all_to_all(total, ('x', 'rj'), 0, 0, tiled=True)  18.7 us
    ppermute x6, starting transfers between devices, spread_out(): lax.ppermute(parts[t], axis, [(a, (a + t) % N) for a in range(N)])  18 us
    ppermute x2, starting transfers between devices, beside_ring(): return lax.ppermute(x, ('zh', 'core'), pairs)  17.1 us
    all_to_all x1, starting transfers between devices, body(): bias = lax.all_to_all(bias, 'rj', 0, 0, tiled=True)  4.19 us
    ppermute x2, starting transfers between devices, body(): spread.append(lax.ppermute(kv, ('core', 'ri', 'rj'), steps))  3.89 us
    ppermute x6, waiting for transfers between devices, spread_out(): lax.ppermute(parts[t], axis, [(a, (a + t) % N) for a in range(N)])  3.77 us
    all_to_all x1, starting transfers between devices, body(): mine = lax.all_to_all(copies, 'x', 0, 0, tiled=True).reshape(-1, ROWS)  3.47 us
  transfers between devices with their start and end apart: 15, of which 7 were waited for; matrix products, arithmetic and copies ran while one was open for 2% of the time, Pallas kernels for 1%

profile of v21, /device:TPU:1, one launch (start us, length us, event | category | flops | bytes accessed | tf_op | source)
XLA Modules:
  0.0 105.7 jit_solution(2544493454423488906)
XLA Ops:
  0.7 1.0 pad_maximum_fusion.2
  1.6 8.8 %collective-permute-start = (bf16[2,128,256]{2,1,0:T(8,128)(2,1)S(1)}, bf16[2,128,256]{2,1,0:T(8,128)(2,1)S(1)}, u32[]{:S(2)}, u32[]{:S(2)}) collective-permute-start(bf16[2,128,256]{2,1,0:T(8,128)(2,1)S(1)} %pad_maximum_fusion.2), channel_id=1, source_target_pairs={{0,16},{16,0},{1,17},{17,1},{2,18},{18,2},{3,19},{19,3},{4,20},{20... | collective-permute-start | bytes 393224 | tf_op jit(solution)/shard_map/ppermute | solution.py:249
  10.5 0.8 dynamic-slice_bitcast_fusion
  11.3 0.1 collective-permute-done
  11.4 1.9 %collective-permute-start.2 = (bf16[4,128,256]{2,1,0:T(8,128)(2,1)S(1)}, bf16[4,128,256]{2,1,0:T(8,128)(2,1)S(1)}, u32[]{:S(2)}, u32[]{:S(2)}) collective-permute-start(bf16[4,128,256]{2,1,0:T(8,128)(2,1)S(1)} %pad_maximum_fusion.1), channel_id=1, source_target_pairs={{0,4},{1,8},{2,12},{3,0},{4,9},{5,13},{6,1},{7,5},{8,14},{9,2},{10... | collective-permute-start | bytes 786440 | tf_op jit(solution)/shard_map/ppermute | solution.py:284
  13.4 2.0 %collective-permute-start.1 = (bf16[4,128,256]{2,1,0:T(8,128)(2,1)S(1)}, bf16[4,128,256]{2,1,0:T(8,128)(2,1)S(1)}, u32[]{:S(2)}, u32[]{:S(2)}) collective-permute-start(bf16[4,128,256]{2,1,0:T(8,128)(2,1)S(1)} %pad_maximum_fusion.1), channel_id=1, source_target_pairs={{0,0},{1,4},{2,8},{3,12},{4,5},{5,9},{6,13},{7,1},{8,10},{9,14},{1... | collective-permute-start | bytes 786440 | tf_op jit(solution)/shard_map/ppermute | solution.py:284
  15.3 4.2 %all-to-all-start = ((bf16[4,256,256]{2,1,0:T(8,128)(2,1)}), bf16[4,256,256]{2,1,0:T(8,128)(2,1)S(1)}, u32[]{:S(2)}, u32[]{:S(2)}) async-start(bf16[4,256,256]{2,1,0:T(8,128)(2,1)} %dynamic-slice_bitcast_fusion), calls=%async_computation | async-start | bytes 1048576 | tf_op jit(solution)/shard_map/all_to_all | solution.py:285
  19.5 3.1 %collective-permute-done.1.first = bf16[4,128,256]{2,1,0:T(8,128)(2,1)S(1)} collective-permute-done((bf16[4,128,256]{2,1,0:T(8,128)(2,1)S(1)}, bf16[4,128,256]{2,1,0:T(8,128)(2,1)S(1)}, u32[]{:S(2)}, u32[]{:S(2)}) %collective-permute-start.1) | collective-permute-done | bytes 262176 | tf_op jit(solution)/shard_map/ppermute | solution.py:284
  22.7 3.4 %collective-permute-start.3 = (bf16[704,256]{1,0:T(8,128)(2,1)S(1)}, bf16[704,256]{1,0:T(8,128)(2,1)S(1)}, u32[]{:S(2)}, u32[]{:S(2)}) collective-permute-start(bf16[704,256]{1,0:T(8,128)(2,1)S(1)} %shard_map.93), channel_id=1, source_target_pairs={{0,16},{16,0},{1,17},{17,1},{2,18},{18,2},{3,19},{19,3},{4,20},{20... | collective-permute-start | bytes 1081352 | tf_op jit(solution)/shard_map/ppermute | solution.py:249
  26.1 1.1 %all-to-all-done.bias = bf16[4,256,256]{2,1,0:T(8,128)(2,1)S(1)} async-done(((bf16[4,256,256]{2,1,0:T(8,128)(2,1)}), bf16[4,256,256]{2,1,0:T(8,128)(2,1)S(1)}, u32[]{:S(2)}, u32[]{:S(2)}) %all-to-all-start) | async-done | bytes 524320 | tf_op jit(solution)/shard_map/all_to_all | solution.py:285
  27.1 0.2 collective-permute-done.3.given
  27.3 3.4 %shard_map.94 = (bf16[16,64,256]{2,1,0:T(8,128)(2,1)S(1)}, bf16[4,32,256]{2,1,0:T(8,128)(2,1)S(1)}, bf16[4,4,64,256]{3,2,1,0:T(8,128)(2,1)S(1)}) custom-call(bf16[2,64,256]{2,1,0:T(8,128)(2,1)S(1)} %bitcast.20, bf16[2,64,256]{2,1,0:T(8,128)(2,1)S(1)} %bitcast.22, bf16[2,64,256]{2,1,0:T(8,128)(2,1)S(1)} %bitcast.24, ...), custom_call_target="tpu_custom_call" | custom-call | flops 335544320 | bytes 6291456 | tf_op jit(solution)/shard_map/pallas_call | solution.py:133
  30.7 18.7 %all_to_all.15 = bf16[16,64,256]{2,1,0:T(8,128)(2,1)S(1)} all-to-all(bf16[16,64,256]{2,1,0:T(8,128)(2,1)S(1)} %get-tuple-element.23), channel_id=1, replica_groups=mesh['zh'=4,'x'=4,'core'=2,'ri'=4,'rj'=4] {'x','rj'}, dimensions={0} | all-to-all | bytes 1048576 | tf_op jit(solution)/shard_map/all_to_all | solution.py:296
  49.4 0.1 reduce_sum.12.after
  49.4 11.9 %collective-permute-start.4 = (bf16[4,64,256]{2,1,0:T(8,128)(2,1)S(1)}, bf16[4,64,256]{2,1,0:T(8,128)(2,1)S(1)}, u32[]{:S(2)}, u32[]{:S(2)}) collective-permute-start(bf16[4,64,256]{2,1,0:T(8,128)(2,1)S(1)} %reduce_sum.12.after), channel_id=1, source_target_pairs={{0,128},{128,0},{256,384},{384,256},{16,400},{144,272},{272,144},{... | collective-permute-start | bytes 393224 | tf_op jit(solution)/shard_map/ppermute | solution.py:262
  61.4 2.3 %collective-permute-start.6 = (bf16[4,64,256]{2,1,0:T(8,128)(2,1)S(1)}, bf16[4,64,256]{2,1,0:T(8,128)(2,1)S(1)}, u32[]{:S(2)}, u32[]{:S(2)}) collective-permute-start(bf16[4,64,256]{2,1,0:T(8,128)(2,1)S(1)} %get-tuple-element.26), channel_id=1, source_target_pairs={{0,1},{1,2},{2,3},{3,0},{4,5},{5,6},{6,7},{7,4},{8,9},{9,10},{10,1... | collective-permute-start | bytes 393224 | tf_op jit(solution)/shard_map/ppermute | solution.py:292
  63.8 3.6 %collective-permute-start.7 = (bf16[4,64,256]{2,1,0:T(8,128)(2,1)S(1)}, bf16[4,64,256]{2,1,0:T(8,128)(2,1)S(1)}, u32[]{:S(2)}, u32[]{:S(2)}) collective-permute-start(bf16[4,64,256]{2,1,0:T(8,128)(2,1)S(1)} %get-tuple-element.27), channel_id=1, source_target_pairs={{0,2},{1,3},{2,0},{3,1},{4,6},{5,7},{6,4},{7,5},{8,10},{9,11},{10,... | collective-permute-start | bytes 393224 | tf_op jit(solution)/shard_map/ppermute | solution.py:292
  67.4 3.1 %collective-permute-start.8 = (bf16[4,64,256]{2,1,0:T(8,128)(2,1)S(1)}, bf16[4,64,256]{2,1,0:T(8,128)(2,1)S(1)}, u32[]{:S(2)}, u32[]{:S(2)}) collective-permute-start(bf16[4,64,256]{2,1,0:T(8,128)(2,1)S(1)} %get-tuple-element.28), channel_id=1, source_target_pairs={{0,3},{1,0},{2,1},{3,2},{4,7},{5,4},{6,5},{7,6},{8,11},{9,8},{10,9... | collective-permute-start | bytes 393224 | tf_op jit(solution)/shard_map/ppermute | solution.py:292
  70.5 5.2 %collective-permute-start.5 = (bf16[4,64,256]{2,1,0:T(8,128)(2,1)S(1)}, bf16[4,64,256]{2,1,0:T(8,128)(2,1)S(1)}, u32[]{:S(2)}, u32[]{:S(2)}) collective-permute-start(bf16[4,64,256]{2,1,0:T(8,128)(2,1)S(1)} %add_convert_fusion.2.after), channel_id=1, source_target_pairs={{0,384},{128,256},{256,128},{384,0},{16,144},{144,16},{272,400},{4... | collective-permute-start | bytes 393224 | tf_op jit(solution)/shard_map/ppermute | solution.py:262
  75.8 0.1 shard_map.96
  75.9 2.4 %collective-permute-start.9 = (bf16[4,64,256]{2,1,0:T(8,128)(2,1)S(1)}, bf16[4,64,256]{2,1,0:T(8,128)(2,1)S(1)}, u32[]{:S(2)}, u32[]{:S(2)}) collective-permute-start(bf16[4,64,256]{2,1,0:T(8,128)(2,1)S(1)} %get-tuple-element.30), channel_id=1, source_target_pairs={{0,4},{4,8},{8,12},{12,0},{1,5},{5,9},{9,13},{13,1},{2,6},{6,10},{... | collective-permute-start | bytes 393224 | tf_op jit(solution)/shard_map/ppermute | solution.py:292
  78.3 2.6 %collective-permute-start.10 = (bf16[4,64,256]{2,1,0:T(8,128)(2,1)S(1)}, bf16[4,64,256]{2,1,0:T(8,128)(2,1)S(1)}, u32[]{:S(2)}, u32[]{:S(2)}) collective-permute-start(bf16[4,64,256]{2,1,0:T(8,128)(2,1)S(1)} %get-tuple-element.31), channel_id=1, source_target_pairs={{0,8},{4,12},{8,0},{12,4},{1,9},{5,13},{9,1},{13,5},{2,10},{6,14},... | collective-permute-start | bytes 393224 | tf_op jit(solution)/shard_map/ppermute | solution.py:292
  80.8 4.1 %collective-permute-start.11 = (bf16[4,64,256]{2,1,0:T(8,128)(2,1)S(1)}, bf16[4,64,256]{2,1,0:T(8,128)(2,1)S(1)}, u32[]{:S(2)}, u32[]{:S(2)}) collective-permute-start(bf16[4,64,256]{2,1,0:T(8,128)(2,1)S(1)} %get-tuple-element.32), channel_id=1, source_target_pairs={{0,12},{4,0},{8,4},{12,8},{1,13},{5,1},{9,5},{13,9},{2,14},{6,2},{... | collective-permute-start | bytes 393224 | tf_op jit(solution)/shard_map/ppermute | solution.py:292
  85.0 0.8 broadcast_in_dim.3
  85.8 3.5 %all-to-all-start.2 = ((bf16[4,4,64,256]{3,2,1,0:T(8,128)(2,1)}), bf16[4,4,64,256]{3,2,1,0:T(8,128)(2,1)S(1)}, u32[]{:S(2)}, u32[]{:S(2)}) async-start(bf16[4,4,64,256]{3,2,1,0:T(8,128)(2,1)} %broadcast_in_dim.3), calls=%async_computation.2 | async-start | bytes 1048576 | tf_op jit(solution)/shard_map/all_to_all | solution.py:305
  89.3 3.8 %collective-permute-done.10 = bf16[4,64,256]{2,1,0:T(8,128)(2,1)S(1)} collective-permute-done((bf16[4,64,256]{2,1,0:T(8,128)(2,1)S(1)}, bf16[4,64,256]{2,1,0:T(8,128)(2,1)S(1)}, u32[]{:S(2)}, u32[]{:S(2)}) %collective-permute-start.10) | collective-permute-done | bytes 131104 | tf_op jit(solution)/shard_map/ppermute | solution.py:292
  93.1 0.1 add_convert_fusion
  93.2 3.0 %all-to-all-done.2 = bf16[4,4,64,256]{3,2,1,0:T(8,128)(2,1)S(1)} async-done(((bf16[4,4,64,256]{3,2,1,0:T(8,128)(2,1)}), bf16[4,4,64,256]{3,2,1,0:T(8,128)(2,1)S(1)}, u32[]{:S(2)}, u32[]{:S(2)}) %all-to-all-start.2) | async-done | bytes 524320 | tf_op jit(solution)/shard_map/all_to_all | solution.py:305
  96.2 6.7 %collective-permute-start.12 = (bf16[1216,256]{1,0:T(8,128)(2,1)S(1)}, bf16[1216,256]{1,0:T(8,128)(2,1)S(1)}, u32[]{:S(2)}, u32[]{:S(2)}) collective-permute-start(bf16[1216,256]{1,0:T(8,128)(2,1)S(1)} %pad_maximum_fusion), channel_id=1, source_target_pairs={{0,16},{16,0},{1,17},{17,1},{2,18},{18,2},{3,19},{19,3},{4,20},{20... | collective-permute-start | bytes 1867784 | tf_op jit(solution)/shard_map/ppermute | solution.py:249
  103.0 1.0 shard_map.97.before
  104.0 0.6 collective-permute-done.12.x_ref
  104.6 1.1 %shard_map.98 = (f32[8,256,256]{2,1,0:T(8,128)}, bf16[2,64,256]{2,1,0:T(8,128)(2,1)}, bf16[2,64,256]{2,1,0:T(8,128)(2,1)}, bf16[2,64,256]{2,1,0:T(8,128)(2,1)}) custom-call(bf16[1216,256]{1,0:T(8,128)(2,1)S(1)} %collective-permute-done.12.x_ref, bf16[2,96,256]{2,1,0:T(8,128)(2,1)S(1)} %get-tuple-element.38.own_ref, ...), custom_call_target="tpu_custom_call", output_to_operand_aliasing={{0}: (2, {})} | custom-call | flops 262144 | bytes 2097152 | tf_op jit(solution)/shard_map/pallas_call | solution.py:232
  (27 shorter events, 0.3 us)
Async XLA Ops:
  0.6 9.8 %copy-start = (bf16[8,256,256]{2,1,0:T(8,128)(2,1)S(1)}, bf16[8,256,256]{2,1,0:T(8,128)(2,1)}, u32[]{:S(2)}) copy-start(bf16[8,256,256]{2,1,0:T(8,128)(2,1)} %param.9) | copy-start | bytes 3145732
  0.6 10.8 %copy-start.4 = (bf16[2,256,64]{1,2,0:T(8,128)(2,1)S(1)}, bf16[2,256,64]{1,2,0:T(8,128)(2,1)}, u32[]{:S(2)}) copy-start(bf16[2,256,64]{1,2,0:T(8,128)(2,1)} %param.8) | copy-start | bytes 196612
  0.7 10.8 %copy-start.5 = (bf16[2,256,64]{1,2,0:T(8,128)(2,1)S(1)}, bf16[2,256,64]{1,2,0:T(8,128)(2,1)}, u32[]{:S(2)}) copy-start(bf16[2,256,64]{1,2,0:T(8,128)(2,1)} %param.7) | copy-start | bytes 196612
  1.6 9.8 %collective-permute-start = (bf16[2,128,256]{2,1,0:T(8,128)(2,1)S(1)}, bf16[2,128,256]{2,1,0:T(8,128)(2,1)S(1)}, u32[]{:S(2)}, u32[]{:S(2)}) collective-permute-start(bf16[2,128,256]{2,1,0:T(8,128)(2,1)S(1)} %pad_maximum_fusion.2), channel_id=1, source_target_pairs={{0,16},{16,0},{1,17},{17,1},{2,18},{18,2},{3,19},{19,3},{4,20},{20... | collective-permute-start | bytes 393224 | tf_op jit(solution)/shard_map/ppermute | solution.py:249
  10.5 12.1 %copy-start.1 = (bf16[2,256,64]{1,2,0:T(8,128)(2,1)S(1)}, bf16[2,256,64]{1,2,0:T(8,128)(2,1)}, u32[]{:S(2)}) copy-start(bf16[2,256,64]{1,2,0:T(8,128)(2,1)} %param.6) | copy-start | bytes 196612
  10.5 12.1 %copy-start.2 = (bf16[2,256,64]{1,2,0:T(8,128)(2,1)S(1)}, bf16[2,256,64]{1,2,0:T(8,128)(2,1)}, u32[]{:S(2)}) copy-start(bf16[2,256,64]{1,2,0:T(8,128)(2,1)} %param.11) | copy-start | bytes 196612
  10.5 12.1 %copy-start.3 = (bf16[2,256,64]{1,2,0:T(8,128)(2,1)S(1)}, bf16[2,256,64]{1,2,0:T(8,128)(2,1)}, u32[]{:S(2)}) copy-start(bf16[2,256,64]{1,2,0:T(8,128)(2,1)} %param.10) | copy-start | bytes 196612
  11.4 8.1 %collective-permute-start.2 = (bf16[4,128,256]{2,1,0:T(8,128)(2,1)S(1)}, bf16[4,128,256]{2,1,0:T(8,128)(2,1)S(1)}, u32[]{:S(2)}, u32[]{:S(2)}) collective-permute-start(bf16[4,128,256]{2,1,0:T(8,128)(2,1)S(1)} %pad_maximum_fusion.1), channel_id=1, source_target_pairs={{0,4},{1,8},{2,12},{3,0},{4,9},{5,13},{6,1},{7,5},{8,14},{9,2},{10... | collective-permute-start | bytes 786440 | tf_op jit(solution)/shard_map/ppermute | solution.py:284
  13.4 9.2 %collective-permute-start.1 = (bf16[4,128,256]{2,1,0:T(8,128)(2,1)S(1)}, bf16[4,128,256]{2,1,0:T(8,128)(2,1)S(1)}, u32[]{:S(2)}, u32[]{:S(2)}) collective-permute-start(bf16[4,128,256]{2,1,0:T(8,128)(2,1)S(1)} %pad_maximum_fusion.1), channel_id=1, source_target_pairs={{0,0},{1,4},{2,8},{3,12},{4,5},{5,9},{6,13},{7,1},{8,10},{9,14},{1... | collective-permute-start | bytes 786440 | tf_op jit(solution)/shard_map/ppermute | solution.py:284
  15.3 11.8 %all-to-all-start = ((bf16[4,256,256]{2,1,0:T(8,128)(2,1)}), bf16[4,256,256]{2,1,0:T(8,128)(2,1)S(1)}, u32[]{:S(2)}, u32[]{:S(2)}) async-start(bf16[4,256,256]{2,1,0:T(8,128)(2,1)} %dynamic-slice_bitcast_fusion), calls=%async_computation | async-start | bytes 1048576 | tf_op jit(solution)/shard_map/all_to_all | solution.py:285
  22.7 4.7 %collective-permute-start.3 = (bf16[704,256]{1,0:T(8,128)(2,1)S(1)}, bf16[704,256]{1,0:T(8,128)(2,1)S(1)}, u32[]{:S(2)}, u32[]{:S(2)}) collective-permute-start(bf16[704,256]{1,0:T(8,128)(2,1)S(1)} %shard_map.93), channel_id=1, source_target_pairs={{0,16},{16,0},{1,17},{17,1},{2,18},{18,2},{3,19},{19,3},{4,20},{20... | collective-permute-start | bytes 1081352 | tf_op jit(solution)/shard_map/ppermute | solution.py:249
  49.4 21.0 %collective-permute-start.4 = (bf16[4,64,256]{2,1,0:T(8,128)(2,1)S(1)}, bf16[4,64,256]{2,1,0:T(8,128)(2,1)S(1)}, u32[]{:S(2)}, u32[]{:S(2)}) collective-permute-start(bf16[4,64,256]{2,1,0:T(8,128)(2,1)S(1)} %reduce_sum.12.after), channel_id=1, source_target_pairs={{0,128},{128,0},{256,384},{384,256},{16,400},{144,272},{272,144},{... | collective-permute-start | bytes 393224 | tf_op jit(solution)/shard_map/ppermute | solution.py:262
  61.4 14.3 %collective-permute-start.6 = (bf16[4,64,256]{2,1,0:T(8,128)(2,1)S(1)}, bf16[4,64,256]{2,1,0:T(8,128)(2,1)S(1)}, u32[]{:S(2)}, u32[]{:S(2)}) collective-permute-start(bf16[4,64,256]{2,1,0:T(8,128)(2,1)S(1)} %get-tuple-element.26), channel_id=1, source_target_pairs={{0,1},{1,2},{2,3},{3,0},{4,5},{5,6},{6,7},{7,4},{8,9},{9,10},{10,1... | collective-permute-start | bytes 393224 | tf_op jit(solution)/shard_map/ppermute | solution.py:292
  63.8 12.0 %collective-permute-start.7 = (bf16[4,64,256]{2,1,0:T(8,128)(2,1)S(1)}, bf16[4,64,256]{2,1,0:T(8,128)(2,1)S(1)}, u32[]{:S(2)}, u32[]{:S(2)}) collective-permute-start(bf16[4,64,256]{2,1,0:T(8,128)(2,1)S(1)} %get-tuple-element.27), channel_id=1, source_target_pairs={{0,2},{1,3},{2,0},{3,1},{4,6},{5,7},{6,4},{7,5},{8,10},{9,11},{10,... | collective-permute-start | bytes 393224 | tf_op jit(solution)/shard_map/ppermute | solution.py:292
  67.4 8.4 %collective-permute-start.8 = (bf16[4,64,256]{2,1,0:T(8,128)(2,1)S(1)}, bf16[4,64,256]{2,1,0:T(8,128)(2,1)S(1)}, u32[]{:S(2)}, u32[]{:S(2)}) collective-permute-start(bf16[4,64,256]{2,1,0:T(8,128)(2,1)S(1)} %get-tuple-element.28), channel_id=1, source_target_pairs={{0,3},{1,0},{2,1},{3,2},{4,7},{5,4},{6,5},{7,6},{8,11},{9,8},{10,9... | collective-permute-start | bytes 393224 | tf_op jit(solution)/shard_map/ppermute | solution.py:292
  70.5 14.4 %collective-permute-start.5 = (bf16[4,64,256]{2,1,0:T(8,128)(2,1)S(1)}, bf16[4,64,256]{2,1,0:T(8,128)(2,1)S(1)}, u32[]{:S(2)}, u32[]{:S(2)}) collective-permute-start(bf16[4,64,256]{2,1,0:T(8,128)(2,1)S(1)} %add_convert_fusion.2.after), channel_id=1, source_target_pairs={{0,384},{128,256},{256,128},{384,0},{16,144},{144,16},{272,400},{4... | collective-permute-start | bytes 393224 | tf_op jit(solution)/shard_map/ppermute | solution.py:262
  75.9 13.4 %collective-permute-start.9 = (bf16[4,64,256]{2,1,0:T(8,128)(2,1)S(1)}, bf16[4,64,256]{2,1,0:T(8,128)(2,1)S(1)}, u32[]{:S(2)}, u32[]{:S(2)}) collective-permute-start(bf16[4,64,256]{2,1,0:T(8,128)(2,1)S(1)} %get-tuple-element.30), channel_id=1, source_target_pairs={{0,4},{4,8},{8,12},{12,0},{1,5},{5,9},{9,13},{13,1},{2,6},{6,10},{... | collective-permute-start | bytes 393224 | tf_op jit(solution)/shard_map/ppermute | solution.py:292
  78.3 14.8 %collective-permute-start.10 = (bf16[4,64,256]{2,1,0:T(8,128)(2,1)S(1)}, bf16[4,64,256]{2,1,0:T(8,128)(2,1)S(1)}, u32[]{:S(2)}, u32[]{:S(2)}) collective-permute-start(bf16[4,64,256]{2,1,0:T(8,128)(2,1)S(1)} %get-tuple-element.31), channel_id=1, source_target_pairs={{0,8},{4,12},{8,0},{12,4},{1,9},{5,13},{9,1},{13,5},{2,10},{6,14},... | collective-permute-start | bytes 393224 | tf_op jit(solution)/shard_map/ppermute | solution.py:292
  80.8 12.2 %collective-permute-start.11 = (bf16[4,64,256]{2,1,0:T(8,128)(2,1)S(1)}, bf16[4,64,256]{2,1,0:T(8,128)(2,1)S(1)}, u32[]{:S(2)}, u32[]{:S(2)}) collective-permute-start(bf16[4,64,256]{2,1,0:T(8,128)(2,1)S(1)} %get-tuple-element.32), channel_id=1, source_target_pairs={{0,12},{4,0},{8,4},{12,8},{1,13},{5,1},{9,5},{13,9},{2,14},{6,2},{... | collective-permute-start | bytes 393224 | tf_op jit(solution)/shard_map/ppermute | solution.py:292
  85.8 10.4 %all-to-all-start.2 = ((bf16[4,4,64,256]{3,2,1,0:T(8,128)(2,1)}), bf16[4,4,64,256]{3,2,1,0:T(8,128)(2,1)S(1)}, u32[]{:S(2)}, u32[]{:S(2)}) async-start(bf16[4,4,64,256]{3,2,1,0:T(8,128)(2,1)} %broadcast_in_dim.3), calls=%async_computation.2 | async-start | bytes 1048576 | tf_op jit(solution)/shard_map/all_to_all | solution.py:305
  96.2 8.4 %collective-permute-start.12 = (bf16[1216,256]{1,0:T(8,128)(2,1)S(1)}, bf16[1216,256]{1,0:T(8,128)(2,1)S(1)}, u32[]{:S(2)}, u32[]{:S(2)}) collective-permute-start(bf16[1216,256]{1,0:T(8,128)(2,1)S(1)} %pad_maximum_fusion), channel_id=1, source_target_pairs={{0,16},{16,0},{1,17},{17,1},{2,18},{18,2},{3,19},{19,3},{4,20},{20... | collective-permute-start | bytes 1867784 | tf_op jit(solution)/shard_map/ppermute | solution.py:249

commit v22 on v21

--- a/solution.py
+++ b/solution.py
@@ -253,6 +253,24 @@
     return (a.astype(F32) + b.astype(F32)).astype(BF)
 
 
+def repeat_kernel(a_ref, b_ref, out):
+    total = (a_ref[...].astype(F32) + b_ref[...].astype(F32)).astype(BF)
+    for t in range(N):
+        out[t] = total
+
+
+def repeat(a, b):
+    vmem = pl.BlockSpec(memory_space=pltpu.VMEM)
+    return pl.pallas_call(
+        repeat_kernel,
+        out_shape=jax.ShapeDtypeStruct((N, *a.shape), BF),
+        in_specs=[vmem] * 2,
+        out_specs=vmem,
+        compiler_params=pltpu.CompilerParams(vmem_limit_bytes=8 * 2**20),
+        cost_estimate=pl.CostEstimate(flops=2**16, bytes_accessed=2**20, transcendentals=0),
+    )(a, b)
+
+
 def beside_ring(x, step):
     pairs = []
     for core in range(2):
@@ -300,8 +318,7 @@
     total = add(total, other)
     other = beside_ring(total, 1)
     parts = spread_out(hand_on(choose_kernel, total, *parts), "ri")
-    total = add(total, other)
-    copies = jnp.broadcast_to(total, (N, *total.shape))
+    copies = repeat(total, other)
     mine = lax.all_to_all(copies, "x", 0, 0, tiled=True).reshape(-1, ROWS)
 
     dkv = sum(x.astype(F32) for x in parts).astype(BF)

time: 106 us -> 106 us (level)
  transfers between devices with their start and end apart: 15 -> 15, of which waited for: 7 -> 7; matrix products, arithmetic and copies ran while one was open for 2% -> 1% of each run, Pallas kernels for 1% -> 2%
where the time goes in v22:
time: 106 us
  starting transfers between devices  65.6 us (62%)
  blocking collectives  18.7 us (18%)
  waiting for transfers between devices  11.9 us (11%)
  Pallas kernels  6.49 us (6%)
  other arithmetic  1.23 us (1%)
    ppermute x3, starting transfers between devices, swap(): lax.ppermute(x, axis, [(a, b) for a, b in pairs] + [(b, a) for a, b in pa...  18.9 us
    all_to_all x1, blocking collectives, body(): spread = lax.all_to_all(total, ('x', 'rj'), 0, 0, tiled=True)  18.7 us
    ppermute x6, starting transfers between devices, spread_out(): lax.ppermute(parts[t], axis, [(a, (a + t) % N) for a in range(N)])  18 us
    ppermute x2, starting transfers between devices, beside_ring(): return lax.ppermute(x, ('zh', 'core'), pairs)  17.1 us
    all_to_all x1, starting transfers between devices, body(): bias = lax.all_to_all(bias, 'rj', 0, 0, tiled=True)  4.19 us
    ppermute x2, starting transfers between devices, body(): spread.append(lax.ppermute(kv, ('core', 'ri', 'rj'), steps))  3.89 us
    ppermute x6, waiting for transfers between devices, spread_out(): lax.ppermute(parts[t], axis, [(a, (a + t) % N) for a in range(N)])  3.83 us
    all_to_all x1, starting transfers between devices, body(): mine = lax.all_to_all(copies, 'x', 0, 0, tiled=True).reshape(-1, ROWS)  3.47 us
  transfers between devices with their start and end apart: 15, of which 7 were waited for; matrix products, arithmetic and copies ran while one was open for 1% of the time, Pallas kernels for 2%

profile of v22, /device:TPU:1, one launch (start us, length us, event | category | flops | bytes accessed | tf_op | source)
XLA Modules:
  0.0 105.7 jit_solution(6133637152468323589)
XLA Ops:
  0.7 1.0 pad_maximum_fusion.2
  1.6 8.8 %collective-permute-start = (bf16[2,128,256]{2,1,0:T(8,128)(2,1)S(1)}, bf16[2,128,256]{2,1,0:T(8,128)(2,1)S(1)}, u32[]{:S(2)}, u32[]{:S(2)}) collective-permute-start(bf16[2,128,256]{2,1,0:T(8,128)(2,1)S(1)} %pad_maximum_fusion.2), channel_id=1, source_target_pairs={{0,16},{16,0},{1,17},{17,1},{2,18},{18,2},{3,19},{19,3},{4,20},{20... | collective-permute-start | bytes 393224 | tf_op jit(solution)/shard_map/ppermute | solution.py:249
  10.5 0.8 dynamic-slice_bitcast_fusion
  11.3 0.1 collective-permute-done
  11.4 1.9 %collective-permute-start.2 = (bf16[4,128,256]{2,1,0:T(8,128)(2,1)S(1)}, bf16[4,128,256]{2,1,0:T(8,128)(2,1)S(1)}, u32[]{:S(2)}, u32[]{:S(2)}) collective-permute-start(bf16[4,128,256]{2,1,0:T(8,128)(2,1)S(1)} %pad_maximum_fusion.1), channel_id=1, source_target_pairs={{0,4},{1,8},{2,12},{3,0},{4,9},{5,13},{6,1},{7,5},{8,14},{9,2},{10... | collective-permute-start | bytes 786440 | tf_op jit(solution)/shard_map/ppermute | solution.py:302
  13.4 2.0 %collective-permute-start.1 = (bf16[4,128,256]{2,1,0:T(8,128)(2,1)S(1)}, bf16[4,128,256]{2,1,0:T(8,128)(2,1)S(1)}, u32[]{:S(2)}, u32[]{:S(2)}) collective-permute-start(bf16[4,128,256]{2,1,0:T(8,128)(2,1)S(1)} %pad_maximum_fusion.1), channel_id=1, source_target_pairs={{0,0},{1,4},{2,8},{3,12},{4,5},{5,9},{6,13},{7,1},{8,10},{9,14},{1... | collective-permute-start | bytes 786440 | tf_op jit(solution)/shard_map/ppermute | solution.py:302
  15.3 4.2 %all-to-all-start = ((bf16[4,256,256]{2,1,0:T(8,128)(2,1)}), bf16[4,256,256]{2,1,0:T(8,128)(2,1)S(1)}, u32[]{:S(2)}, u32[]{:S(2)}) async-start(bf16[4,256,256]{2,1,0:T(8,128)(2,1)} %dynamic-slice_bitcast_fusion), calls=%async_computation | async-start | bytes 1048576 | tf_op jit(solution)/shard_map/all_to_all | solution.py:303
  19.5 3.1 %collective-permute-done.1.first = bf16[4,128,256]{2,1,0:T(8,128)(2,1)S(1)} collective-permute-done((bf16[4,128,256]{2,1,0:T(8,128)(2,1)S(1)}, bf16[4,128,256]{2,1,0:T(8,128)(2,1)S(1)}, u32[]{:S(2)}, u32[]{:S(2)}) %collective-permute-start.1) | collective-permute-done | bytes 262176 | tf_op jit(solution)/shard_map/ppermute | solution.py:302
  22.7 3.4 %collective-permute-start.3 = (bf16[704,256]{1,0:T(8,128)(2,1)S(1)}, bf16[704,256]{1,0:T(8,128)(2,1)S(1)}, u32[]{:S(2)}, u32[]{:S(2)}) collective-permute-start(bf16[704,256]{1,0:T(8,128)(2,1)S(1)} %shard_map.93), channel_id=1, source_target_pairs={{0,16},{16,0},{1,17},{17,1},{2,18},{18,2},{3,19},{19,3},{4,20},{20... | collective-permute-start | bytes 1081352 | tf_op jit(solution)/shard_map/ppermute | solution.py:249
  26.1 1.1 %all-to-all-done.bias = bf16[4,256,256]{2,1,0:T(8,128)(2,1)S(1)} async-done(((bf16[4,256,256]{2,1,0:T(8,128)(2,1)}), bf16[4,256,256]{2,1,0:T(8,128)(2,1)S(1)}, u32[]{:S(2)}, u32[]{:S(2)}) %all-to-all-start) | async-done | bytes 524320 | tf_op jit(solution)/shard_map/all_to_all | solution.py:303
  27.1 0.2 collective-permute-done.3.given
  27.3 3.4 %shard_map.94 = (bf16[16,64,256]{2,1,0:T(8,128)(2,1)S(1)}, bf16[4,32,256]{2,1,0:T(8,128)(2,1)S(1)}, bf16[4,4,64,256]{3,2,1,0:T(8,128)(2,1)S(1)}) custom-call(bf16[2,64,256]{2,1,0:T(8,128)(2,1)S(1)} %bitcast.20, bf16[2,64,256]{2,1,0:T(8,128)(2,1)S(1)} %bitcast.22, bf16[2,64,256]{2,1,0:T(8,128)(2,1)S(1)} %bitcast.24, ...), custom_call_target="tpu_custom_call" | custom-call | flops 335544320 | bytes 6291456 | tf_op jit(solution)/shard_map/pallas_call | solution.py:133
  30.7 18.7 %all_to_all.15 = bf16[16,64,256]{2,1,0:T(8,128)(2,1)S(1)} all-to-all(bf16[16,64,256]{2,1,0:T(8,128)(2,1)S(1)} %get-tuple-element.23), channel_id=1, replica_groups=mesh['zh'=4,'x'=4,'core'=2,'ri'=4,'rj'=4] {'x','rj'}, dimensions={0} | all-to-all | bytes 1048576 | tf_op jit(solution)/shard_map/all_to_all | solution.py:314
  49.4 0.1 reduce_sum.12.after
  49.4 11.9 %collective-permute-start.4 = (bf16[4,64,256]{2,1,0:T(8,128)(2,1)S(1)}, bf16[4,64,256]{2,1,0:T(8,128)(2,1)S(1)}, u32[]{:S(2)}, u32[]{:S(2)}) collective-permute-start(bf16[4,64,256]{2,1,0:T(8,128)(2,1)S(1)} %reduce_sum.12.after), channel_id=1, source_target_pairs={{0,128},{128,0},{256,384},{384,256},{16,400},{144,272},{272,144},{... | collective-permute-start | bytes 393224 | tf_op jit(solution)/shard_map/ppermute | solution.py:280
  61.4 2.3 %collective-permute-start.6 = (bf16[4,64,256]{2,1,0:T(8,128)(2,1)S(1)}, bf16[4,64,256]{2,1,0:T(8,128)(2,1)S(1)}, u32[]{:S(2)}, u32[]{:S(2)}) collective-permute-start(bf16[4,64,256]{2,1,0:T(8,128)(2,1)S(1)} %get-tuple-element.26), channel_id=1, source_target_pairs={{0,1},{1,2},{2,3},{3,0},{4,5},{5,6},{6,7},{7,4},{8,9},{9,10},{10,1... | collective-permute-start | bytes 393224 | tf_op jit(solution)/shard_map/ppermute | solution.py:310
  63.8 3.6 %collective-permute-start.7 = (bf16[4,64,256]{2,1,0:T(8,128)(2,1)S(1)}, bf16[4,64,256]{2,1,0:T(8,128)(2,1)S(1)}, u32[]{:S(2)}, u32[]{:S(2)}) collective-permute-start(bf16[4,64,256]{2,1,0:T(8,128)(2,1)S(1)} %get-tuple-element.27), channel_id=1, source_target_pairs={{0,2},{1,3},{2,0},{3,1},{4,6},{5,7},{6,4},{7,5},{8,10},{9,11},{10,... | collective-permute-start | bytes 393224 | tf_op jit(solution)/shard_map/ppermute | solution.py:310
  67.4 3.1 %collective-permute-start.8 = (bf16[4,64,256]{2,1,0:T(8,128)(2,1)S(1)}, bf16[4,64,256]{2,1,0:T(8,128)(2,1)S(1)}, u32[]{:S(2)}, u32[]{:S(2)}) collective-permute-start(bf16[4,64,256]{2,1,0:T(8,128)(2,1)S(1)} %get-tuple-element.28), channel_id=1, source_target_pairs={{0,3},{1,0},{2,1},{3,2},{4,7},{5,4},{6,5},{7,6},{8,11},{9,8},{10,9... | collective-permute-start | bytes 393224 | tf_op jit(solution)/shard_map/ppermute | solution.py:310
  70.5 5.2 %collective-permute-start.5 = (bf16[4,64,256]{2,1,0:T(8,128)(2,1)S(1)}, bf16[4,64,256]{2,1,0:T(8,128)(2,1)S(1)}, u32[]{:S(2)}, u32[]{:S(2)}) collective-permute-start(bf16[4,64,256]{2,1,0:T(8,128)(2,1)S(1)} %add_convert_fusion.1.a_ref.after), channel_id=1, source_target_pairs={{0,384},{128,256},{256,128},{384,0},{16,144},{144,16},{272,400},{4... | collective-permute-start | bytes 393224 | tf_op jit(solution)/shard_map/ppermute | solution.py:280
  75.8 0.1 shard_map.97
  75.9 2.4 %collective-permute-start.9 = (bf16[4,64,256]{2,1,0:T(8,128)(2,1)S(1)}, bf16[4,64,256]{2,1,0:T(8,128)(2,1)S(1)}, u32[]{:S(2)}, u32[]{:S(2)}) collective-permute-start(bf16[4,64,256]{2,1,0:T(8,128)(2,1)S(1)} %get-tuple-element.30), channel_id=1, source_target_pairs={{0,4},{4,8},{8,12},{12,0},{1,5},{5,9},{9,13},{13,1},{2,6},{6,10},{... | collective-permute-start | bytes 393224 | tf_op jit(solution)/shard_map/ppermute | solution.py:310
  78.3 2.6 %collective-permute-start.10 = (bf16[4,64,256]{2,1,0:T(8,128)(2,1)S(1)}, bf16[4,64,256]{2,1,0:T(8,128)(2,1)S(1)}, u32[]{:S(2)}, u32[]{:S(2)}) collective-permute-start(bf16[4,64,256]{2,1,0:T(8,128)(2,1)S(1)} %get-tuple-element.31), channel_id=1, source_target_pairs={{0,8},{4,12},{8,0},{12,4},{1,9},{5,13},{9,1},{13,5},{2,10},{6,14},... | collective-permute-start | bytes 393224 | tf_op jit(solution)/shard_map/ppermute | solution.py:310
  80.8 4.1 %collective-permute-start.11 = (bf16[4,64,256]{2,1,0:T(8,128)(2,1)S(1)}, bf16[4,64,256]{2,1,0:T(8,128)(2,1)S(1)}, u32[]{:S(2)}, u32[]{:S(2)}) collective-permute-start(bf16[4,64,256]{2,1,0:T(8,128)(2,1)S(1)} %get-tuple-element.32), channel_id=1, source_target_pairs={{0,12},{4,0},{8,4},{12,8},{1,13},{5,1},{9,5},{13,9},{2,14},{6,2},{... | collective-permute-start | bytes 393224 | tf_op jit(solution)/shard_map/ppermute | solution.py:310
  84.9 0.8 shard_map.95
  85.8 3.5 %all-to-all-start.2 = ((bf16[4,4,64,256]{3,2,1,0:T(8,128)(2,1)}), bf16[4,4,64,256]{3,2,1,0:T(8,128)(2,1)S(1)}, u32[]{:S(2)}, u32[]{:S(2)}) async-start(bf16[4,4,64,256]{3,2,1,0:T(8,128)(2,1)} %shard_map.95), calls=%async_computation.2 | async-start | bytes 1048576 | tf_op jit(solution)/shard_map/all_to_all | solution.py:322
  89.3 3.8 %collective-permute-done.10 = bf16[4,64,256]{2,1,0:T(8,128)(2,1)S(1)} collective-permute-done((bf16[4,64,256]{2,1,0:T(8,128)(2,1)S(1)}, bf16[4,64,256]{2,1,0:T(8,128)(2,1)S(1)}, u32[]{:S(2)}, u32[]{:S(2)}) %collective-permute-start.10) | collective-permute-done | bytes 131104 | tf_op jit(solution)/shard_map/ppermute | solution.py:310
  93.1 0.1 add_convert_fusion
  93.2 3.0 %all-to-all-done.2 = bf16[4,4,64,256]{3,2,1,0:T(8,128)(2,1)S(1)} async-done(((bf16[4,4,64,256]{3,2,1,0:T(8,128)(2,1)}), bf16[4,4,64,256]{3,2,1,0:T(8,128)(2,1)S(1)}, u32[]{:S(2)}, u32[]{:S(2)}) %all-to-all-start.2) | async-done | bytes 524320 | tf_op jit(solution)/shard_map/all_to_all | solution.py:322
  96.2 6.7 %collective-permute-start.12 = (bf16[1216,256]{1,0:T(8,128)(2,1)S(1)}, bf16[1216,256]{1,0:T(8,128)(2,1)S(1)}, u32[]{:S(2)}, u32[]{:S(2)}) collective-permute-start(bf16[1216,256]{1,0:T(8,128)(2,1)S(1)} %pad_maximum_fusion), channel_id=1, source_target_pairs={{0,16},{16,0},{1,17},{17,1},{2,18},{18,2},{3,19},{19,3},{4,20},{20... | collective-permute-start | bytes 1867784 | tf_op jit(solution)/shard_map/ppermute | solution.py:249
  102.9 1.0 shard_map.98.before
  103.9 0.6 collective-permute-done.12.x_ref
  104.6 1.1 %shard_map.99 = (f32[8,256,256]{2,1,0:T(8,128)}, bf16[2,64,256]{2,1,0:T(8,128)(2,1)}, bf16[2,64,256]{2,1,0:T(8,128)(2,1)}, bf16[2,64,256]{2,1,0:T(8,128)(2,1)}) custom-call(bf16[1216,256]{1,0:T(8,128)(2,1)S(1)} %collective-permute-done.12.x_ref, bf16[2,96,256]{2,1,0:T(8,128)(2,1)S(1)} %get-tuple-element.38.own_ref, ...), custom_call_target="tpu_custom_call", output_to_operand_aliasing={{0}: (2, {})} | custom-call | flops 262144 | bytes 2097152 | tf_op jit(solution)/shard_map/pallas_call | solution.py:232
  (26 shorter events, 0.2 us)
Async XLA Ops:
  0.6 9.8 %copy-start = (bf16[8,256,256]{2,1,0:T(8,128)(2,1)S(1)}, bf16[8,256,256]{2,1,0:T(8,128)(2,1)}, u32[]{:S(2)}) copy-start(bf16[8,256,256]{2,1,0:T(8,128)(2,1)} %param.9) | copy-start | bytes 3145732
  0.6 10.8 %copy-start.4 = (bf16[2,256,64]{1,2,0:T(8,128)(2,1)S(1)}, bf16[2,256,64]{1,2,0:T(8,128)(2,1)}, u32[]{:S(2)}) copy-start(bf16[2,256,64]{1,2,0:T(8,128)(2,1)} %param.8) | copy-start | bytes 196612
  0.7 10.8 %copy-start.5 = (bf16[2,256,64]{1,2,0:T(8,128)(2,1)S(1)}, bf16[2,256,64]{1,2,0:T(8,128)(2,1)}, u32[]{:S(2)}) copy-start(bf16[2,256,64]{1,2,0:T(8,128)(2,1)} %param.7) | copy-start | bytes 196612
  1.6 9.8 %collective-permute-start = (bf16[2,128,256]{2,1,0:T(8,128)(2,1)S(1)}, bf16[2,128,256]{2,1,0:T(8,128)(2,1)S(1)}, u32[]{:S(2)}, u32[]{:S(2)}) collective-permute-start(bf16[2,128,256]{2,1,0:T(8,128)(2,1)S(1)} %pad_maximum_fusion.2), channel_id=1, source_target_pairs={{0,16},{16,0},{1,17},{17,1},{2,18},{18,2},{3,19},{19,3},{4,20},{20... | collective-permute-start | bytes 393224 | tf_op jit(solution)/shard_map/ppermute | solution.py:249
  10.5 12.1 %copy-start.1 = (bf16[2,256,64]{1,2,0:T(8,128)(2,1)S(1)}, bf16[2,256,64]{1,2,0:T(8,128)(2,1)}, u32[]{:S(2)}) copy-start(bf16[2,256,64]{1,2,0:T(8,128)(2,1)} %param.6) | copy-start | bytes 196612
  10.5 12.1 %copy-start.2 = (bf16[2,256,64]{1,2,0:T(8,128)(2,1)S(1)}, bf16[2,256,64]{1,2,0:T(8,128)(2,1)}, u32[]{:S(2)}) copy-start(bf16[2,256,64]{1,2,0:T(8,128)(2,1)} %param.11) | copy-start | bytes 196612
  10.5 12.1 %copy-start.3 = (bf16[2,256,64]{1,2,0:T(8,128)(2,1)S(1)}, bf16[2,256,64]{1,2,0:T(8,128)(2,1)}, u32[]{:S(2)}) copy-start(bf16[2,256,64]{1,2,0:T(8,128)(2,1)} %param.10) | copy-start | bytes 196612
  11.4 8.1 %collective-permute-start.2 = (bf16[4,128,256]{2,1,0:T(8,128)(2,1)S(1)}, bf16[4,128,256]{2,1,0:T(8,128)(2,1)S(1)}, u32[]{:S(2)}, u32[]{:S(2)}) collective-permute-start(bf16[4,128,256]{2,1,0:T(8,128)(2,1)S(1)} %pad_maximum_fusion.1), channel_id=1, source_target_pairs={{0,4},{1,8},{2,12},{3,0},{4,9},{5,13},{6,1},{7,5},{8,14},{9,2},{10... | collective-permute-start | bytes 786440 | tf_op jit(solution)/shard_map/ppermute | solution.py:302
  13.4 9.2 %collective-permute-start.1 = (bf16[4,128,256]{2,1,0:T(8,128)(2,1)S(1)}, bf16[4,128,256]{2,1,0:T(8,128)(2,1)S(1)}, u32[]{:S(2)}, u32[]{:S(2)}) collective-permute-start(bf16[4,128,256]{2,1,0:T(8,128)(2,1)S(1)} %pad_maximum_fusion.1), channel_id=1, source_target_pairs={{0,0},{1,4},{2,8},{3,12},{4,5},{5,9},{6,13},{7,1},{8,10},{9,14},{1... | collective-permute-start | bytes 786440 | tf_op jit(solution)/shard_map/ppermute | solution.py:302
  15.3 11.8 %all-to-all-start = ((bf16[4,256,256]{2,1,0:T(8,128)(2,1)}), bf16[4,256,256]{2,1,0:T(8,128)(2,1)S(1)}, u32[]{:S(2)}, u32[]{:S(2)}) async-start(bf16[4,256,256]{2,1,0:T(8,128)(2,1)} %dynamic-slice_bitcast_fusion), calls=%async_computation | async-start | bytes 1048576 | tf_op jit(solution)/shard_map/all_to_all | solution.py:303
  22.7 4.7 %collective-permute-start.3 = (bf16[704,256]{1,0:T(8,128)(2,1)S(1)}, bf16[704,256]{1,0:T(8,128)(2,1)S(1)}, u32[]{:S(2)}, u32[]{:S(2)}) collective-permute-start(bf16[704,256]{1,0:T(8,128)(2,1)S(1)} %shard_map.93), channel_id=1, source_target_pairs={{0,16},{16,0},{1,17},{17,1},{2,18},{18,2},{3,19},{19,3},{4,20},{20... | collective-permute-start | bytes 1081352 | tf_op jit(solution)/shard_map/ppermute | solution.py:249
  49.4 21.0 %collective-permute-start.4 = (bf16[4,64,256]{2,1,0:T(8,128)(2,1)S(1)}, bf16[4,64,256]{2,1,0:T(8,128)(2,1)S(1)}, u32[]{:S(2)}, u32[]{:S(2)}) collective-permute-start(bf16[4,64,256]{2,1,0:T(8,128)(2,1)S(1)} %reduce_sum.12.after), channel_id=1, source_target_pairs={{0,128},{128,0},{256,384},{384,256},{16,400},{144,272},{272,144},{... | collective-permute-start | bytes 393224 | tf_op jit(solution)/shard_map/ppermute | solution.py:280
  61.4 14.3 %collective-permute-start.6 = (bf16[4,64,256]{2,1,0:T(8,128)(2,1)S(1)}, bf16[4,64,256]{2,1,0:T(8,128)(2,1)S(1)}, u32[]{:S(2)}, u32[]{:S(2)}) collective-permute-start(bf16[4,64,256]{2,1,0:T(8,128)(2,1)S(1)} %get-tuple-element.26), channel_id=1, source_target_pairs={{0,1},{1,2},{2,3},{3,0},{4,5},{5,6},{6,7},{7,4},{8,9},{9,10},{10,1... | collective-permute-start | bytes 393224 | tf_op jit(solution)/shard_map/ppermute | solution.py:310
  63.8 12.0 %collective-permute-start.7 = (bf16[4,64,256]{2,1,0:T(8,128)(2,1)S(1)}, bf16[4,64,256]{2,1,0:T(8,128)(2,1)S(1)}, u32[]{:S(2)}, u32[]{:S(2)}) collective-permute-start(bf16[4,64,256]{2,1,0:T(8,128)(2,1)S(1)} %get-tuple-element.27), channel_id=1, source_target_pairs={{0,2},{1,3},{2,0},{3,1},{4,6},{5,7},{6,4},{7,5},{8,10},{9,11},{10,... | collective-permute-start | bytes 393224 | tf_op jit(solution)/shard_map/ppermute | solution.py:310
  67.4 8.4 %collective-permute-start.8 = (bf16[4,64,256]{2,1,0:T(8,128)(2,1)S(1)}, bf16[4,64,256]{2,1,0:T(8,128)(2,1)S(1)}, u32[]{:S(2)}, u32[]{:S(2)}) collective-permute-start(bf16[4,64,256]{2,1,0:T(8,128)(2,1)S(1)} %get-tuple-element.28), channel_id=1, source_target_pairs={{0,3},{1,0},{2,1},{3,2},{4,7},{5,4},{6,5},{7,6},{8,11},{9,8},{10,9... | collective-permute-start | bytes 393224 | tf_op jit(solution)/shard_map/ppermute | solution.py:310
  70.5 14.4 %collective-permute-start.5 = (bf16[4,64,256]{2,1,0:T(8,128)(2,1)S(1)}, bf16[4,64,256]{2,1,0:T(8,128)(2,1)S(1)}, u32[]{:S(2)}, u32[]{:S(2)}) collective-permute-start(bf16[4,64,256]{2,1,0:T(8,128)(2,1)S(1)} %add_convert_fusion.1.a_ref.after), channel_id=1, source_target_pairs={{0,384},{128,256},{256,128},{384,0},{16,144},{144,16},{272,400},{4... | collective-permute-start | bytes 393224 | tf_op jit(solution)/shard_map/ppermute | solution.py:280
  75.9 13.4 %collective-permute-start.9 = (bf16[4,64,256]{2,1,0:T(8,128)(2,1)S(1)}, bf16[4,64,256]{2,1,0:T(8,128)(2,1)S(1)}, u32[]{:S(2)}, u32[]{:S(2)}) collective-permute-start(bf16[4,64,256]{2,1,0:T(8,128)(2,1)S(1)} %get-tuple-element.30), channel_id=1, source_target_pairs={{0,4},{4,8},{8,12},{12,0},{1,5},{5,9},{9,13},{13,1},{2,6},{6,10},{... | collective-permute-start | bytes 393224 | tf_op jit(solution)/shard_map/ppermute | solution.py:310
  78.3 14.8 %collective-permute-start.10 = (bf16[4,64,256]{2,1,0:T(8,128)(2,1)S(1)}, bf16[4,64,256]{2,1,0:T(8,128)(2,1)S(1)}, u32[]{:S(2)}, u32[]{:S(2)}) collective-permute-start(bf16[4,64,256]{2,1,0:T(8,128)(2,1)S(1)} %get-tuple-element.31), channel_id=1, source_target_pairs={{0,8},{4,12},{8,0},{12,4},{1,9},{5,13},{9,1},{13,5},{2,10},{6,14},... | collective-permute-start | bytes 393224 | tf_op jit(solution)/shard_map/ppermute | solution.py:310
  80.8 12.2 %collective-permute-start.11 = (bf16[4,64,256]{2,1,0:T(8,128)(2,1)S(1)}, bf16[4,64,256]{2,1,0:T(8,128)(2,1)S(1)}, u32[]{:S(2)}, u32[]{:S(2)}) collective-permute-start(bf16[4,64,256]{2,1,0:T(8,128)(2,1)S(1)} %get-tuple-element.32), channel_id=1, source_target_pairs={{0,12},{4,0},{8,4},{12,8},{1,13},{5,1},{9,5},{13,9},{2,14},{6,2},{... | collective-permute-start | bytes 393224 | tf_op jit(solution)/shard_map/ppermute | solution.py:310
  85.8 10.4 %all-to-all-start.2 = ((bf16[4,4,64,256]{3,2,1,0:T(8,128)(2,1)}), bf16[4,4,64,256]{3,2,1,0:T(8,128)(2,1)S(1)}, u32[]{:S(2)}, u32[]{:S(2)}) async-start(bf16[4,4,64,256]{3,2,1,0:T(8,128)(2,1)} %shard_map.95), calls=%async_computation.2 | async-start | bytes 1048576 | tf_op jit(solution)/shard_map/all_to_all | solution.py:322
  96.2 8.4 %collective-permute-start.12 = (bf16[1216,256]{1,0:T(8,128)(2,1)S(1)}, bf16[1216,256]{1,0:T(8,128)(2,1)S(1)}, u32[]{:S(2)}, u32[]{:S(2)}) collective-permute-start(bf16[1216,256]{1,0:T(8,128)(2,1)S(1)} %pad_maximum_fusion), channel_id=1, source_target_pairs={{0,16},{16,0},{1,17},{17,1},{2,18},{18,2},{3,19},{19,3},{4,20},{20... | collective-permute-start | bytes 1867784 | tf_op jit(solution)/shard_map/ppermute | solution.py:249
